TPU v7x, 32 devices: a whole 2x2x4 slice. The times are simulated.
32 devices in a mesh: rows: 8 (over z, x), seq: 4 (over y, core).
Axes of the slice: x: 2, y: 2, z: 4, core: 2. Of those that a mesh axis runs over, the one named last changes fastest.
Arguments:
- frames_in: bfloat16 [16, 4096, 512], P('rows', 'seq'), may hold values from -6 to 6
- lengths: int32 [16, 4], P('rows'), may hold values from 1 to 2048, 4096 in all within a row
- bw_ids: int32 [16, 4], P('rows'), may hold values from 0 to 3
- owner_list: int32 [137], replicated, may hold values from 0 to 7, as said below
- master: float32 [216, 32, 512], P('rows')
- moment1: float32 [216, 32, 512], P('rows')
- moment2: float32 [216, 32, 512], P('rows'), as said below
- wave_grad: bfloat16 [16, 1310720], P('rows', 'seq'), may hold values from -6 to 6
Outputs:
- waveform: float32 [16, 1310720], P('rows', 'seq')
- input_grad: float32 [16, 4096, 512], P('rows', 'seq')
- new_master: float32 [216, 32, 512], P('rows')
- new_moment1: float32 [216, 32, 512], P('rows')
- new_moment2: float32 [216, 32, 512], P('rows')
Inputs may be any that keep to these rules, and one draw needn't show every extreme that they name: `owner_list`: no index along rows owns more than 27 buckets, and some index owns exactly 27. `moment2`: every entry is positive.
All inputs are finite; a program needn't handle non-finite values.
Results may differ from a plain program's by a relative error of at most 0.012.
The roundings to bfloat16 on the way count: a program that leaves them out, or rounds other values in their place, can miss the bound.
Values may be sent and summed in bfloat16 or wider, within the bound.
No kernel may reach another device: no remote copies, remote signals or barrier semaphores. Data moves between devices by JAX's collectives and lax.ppermute only.
A program may use at most 192 MiB of HBM per device.

v0:
```python
import math

import jax
import jax.numpy as jnp
from jax import lax
from jax.sharding import PartitionSpec as P

FF = 1536
NFFT = 1280
HOP = 320
NBW = 4
KW = 7
UTT = 4
BR = 32
STEP_COUNT = 6
BINS = 641
NOUT = 1282
VROWS = 20
IN_ROWS = 3
HEAD_ROWS = 3
PR = 4380
NB = 137


NORM_EPS = 1e-06
ENV_FLOOR = 0.5
BETA_ONE = 0.8
BETA_TWO = 0.9
LEARN_RATE = 0.04
WEIGHT_DECAY = 0.01
ADAM_EPS = 1e-08


def padded(block, sides, width):
    for axis, dim in sides:
        count = lax.axis_size(axis)
        forward = [(i, i + 1) for i in range(count - 1)]
        backward = [(target, source) for source, target in forward]
        low = lax.ppermute(
            lax.slice_in_dim(block, block.shape[dim] - width, None, axis=dim), axis, forward
        )
        high = lax.ppermute(lax.slice_in_dim(block, 0, width, axis=dim), axis, backward)
        block = jnp.concatenate([low, block, high], axis=dim)
    return block


def from_behind(block, axis, distance):
    devices = range(lax.axis_size(axis))
    route = [(i - distance, i) for i in devices if i - distance in devices]
    return lax.ppermute(block, axis, route)


def slot_maps(owner_list, owner_count, slot_count):
    bucket_count = owner_list.shape[0]
    bucket_index = jnp.arange(bucket_count, dtype=jnp.int32)
    same_owner = owner_list[None, :] == owner_list[:, None]
    before = bucket_index[None, :] < bucket_index[:, None]
    slot_rank = jnp.sum((same_owner & before).astype(jnp.int32), axis=1)
    bucket_place = owner_list * slot_count + slot_rank
    targets = jnp.arange(owner_count * slot_count, dtype=jnp.int32)
    slot_match = bucket_place[None, :] == targets[:, None]
    found_bucket = jnp.sum(slot_match.astype(jnp.int32) * bucket_index[None, :], axis=1)
    source = jnp.where(jnp.any(slot_match, axis=1), found_bucket, bucket_count)
    return (bucket_place, source)


def synthesis_table():
    bin_index = jnp.arange(BINS, dtype=jnp.int32)[:, None]
    tap_index = jnp.arange(NFFT, dtype=jnp.int32)[None, :]
    turns = bin_index * tap_index % NFFT
    angle = turns.astype(jnp.float32) * (2.0 * math.pi / NFFT)
    edge_bin = (bin_index == 0) | (bin_index == NFFT // 2)
    factor = jnp.where(edge_bin, 1.0, 2.0).astype(jnp.float32) / NFFT
    return jnp.concatenate([factor * jnp.cos(angle), -factor * jnp.sin(angle)], axis=0)


def hann_window():
    angle = jnp.arange(NFFT, dtype=jnp.int32).astype(jnp.float32) * (2.0 * math.pi / NFFT)
    return 0.5 - 0.5 * jnp.cos(angle)


def segment_ids(lengths, first_index, span):
    starts = jnp.cumsum(lengths, axis=1) - lengths
    frame_index = first_index + jnp.arange(span, dtype=jnp.int32)
    return jnp.sum((starts[:, None, :] <= frame_index[None, :, None]).astype(jnp.int32), axis=2) - 1


def layer_norm(values):
    row_mean = jnp.mean(values, axis=-1, keepdims=True)
    centered = values - row_mean
    return centered * lax.rsqrt(jnp.mean(centered * centered, axis=-1, keepdims=True) + NORM_EPS)


def ada_norm(values, scale_rows, shift_rows):
    return layer_norm(values) * scale_rows + shift_rows


def final_norm(values, norm_gain, norm_bias):
    return layer_norm(values) * norm_gain[None, :] + norm_bias[None, :]


def exact_gelu(values):
    return jax.nn.gelu(values, approximate=False)


def contract(left_side, right_side, left_dim, right_dim):
    return lax.dot_general(
        left_side,
        right_side,
        (((left_dim,), (right_dim,)), ((), ())),
        preferred_element_type=jnp.float32,
    )


def local(frames_in, lengths, bw_ids, owner_list, master, moment1, moment2, wave_grad):
    rows_here, frames_here, channels = frames_in.shape
    slot_count = master.shape[0]
    frame_count = rows_here * frames_here
    lap_count = NFFT // HOP
    rim_width = (KW - 1) // 2
    margin = max(rim_width, lap_count - 1)
    bucket_place, source = slot_maps(owner_list, lax.axis_size("rows"), slot_count)
    gathered = lax.all_gather(master.astype(jnp.bfloat16), "rows", axis=0, tiled=True)
    buckets = jnp.take(gathered, bucket_place, axis=0)
    weight_table = buckets.reshape(-1, channels)[:PR]
    w_in = weight_table[:FF]
    w_out = weight_table[FF : 2 * FF]
    w_head = weight_table[2 * FF : 2 * FF + NOUT]
    row_start = 2 * FF + NOUT
    channel_rows = weight_table[row_start : row_start + VROWS].astype(jnp.float32)
    row_start = row_start + VROWS
    bias_in = weight_table[row_start : row_start + IN_ROWS].reshape(-1).astype(jnp.float32)
    row_start = row_start + IN_ROWS
    bias_head = (
        weight_table[row_start : row_start + HEAD_ROWS].reshape(-1)[:NOUT].astype(jnp.float32)
    )
    conv_weight = channel_rows[:KW]
    conv_bias = channel_rows[KW]
    ada_scale = channel_rows[KW + 1 : KW + 1 + NBW]
    ada_shift = channel_rows[KW + 1 + NBW : KW + 1 + 2 * NBW]
    vec_base = KW + 1 + 2 * NBW
    bias_out = channel_rows[vec_base]
    layer_scale = channel_rows[vec_base + 1]
    norm_gain = channel_rows[vec_base + 2]
    norm_bias = channel_rows[vec_base + 3]
    first_index = lax.axis_index("seq") * frames_here - margin
    segment = segment_ids(lengths, first_index, frames_here + 2 * margin)
    own_segment = segment[:, margin : margin + frames_here]
    halo_frames = padded(frames_in, (("seq", 1),), rim_width)
    wide_frames = halo_frames.astype(jnp.float32)
    conv_keep = []
    conv_out = jnp.zeros((rows_here, frames_here, channels), jnp.float32) + conv_bias
    for tap_index in range(KW):
        lower = margin - rim_width + tap_index
        keep = (segment[:, lower : lower + frames_here] == own_segment).astype(jnp.float32)[
            :, :, None
        ]
        conv_keep.append(keep)
        conv_out = (
            conv_out
            + keep * wide_frames[:, tap_index : tap_index + frames_here] * conv_weight[tap_index]
        )
    conv_out = conv_out.reshape(frame_count, channels)
    utt_pick = (own_segment[:, :, None] == jnp.arange(UTT, dtype=jnp.int32)[None, None, :]).astype(
        jnp.int32
    )
    frame_ids = jnp.sum(utt_pick * bw_ids[:, None, :], axis=2).reshape(frame_count)
    bw_onehot = (frame_ids[:, None] == jnp.arange(NBW, dtype=jnp.int32)[None, :]).astype(
        jnp.float32
    )
    scale_rows = jnp.dot(bw_onehot, ada_scale, precision=lax.Precision.HIGHEST)
    shift_rows = jnp.dot(bw_onehot, ada_shift, precision=lax.Precision.HIGHEST)
    ada_value, ada_back = jax.vjp(ada_norm, conv_out, scale_rows, shift_rows)
    ada_low = ada_value.astype(jnp.bfloat16)
    hidden_pre = contract(ada_low, w_in, 1, 1) + bias_in[None, :]
    act_value, gelu_back = jax.vjp(exact_gelu, hidden_pre)
    act_low = act_value.astype(jnp.bfloat16)
    branch = contract(act_low, w_out, 1, 0) + bias_out[None, :]
    frames_flat = frames_in.reshape(frame_count, channels).astype(jnp.float32)
    residual = frames_flat + layer_scale[None, :] * branch
    normed_value, final_back = jax.vjp(final_norm, residual, norm_gain, norm_bias)
    normed_low = normed_value.astype(jnp.bfloat16)
    head_out = contract(normed_low, w_head, 1, 1) + bias_head[None, :]
    magnitude = jnp.exp(head_out[:, :BINS])
    phase_angle = head_out[:, BINS:]
    real_part = magnitude * jnp.cos(phase_angle)
    imag_part = magnitude * jnp.sin(phase_angle)
    spectrum_low = jnp.concatenate([real_part, imag_part], axis=1).astype(jnp.bfloat16)
    synthesis = synthesis_table().astype(jnp.bfloat16)
    signal = contract(spectrum_low, synthesis, 1, 0)
    window_rows = hann_window().reshape(lap_count, HOP)
    pieces = signal.reshape(rows_here, frames_here, lap_count, HOP) * window_rows[None, None, :, :]
    lap_keep = []
    numerator = jnp.zeros((rows_here, frames_here + lap_count - 1, HOP), jnp.float32)
    envelope = jnp.zeros((rows_here, frames_here, HOP), jnp.float32)
    for lap_index in range(lap_count):
        ahead = margin + lap_index
        keep = (segment[:, ahead : ahead + frames_here] == own_segment).astype(jnp.float32)[
            :, :, None
        ]
        lap_keep.append(keep)
        numerator = numerator + jnp.pad(
            keep * pieces[:, :, lap_index], ((0, 0), (lap_index, lap_count - 1 - lap_index), (0, 0))
        )
        behind = margin - lap_index
        back_keep = (segment[:, behind : behind + frames_here] == own_segment).astype(jnp.float32)[
            :, :, None
        ]
        envelope = envelope + back_keep * (window_rows[lap_index] ** 2)[None, None, :]
    arrived = from_behind(numerator[:, frames_here:], "seq", 1)
    numerator = numerator[:, :frames_here] + jnp.pad(
        arrived, ((0, 0), (0, frames_here - lap_count + 1), (0, 0))
    )
    denominator = jnp.maximum(envelope, ENV_FLOOR)
    waveform = (numerator / denominator).reshape(rows_here, frames_here * HOP)
    scaled = wave_grad.astype(jnp.float32).reshape(rows_here, frames_here, HOP) / denominator
    later_rows = from_behind(scaled[:, : lap_count - 1], "seq", -1)
    reach_rows = jnp.concatenate([scaled, later_rows], axis=1)
    signal_grad = jnp.stack(
        [
            lap_keep[lap_index]
            * window_rows[lap_index][None, None, :]
            * reach_rows[:, lap_index : lap_index + frames_here]
            for lap_index in range(lap_count)
        ],
        axis=2,
    )
    signal_low = signal_grad.reshape(frame_count, NFFT).astype(jnp.bfloat16)
    spec_grad = contract(signal_low, synthesis, 1, 1)
    real_grad = spec_grad[:, :BINS]
    imag_grad = spec_grad[:, BINS:]
    head_grad = jnp.concatenate(
        [
            real_grad * real_part + imag_grad * imag_part,
            imag_grad * real_part - real_grad * imag_part,
        ],
        axis=1,
    ).astype(jnp.bfloat16)
    grad_w_head = contract(head_grad, normed_low, 0, 0)
    grad_b_head = jnp.sum(head_grad, axis=0, dtype=jnp.float32)
    normed_grad = contract(head_grad, w_head, 1, 0)
    residual_grad, grad_gain, grad_bias = final_back(normed_grad)
    branch_low = (layer_scale[None, :] * residual_grad).astype(jnp.bfloat16)
    grad_layer_scale = jnp.sum(residual_grad * branch, axis=0)
    grad_w_out = contract(act_low, branch_low, 0, 0)
    grad_b_out = jnp.sum(branch_low, axis=0, dtype=jnp.float32)
    act_grad = contract(branch_low, w_out, 1, 1)
    pre_low = gelu_back(act_grad)[0].astype(jnp.bfloat16)
    grad_w_in = contract(pre_low, ada_low, 0, 0)
    grad_b_in = jnp.sum(pre_low, axis=0, dtype=jnp.float32)
    ada_grad = contract(pre_low, w_in, 1, 0)
    conv_grad, scale_grad_rows, shift_grad_rows = ada_back(ada_grad)
    grad_scales = lax.dot_general(
        bw_onehot, scale_grad_rows, (((0,), (0,)), ((), ())), precision=lax.Precision.HIGHEST
    )
    grad_shifts = lax.dot_general(
        bw_onehot, shift_grad_rows, (((0,), (0,)), ((), ())), precision=lax.Precision.HIGHEST
    )
    conv_rows = conv_grad.reshape(rows_here, frames_here, channels)
    grad_conv_b = jnp.sum(conv_grad, axis=0)
    grad_conv_w = jnp.stack(
        [
            jnp.sum(
                conv_keep[tap_index]
                * conv_rows
                * wide_frames[:, tap_index : tap_index + frames_here],
                axis=(0, 1),
            )
            for tap_index in range(KW)
        ],
        axis=0,
    )
    halo_grad = padded(conv_rows, (("seq", 1),), rim_width)
    input_grad = residual_grad.reshape(rows_here, frames_here, channels)
    for tap_index in range(KW):
        lower = margin + rim_width - tap_index
        keep = (segment[:, lower : lower + frames_here] == own_segment).astype(jnp.float32)[
            :, :, None
        ]
        begin = 2 * rim_width - tap_index
        input_grad = (
            input_grad + conv_weight[tap_index] * keep * halo_grad[:, begin : begin + frames_here]
        )
    vec_grads = jnp.concatenate(
        [
            grad_conv_w,
            grad_conv_b[None, :],
            grad_scales,
            grad_shifts,
            jnp.stack([grad_b_out, grad_layer_scale, grad_gain, grad_bias], axis=0),
        ],
        axis=0,
    )
    in_rows = grad_b_in.reshape(IN_ROWS, channels)
    head_rows = jnp.pad(grad_b_head, (0, HEAD_ROWS * channels - NOUT)).reshape(HEAD_ROWS, channels)
    grad_table = jnp.concatenate(
        [grad_w_in, grad_w_out, grad_w_head, vec_grads, in_rows, head_rows], axis=0
    )
    grad_buckets = jnp.pad(grad_table, ((0, NB * BR - PR), (0, 0))).reshape(NB, BR, channels)
    empty_bucket = jnp.zeros((1, BR, channels), jnp.float32)
    summed = lax.psum(grad_buckets, ("rows", "seq"))
    extended = jnp.concatenate([summed, empty_bucket], axis=0)
    my_sources = lax.dynamic_slice_in_dim(source, lax.axis_index("rows") * slot_count, slot_count)
    reduced = jnp.take(extended, my_sources, axis=0)
    first_new = BETA_ONE * moment1 + (1.0 - BETA_ONE) * reduced
    second_new = BETA_TWO * moment2 + (1.0 - BETA_TWO) * reduced * reduced
    first_fix = 1.0 - BETA_ONE**STEP_COUNT
    second_fix = 1.0 - BETA_TWO**STEP_COUNT
    master_new = master - LEARN_RATE * (
        first_new / first_fix / (jnp.sqrt(second_new / second_fix) + ADAM_EPS)
        + WEIGHT_DECAY * master
    )
    return (waveform, input_grad, master_new, first_new, second_new)


def solution(mesh):
    in_specs = (
        P("rows", "seq", None),
        P("rows", None),
        P("rows", None),
        P(),
        P("rows", None, None),
        P("rows", None, None),
        P("rows", None, None),
        P("rows", "seq"),
    )
    out_specs = (
        P("rows", "seq"),
        P("rows", "seq", None),
        P("rows", None, None),
        P("rows", None, None),
        P("rows", None, None),
    )
    return jax.shard_map(local, mesh=mesh, in_specs=in_specs, out_specs=out_specs, check_vma=False)
```

profile of v0, /device:TPU:0, one launch (start us, length us, event | category | flops | bytes accessed | tf_op | source)
XLA Modules:
  0.0 546.3 jit_solution(15566940357598605938)
XLA Ops:
  7.2 2.5 convert_element_type.160
  15.8 2.7 reshape.271
  21.1 2.9 fusion.48
  26.2 2.7 reshape.270
  33.0 2.8 fusion.47
  35.9 15.2 %multiply_convert_fusion.2 = (bf16[641,1280]{1,0:T(8,128)(2,1)}, bf16[641,1280]{1,0:T(8,128)(2,1)}) fusion(f32[641]{0:T(1024)S(1)} %fusion.74, f32[641]{0:T(1024)S(1)} %select_multiply_fusion), kind=kLoop, calls=%fused_computation.89 | loop fusion | flops 10666240 | bytes 3287048 | tf_op jit(solution)/shard_map/convert.12
  51.9 9.4 %concatenate.35 = bf16[2,1030,512]{2,1,0:T(8,128)(2,1)S(1)} concatenate(bf16[2,3,512]{2,1,0:T(4,128)(2,1)S(1)} %collective-permute-done, bf16[2,1024,512]{2,1,0:T(8,128)(2,1)} %param.8, bf16[2,3,512]{2,1,0:T(4,128)(2,1)S(1)} %collective-permute-done.1), dimensions={1} | concatenate | bytes 4218880 | tf_op jit(solution)/shard_map/concatenate | solution.py:43
  61.3 2.6 convert_element_type.164
  63.8 4.7 fusion.55
  68.5 3.2 pad_maximum_fusion.1
  71.7 10.2 %copy.40 = bf16[2,1024,4,320]{1,0,3,2:T(2,128)(2,1)} copy(bf16[2,1024,4,320]{1,3,0,2:T(8,128)(2,1)} %pad_maximum_fusion.1) | data formatting | bytes 10485760 | tf_op jit(solution)/shard_map/stack | solution.py:219
  81.9 4.8 copy.45
  86.7 9.7 %fusion.49 = f32[2048,1282]{0,1:T(8,128)} fusion(bf16[2048,1280]{0,1:T(8,128)(2,1)S(1)} %bitcast.122, bf16[641,1280]{1,0:T(8,128)(2,1)S(1)} %copy-done.20, bf16[641,1280]{1,0:T(8,128)(2,1)S(1)} %copy-done.21), kind=kOutput, calls=%fused_computation.122 | convolution fusion | flops 6727936000 | bytes 19026944 | tf_op jit(solution)/shard_map/dot_general | solution.py:107
  96.5 25.9 %all-gather.2.cloned.1.call-done = bf16[216,32,512]{2,1,0:T(8,128)(2,1)} async-done(((bf16[27,32,512]{2,1,0:T(8,128)(2,1)}), bf16[216,32,512]{2,1,0:T(8,128)(2,1)}) %all-gather.2.cloned.1.call-update) | async-done | bytes 7077904 | tf_op jit(solution)/shard_map/all_gather | solution.py:123
  122.3 10.9 %gather_fusion = bf16[137,32,512]{2,1,0:T(8,128)(2,1)} fusion(bf16[216,32,512]{2,1,0:T(8,128)(2,1)} %all-gather.2.cloned.1.call-done, s32[1024]{0:T(1024)S(1)} %pad_clamp_fusion.1), kind=kCustom, calls=%fused_computation | custom fusion | bytes 8978980 | tf_op jit(solution)/shard_map/jit(_take)/gather | solution.py:124
  133.3 4.1 bitcast_select_fusion
  137.5 2.6 broadcast_select_fusion
  140.2 2.4 slice-done
  142.7 6.1 %fusion.88 = (f32[2,1024]{1,0:T(2,128)S(1)}, f32[2,1024,512]{2,1,0:T(8,128)S(1)}) fusion(f32[512]{0:T(512)S(1)} %bitcast.134, f32[2,1030,512]{2,1,0:T(8,128)S(1)} %bitcast.114, f32[2,1024]{1,0:T(2,128)S(1)} %get-tuple-element.69, f32[512]{0:T(512)S(1)} %bitcast.136, f32[2,1024]{1,0:T(2,128)S(1)} %get-tuple-element.70, f32[512]{0:T(512)S(1)} %bitcast.138, ...), kind=kLoop, calls=%fused_computation.211 | loop fusion | flops 22018048 | bytes 33628160 | tf_op jit(solution)/shard_map/jvp()/reduce_sum | solution.py:89
  152.1 2.5 fusion.60
  157.8 4.0 add_convert_fusion.3
  161.8 31.4 %multiply_convert_fusion = (bf16[2048,1536]{1,0:T(8,128)(2,1)S(1)}, f32[2048,1536]{1,0:T(8,128)}, f32[2048,1536]{1,0:T(8,128)}) fusion(f32[1536]{0:T(1024)S(1)} %reshape.280, bf16[2048,512]{1,0:T(8,128)(2,1)S(1)} %add_convert_fusion.3, bf16[1536,512]{1,0:T(8,128)(2,1)S(1)} %bitcast.123), kind=kOutput, calls=%fused_computation.6 | convolution fusion | flops 3428843520 | bytes 35133440 | tf_op jit(solution)/shard_map/dot_general | solution.py:107
  193.2 5.6 %fusion.86 = (f32[2048]{0:T(1024)S(1)}, f32[2048,512]{1,0:T(8,128)S(1)}, f32[2048,512]{1,0:T(8,128)}) fusion(f32[512]{0:T(512)S(1)} %bitcast.159, f32[512]{0:T(512)S(1)} %bitcast.157, bf16[2,1024,512]{2,1,0:T(8,128)(2,1)S(1)} %copy-done.16, bf16[2048,1536]{1,0:T(8,128)(2,1)S(1)} %get-tuple-element.32, bf16[1536,512]{1,0:T(8,128)(2,1)S(1)} %bitcast.125), kind=kOutput, calls=%fused_computation.210 | convolution fusion | flops 3226466304 | bytes 18362368 | tf_op jit(solution)/shard_map/dot_general | solution.py:107
  201.6 5.8 %convolution_add_fusion = f32[2048,1282]{0,1:T(8,128)S(1)} fusion(f32[1282]{0:T(1024)S(1)} %slice_convert_fusion.1, bf16[4384,512]{1,0:T(8,128)(2,1)} %copy-done.13, f32[2048,512]{1,0:T(8,128)} %copy-done.8, f32[512]{0:T(512)S(1)} %bitcast.169, f32[512]{0:T(512)S(1)} %bitcast.163, f32[2048]{0:T(1024)S(1)} %fusion.70, f32[2048]{0:T(1024)S(1)} %broadcast_multiply_fusion), kind=kOutput, calls=%fused_computation.22 | convolution fusion | flops 2696417280 | bytes 16040968 | tf_op jit(solution)/shard_map/dot_general | solution.py:107
  207.5 24.2 %add_convert_fusion.1 = (bf16[2048,641]{0,1:T(8,128)(2,1)S(1)}, bf16[2048,641]{0,1:T(8,128)(2,1)S(1)}, bf16[2048,641]{0,1:T(8,128)(2,1)}, bf16[2048,641]{0,1:T(8,128)(2,1)}) fusion(f32[2048,1282]{0,1:T(8,128)} %fusion.49, f32[2048,1282]{0,1:T(8,128)S(1)} %convolution_add_fusion), kind=kLoop, calls=%fused_computation.31 | loop fusion | flops 15753216 | bytes 31506432 | tf_op jit(solution)/shard_map/convert.2
  233.9 6.2 %multiply_reduce_fusion = (f32[512]{0:T(512)S(1)}, f32[2048]{0:T(1024)S(1)}, f32[512]{0:T(512)S(1)}, f32[2048,512]{1,0:T(8,128)S(1)}) fusion(f32[2048,512]{1,0:T(8,128)S(1)} %copy-done.9, f32[2048]{0:T(1024)S(1)} %fusion.70, f32[2048]{0:T(1024)S(1)} %broadcast_multiply_fusion, f32[512]{0:T(512)S(1)} %bitcast.164, bf16[4384,512]{1,0:T(8,128)(2,1)} %copy-done.13, ...), kind=kOutput, calls=%fused_computation.64 | convolution fusion | flops 2707436544 | bytes 14989312 | tf_op jit(solution)/shard_map/dot_general | solution.py:107
  240.1 4.6 fusion.52
  249.5 3.6 fusion.95
  253.1 16.6 %convert_reduce_fusion = (f32[1536]{0:T(1024)S(1)}, bf16[2048,1536]{1,0:T(8,128)(2,1)}) fusion(f32[2048,1536]{1,0:T(8,128)} %get-tuple-element.33, bf16[2048,512]{1,0:T(8,128)(2,1)} %copy-done.19, bf16[1536,512]{1,0:T(8,128)(2,1)} %bitcast.126, f32[2048,1536]{1,0:T(8,128)} %get-tuple-element.84, f32[1536]{0:T(1024)S(1)} %reshape.280), kind=kOutput, calls=%fused_computation.4 | convolution fusion | flops 3274701312 | bytes 35139584 | tf_op jit(solution)/shard_map/dot_general | solution.py:107
  269.7 6.7 %multiply_reduce_fusion.9 = (f32[2048]{0:T(1024)S(1)}, f32[2048,512]{1,0:T(8,128)S(1)}) fusion(f32[2048,512]{1,0:T(8,128)S(1)} %copy-done.4, f32[2048,512]{1,0:T(8,128)S(1)} %copy-done.6, bf16[2048,1536]{1,0:T(8,128)(2,1)} %get-tuple-element.90, bf16[1536,512]{1,0:T(8,128)(2,1)} %bitcast.124), kind=kOutput, calls=%fused_computation.76 | convolution fusion | flops 3224369152 | bytes 20455424 | tf_op jit(solution)/shard_map/dot_general | solution.py:107
  276.4 5.1 fusion.94
  285.5 5.5 %fusion.84 = (f32[2048]{0:T(1024)S(1)}, f32[2048,512]{1,0:T(8,128)S(1)}) fusion(f32[2048]{0:T(1024)S(1)} %fusion.69, f32[2048]{0:T(1024)S(1)} %copy-done.39, f32[2048,512]{1,0:T(8,128)} %copy-done.7, f32[2048,512]{1,0:T(8,128)} %fusion.60, f32[2048]{0:T(1024)S(1)} %bitcast.132, f32[2,1024,512]{2,1,0:T(8,128)} %copy-done), kind=kLoop, calls=%fused_computation.208 | loop fusion | flops 7337984 | bytes 16809984 | tf_op jit(solution)/shard_map/transpose(jvp())/reduce_sum | solution.py:90
  291.5 3.2 slice-done.2
  294.7 5.3 multiply_reduce_fusion.2
  300.1 27.2 %concatenate.42 = f32[4380,512]{1,0:T(8,128)} concatenate(f32[1536,512]{1,0:T(8,128)} %fusion.94, f32[1536,512]{1,0:T(8,128)S(1)} %fusion.95, f32[1282,512]{1,0:T(8,128)} %fusion.52, f32[1,512]{1,0:T(1,128)S(1)} %bitcast.156, f32[1,512]{1,0:T(1,128)S(1)} %bitcast.155, f32[1,512]{1,0:T(1,128)S(1)} %bitcast.154, f32[1,512]{1,0:T(1,128)S(1)} %bitcast.153, f32[1,512]{1,0:T(1,128)S(1)} %bitcast.152, ...), dimensions={0} | concatenate | bytes 17940480 | tf_op jit(solution)/shard_map/concatenate | solution.py:296
  327.2 8.1 %pad.35 = f32[4384,512]{1,0:T(8,128)} pad(f32[4380,512]{1,0:T(8,128)} %concatenate.42, f32[]{:T(128)} %constant.72.clone.1), padding=0_4x0_0 | pad | bytes 17948676 | tf_op jit(solution)/shard_map/jit(_pad)/pad | solution.py:299
  337.1 13.9 %fusion.6 = f32[2048,1280]{0,1:T(8,128)} fusion(bf16[2048,641]{0,1:T(8,128)(2,1)} %get-tuple-element.41, bf16[2048,641]{0,1:T(8,128)(2,1)S(1)} %copy-done.15, bf16[641,1280]{1,0:T(8,128)(2,1)} %get-tuple-element.91, bf16[641,1280]{1,0:T(8,128)(2,1)} %get-tuple-element.92), kind=kOutput, calls=%fused_computation.34 | convolution fusion | flops 6738438144 | bytes 19018752 | tf_op jit(solution)/shard_map/dot_general | solution.py:107
  350.9 14.4 %reshape.268 = f32[2,1024,4,320]{1,0,3,2:T(2,128)} reshape(f32[2048,1280]{0,1:T(8,128)} %fusion.6) | data formatting | bytes 20971520 | tf_op jit(solution)/shard_map/reshape | solution.py:192
  365.4 8.5 %copy_multiply_fusion = f32[2,1024,4,320]{1,3,0,2:T(8,128)S(1)} fusion(f32[2,1024,4,320]{1,0,3,2:T(2,128)} %reshape.268, f32[4,320]{1,0:T(4,128)S(1)} %copy-done.52), kind=kLoop, calls=%fused_computation.21 | loop fusion | flops 2621440 | bytes 20976640 | tf_op jit(solution)/shard_map/mul | solution.py:192
  382.3 4.4 collective-permute-start.5
  386.8 2.4 fusion.43
  389.2 2.6 copy.36
  391.9 4.1 reshape.269
  396.1 20.3 %fusion.13 = f32[2,1024,512]{2,1,0:T(8,128)} fusion(f32[2,3,512]{2,1,0:T(4,128)S(1)} %collective-permute-done.5, f32[2,3,512]{2,1,0:T(4,128)S(1)} %collective-permute-done.4, f32[2,1024,512]{2,1,0:T(8,128)} %bitcast.119, f32[2,1024,512]{2,1,0:T(8,128)} %bitcast.118, f32[512]{0:T(512)S(1)} %bitcast.135, f32[2,1024]{1,0:T(2,128)S(1)} %copy-done.31, ...), kind=kLoop, calls=%fused_computation.46 | loop fusion | flops 27262976 | bytes 12670976 | tf_op jit(solution)/shard_map/add | solution.py:282
  416.3 103.8 %all-reduce.10.cloned.1.call-done = f32[137,32,512]{2,1,0:T(8,128)} async-done(((f32[137,32,512]{2,1,0:T(8,128)}), f32[137,32,512]{2,1,0:T(8,128)}) %all-reduce.10.cloned.1.call-update) | async-done | bytes 8978448 | tf_op jit(solution)/shard_map/psum | solution.py:301
  520.2 9.1 %concatenate.43 = f32[138,32,512]{2,1,0:T(8,128)} pad(f32[137,32,512]{2,1,0:T(8,128)} %all-reduce.10.cloned.1.call-done, f32[]{:T(128)} %constant.72.clone.1), padding=0_1x0_0x0_0 | pad | bytes 18022404 | tf_op jit(solution)/shard_map/concatenate | solution.py:302
  529.3 4.5 gather_fusion.1
  533.8 5.5 %multiply_subtract_fusion = (f32[27,32,512]{2,1,0:T(8,128)}, f32[27,32,512]{2,1,0:T(8,128)}, f32[27,32,512]{2,1,0:T(8,128)}) fusion(f32[27,32,512]{2,1,0:T(8,128)S(1)} %copy-done.12, f32[27,32,512]{2,1,0:T(8,128)S(1)} %gather_fusion.1, pred[27]{0:T(512)(128)(4,1)S(1)} %copy-done.68, f32[27,32,512]{2,1,0:T(8,128)} %param.13, f32[27,32,512]{2,1,0:T(8,128)} %param.14), kind=kLoop, calls=%fused_computation.127 | loop fusion | flops 7077888 | bytes 12386331 | tf_op jit(solution)/shard_map/sub | solution.py:309
  (236 shorter events, 46.5 us)
Async XLA Ops:
  7.2 115.2 %all-gather.2.cloned.1.call-start = ((), (), s32[]{:S(2)}) async-start(), calls=%async_computation | async-start | bytes 7962624 | tf_op jit(solution)/shard_map/all_gather | solution.py:123
  9.8 510.4 %all-reduce.10.cloned.1.call-start = ((), (), s32[]{:S(2)}) async-start(), calls=%async_computation.1 | async-start | bytes 17956864 | tf_op jit(solution)/shard_map/psum | solution.py:301
  10.6 41.3 %collective-permute-start = (bf16[2,3,512]{2,1,0:T(4,128)(2,1)S(1)}, bf16[2,3,512]{2,1,0:T(4,128)(2,1)S(1)}, u32[]{:S(2)}, u32[]{:S(2)}) collective-permute-start(bf16[2,3,512]{2,1,0:T(4,128)(2,1)S(1)} %get-tuple-element.55), channel_id=1, source_target_pairs={{0,1},{1,2},{2,3},{4,5},{5,6},{6,7},{8,9},{9,10},{10,11},{12,13},{... | collective-permute-start | bytes 18440 | tf_op jit(solution)/shard_map/ppermute | solution.py:39
  12.9 38.9 %collective-permute-start.1 = (bf16[2,3,512]{2,1,0:T(4,128)(2,1)S(1)}, bf16[2,3,512]{2,1,0:T(4,128)(2,1)S(1)}, u32[]{:S(2)}, u32[]{:S(2)}) collective-permute-start(bf16[2,3,512]{2,1,0:T(4,128)(2,1)S(1)} %get-tuple-element.54), channel_id=1, source_target_pairs={{1,0},{2,1},{3,2},{5,4},{6,5},{7,6},{9,8},{10,9},{11,10},{13,12},{... | collective-permute-start | bytes 18440 | tf_op jit(solution)/shard_map/ppermute | solution.py:42
  20.9 12.1 %copy-start.44 = (f32[320]{0:T(512)}, f32[320]{0:T(512)S(1)}, u32[]{:S(2)}) copy-start(f32[320]{0:T(512)S(1)} %get-tuple-element.75) | copy-start | bytes 3844
  20.9 12.1 %copy-start.46 = (f32[320]{0:T(512)}, f32[320]{0:T(512)S(1)}, u32[]{:S(2)}) copy-start(f32[320]{0:T(512)S(1)} %get-tuple-element.76) | copy-start | bytes 3844
  20.9 12.1 %copy-start.48 = (f32[320]{0:T(512)}, f32[320]{0:T(512)S(1)}, u32[]{:S(2)}) copy-start(f32[320]{0:T(512)S(1)} %get-tuple-element.77) | copy-start | bytes 3844
  20.9 12.1 %copy-start.50 = (f32[320]{0:T(512)}, f32[320]{0:T(512)S(1)}, u32[]{:S(2)}) copy-start(f32[320]{0:T(512)S(1)} %get-tuple-element.78) | copy-start | bytes 3844
  21.1 119.1 %copy-start.24 = (f32[2,1024]{1,0:T(2,128)}, f32[2,1024]{1,0:T(2,128)S(1)}, u32[]{:S(2)}) copy-start(f32[2,1024]{1,0:T(2,128)S(1)} %get-tuple-element.68) | copy-start | bytes 24580
  21.1 119.1 %copy-start.26 = (f32[2,1024]{1,0:T(2,128)}, f32[2,1024]{1,0:T(2,128)S(1)}, u32[]{:S(2)}) copy-start(f32[2,1024]{1,0:T(2,128)S(1)} %get-tuple-element.72) | copy-start | bytes 24580
  21.1 119.1 %copy-start.28 = (f32[2,1024]{1,0:T(2,128)}, f32[2,1024]{1,0:T(2,128)S(1)}, u32[]{:S(2)}) copy-start(f32[2,1024]{1,0:T(2,128)S(1)} %get-tuple-element.73) | copy-start | bytes 24580
  21.1 119.1 %copy-start.30 = (f32[2,1024]{1,0:T(2,128)}, f32[2,1024]{1,0:T(2,128)S(1)}, u32[]{:S(2)}) copy-start(f32[2,1024]{1,0:T(2,128)S(1)} %get-tuple-element.69) | copy-start | bytes 24580
  21.1 119.1 %copy-start.32 = (f32[2,1024]{1,0:T(2,128)}, f32[2,1024]{1,0:T(2,128)S(1)}, u32[]{:S(2)}) copy-start(f32[2,1024]{1,0:T(2,128)S(1)} %get-tuple-element.70) | copy-start | bytes 24580
  21.1 119.1 %copy-start.34 = (f32[2,1024]{1,0:T(2,128)}, f32[2,1024]{1,0:T(2,128)S(1)}, u32[]{:S(2)}) copy-start(f32[2,1024]{1,0:T(2,128)S(1)} %get-tuple-element.71) | copy-start | bytes 24580
  24.8 39.0 %collective-permute-start.3 = (f32[2,3,320]{1,2,0:T(8,128)}, f32[2,3,320]{1,2,0:T(8,128)}, u32[]{:S(2)}, u32[]{:S(2)}) collective-permute-start(f32[2,3,320]{1,2,0:T(8,128)} %slice.387), channel_id=1, source_target_pairs={{1,0},{2,1},{3,2},{5,4},{6,5},{7,6},{9,8},{10,9},{11,10},{13,12},{... | collective-permute-start | bytes 23048 | tf_op jit(solution)/shard_map/ppermute | solution.py:50
  26.2 6.7 %copy-start.69 = (s32[2,4]{1,0:T(2,128)S(1)}, s32[2,4]{1,0:T(2,128)}, u32[]{:S(2)}) copy-start(s32[2,4]{1,0:T(2,128)} %param.10) | copy-start | bytes 100
  51.8 105.1 %copy-start.36 = (s32[1,8,2,128]{3,1,2,0:T(8,128)}, s32[1,8,2,128]{3,1,2,0:T(8,128)S(1)}, u32[]{:S(2)}) copy-start(s32[1,8,2,128]{3,1,2,0:T(8,128)S(1)} %copy.53) | copy-start | bytes 24580
  137.4 14.7 %copy-start.13 = (bf16[4384,512]{1,0:T(8,128)(2,1)}, bf16[4384,512]{1,0:T(8,128)(2,1)S(1)}, u32[]{:S(2)}) copy-start(bf16[4384,512]{1,0:T(8,128)(2,1)S(1)} %bitcast_select_fusion) | copy-start | bytes 13467652
  137.4 5.3 slice-start
  137.5 5.2 slice-start.1
  140.1 8.7 %copy-start.53 = (f32[1,512]{1,0:T(1,128)}, f32[1,512]{1,0:T(1,128)S(1)}, u32[]{:S(2)}) copy-start(f32[1,512]{1,0:T(1,128)S(1)} %get-tuple-element.59) | copy-start | bytes 6148
  140.1 8.7 %copy-start.55 = (f32[1,512]{1,0:T(1,128)}, f32[1,512]{1,0:T(1,128)S(1)}, u32[]{:S(2)}) copy-start(f32[1,512]{1,0:T(1,128)S(1)} %get-tuple-element.60) | copy-start | bytes 6148
  140.1 8.7 %copy-start.57 = (f32[1,512]{1,0:T(1,128)}, f32[1,512]{1,0:T(1,128)S(1)}, u32[]{:S(2)}) copy-start(f32[1,512]{1,0:T(1,128)S(1)} %get-tuple-element.61) | copy-start | bytes 6148
  140.1 8.7 %copy-start.59 = (f32[1,512]{1,0:T(1,128)}, f32[1,512]{1,0:T(1,128)S(1)}, u32[]{:S(2)}) copy-start(f32[1,512]{1,0:T(1,128)S(1)} %get-tuple-element.62) | copy-start | bytes 6148
  140.2 8.7 %copy-start.61 = (f32[1,512]{1,0:T(1,128)}, f32[1,512]{1,0:T(1,128)S(1)}, u32[]{:S(2)}) copy-start(f32[1,512]{1,0:T(1,128)S(1)} %get-tuple-element.63) | copy-start | bytes 6148
  140.2 8.7 %copy-start.63 = (f32[1,512]{1,0:T(1,128)}, f32[1,512]{1,0:T(1,128)S(1)}, u32[]{:S(2)}) copy-start(f32[1,512]{1,0:T(1,128)S(1)} %get-tuple-element.64) | copy-start | bytes 6148
  140.2 8.7 %copy-start.65 = (f32[1,512]{1,0:T(1,128)}, f32[1,512]{1,0:T(1,128)S(1)}, u32[]{:S(2)}) copy-start(f32[1,512]{1,0:T(1,128)S(1)} %get-tuple-element.65) | copy-start | bytes 6148
  149.7 7.2 %copy-start.38 = (f32[2048]{0:T(1024)}, f32[2048]{0:T(1024)S(1)}, u32[]{:S(2)}) copy-start(f32[2048]{0:T(1024)S(1)} %bitcast_rsqrt_fusion) | copy-start | bytes 24580
  157.8 35.4 %copy-start.23 = (bf16[48,32,512]{2,1,0:T(8,128)(2,1)}, bf16[48,32,512]{2,1,0:T(8,128)(2,1)S(1)}, u32[]{:S(2)}) copy-start(bf16[48,32,512]{2,1,0:T(8,128)(2,1)S(1)} %get-tuple-element.45) | copy-start | bytes 4718596
  161.8 31.4 %copy-start.17 = (bf16[2048,512]{1,0:T(8,128)(2,1)}, bf16[2048,512]{1,0:T(8,128)(2,1)S(1)}, u32[]{:S(2)}) copy-start(bf16[2048,512]{1,0:T(8,128)(2,1)S(1)} %add_convert_fusion.3) | copy-start | bytes 6291460
  161.8 31.4 %copy-start.16 = (bf16[2,1024,512]{2,1,0:T(8,128)(2,1)S(1)}, bf16[2,1024,512]{2,1,0:T(8,128)(2,1)}, u32[]{:S(2)}) copy-start(bf16[2,1024,512]{2,1,0:T(8,128)(2,1)} %param.8) | copy-start | bytes 6291460
  193.2 5.6 %copy-start.71 = (bf16[2048,1536]{1,0:T(8,128)(2,1)}, bf16[2048,1536]{1,0:T(8,128)(2,1)S(1)}, u32[]{:S(2)}) copy-start(bf16[2048,1536]{1,0:T(8,128)(2,1)S(1)} %get-tuple-element.32) | copy-start | bytes 18874372
  247.5 5.6 %copy-start.5 = (f32[2048,512]{1,0:T(8,128)}, f32[2048,512]{1,0:T(8,128)S(1)}, u32[]{:S(2)}) copy-start(f32[2048,512]{1,0:T(8,128)S(1)} %get-tuple-element.21) | copy-start | bytes 12582916
  253.1 16.6 %copy-start.4 = (f32[2048,512]{1,0:T(8,128)S(1)}, f32[2048,512]{1,0:T(8,128)}, u32[]{:S(2)}) copy-start(f32[2048,512]{1,0:T(8,128)} %bitcast_subtract_fusion) | copy-start | bytes 12582916
  253.1 16.6 %copy-start.6 = (f32[2048,512]{1,0:T(8,128)S(1)}, f32[2048,512]{1,0:T(8,128)}, u32[]{:S(2)}) copy-start(f32[2048,512]{1,0:T(8,128)} %fusion.60) | copy-start | bytes 12582916
  269.7 6.7 %copy-start.18 = (bf16[2048,512]{1,0:T(8,128)(2,1)S(1)}, bf16[2048,512]{1,0:T(8,128)(2,1)}, u32[]{:S(2)}) copy-start(bf16[2048,512]{1,0:T(8,128)(2,1)} %copy-done.17) | copy-start | bytes 6291460
  269.7 6.7 %copy-start.70 = (bf16[2048,1536]{1,0:T(8,128)(2,1)S(1)}, bf16[2048,1536]{1,0:T(8,128)(2,1)}, u32[]{:S(2)}) copy-start(bf16[2048,1536]{1,0:T(8,128)(2,1)} %get-tuple-element.90) | copy-start | bytes 18874372
  276.4 7.3 %copy-start.7 = (f32[2048,512]{1,0:T(8,128)}, f32[2048,512]{1,0:T(8,128)S(1)}, u32[]{:S(2)}) copy-start(f32[2048,512]{1,0:T(8,128)S(1)} %get-tuple-element.88) | copy-start | bytes 12582916
  291.5 8.6 %copy-start.2 = (f32[2048,512]{1,0:T(8,128)}, f32[2048,512]{1,0:T(8,128)S(1)}, u32[]{:S(2)}) copy-start(f32[2048,512]{1,0:T(8,128)S(1)} %get-tuple-element.25) | copy-start | bytes 12582916
  350.9 14.4 %copy-start.52 = (f32[4,320]{1,0:T(4,128)S(1)}, f32[4,320]{1,0:T(4,128)}, u32[]{:S(2)}) copy-start(f32[4,320]{1,0:T(4,128)} %multiply_subtract_fusion.2) | copy-start | bytes 15364
  376.4 10.4 %copy-start.45 = (f32[320]{0:T(512)S(1)}, f32[320]{0:T(512)}, u32[]{:S(2)}) copy-start(f32[320]{0:T(512)} %copy-done.44) | copy-start | bytes 3844
  376.4 10.4 %copy-start.47 = (f32[320]{0:T(512)S(1)}, f32[320]{0:T(512)}, u32[]{:S(2)}) copy-start(f32[320]{0:T(512)} %copy-done.46) | copy-start | bytes 3844
  376.4 10.4 %copy-start.49 = (f32[320]{0:T(512)S(1)}, f32[320]{0:T(512)}, u32[]{:S(2)}) copy-start(f32[320]{0:T(512)} %copy-done.48) | copy-start | bytes 3844
  376.4 10.4 %copy-start.51 = (f32[320]{0:T(512)S(1)}, f32[320]{0:T(512)}, u32[]{:S(2)}) copy-start(f32[320]{0:T(512)} %copy-done.50) | copy-start | bytes 3844
  376.4 10.3 %collective-permute-start.2 = (f32[2,3,320]{1,2,0:T(8,128)S(1)}, f32[2,3,320]{1,2,0:T(8,128)S(1)}, u32[]{:S(2)}, u32[]{:S(2)}) collective-permute-start(f32[2,3,320]{1,2,0:T(8,128)S(1)} %pad_add_fusion.1), channel_id=1, source_target_pairs={{0,1},{1,2},{2,3},{4,5},{5,6},{6,7},{8,9},{9,10},{10,11},{12,13},{... | collective-permute-start | bytes 23048 | tf_op jit(solution)/shard_map/ppermute | solution.py:50
  381.1 14.9 %collective-permute-start.4 = (f32[2,3,512]{2,1,0:T(4,128)S(1)}, f32[2,3,512]{2,1,0:T(4,128)S(1)}, u32[]{:S(2)}, u32[]{:S(2)}) collective-permute-start(f32[2,3,512]{2,1,0:T(4,128)S(1)} %get-tuple-element.49), channel_id=1, source_target_pairs={{1,0},{2,1},{3,2},{5,4},{6,5},{7,6},{9,8},{10,9},{11,10},{13,12},{... | collective-permute-start | bytes 36872 | tf_op jit(solution)/shard_map/ppermute | solution.py:42
  382.3 13.6 %collective-permute-start.5 = (f32[2,3,512]{2,1,0:T(4,128)S(1)}, f32[2,3,512]{2,1,0:T(4,128)S(1)}, u32[]{:S(2)}, u32[]{:S(2)}) collective-permute-start(f32[2,3,512]{2,1,0:T(4,128)S(1)} %get-tuple-element.50), channel_id=1, source_target_pairs={{0,1},{1,2},{2,3},{4,5},{5,6},{6,7},{8,9},{9,10},{10,11},{12,13},{... | collective-permute-start | bytes 36872 | tf_op jit(solution)/shard_map/ppermute | solution.py:39
  416.3 117.4 %copy-start.68 = (pred[27]{0:T(512)(128)(4,1)S(1)}, pred[27]{0:T(512)(128)(4,1)}, u32[]{:S(2)}) copy-start(pred[27]{0:T(512)(128)(4,1)} %get-tuple-element.18) | copy-start | bytes 85
  (38 other events, 134.6 us)
Sparse Core Ops, SparseCore 0:
  10.8 111.5 all-gather.1
  335.5 184.6 all-reduce.9
where the time goes:
time: 556 us; the launch traced here: 546 us
  other arithmetic  136 us (24%)
  local copies, waits for them, and re-layouts  133 us (24%)
  waiting for transfers between devices  130 us (23%)
  matrix products  119 us (21%)
  between operations  15.7 us (3%)
  starting transfers between devices  12.2 us (2%)
    dot_general x11, matrix products, contract(): lax.dot_general(left_side, right_side, (((left_dim,), (right_dim,)), ((),...  109 us
    psum x1, waiting for transfers between devices, local(): summed = lax.psum(grad_buckets, ('rows', 'seq'))  104 us
    another operation x3, other arithmetic  42.2 us
    concatenate x1, local copies, waits for them, and re-layouts, local(): jnp.concatenate([grad_w_in, grad_w_out, grad_w_head, vec_grads, in_rows,...  27.2 us
    all_gather x1, waiting for transfers between devices, local(): lax.all_gather(master.astype(jnp.bfloat16), 'rows', axis=0, tiled=True)  25.9 us
    add x1, other arithmetic, local(): input_grad + conv_weight[tap_index] * keep * halo_grad[:, begin:begin + f...  20.3 us
    unnamed x159, local copies, waits for them, and re-layouts  17.5 us
    reshape x1, local copies, waits for them, and re-layouts, local(): signal.reshape(rows_here, frames_here, lap_count, HOP)  14.4 us
  transfers between devices with their start and end apart: 8, of which 2 were waited for; matrix products, arithmetic and copies ran while one was open for 28% of the time, Pallas kernels for 0%

commit v1 on v0

v1 whole, which is shorter than its diff:
```python
import functools
import math

import jax
import jax.numpy as jnp
import numpy as np
from jax import lax
from jax.experimental import pallas as pl
from jax.experimental.pallas import tpu as pltpu
from jax.sharding import PartitionSpec as P

FF = 1536
NFFT = 1280
HOP = 320
NBW = 4
KW = 7
UTT = 4
BR = 32
STEP_COUNT = 6
BINS = 641
NOUT = 1282
VROWS = 20
IN_ROWS = 3
HEAD_ROWS = 3
NB = 137

NORM_EPS = 1e-06
ENV_FLOOR = 0.5
BETA_ONE = 0.8
BETA_TWO = 0.9
LEARN_RATE = 0.04
WEIGHT_DECAY = 0.01
ADAM_EPS = 1e-08

LAPS = NFFT // HOP
RIM = (KW - 1) // 2
LAP_PAD = 384
BIN_PAD = 768
HALF = BR // 2
QUART = BR // 4
EDGE = 8
TILE = 256
CHUNK = 512
AXES = ("rows", "seq")

F32 = jnp.float32
BF16 = jnp.bfloat16
MIB = 1 << 20


def synthesis_table():
    k = np.arange(BINS)[:, None]
    n = np.arange(NFFT)[None, :]
    angle = (k * n % NFFT) * (2.0 * math.pi / NFFT)
    factor = np.where((k == 0) | (k == NFFT // 2), 1.0, 2.0) / NFFT
    out = np.zeros((2, BIN_PAD, LAPS, LAP_PAD), np.float32)
    out[0, :BINS, :, :HOP] = (factor * np.cos(angle)).reshape(BINS, LAPS, HOP)
    out[1, :BINS, :, :HOP] = (-factor * np.sin(angle)).reshape(BINS, LAPS, HOP)
    return out.reshape(2 * BIN_PAD, LAPS * LAP_PAD).astype(jnp.bfloat16)


def window_tables():
    window = 0.5 - 0.5 * np.cos(np.arange(NFFT) * (2.0 * math.pi / NFFT))
    rows = np.zeros((LAPS, LAP_PAD), np.float64)
    rows[:, :HOP] = window.reshape(LAPS, HOP)
    envelope = np.cumsum(rows**2, axis=0)
    return np.concatenate([rows, 1.0 / np.maximum(envelope, ENV_FLOOR)], axis=0).astype(np.float32)


def ring_of(count):
    if count != 8:
        return None
    return [0, 2, 4, 6, 7, 5, 3, 1]


def ring_step(ring, shift, seq_count):
    where = {r: i for i, r in enumerate(ring)}
    pairs = []
    for r in ring:
        target = ring[(where[r] + shift) % len(ring)]
        pairs += [(r * seq_count + s, target * seq_count + s) for s in range(seq_count)]
    return pairs


def seq_swap(value, bit):
    count = lax.axis_size("seq")
    return lax.ppermute(value, "seq", [(s, s ^ bit) for s in range(count)])


def rows_swap(value, bit):
    count = lax.axis_size("rows")
    return lax.ppermute(value, "rows", [(r, r ^ bit) for r in range(count)])


def shifted(value, distance):
    devices = range(lax.axis_size("seq"))
    return lax.ppermute(
        value, "seq", [(i - distance, i) for i in devices if i - distance in devices]
    )


def dot(a, b, dims):
    return lax.dot_general(a, b, (dims, ((), ())), preferred_element_type=F32)


NN = ((1,), (0,))
NT = ((1,), (1,))
TN = ((0,), (0,))


def frame_reach(meta, row, first, count, utts):
    index = first + lax.broadcasted_iota(jnp.int32, (count, 128), 0)
    start = jnp.zeros_like(index)
    end = jnp.zeros_like(index) + meta[row, 1]
    for u in range(1, utts):
        inside = index >= meta[row, u]
        start = jnp.where(inside, meta[row, u], start)
        end = jnp.where(inside, meta[row, u + 1], end)
    return index - start, end - 1 - index


def lanes(mask, count):
    return jnp.concatenate([mask] * count, axis=1)


def by_reach(reach, table, base, count):
    picked = jnp.broadcast_to(table[base + LAPS - 1 : base + LAPS], (reach.shape[0], LAP_PAD))
    for j in range(LAPS - 2, -1, -1):
        picked = jnp.where(lanes(reach == j, LAP_PAD // 128), table[base + j : base + j + 1], picked)
    return picked


def fold(values):
    rows, columns = values.shape
    return jnp.sum(values.reshape(rows // 8, 8, columns), axis=0)


def sincos(angle):
    turns = jnp.round(angle * (1.0 / math.pi))
    rest = angle - turns * 3.140625
    rest = rest - turns * 9.670257568359375e-4
    rest = rest - turns * 6.2771141529083251953e-7
    rest = rest - turns * 1.2154201256553420e-10
    half = turns * 0.5
    sign = 1.0 - 4.0 * (half - jnp.floor(half))
    sq = rest * rest
    sine = rest + rest * sq * (
        -1.6666667163e-01
        + sq * (8.3333337680e-03 + sq * (-1.9841270114e-04 + sq * (2.7557314297e-06 - sq * 2.5050759689e-08)))
    )
    cosine = 1.0 + sq * (
        -0.5
        + sq
        * (
            4.1666667908e-02
            + sq
            * (-1.3888889225e-03 + sq * (2.4801587642e-05 + sq * (-2.7557314297e-07 + sq * 2.0875723372e-09)))
        )
    )
    return sine * sign, cosine * sign


ANGLE_LIMIT = 8192.0


def pre_body(meta, wave_ref, synth_ref, win_ref, out_ref, scaled, *, tiles, utts):
    step = pl.program_id(0)
    row, first = step // tiles, (step % tiles) * TILE
    base = meta[row, 2 * utts + 1] + first
    reach, left = frame_reach(meta, row, base, TILE + EDGE, utts)
    wave = wave_ref[row, pl.ds(pl.multiple_of(first, TILE), TILE + 2 * EDGE), :].astype(F32)
    scaled[...] = wave[: TILE + EDGE] * by_reach(reach, win_ref, LAPS, LAP_PAD)
    parts = []
    for j in range(LAPS):
        part = scaled[j : j + TILE, :] * win_ref[j : j + 1, :]
        if j:
            part = jnp.where(lanes(left[:TILE] >= j, LAP_PAD // 128), part, 0.0)
        parts.append(part.astype(BF16))
    signal = jnp.concatenate(parts, axis=1)
    for c in range(0, 2 * BIN_PAD, 512):
        out_ref[:, c : c + 512] = dot(signal, synth_ref[c : c + 512, :], NT).astype(BF16)


def spectrum_cotangent(meta, wave, synth, win, rows, frames, utts):
    tiles = frames // TILE
    count = rows * frames
    return pl.pallas_call(
        functools.partial(pre_body, tiles=tiles, utts=utts),
        grid=(rows * tiles,),
        in_specs=[
            pl.BlockSpec(memory_space=pltpu.SMEM),
            pl.BlockSpec(memory_space=pltpu.VMEM),
            pl.BlockSpec(memory_space=pltpu.VMEM),
            pl.BlockSpec(memory_space=pltpu.VMEM),
        ],
        out_specs=pl.BlockSpec((TILE, 2 * BIN_PAD), lambda i: (i, 0)),
        out_shape=jax.ShapeDtypeStruct((count, 2 * BIN_PAD), BF16),
        scratch_shapes=[pltpu.VMEM((TILE + EDGE, LAP_PAD), F32)],
        compiler_params=pltpu.CompilerParams(vmem_limit_bytes=40 * MIB),
        cost_estimate=pl.CostEstimate(
            flops=2 * count * 1536 * 1536, bytes_accessed=count * 1536 * 2 + 8 * MIB, transcendentals=0
        ),
        name="spectrum_cotangent",
    )(meta, wave, synth, win)


def forward_body(
    meta,
    places,
    x_ref,
    cot_ref,
    *rest,
    parts,
    tiles,
    utts,
):
    sources = rest[:parts]
    (
        table,
        spec_ref,
        act_ref,
        der_ref,
        ada_ref,
        low_ref,
        resg_ref,
        xc_ref,
        rc_ref,
        send_ref,
        keep_ref,
        tail_ref,
        sums_ref,
        bsum_ref,
        xs,
        w_head,
        b_head,
        grad,
        hg,
        sem,
    ) = rest[parts:]
    step = pl.program_id(0)
    steps = pl.num_programs(0)
    core = meta[0, 2 * utts + 2]
    channels = x_ref.shape[2]

    @pl.when(step == 0)
    def _():
        def go(start):
            base = 0
            for index, ref in enumerate(sources):
                slots = ref.shape[0]
                side = core if index % 2 == 0 else 1 - core

                def one(s, carry, ref=ref, base=base, side=side):
                    bucket = places[0, base + s]

                    @pl.when(bucket < NB)
                    def _():
                        at = pl.multiple_of(bucket * BR + side * HALF, HALF)
                        copy = pltpu.make_async_copy(ref.at[s], table.at[pl.ds(at, HALF), :], sem)
                        if start:
                            copy.start()
                        else:
                            copy.wait()

                    return carry

                lax.fori_loop(0, slots, one, 0)
                if index % 2 == 1:
                    base = base + slots

        go(True)
        grad[...] = jnp.zeros_like(grad)
        sums_ref[...] = jnp.zeros_like(sums_ref)
        bsum_ref[...] = jnp.zeros_like(bsum_ref)
        go(False)
        head_at = 2 * FF
        w_head[0:640, :] = table[head_at : head_at + 640, :]
        edge = table[head_at + 640 : head_at + 640 + 656, :].astype(F32)
        inside = lax.broadcasted_iota(jnp.int32, (128, channels), 0)
        w_head[640:768, :] = jnp.where(inside < 1, edge[0:128], 0.0).astype(BF16)
        w_head[768:1408, :] = edge[1:641].astype(BF16)
        w_head[1408:1536, :] = jnp.where(inside < 1, edge[641:642], 0.0).astype(BF16)
        last = table[2 * FF + 1280 : 2 * FF + 1280 + BR, :].astype(F32)
        wide = jnp.concatenate([last[25:26], last[26:27], last[27:28]], axis=1)
        wide = jnp.broadcast_to(wide, (8, 3 * channels))
        column = lax.broadcasted_iota(jnp.int32, (8, BIN_PAD), 1)
        b_head[:, 0:BIN_PAD] = jnp.where(column < BINS, wide[:, 0:BIN_PAD], 0.0)
        moved = pltpu.roll(wide, 3 * channels - BINS, 1)
        b_head[:, BIN_PAD:] = jnp.where(column < BINS, moved[:, 0:BIN_PAD], 0.0)

    row, first = step // tiles, (step % tiles) * TILE
    base = meta[row, 2 * utts + 1] + first
    reach, left = frame_reach(meta, row, base, TILE, utts)
    last = table[2 * FF + 1280 : 2 * FF + 1280 + BR, :].astype(F32)
    vec = lambda v: last[2 + v : 3 + v]
    xs[...] = x_ref[row, pl.ds(pl.multiple_of(first, TILE), TILE + 2 * EDGE), :].astype(F32)
    conv = jnp.zeros((TILE, channels), F32) + vec(KW)
    for k in range(KW):
        offset = k - RIM
        moved = xs[EDGE + offset : EDGE + offset + TILE, :]
        if offset < 0:
            moved = jnp.where(lanes(reach >= -offset, channels // 128), moved, 0.0)
        elif offset > 0:
            moved = jnp.where(lanes(left >= offset, channels // 128), moved, 0.0)
        conv = conv + moved * vec(k)
    mean = jnp.mean(conv, axis=1, keepdims=True)
    conv = conv - mean
    rc = lax.rsqrt(jnp.mean(conv * conv, axis=1, keepdims=True) + NORM_EPS)
    xc = conv * rc
    xc_ref[...] = xc
    rc_ref[...] = jnp.broadcast_to(rc, (TILE, 128))
    index = base + lax.broadcasted_iota(jnp.int32, (TILE, 128), 0)

    def pick(offset):
        def of(u):
            wanted = meta[row, utts + 1 + u]
            value = vec(offset)
            for b in range(1, NBW):
                value = jnp.where(wanted == b, vec(offset + b), value)
            return value

        value = jnp.broadcast_to(of(0), (TILE, channels))
        for u in range(1, utts):
            value = jnp.where(lanes(index >= meta[row, u], channels // 128), of(u), value)
        return value

    ada = (xc * pick(KW + 1) + pick(KW + 1 + NBW)).astype(BF16)
    ada_ref[...] = ada
    for c in range(IN_ROWS):
        span = slice(c * CHUNK, (c + 1) * CHUNK)
        pre = dot(ada, table[span, :], NT) + last[2 + VROWS + c : 3 + VROWS + c]
        phi = 0.5 + 0.5 * lax.erf(pre * math.sqrt(0.5))
        act_ref[:, span] = (pre * phi).astype(BF16)
        bell = jnp.exp(-0.5 * pre * pre) * (1.0 / math.sqrt(2.0 * math.pi))
        der_ref[:, span] = (phi + pre * bell).astype(BF16)
    vec_at = KW + 1 + 2 * NBW
    branch = dot(act_ref[...], table[FF : 2 * FF, :], NN) + vec(vec_at)
    residual = xs[EDGE : EDGE + TILE, :] + vec(vec_at + 1) * branch
    residual = residual - jnp.mean(residual, axis=1, keepdims=True)
    rn = lax.rsqrt(jnp.mean(residual * residual, axis=1, keepdims=True) + NORM_EPS)
    xn = residual * rn
    normed = (xn * vec(vec_at + 2) + vec(vec_at + 3)).astype(BF16)
    def head(c, turn):
        logs = dot(normed, w_head[c : c + 256, :], NT) + b_head[0:1, c : c + 256]
        angle = (
            dot(normed, w_head[BIN_PAD + c : BIN_PAD + c + 256, :], NT)
            + b_head[0:1, BIN_PAD + c : BIN_PAD + c + 256]
        )
        size = jnp.exp(logs)
        sine, cosine = turn(angle)
        real, imag = size * cosine, size * sine
        spec_ref[:, c : c + 256] = real.astype(BF16)
        spec_ref[:, BIN_PAD + c : BIN_PAD + c + 256] = imag.astype(BF16)
        dre = cot_ref[:, c : c + 256].astype(F32)
        dim = cot_ref[:, BIN_PAD + c : BIN_PAD + c + 256].astype(F32)
        hg[:, c : c + 256] = (dre * real + dim * imag).astype(BF16)
        hg[:, BIN_PAD + c : BIN_PAD + c + 256] = (dim * real - dre * imag).astype(BF16)
        return jnp.max(jnp.abs(angle).reshape(TILE // 8, 8, 256), axis=0)

    widest = head(0, sincos)
    for c in range(256, BIN_PAD, 256):
        widest = jnp.maximum(widest, head(c, sincos))

    @pl.when(jnp.max(widest) > ANGLE_LIMIT)
    def _():
        for c in range(0, BIN_PAD, 256):
            head(c, lambda angle: (jnp.sin(angle), jnp.cos(angle)))

    bsum_ref[...] += fold(hg[...].astype(F32))
    grad[...] += dot(hg[...], normed, TN)
    ngrad = dot(hg[...], w_head[...], NN)
    e = ngrad * vec(vec_at + 2)
    resg = rn * (
        e - jnp.mean(e, axis=1, keepdims=True) - xn * jnp.mean(e * xn, axis=1, keepdims=True)
    )
    resg_ref[...] = resg
    low = (vec(vec_at + 1) * resg).astype(BF16)
    low_ref[...] = low
    sums_ref[0] += fold(low.astype(F32))
    sums_ref[1] += fold(resg * branch)
    sums_ref[2] += fold(ngrad * xn)
    sums_ref[3] += fold(ngrad)

    @pl.when(step == steps - 1)
    def _():
        grad[767:768, :] = grad[640:641, :]
        for b in range(40):
            at = b * BR if b < 20 else b * BR + 127
            low_half = grad[at : at + HALF, :].astype(BF16)
            high_half = grad[at + HALF : at + BR, :].astype(BF16)
            keep_ref[b] = jnp.where(core == 0, low_half, high_half)
            send_ref[b] = jnp.where(core == 0, high_half, low_half)
        tail_ref[...] = grad[1407:1415, :]


def forward(meta, places, xpad, cot, sources, rows, frames, utts):
    tiles = frames // TILE
    count = rows * frames
    channels = xpad.shape[2]
    wide = pl.BlockSpec((TILE, FF), lambda i: (i, 0))
    slim = pl.BlockSpec((TILE, channels), lambda i: (i, 0))
    whole = pl.BlockSpec(memory_space=pltpu.VMEM)
    smem = pl.BlockSpec(memory_space=pltpu.SMEM)
    shape = jax.ShapeDtypeStruct
    return pl.pallas_call(
        functools.partial(forward_body, parts=len(sources), tiles=tiles, utts=utts),
        grid=(rows * tiles,),
        in_specs=[smem, smem, whole, wide] + [pl.BlockSpec(memory_space=pl.ANY)] * len(sources),
        out_specs=[whole, wide, wide, wide, slim, slim, slim, slim]
        + [pl.BlockSpec((TILE, 128), lambda i: (i, 0))]
        + [whole] * 5,
        out_shape=[
            shape((NB * BR, channels), BF16),
            shape((count, FF), BF16),
            shape((count, FF), BF16),
            shape((count, FF), BF16),
            shape((count, channels), BF16),
            shape((count, channels), BF16),
            shape((count, channels), F32),
            shape((count, channels), F32),
            shape((count, 128), F32),
            shape((40, HALF, channels), BF16),
            shape((40, HALF, channels), BF16),
            shape((8, channels), F32),
            shape((4, 8, channels), F32),
            shape((8, 2 * BIN_PAD), F32),
        ],
        scratch_shapes=[
            pltpu.VMEM((TILE + 2 * EDGE, channels), F32),
            pltpu.VMEM((2 * BIN_PAD, channels), BF16),
            pltpu.VMEM((8, 2 * BIN_PAD), F32),
            pltpu.VMEM((2 * BIN_PAD, channels), F32),
            pltpu.VMEM((TILE, 2 * BIN_PAD), BF16),
            pltpu.SemaphoreType.DMA,
        ],
        compiler_params=pltpu.CompilerParams(vmem_limit_bytes=56 * MIB),
        cost_estimate=pl.CostEstimate(
            flops=10 * count * 1536 * 512, bytes_accessed=40 * MIB, transcendentals=count * 4096
        ),
        name="forward",
    )(meta, places, xpad, cot, *sources)


def mlp_body(meta, low_ref, act_ref, der_ref, ada_ref, wout_ref, pre_ref, send_ref, keep_ref, bsum_ref, gout, gin, *, utts):
    step = pl.program_id(0)
    core = meta[0, 2 * utts + 2]

    @pl.when(step == 0)
    def _():
        gout[...] = jnp.zeros_like(gout)
        gin[...] = jnp.zeros_like(gin)
        bsum_ref[...] = jnp.zeros_like(bsum_ref)

    low = low_ref[...]
    agrad = dot(low, wout_ref[...], NT)
    pre = (agrad * der_ref[...].astype(F32)).astype(BF16)
    pre_ref[...] = pre
    bsum_ref[...] += fold(pre.astype(F32))
    gout[...] += dot(act_ref[...], low, TN)
    gin[...] += dot(pre, ada_ref[...], TN)

    @pl.when(step == pl.num_programs(0) - 1)
    def _():
        buckets = CHUNK // BR
        for at, ref in ((0, gin), (buckets, gout)):
            for b in range(buckets):
                low_half = ref[b * BR : b * BR + HALF, :].astype(BF16)
                high_half = ref[b * BR + HALF : b * BR + BR, :].astype(BF16)
                keep_ref[at + b] = jnp.where(core == 0, low_half, high_half)
                send_ref[at + b] = jnp.where(core == 0, high_half, low_half)


def mlp_backward(chunk, meta, low, act, der, ada, table, utts):
    count, channels = low.shape
    tile = 512
    shape = jax.ShapeDtypeStruct
    slim = pl.BlockSpec((tile, channels), lambda i: (i, 0))
    part = pl.BlockSpec((tile, CHUNK), lambda i: (i, chunk))
    buckets = 2 * CHUNK // BR
    whole = pl.BlockSpec(memory_space=pltpu.VMEM)
    return pl.pallas_call(
        functools.partial(mlp_body, utts=utts),
        grid=(count // tile,),
        in_specs=[
            pl.BlockSpec(memory_space=pltpu.SMEM),
            slim,
            part,
            part,
            slim,
            pl.BlockSpec((CHUNK, channels), lambda i: (FF // CHUNK + chunk, 0)),
        ],
        out_specs=[pl.BlockSpec((tile, CHUNK), lambda i: (i, 0)), whole, whole, whole],
        out_shape=[
            shape((count, CHUNK), BF16),
            shape((buckets, HALF, channels), BF16),
            shape((buckets, HALF, channels), BF16),
            shape((8, CHUNK), F32),
        ],
        scratch_shapes=[pltpu.VMEM((CHUNK, channels), F32), pltpu.VMEM((CHUNK, channels), F32)],
        compiler_params=pltpu.CompilerParams(vmem_limit_bytes=40 * MIB),
        cost_estimate=pl.CostEstimate(
            flops=6 * count * CHUNK * 512, bytes_accessed=12 * MIB, transcendentals=0
        ),
        name=f"mlp_backward_{chunk}",
    )(meta, low, act, der, ada, table)


def conv_body(
    meta,
    x_ref,
    pre0,
    pre1,
    pre2,
    table,
    xc_ref,
    rc_ref,
    resg_ref,
    tail_ref,
    sums_ref,
    hsum_ref,
    bsum0,
    bsum1,
    bsum2,
    out_ref,
    edge_ref,
    vec_ref,
    xs,
    cg,
    part,
    *,
    tiles,
    utts,
):
    phase = pl.program_id(0)
    step = pl.program_id(1)
    steps = pl.num_programs(1)
    row, first = step // tiles, (step % tiles) * TILE
    channels = x_ref.shape[2]
    frames = tiles * TILE
    base = meta[row, 2 * utts + 1] + first
    last = table[2 * FF + 1280 : 2 * FF + 1280 + BR, :].astype(F32)
    vec = lambda v: last[2 + v : 3 + v]
    at = pl.multiple_of(first, TILE)
    reach, left = frame_reach(meta, row, base, TILE, utts)

    @pl.when((phase == 0) & (step == 0))
    def _():
        part[...] = jnp.zeros_like(part)
        cg[...] = jnp.zeros_like(cg)

    @pl.when(phase == 0)
    def _():
        agrad = dot(pre0[...], table[0:CHUNK, :], NN)
        agrad += dot(pre1[...], table[CHUNK : 2 * CHUNK, :], NN)
        agrad += dot(pre2[...], table[2 * CHUNK : 3 * CHUNK, :], NN)
        xc = xc_ref[...]
        rc = rc_ref[:, 0:1]
        index = base + lax.broadcasted_iota(jnp.int32, (TILE, 128), 0)
        scaled = agrad * xc
        scale = None
        for u in range(utts):
            low, high = meta[row, u], meta[row, u + 1]
            wanted = meta[row, utts + 1 + u]
            value = vec(KW + 1)
            for b in range(1, NBW):
                value = jnp.where(wanted == b, vec(KW + 1 + b), value)
            if u == 0:
                scale = jnp.broadcast_to(value, (TILE, channels))
            else:
                scale = jnp.where(lanes(index >= low, channels // 128), value, scale)

            @pl.when((low < base + TILE) & (high > base))
            def _(wanted=wanted, low=low, high=high):
                inside = lanes((index >= low) & (index < high), channels // 128)
                part[KW + 1 + wanted] += fold(jnp.where(inside, scaled, 0.0))
                part[KW + 1 + NBW + wanted] += fold(jnp.where(inside, agrad, 0.0))

        ec = agrad * scale
        cgrad = rc * (
            ec - jnp.mean(ec, axis=1, keepdims=True) - xc * jnp.mean(ec * xc, axis=1, keepdims=True)
        )
        cg[row, pl.ds(pl.multiple_of(first + EDGE, EDGE), TILE), :] = cgrad
        xs[...] = x_ref[row, pl.ds(at, TILE + 2 * EDGE), :].astype(F32)
        part[KW] += fold(cgrad)
        for k in range(KW):
            offset = k - RIM
            moved = xs[EDGE + offset : EDGE + offset + TILE, :] * cgrad
            if offset < 0:
                moved = jnp.where(lanes(reach >= -offset, channels // 128), moved, 0.0)
            elif offset > 0:
                moved = jnp.where(lanes(left >= offset, channels // 128), moved, 0.0)
            part[k] += fold(moved)

    @pl.when(phase == 1)
    def _():
        xs[...] = cg[row, pl.ds(at, TILE + 2 * EDGE), :]
        total = resg_ref[...]
        for k in range(KW):
            offset = RIM - k
            moved = xs[EDGE + offset : EDGE + offset + TILE, :]
            if offset < 0:
                moved = jnp.where(lanes(reach >= -offset, channels // 128), moved, 0.0)
            elif offset > 0:
                moved = jnp.where(lanes(left >= offset, channels // 128), moved, 0.0)
            total = total + moved * vec(k)
        out_ref[0] = total

    @pl.when((phase == 1) & (step == steps - 1))
    def _():
        for r in range(cg.shape[0]):
            edge_ref[r, 0] = cg[r, EDGE : 2 * EDGE, :]
            edge_ref[r, 1] = cg[r, frames : frames + EDGE, :]
        vec_ref[0:8, :] = jnp.zeros((8, channels), F32)
        vec_ref[0:2, :] = tail_ref[0:2, :]
        for v in range(VROWS):
            rows_of = part[v] if v < KW + 1 + 2 * NBW else sums_ref[v - (KW + 1 + 2 * NBW)]
            vec_ref[2 + v : 3 + v, :] = jnp.sum(rows_of, axis=0, keepdims=True)
        for c, ref in enumerate((bsum0, bsum1, bsum2)):
            vec_ref[2 + VROWS + c : 3 + VROWS + c, :] = jnp.sum(ref[...], axis=0, keepdims=True)
        flat = jnp.broadcast_to(
            jnp.sum(hsum_ref[...], axis=0, keepdims=True), (8, 2 * BIN_PAD)
        )
        column = lax.broadcasted_iota(jnp.int32, (8, 3 * channels), 1)
        moved = pltpu.roll(flat, 2 * BIN_PAD - (BIN_PAD - BINS), 1)
        joined = jnp.where(column < BINS, flat, moved)
        joined = jnp.where(column < NOUT, joined, 0.0)
        for c in range(HEAD_ROWS):
            at_row = 2 + VROWS + IN_ROWS + c
            vec_ref[at_row : at_row + 1, :] = joined[0:1, c * channels : (c + 1) * channels]
        vec_ref[28:32, :] = jnp.zeros((4, channels), F32)


def conv_backward(meta, xpad, pres, table, xc, rc, resg, tail, sums, hsum, bsums, rows, frames, utts):
    tiles = frames // TILE
    steps = rows * tiles
    count, channels = resg.shape
    shape = jax.ShapeDtypeStruct
    whole = pl.BlockSpec(memory_space=pltpu.VMEM)
    early = lambda p, i: (jnp.where(p == 0, i, steps - 1), 0)
    late = lambda p, i: (jnp.where(p == 0, 0, i), 0)
    late_out = lambda p, i: (jnp.where(p == 0, 0, i // tiles), jnp.where(p == 0, 0, i % tiles), 0)
    return pl.pallas_call(
        functools.partial(conv_body, tiles=tiles, utts=utts),
        grid=(2, steps),
        in_specs=[pl.BlockSpec(memory_space=pltpu.SMEM), whole]
        + [pl.BlockSpec((TILE, CHUNK), early)] * 3
        + [whole, pl.BlockSpec((TILE, channels), early), pl.BlockSpec((TILE, 128), early)]
        + [pl.BlockSpec((TILE, channels), late)]
        + [whole] * 6,
        out_specs=[pl.BlockSpec((1, TILE, channels), late_out), whole, whole],
        out_shape=[
            shape((rows, frames, channels), F32),
            shape((rows, 2, EDGE, channels), F32),
            shape((BR, channels), F32),
        ],
        scratch_shapes=[
            pltpu.VMEM((TILE + 2 * EDGE, channels), F32),
            pltpu.VMEM((rows, frames + 2 * EDGE, channels), F32),
            pltpu.VMEM((KW + 1 + 2 * NBW, 8, channels), F32),
        ],
        compiler_params=pltpu.CompilerParams(vmem_limit_bytes=56 * MIB),
        cost_estimate=pl.CostEstimate(
            flops=2 * count * 1536 * 512, bytes_accessed=24 * MIB, transcendentals=0
        ),
        name="conv_backward",
    )(meta, xpad, *pres, table, xc, rc, resg, tail, sums, hsum, *bsums)


def wave_body(meta, spec_ref, synth_ref, win_ref, out_ref, over_ref, held, *, tiles, utts):
    step = pl.program_id(0)
    row, first = step // tiles, (step % tiles) * TILE
    base = meta[row, 2 * utts + 1] + first
    reach, _ = frame_reach(meta, row, base, TILE + EDGE, utts)

    @pl.when(step % tiles == 0)
    def _():
        held[:, 0:EDGE, :] = jnp.zeros((LAPS, EDGE, LAP_PAD), F32)

    for j in range(LAPS):
        span = slice(j * LAP_PAD, (j + 1) * LAP_PAD)
        piece = dot(spec_ref[...], synth_ref[:, span], NN) * win_ref[j : j + 1, :]
        held[j, EDGE : EDGE + TILE, :] = piece
        held[j, EDGE + TILE :, :] = jnp.zeros((EDGE, LAP_PAD), F32)
    total = held[0, EDGE:, :]
    for j in range(1, LAPS):
        moved = held[j, EDGE - j : EDGE - j + TILE + EDGE, :]
        total = total + jnp.where(lanes(reach >= j, LAP_PAD // 128), moved, 0.0)
    out_ref[0] = total[:TILE] * by_reach(reach[:TILE], win_ref, LAPS, LAP_PAD)
    over_ref[row] = total[TILE:]
    held[:, 0:EDGE, :] = held[:, TILE : TILE + EDGE, :]


def wave_forward(meta, spec, synth, win, rows, frames, utts):
    tiles = frames // TILE
    count = rows * frames
    shape = jax.ShapeDtypeStruct
    whole = pl.BlockSpec(memory_space=pltpu.VMEM)
    return pl.pallas_call(
        functools.partial(wave_body, tiles=tiles, utts=utts),
        grid=(rows * tiles,),
        in_specs=[
            pl.BlockSpec(memory_space=pltpu.SMEM),
            pl.BlockSpec((TILE, 2 * BIN_PAD), lambda i: (i, 0)),
            whole,
            whole,
        ],
        out_specs=[
            pl.BlockSpec((1, TILE, LAP_PAD), lambda i: (i // tiles, i % tiles, 0)),
            whole,
        ],
        out_shape=[shape((rows, frames, LAP_PAD), F32), shape((rows, EDGE, LAP_PAD), F32)],
        scratch_shapes=[pltpu.VMEM((LAPS, TILE + 2 * EDGE, LAP_PAD), F32)],
        compiler_params=pltpu.CompilerParams(vmem_limit_bytes=40 * MIB),
        cost_estimate=pl.CostEstimate(
            flops=2 * count * 1536 * 1536, bytes_accessed=16 * MIB, transcendentals=0
        ),
        name="wave_forward",
    )(meta, spec, synth, win)


def slot_body(places, *refs, bounds):
    count = len(bounds)
    outs = refs[2 * count :]
    slots = outs[0].shape[0]
    for index, out in enumerate(outs):

        def one(s, carry, out=out, index=index):
            bucket = places[0, index * slots + s]
            for (start, stop), keep, came in zip(bounds, refs[:count], refs[count : 2 * count]):

                @pl.when((bucket >= start) & (bucket < stop))
                def _(keep=keep, came=came, start=start):
                    out[s] = (keep[bucket - start].astype(F32) + came[bucket - start].astype(F32)).astype(BF16)

            @pl.when(bucket >= NB - 1)
            def _():
                out[s] = jnp.zeros(out.shape[1:], BF16)

            return carry

        lax.fori_loop(0, slots, one, 0)


def to_slots(places, keeps, cames, bounds, owners, slots):
    channels = keeps[0].shape[2]
    whole = pl.BlockSpec(memory_space=pltpu.VMEM)
    return pl.pallas_call(
        functools.partial(slot_body, bounds=bounds),
        in_specs=[pl.BlockSpec(memory_space=pltpu.SMEM)] + [whole] * (2 * len(bounds)),
        out_specs=[whole] * owners,
        out_shape=[jax.ShapeDtypeStruct((slots, QUART, channels), BF16)] * owners,
        compiler_params=pltpu.CompilerParams(vmem_limit_bytes=40 * MIB),
        cost_estimate=pl.CostEstimate(flops=0, bytes_accessed=8 * MIB, transcendentals=0),
        name="to_slots",
    )(places, *keeps, *cames)


def adam_body(places, grad_ref, last_ref, master, first, second, out_master, out_first, out_second):
    bucket = places[0, pl.program_id(0)]
    grad = grad_ref[0].astype(F32)
    grad = jnp.where(bucket == NB - 1, last_ref[...], grad)
    grad = jnp.where(bucket < NB, grad, 0.0)
    old = master[0]
    one = BETA_ONE * first[0] + (1.0 - BETA_ONE) * grad
    two = BETA_TWO * second[0] + (1.0 - BETA_TWO) * grad * grad
    one_fix = 1.0 / (1.0 - BETA_ONE**STEP_COUNT)
    two_fix = 1.0 / (1.0 - BETA_TWO**STEP_COUNT)
    out_first[0] = one
    out_second[0] = two
    out_master[0] = old - LEARN_RATE * (
        one * one_fix / (jnp.sqrt(two * two_fix) + ADAM_EPS) + WEIGHT_DECAY * old
    )


def adam(places, grad, last, master, first, second):
    slots, depth, channels = master.shape
    block = pl.BlockSpec((1, depth, channels), lambda i: (i, 0, 0))
    return pl.pallas_call(
        adam_body,
        grid=(slots,),
        in_specs=[
            pl.BlockSpec(memory_space=pltpu.SMEM),
            block,
            pl.BlockSpec(memory_space=pltpu.VMEM),
            block,
            block,
            block,
        ],
        out_specs=[block] * 3,
        out_shape=[jax.ShapeDtypeStruct(master.shape, F32)] * 3,
        compiler_params=pltpu.CompilerParams(vmem_limit_bytes=40 * MIB),
        cost_estimate=pl.CostEstimate(flops=0, bytes_accessed=12 * MIB, transcendentals=0),
        name="adam",
    )(places, grad, last, master, first, second)


def local(frames_in, lengths, bw_ids, owner_list, master, moment1, moment2, wave_grad):
    rows, frames, channels = frames_in.shape
    slots = master.shape[0]
    utts = lengths.shape[1]
    owners = lax.axis_size("rows")
    seqs = lax.axis_size("seq")
    row_at = lax.axis_index("rows")
    seq_at = lax.axis_index("seq")
    core, plane = seq_at % 2, seq_at // 2
    ring = ring_of(owners)

    bucket_index = jnp.arange(NB, dtype=jnp.int32)
    same = owner_list[None, :] == owner_list[:, None]
    rank = jnp.sum((same & (bucket_index[None, :] < bucket_index[:, None])).astype(jnp.int32), axis=1)
    place = owner_list * slots + rank

    def held_by(owner_ids):
        targets = (owner_ids[:, None] * slots + jnp.arange(slots, dtype=jnp.int32)[None, :]).reshape(-1)
        match = place[None, :] == targets[:, None]
        return (NB + jnp.sum(match.astype(jnp.int32) * (bucket_index[None, :] - NB), axis=1))[None, :]

    mine = lax.dynamic_slice_in_dim(master, core * HALF, HALF, axis=1).astype(BF16)
    if ring:
        order = jnp.asarray(ring, jnp.int32)
        where = jnp.sum(jnp.where(order == row_at, jnp.arange(owners, dtype=jnp.int32), 0))
        offsets = [0]
        pieces = [mine]
        ahead = back = mine
        for hop in range(owners // 2):
            ahead = lax.ppermute(ahead, AXES, ring_step(ring, 1, seqs))
            pieces.append(ahead)
            offsets.append(-(hop + 1))
            if hop < owners // 2 - 1:
                back = lax.ppermute(back, AXES, ring_step(ring, -1, seqs))
                pieces.append(back)
                offsets.append(hop + 1)
        at = (where + jnp.asarray(offsets, jnp.int32)) % owners
        owner_ids = jnp.sum(
            jnp.where(at[:, None] == jnp.arange(owners, dtype=jnp.int32)[None, :], order[None, :], 0), axis=1
        )
    else:
        pieces = [lax.all_gather(mine, "rows", axis=0, tiled=True)]
        owner_ids = jnp.arange(owners, dtype=jnp.int32)
    sources = []
    for piece in pieces:
        sources += [piece, seq_swap(piece, 1)]
    places = held_by(owner_ids)

    starts = [jnp.zeros((rows, 1), jnp.int32)]
    for u in range(utts):
        starts.append(starts[-1] + lengths[:, u : u + 1])
    spot = jnp.broadcast_to(jnp.stack([seq_at * frames, core])[None, :], (rows, 2)).astype(jnp.int32)
    meta = jnp.concatenate(starts + [bw_ids, spot], axis=1)

    low = shifted(frames_in[:, frames - RIM :], 1)
    high = shifted(frames_in[:, :RIM], -1)
    gap = jnp.zeros((rows, EDGE - RIM, channels), BF16)
    xpad = jnp.concatenate([gap, low, frames_in, high, gap], axis=1)
    blocks = wave_grad.reshape(rows, frames, HOP)
    later = shifted(blocks[:, : LAPS - 1], -1)
    wave = jnp.concatenate(
        [blocks, later, jnp.zeros((rows, 2 * EDGE - LAPS + 1, HOP), BF16)], axis=1
    )
    wave = jnp.pad(wave, ((0, 0), (0, 0), (0, LAP_PAD - HOP)))
    synth = jnp.asarray(synthesis_table())
    win = jnp.asarray(window_tables())

    cot = spectrum_cotangent(meta, wave, synth, win, rows, frames, utts)
    (table, spec, act, der, ada, low_grad, resg, xc, rc, send, keep, tail, sums, hsum) = forward(
        meta, places, xpad, cot, sources, rows, frames, utts
    )

    def seq_sum(send, keep):
        both = (keep.astype(F32) + seq_swap(send, 1).astype(F32)).astype(BF16)
        stay = lax.dynamic_slice_in_dim(both, plane * QUART, QUART, axis=1)
        leave = lax.dynamic_slice_in_dim(both, (1 - plane) * QUART, QUART, axis=1)
        return stay, seq_swap(leave, 2)

    keeps, cames, bounds = [], [], []
    stay, came = seq_sum(send, keep)
    keeps.append(stay)
    cames.append(came)
    bounds.append((2 * FF // BR, NB - 1))
    pres, bsums = [], []
    per = CHUNK // BR
    for chunk in range(FF // CHUNK):
        pre, send, keep, bsum = mlp_backward(chunk, meta, low_grad, act, der, ada, table, utts)
        pres.append(pre)
        bsums.append(bsum)
        stay, came = seq_sum(send, keep)
        for at in (0, 1):
            keeps.append(stay[at * per : (at + 1) * per])
            cames.append(came[at * per : (at + 1) * per])
            begin = at * FF // BR + chunk * per
            bounds.append((begin, begin + per))
    if ring:
        chunks = to_slots(places, keeps, cames, tuple(bounds), owners, slots)
        by_offset = dict(zip(offsets, chunks))
        half = owners // 2
        plus = lambda a, b: (a.astype(F32) + b.astype(F32)).astype(BF16)
        up = by_offset[-half]
        for hop in range(half - 1, -1, -1):
            up = lax.ppermute(up, AXES, ring_step(ring, 1, seqs))
            if hop:
                up = plus(up, by_offset[hop])
        down = by_offset[-(half - 1)]
        for hop in range(half - 2, -1, -1):
            down = lax.ppermute(down, AXES, ring_step(ring, -1, seqs))
            if hop:
                down = plus(down, by_offset[-hop])
        total = (by_offset[0].astype(F32) + up.astype(F32) + down.astype(F32)).astype(BF16)
    else:
        [chunks] = to_slots(places, keeps, cames, tuple(bounds), 1, owners * slots)
        total = lax.psum_scatter(chunks, "rows", scatter_dimension=0, tiled=True)
    other = seq_swap(total, 2)
    pair = jnp.where(plane == 0, jnp.concatenate([total, other], axis=1), jnp.concatenate([other, total], axis=1))
    other = seq_swap(pair, 1)
    full = jnp.where(core == 0, jnp.concatenate([pair, other], axis=1), jnp.concatenate([other, pair], axis=1))

    input_grad, edges, last = conv_backward(
        meta, xpad, pres, table, xc, rc, resg, tail, sums, hsum, bsums, rows, frames, utts
    )
    if ring:
        for bit in (1, 2):
            last = last + seq_swap(last, bit)
        for bit in (1, 2, 4):
            last = last + rows_swap(last, bit)
    else:
        last = lax.psum(last, AXES)
    index = seq_at * frames + jnp.arange(frames, dtype=jnp.int32)
    seg = jnp.sum((meta[:, None, 1:utts] <= index[None, :, None]).astype(jnp.int32), axis=2)
    taps = table[2 * FF + NOUT : 2 * FF + NOUT + KW].astype(F32)
    from_low = shifted(edges[:, 1, EDGE - RIM :], 1)
    from_high = shifted(edges[:, 0, :RIM], -1)
    seg_at = lambda i: jnp.sum((meta[:, 1:utts] <= i).astype(jnp.int32), axis=1)
    begin = seq_at * frames
    low_fix, high_fix = [], []
    for i in range(RIM):
        fix = jnp.zeros((rows, channels), F32)
        for k in range(KW):
            source = i - k + RIM
            if source < 0:
                same_seg = (seg_at(begin + source) == seg_at(begin + i)).astype(F32)
                fix = fix + taps[k] * same_seg[:, None] * from_low[:, source + RIM]
        low_fix.append(fix)
        fix = jnp.zeros((rows, channels), F32)
        here = frames - RIM + i
        for k in range(KW):
            source = here - k + RIM
            if source >= frames:
                same_seg = (seg_at(begin + source) == seg_at(begin + here)).astype(F32)
                fix = fix + taps[k] * same_seg[:, None] * from_high[:, source - frames]
        high_fix.append(fix)
    input_grad = input_grad.at[:, :RIM].add(jnp.stack(low_fix, axis=1))
    input_grad = input_grad.at[:, frames - RIM :].add(jnp.stack(high_fix, axis=1))

    out, over = wave_forward(meta, spec, synth, win, rows, frames, utts)
    arrived = shifted(over, 1)
    first_reach = []
    for b in range(LAPS - 1):
        i = begin + b
        start = jnp.max(jnp.where(meta[:, :utts] <= i, meta[:, :utts], 0), axis=1)
        first_reach.append(i - start)
    reach = jnp.stack(first_reach, axis=1)
    scale = jnp.broadcast_to(win[2 * LAPS - 1], (rows, LAPS - 1, LAP_PAD))
    for j in range(LAPS - 1):
        scale = jnp.where((reach == j)[:, :, None], win[LAPS + j], scale)
    out = out.at[:, : LAPS - 1].add(arrived[:, : LAPS - 1] * scale)
    waveform = out[:, :, :HOP].reshape(rows, frames * HOP)

    held = held_by(row_at[None].astype(jnp.int32))
    new_master, new_first, new_second = adam(held, full, last, master, moment1, moment2)
    return waveform, input_grad, new_master, new_first, new_second


def solution(mesh):
    in_specs = (
        P("rows", "seq", None),
        P("rows", None),
        P("rows", None),
        P(),
        P("rows", None, None),
        P("rows", None, None),
        P("rows", None, None),
        P("rows", "seq"),
    )
    out_specs = (
        P("rows", "seq"),
        P("rows", "seq", None),
        P("rows", None, None),
        P("rows", None, None),
        P("rows", None, None),
    )
    return jax.shard_map(local, mesh=mesh, in_specs=in_specs, out_specs=out_specs, check_vma=False)
```

time: 556 us -> 338 us (0.61); the launches traced: 546 us -> 336 us
  Pallas kernels: 0 us -> 164 us
  other arithmetic: 136 us -> 12.6 us
  matrix products: 119 us -> 0 us
  local copies, waits for them, and re-layouts: 133 us -> 55 us
  waiting for transfers between devices: 130 us -> 54.6 us
  starting transfers between devices: 12.2 us -> 48.4 us
  between operations: 15.7 us -> 1.44 us
    pallas_call x0 -> x9, Pallas kernels: none -> 164 us  [the longest x1 61.1 us: forward(): pl.pallas_call(functools.partial(forward_body, parts=len(sources), tiles=...]
    dot_general x15 -> x0, matrix products: 119 us -> none  [the longest x11 109 us: contract(): lax.dot_general(left_side, right_side, (((left_dim,), (right_dim,)), ((),...]
    psum x1 -> x0, waiting for transfers between devices: 104 us -> none  [local(): summed = lax.psum(grad_buckets, ('rows', 'seq'))]
    ppermute x6 -> x43, waiting for transfers between devices: 0.02 us -> 54.6 us  [the longest x4 21.3 us: local(): ahead = lax.ppermute(ahead, AXES, ring_step(ring, 1, seqs))]
    another operation x6 -> x1, other arithmetic: 50.9 us -> 0.08 us  [local(): jnp.stack([seq_at * frames, core])[None, :]]
    ppermute x6 -> x43, starting transfers between devices: 12.1 us -> 48.4 us  [the longest x6 13.6 us: shifted(): lax.ppermute(value, 'seq', [(i - distance, i) for i in devices if i - dis...]
    concatenate x3, local copies, waits for them, and re-layouts: 45.7 us -> 12.8 us  [the longest x1 6.7 us: local(): xpad = jnp.concatenate([gap, low, frames_in, high, gap], axis=1)]
    all_gather x1 -> x0, waiting for transfers between devices: 25.9 us -> none  [local(): lax.all_gather(master.astype(jnp.bfloat16), 'rows', axis=0, tiled=True)]
  transfers between devices with their start and end apart: 8 -> 43, of which waited for: 2 -> 13; matrix products, arithmetic and copies ran while one was open for 28% -> 12% of each run, Pallas kernels for 0% -> 12%
where the time goes in v1:
time: 338 us; the launch traced here: 336 us
  Pallas kernels  164 us (49%)
  local copies, waits for them, and re-layouts  55 us (16%)
  waiting for transfers between devices  54.6 us (16%)
  starting transfers between devices  48.4 us (14%)
  other arithmetic  12.6 us (4%)
    pallas_call x1, Pallas kernels, forward(): pl.pallas_call(functools.partial(forward_body, parts=len(sources), tiles=...  61.1 us
    pallas_call x1, Pallas kernels, conv_backward(): pl.pallas_call(functools.partial(conv_body, tiles=tiles, utts=utts), grid...  33.2 us
    unnamed x75, local copies, waits for them, and re-layouts  26.6 us
    ppermute x4, waiting for transfers between devices, local(): ahead = lax.ppermute(ahead, AXES, ring_step(ring, 1, seqs))  21.3 us
    pallas_call x3, Pallas kernels, mlp_backward(): pl.pallas_call(functools.partial(mlp_body, utts=utts), grid=(count // til...  18.1 us
    ppermute x20, waiting for transfers between devices, seq_swap(): return lax.ppermute(value, 'seq', [(s, s ^ bit) for s in range(count)])  17.9 us
    pallas_call x1, Pallas kernels, wave_forward(): pl.pallas_call(functools.partial(wave_body, tiles=tiles, utts=utts), grid...  16 us
    ppermute x4, waiting for transfers between devices, local(): up = lax.ppermute(up, AXES, ring_step(ring, 1, seqs))  15.2 us
  transfers between devices with their start and end apart: 43, of which 13 were waited for; matrix products, arithmetic and copies ran while one was open for 12% of the time, Pallas kernels for 12%

profile of v1, /device:TPU:0, one launch (start us, length us, event | category | flops | bytes accessed | tf_op | source)
XLA Modules:
  0.0 335.9 jit_solution(4016886572344388421)
XLA Ops:
  1.9 3.1 collective-permute-start.4
  5.0 2.3 reshape.863
  7.3 2.3 reshape.861
  12.4 3.0 collective-permute-start
  20.2 2.0 collective-permute-start.8
  22.3 9.8 %collective-permute-done.8.rest_6_ = bf16[27,16,512]{2,1,0:T(8,128)(2,1)} collective-permute-done((bf16[27,16,512]{2,1,0:T(8,128)(2,1)S(1)}, bf16[27,16,512]{2,1,0:T(8,128)(2,1)}, u32[]{:S(2)}, u32[]{:S(2)}) %collective-permute-start.8) | collective-permute-done | bytes 442400 | tf_op jit(solution)/shard_map/ppermute | solution.py:826
  32.1 2.5 collective-permute-start.12
  37.4 8.4 %collective-permute-done.12.rest_10_ = bf16[27,16,512]{2,1,0:T(8,128)(2,1)} collective-permute-done((bf16[27,16,512]{2,1,0:T(8,128)(2,1)}, bf16[27,16,512]{2,1,0:T(8,128)(2,1)}, u32[]{:S(2)}, u32[]{:S(2)}) %collective-permute-start.12) | collective-permute-done | bytes 442400 | tf_op jit(solution)/shard_map/ppermute | solution.py:826
  45.9 2.0 collective-permute-start.16
  47.9 6.0 %concatenate.47 = bf16[2,1040,320]{2,1,0:T(8,128)(2,1)S(1)} concatenate(bf16[2,1024,320]{2,1,0:T(8,128)(2,1)} %reshape.861, bf16[2,3,320]{2,1,0:T(4,128)(2,1)S(1)} %collective-permute-done.2, bf16[2,13,320]{2,1,0:T(8,128)(2,1)S(1)} %broadcast_in_dim.101), dimensions={1} | concatenate | bytes 2662400 | tf_op jit(solution)/shard_map/concatenate | solution.py:857
  55.3 3.1 collective-permute-done.16.rest_14_
  58.4 2.3 copy-done.16
  60.7 12.8 %spectrum_cotangent.1.cot_ref = bf16[2048,1536]{1,0:T(8,128)(2,1)S(1)} custom-call(s32[2,11]{1,0:T(2,128)S(1)} %concatenate.45.meta, bf16[2,1040,384]{2,1,0:T(8,128)(2,1)S(1)} %pad.10.wave_ref, bf16[1536,1536]{1,0:T(8,128)(2,1)S(1)} %copy-done.16, f32[8,384]{1,0:T(8,128)S(1)} %copy-done.18), custom_call_target="tpu_custom_call" | custom-call | flops 9663676416 | bytes 14680064 | tf_op jit(solution)/shard_map/spectrum_cotangent/pallas_call | solution.py:187
  73.6 2.7 copy-done.19
  76.3 6.7 %concatenate.46.x_ref = bf16[2,1040,512]{2,1,0:T(8,128)(2,1)} concatenate(bf16[2,5,512]{2,1,0:T(8,128)(2,1)S(1)} %broadcast_in_dim.100, bf16[2,3,512]{2,1,0:T(4,128)(2,1)S(1)} %collective-permute-done, bf16[2,1024,512]{2,1,0:T(8,128)(2,1)S(1)} %copy-done.21, bf16[2,3,512]{2,1,0:T(4,128)(2,1)S(1)} %collective-permute-done.1, bf16[2,5,512]{2,1,0:T(8,128)(2,1)S(1)} %broadcast_in_dim.100), dimensions={1} | concatenate | bytes 4259840 | tf_op jit(solution)/shard_map/concatenate | solution.py:854
  83.9 61.1 %forward.1 = (bf16[4384,512]{1,0:T(8,128)(2,1)}, bf16[2048,1536]{1,0:T(8,128)(2,1)}, bf16[2048,1536]{1,0:T(8,128)(2,1)}, bf16[2048,1536]{1,0:T(8,128)(2,1)}, bf1...) custom-call(s32[2,11]{1,0:T(2,128)} %copy-done.9, ...), custom_call_target="tpu_custom_call" | custom-call | flops 16106127360 | bytes 41943040 | tf_op jit(solution)/shard_map/forward/pallas_call | solution.py:405
  145.0 2.3 copy-done
  148.8 1.6 copy-done.2
  150.4 6.0 %mlp_backward_2.1 = (bf16[2048,512]{1,0:T(8,128)(2,1)S(1)}, bf16[32,16,512]{2,1,0:T(8,128)(2,1)S(1)}, bf16[32,16,512]{2,1,0:T(8,128)(2,1)S(1)}, f32[8,512]{1,0:T(8,128)S(1)}) custom-call(s32[2,11]{1,0:T(2,128)S(1)} %copy-done.10, bf16[2048,512]{1,0:T(8,128)(2,1)S(1)} %copy-done.2, bf16[2048,1536]{1,0:T(8,128)(2,1)} %get-tuple-element.87.act_ref, ...), custom_call_target="tpu_custom_call" | custom-call | flops 3221225472 | bytes 12582912 | tf_op jit(solution)/shard_map/mlp_backward_2/pallas_call | solution.py:481
  157.8 6.0 %mlp_backward_1.1 = (bf16[2048,512]{1,0:T(8,128)(2,1)S(1)}, bf16[32,16,512]{2,1,0:T(8,128)(2,1)S(1)}, bf16[32,16,512]{2,1,0:T(8,128)(2,1)S(1)}, f32[8,512]{1,0:T(8,128)S(1)}) custom-call(s32[2,11]{1,0:T(2,128)S(1)} %copy-done.10, bf16[2048,512]{1,0:T(8,128)(2,1)S(1)} %copy-done.2, bf16[2048,1536]{1,0:T(8,128)(2,1)} %get-tuple-element.87.act_ref, ...), custom_call_target="tpu_custom_call" | custom-call | flops 3221225472 | bytes 12582912 | tf_op jit(solution)/shard_map/mlp_backward_1/pallas_call | solution.py:481
  165.2 6.0 %mlp_backward_0.1 = (bf16[2048,512]{1,0:T(8,128)(2,1)S(1)}, bf16[32,16,512]{2,1,0:T(8,128)(2,1)S(1)}, bf16[32,16,512]{2,1,0:T(8,128)(2,1)S(1)}, f32[8,512]{1,0:T(8,128)S(1)}) custom-call(s32[2,11]{1,0:T(2,128)S(1)} %copy-done.10, bf16[2048,512]{1,0:T(8,128)(2,1)S(1)} %copy-done.2, bf16[2048,1536]{1,0:T(8,128)(2,1)} %get-tuple-element.87.act_ref, ...), custom_call_target="tpu_custom_call" | custom-call | flops 3221225472 | bytes 12582912 | tf_op jit(solution)/shard_map/mlp_backward_0/pallas_call | solution.py:481
  173.2 33.2 %conv_backward.1 = (f32[2,1024,512]{2,1,0:T(8,128)}, f32[2,2,8,512]{3,2,1,0:T(8,128)}, f32[32,512]{1,0:T(8,128)}) custom-call(s32[2,11]{1,0:T(2,128)} %copy-done.9, bf16[2,1040,512]{2,1,0:T(8,128)(2,1)} %concatenate.46.x_ref, bf16[2048,512]{1,0:T(8,128)(2,1)} %copy-done.6, bf16[2048,512]{1,0:T(8,128)(2,1)} %copy-done.5, bf16[2048,512]{1,0:T(8,128)(2,1)} %copy-done.4, ...), custom_call_target="tpu_custom_call" | custom-call | flops 3221225472 | bytes 25165824 | tf_op jit(solution)/shard_map/conv_backward/pallas_call | solution.py:642
  208.4 2.3 copy-done.17
  210.8 2.8 copy-done.20
  213.6 16.0 %wave_forward.1 = (f32[2,1024,384]{2,1,0:T(8,128)S(1)}, f32[2,8,384]{2,1,0:T(8,128)S(1)}) custom-call(s32[2,11]{1,0:T(2,128)S(1)} %copy-done.11, bf16[2048,1536]{1,0:T(8,128)(2,1)S(1)} %copy-done.20, bf16[1536,1536]{1,0:T(8,128)(2,1)S(1)} %copy-done.17, f32[8,384]{1,0:T(8,128)S(1)} %copy-done.18), custom_call_target="tpu_custom_call" | custom-call | flops 9663676416 | bytes 16777216 | tf_op jit(solution)/shard_map/wave_forward/pallas_call | solution.py:698
  232.5 3.0 collective-permute-start.19
  238.7 5.9 %collective-permute-done.28 = bf16[32,8,512]{2,1,0:T(8,128)(2,1)S(1)} collective-permute-done((bf16[32,8,512]{2,1,0:T(8,128)(2,1)S(1)}, bf16[32,8,512]{2,1,0:T(8,128)(2,1)S(1)}, u32[]{:S(2)}, u32[]{:S(2)}) %collective-permute-start.28) | collective-permute-done | bytes 262176 | tf_op jit(solution)/shard_map/ppermute | solution.py:87
  244.6 1.9 collective-permute-start.26
  246.6 3.7 %collective-permute-done.27 = bf16[32,8,512]{2,1,0:T(8,128)(2,1)S(1)} collective-permute-done((bf16[32,8,512]{2,1,0:T(8,128)(2,1)S(1)}, bf16[32,8,512]{2,1,0:T(8,128)(2,1)S(1)}, u32[]{:S(2)}, u32[]{:S(2)}) %collective-permute-start.27) | collective-permute-done | bytes 262176 | tf_op jit(solution)/shard_map/ppermute | solution.py:87
  250.2 1.9 collective-permute-start.25
  252.2 3.7 %collective-permute-done.26 = bf16[32,8,512]{2,1,0:T(8,128)(2,1)S(1)} collective-permute-done((bf16[32,8,512]{2,1,0:T(8,128)(2,1)S(1)}, bf16[32,8,512]{2,1,0:T(8,128)(2,1)S(1)}, u32[]{:S(2)}, u32[]{:S(2)}) %collective-permute-start.26) | collective-permute-done | bytes 262176 | tf_op jit(solution)/shard_map/ppermute | solution.py:87
  255.9 3.7 %collective-permute-start.18 = (f32[2,8,384]{2,1,0:T(8,128)S(1)}, f32[2,8,384]{2,1,0:T(8,128)}, u32[]{:S(2)}, u32[]{:S(2)}) collective-permute-start(f32[2,8,384]{2,1,0:T(8,128)S(1)} %get-tuple-element.85), channel_id=1, source_target_pairs={{0,1},{1,2},{2,3},{4,5},{5,6},{6,7},{8,9},{9,10},{10,11},{12,13},{... | collective-permute-start | bytes 73736 | tf_op jit(solution)/shard_map/ppermute | solution.py:97
  259.6 3.3 collective-permute-done.25.refs_7_
  262.9 12.2 %to_slots.1 = (bf16[27,8,512]{2,1,0:T(8,128)(2,1)S(1)}, bf16[27,8,512]{2,1,0:T(8,128)(2,1)S(1)}, bf16[27,8,512]{2,1,0:T(8,128)(2,1)S(1)}, bf16[27,8,512]{2,1,0:T...) custom-call(s32[1,216]{1,0:T(1,128)S(1)} %bitcast.24, ...), custom_call_target="tpu_custom_call" | custom-call | bytes 8388608 | tf_op jit(solution)/shard_map/to_slots/pallas_call | solution.py:747
  275.1 2.6 collective-permute-start.29
  279.1 4.0 %collective-permute-done.29 = bf16[27,8,512]{2,1,0:T(8,128)(2,1)S(1)} collective-permute-done((bf16[27,8,512]{2,1,0:T(8,128)(2,1)S(1)}, bf16[27,8,512]{2,1,0:T(8,128)(2,1)S(1)}, u32[]{:S(2)}, u32[]{:S(2)}) %collective-permute-start.29) | collective-permute-done | bytes 221216 | tf_op jit(solution)/shard_map/ppermute | solution.py:899
  283.1 2.2 collective-permute-start.30
  285.8 4.3 %collective-permute-done.30 = bf16[27,8,512]{2,1,0:T(8,128)(2,1)S(1)} collective-permute-done((bf16[27,8,512]{2,1,0:T(8,128)(2,1)S(1)}, bf16[27,8,512]{2,1,0:T(8,128)(2,1)S(1)}, u32[]{:S(2)}, u32[]{:S(2)}) %collective-permute-start.30) | collective-permute-done | bytes 221216 | tf_op jit(solution)/shard_map/ppermute | solution.py:899
  290.2 1.8 collective-permute-start.31
  292.4 3.9 %collective-permute-done.31 = bf16[27,8,512]{2,1,0:T(8,128)(2,1)S(1)} collective-permute-done((bf16[27,8,512]{2,1,0:T(8,128)(2,1)S(1)}, bf16[27,8,512]{2,1,0:T(8,128)(2,1)S(1)}, u32[]{:S(2)}, u32[]{:S(2)}) %collective-permute-start.31) | collective-permute-done | bytes 221216 | tf_op jit(solution)/shard_map/ppermute | solution.py:899
  296.4 1.8 collective-permute-start.32
  299.3 3.0 collective-permute-done.32
  305.0 2.2 collective-permute-start.41
  308.6 2.0 maximum_select_fusion.1
  312.7 2.5 collective-permute-start.42
  316.3 4.1 %reshape.862 = f32[2,327680]{1,0:T(2,128)} reshape(f32[2,1024,320]{2,1,0:T(8,128)S(1)} %bitcast.22) | data formatting | bytes 5242880 | tf_op jit(solution)/shard_map/reshape | solution.py:965
  320.4 1.8 maximum_select_fusion.grad_ref
  325.4 10.5 %adam.1 = (f32[27,32,512]{2,1,0:T(8,128)}, f32[27,32,512]{2,1,0:T(8,128)}, f32[27,32,512]{2,1,0:T(8,128)}) custom-call(s32[1,27]{1,0:T(1,128)S(1)} %add_bitcast_fusion.places, bf16[27,32,512]{2,1,0:T(8,128)(2,1)S(1)} %maximum_select_fusion.grad_ref, f32[32,512]{1,0:T(8,128)S(1)} %add.310.last_ref, f32[27,32,512]{2,1,0:T(8,128)S(1)} %copy-done.3, ...), custom_call_target="tpu_custom_call" | custom-call | bytes 12582912 | tf_op jit(solution)/shard_map/adam/pallas_call | solution.py:778
  (200 shorter events, 42.0 us)
Async XLA Ops:
  1.9 34.4 %copy-start.23 = (bf16[27,16,512]{2,1,0:T(8,128)(2,1)}, bf16[27,16,512]{2,1,0:T(8,128)(2,1)S(1)}, u32[]{:S(2)}) copy-start(bf16[27,16,512]{2,1,0:T(8,128)(2,1)S(1)} %dynamic-slice_convert_fusion.rest_0_) | copy-start | bytes 1327108
  1.9 18.3 %collective-permute-start.4 = (bf16[27,16,512]{2,1,0:T(8,128)(2,1)S(1)}, bf16[27,16,512]{2,1,0:T(8,128)(2,1)S(1)}, u32[]{:S(2)}, u32[]{:S(2)}) collective-permute-start(bf16[27,16,512]{2,1,0:T(8,128)(2,1)S(1)} %dynamic-slice_convert_fusion.rest_0_), channel_id=1, source_target_pairs={{0,8},{1,9},{2,10},{3,11},{8,16},{9,17},{10,18},{11,19},{16,24},{1... | collective-permute-start | bytes 1327112 | tf_op jit(solution)/shard_map/ppermute | solution.py:826
  5.0 17.3 %collective-permute-start.6 = (bf16[27,16,512]{2,1,0:T(8,128)(2,1)S(1)}, bf16[27,16,512]{2,1,0:T(8,128)(2,1)S(1)}, u32[]{:S(2)}, u32[]{:S(2)}) collective-permute-start(bf16[27,16,512]{2,1,0:T(8,128)(2,1)S(1)} %dynamic-slice_convert_fusion.rest_0_), channel_id=1, source_target_pairs={{0,4},{1,5},{2,6},{3,7},{8,0},{9,1},{10,2},{11,3},{16,8},{17,9},{1... | collective-permute-start | bytes 1327112 | tf_op jit(solution)/shard_map/ppermute | solution.py:830
  10.3 25.9 %collective-permute-start.2 = (bf16[2,3,320]{2,1,0:T(4,128)(2,1)S(1)}, bf16[2,3,320]{2,1,0:T(4,128)(2,1)S(1)}, u32[]{:S(2)}, u32[]{:S(2)}) collective-permute-start(bf16[2,3,320]{2,1,0:T(4,128)(2,1)S(1)} %slice.297), channel_id=1, source_target_pairs={{1,0},{2,1},{3,2},{5,4},{6,5},{7,6},{9,8},{10,9},{11,10},{13,12},{... | collective-permute-start | bytes 11528 | tf_op jit(solution)/shard_map/ppermute | solution.py:97
  12.4 24.5 %collective-permute-start = (bf16[2,3,512]{2,1,0:T(4,128)(2,1)S(1)}, bf16[2,3,512]{2,1,0:T(4,128)(2,1)S(1)}, u32[]{:S(2)}, u32[]{:S(2)}) collective-permute-start(bf16[2,3,512]{2,1,0:T(4,128)(2,1)S(1)} %get-tuple-element.143), channel_id=1, source_target_pairs={{0,1},{1,2},{2,3},{4,5},{5,6},{6,7},{8,9},{9,10},{10,11},{12,13},{... | collective-permute-start | bytes 18440 | tf_op jit(solution)/shard_map/ppermute | solution.py:97
  15.4 21.6 %collective-permute-start.1 = (bf16[2,3,512]{2,1,0:T(4,128)(2,1)S(1)}, bf16[2,3,512]{2,1,0:T(4,128)(2,1)S(1)}, u32[]{:S(2)}, u32[]{:S(2)}) collective-permute-start(bf16[2,3,512]{2,1,0:T(4,128)(2,1)S(1)} %get-tuple-element.142), channel_id=1, source_target_pairs={{1,0},{2,1},{3,2},{5,4},{6,5},{7,6},{9,8},{10,9},{11,10},{13,12},{... | collective-permute-start | bytes 18440 | tf_op jit(solution)/shard_map/ppermute | solution.py:97
  20.2 33.9 %copy-start.31 = (bf16[27,16,512]{2,1,0:T(8,128)(2,1)}, bf16[27,16,512]{2,1,0:T(8,128)(2,1)S(1)}, u32[]{:S(2)}) copy-start(bf16[27,16,512]{2,1,0:T(8,128)(2,1)S(1)} %collective-permute-done.4.rest_2_) | copy-start | bytes 1327108
  20.2 11.9 %collective-permute-start.8 = (bf16[27,16,512]{2,1,0:T(8,128)(2,1)S(1)}, bf16[27,16,512]{2,1,0:T(8,128)(2,1)}, u32[]{:S(2)}, u32[]{:S(2)}) collective-permute-start(bf16[27,16,512]{2,1,0:T(8,128)(2,1)S(1)} %collective-permute-done.4.rest_2_), channel_id=1, source_target_pairs={{0,8},{1,9},{2,10},{3,11},{8,16},{9,17},{10,18},{11,19},{16,24},{1... | collective-permute-start | bytes 1327112 | tf_op jit(solution)/shard_map/ppermute | solution.py:826
  22.3 15.2 %collective-permute-start.10 = (bf16[27,16,512]{2,1,0:T(8,128)(2,1)S(1)}, bf16[27,16,512]{2,1,0:T(8,128)(2,1)}, u32[]{:S(2)}, u32[]{:S(2)}) collective-permute-start(bf16[27,16,512]{2,1,0:T(8,128)(2,1)S(1)} %collective-permute-done.6.rest_4_), channel_id=1, source_target_pairs={{0,4},{1,5},{2,6},{3,7},{8,0},{9,1},{10,2},{11,3},{16,8},{17,9},{1... | collective-permute-start | bytes 1327112 | tf_op jit(solution)/shard_map/ppermute | solution.py:830
  32.1 13.8 %collective-permute-start.12 = (bf16[27,16,512]{2,1,0:T(8,128)(2,1)}, bf16[27,16,512]{2,1,0:T(8,128)(2,1)}, u32[]{:S(2)}, u32[]{:S(2)}) collective-permute-start(bf16[27,16,512]{2,1,0:T(8,128)(2,1)} %collective-permute-done.8.rest_6_), channel_id=1, source_target_pairs={{0,8},{1,9},{2,10},{3,11},{8,16},{9,17},{10,18},{11,19},{16,24},{1... | collective-permute-start | bytes 1327112 | tf_op jit(solution)/shard_map/ppermute | solution.py:826
  36.2 17.9 %collective-permute-start.3 = (bf16[27,16,512]{2,1,0:T(8,128)(2,1)S(1)}, bf16[27,16,512]{2,1,0:T(8,128)(2,1)}, u32[]{:S(2)}, u32[]{:S(2)}) collective-permute-start(bf16[27,16,512]{2,1,0:T(8,128)(2,1)S(1)} %dynamic-slice_convert_fusion.rest_0_), channel_id=1, source_target_pairs={{0,1},{1,0},{2,3},{3,2},{4,5},{5,4},{6,7},{7,6},{8,9},{9,8},{10,11... | collective-permute-start | bytes 1327112 | tf_op jit(solution)/shard_map/ppermute | solution.py:87
  36.9 17.3 %collective-permute-start.5 = (bf16[27,16,512]{2,1,0:T(8,128)(2,1)S(1)}, bf16[27,16,512]{2,1,0:T(8,128)(2,1)}, u32[]{:S(2)}, u32[]{:S(2)}) collective-permute-start(bf16[27,16,512]{2,1,0:T(8,128)(2,1)S(1)} %collective-permute-done.4.rest_2_), channel_id=1, source_target_pairs={{0,1},{1,0},{2,3},{3,2},{4,5},{5,4},{6,7},{7,6},{8,9},{9,8},{10,11... | collective-permute-start | bytes 1327112 | tf_op jit(solution)/shard_map/ppermute | solution.py:87
  37.0 17.8 %collective-permute-start.7 = (bf16[27,16,512]{2,1,0:T(8,128)(2,1)S(1)}, bf16[27,16,512]{2,1,0:T(8,128)(2,1)}, u32[]{:S(2)}, u32[]{:S(2)}) collective-permute-start(bf16[27,16,512]{2,1,0:T(8,128)(2,1)S(1)} %collective-permute-done.6.rest_4_), channel_id=1, source_target_pairs={{0,1},{1,0},{2,3},{3,2},{4,5},{5,4},{6,7},{7,6},{8,9},{9,8},{10,11... | collective-permute-start | bytes 1327112 | tf_op jit(solution)/shard_map/ppermute | solution.py:87
  37.4 17.4 %collective-permute-start.14 = (bf16[27,16,512]{2,1,0:T(8,128)(2,1)}, bf16[27,16,512]{2,1,0:T(8,128)(2,1)}, u32[]{:S(2)}, u32[]{:S(2)}) collective-permute-start(bf16[27,16,512]{2,1,0:T(8,128)(2,1)} %collective-permute-done.10.rest_8_), channel_id=1, source_target_pairs={{0,4},{1,5},{2,6},{3,7},{8,0},{9,1},{10,2},{11,3},{16,8},{17,9},{1... | collective-permute-start | bytes 1327112 | tf_op jit(solution)/shard_map/ppermute | solution.py:830
  45.9 12.5 %collective-permute-start.16 = (bf16[27,16,512]{2,1,0:T(8,128)(2,1)}, bf16[27,16,512]{2,1,0:T(8,128)(2,1)}, u32[]{:S(2)}, u32[]{:S(2)}) collective-permute-start(bf16[27,16,512]{2,1,0:T(8,128)(2,1)} %collective-permute-done.12.rest_10_), channel_id=1, source_target_pairs={{0,8},{1,9},{2,10},{3,11},{8,16},{9,17},{10,18},{11,19},{16,24},{1... | collective-permute-start | bytes 1327112 | tf_op jit(solution)/shard_map/ppermute | solution.py:826
  54.2 28.8 %collective-permute-start.11 = (bf16[27,16,512]{2,1,0:T(8,128)(2,1)}, bf16[27,16,512]{2,1,0:T(8,128)(2,1)S(1)}, u32[]{:S(2)}, u32[]{:S(2)}) collective-permute-start(bf16[27,16,512]{2,1,0:T(8,128)(2,1)} %collective-permute-done.10.rest_8_), channel_id=1, source_target_pairs={{0,1},{1,0},{2,3},{3,2},{4,5},{5,4},{6,7},{7,6},{8,9},{9,8},{10,11... | collective-permute-start | bytes 1327112 | tf_op jit(solution)/shard_map/ppermute | solution.py:87
  54.3 28.7 %collective-permute-start.9 = (bf16[27,16,512]{2,1,0:T(8,128)(2,1)}, bf16[27,16,512]{2,1,0:T(8,128)(2,1)S(1)}, u32[]{:S(2)}, u32[]{:S(2)}) collective-permute-start(bf16[27,16,512]{2,1,0:T(8,128)(2,1)} %collective-permute-done.8.rest_6_), channel_id=1, source_target_pairs={{0,1},{1,0},{2,3},{3,2},{4,5},{5,4},{6,7},{7,6},{8,9},{9,8},{10,11... | collective-permute-start | bytes 1327112 | tf_op jit(solution)/shard_map/ppermute | solution.py:87
  54.8 28.2 %collective-permute-start.13 = (bf16[27,16,512]{2,1,0:T(8,128)(2,1)}, bf16[27,16,512]{2,1,0:T(8,128)(2,1)}, u32[]{:S(2)}, u32[]{:S(2)}) collective-permute-start(bf16[27,16,512]{2,1,0:T(8,128)(2,1)} %collective-permute-done.12.rest_10_), channel_id=1, source_target_pairs={{0,1},{1,0},{2,3},{3,2},{4,5},{5,4},{6,7},{7,6},{8,9},{9,8},{10,11... | collective-permute-start | bytes 1327112 | tf_op jit(solution)/shard_map/ppermute | solution.py:87
  54.9 28.1 %collective-permute-start.15 = (bf16[27,16,512]{2,1,0:T(8,128)(2,1)}, bf16[27,16,512]{2,1,0:T(8,128)(2,1)}, u32[]{:S(2)}, u32[]{:S(2)}) collective-permute-start(bf16[27,16,512]{2,1,0:T(8,128)(2,1)} %collective-permute-done.14.rest_12_), channel_id=1, source_target_pairs={{0,1},{1,0},{2,3},{3,2},{4,5},{5,4},{6,7},{7,6},{8,9},{9,8},{10,11... | collective-permute-start | bytes 1327112 | tf_op jit(solution)/shard_map/ppermute | solution.py:87
  58.4 24.6 %collective-permute-start.17 = (bf16[27,16,512]{2,1,0:T(8,128)(2,1)}, bf16[27,16,512]{2,1,0:T(8,128)(2,1)}, u32[]{:S(2)}, u32[]{:S(2)}) collective-permute-start(bf16[27,16,512]{2,1,0:T(8,128)(2,1)} %collective-permute-done.16.rest_14_), channel_id=1, source_target_pairs={{0,1},{1,0},{2,3},{3,2},{4,5},{5,4},{6,7},{7,6},{8,9},{9,8},{10,11... | collective-permute-start | bytes 1327112 | tf_op jit(solution)/shard_map/ppermute | solution.py:87
  83.9 61.1 %copy-start.10 = (s32[2,11]{1,0:T(2,128)S(1)}, s32[2,11]{1,0:T(2,128)}, u32[]{:S(2)}) copy-start(s32[2,11]{1,0:T(2,128)} %copy-done.9) | copy-start | bytes 268
  173.2 35.2 %copy-start.11 = (s32[2,11]{1,0:T(2,128)S(1)}, s32[2,11]{1,0:T(2,128)}, u32[]{:S(2)}) copy-start(s32[2,11]{1,0:T(2,128)} %copy-done.9) | copy-start | bytes 268
  206.4 71.4 %collective-permute-start.38 = (f32[32,512]{1,0:T(8,128)}, f32[32,512]{1,0:T(8,128)S(1)}, u32[]{:S(2)}, u32[]{:S(2)}) collective-permute-start(f32[32,512]{1,0:T(8,128)} %get-tuple-element.121), channel_id=1, source_target_pairs={{0,1},{1,0},{2,3},{3,2},{4,5},{5,4},{6,7},{7,6},{8,9},{9,8},{10,11... | collective-permute-start | bytes 196616 | tf_op jit(solution)/shard_map/ppermute | solution.py:87
  206.7 24.4 %collective-permute-start.24 = (bf16[32,16,512]{2,1,0:T(8,128)(2,1)S(1)}, bf16[32,16,512]{2,1,0:T(8,128)(2,1)S(1)}, u32[]{:S(2)}, u32[]{:S(2)}) collective-permute-start(bf16[32,16,512]{2,1,0:T(8,128)(2,1)S(1)} %get-tuple-element.112), channel_id=1, source_target_pairs={{0,1},{1,0},{2,3},{3,2},{4,5},{5,4},{6,7},{7,6},{8,9},{9,8},{10,11... | collective-permute-start | bytes 1572872 | tf_op jit(solution)/shard_map/ppermute | solution.py:87
  207.0 25.5 %collective-permute-start.23 = (bf16[32,16,512]{2,1,0:T(8,128)(2,1)S(1)}, bf16[32,16,512]{2,1,0:T(8,128)(2,1)S(1)}, u32[]{:S(2)}, u32[]{:S(2)}) collective-permute-start(bf16[32,16,512]{2,1,0:T(8,128)(2,1)S(1)} %get-tuple-element.110), channel_id=1, source_target_pairs={{0,1},{1,0},{2,3},{3,2},{4,5},{5,4},{6,7},{7,6},{8,9},{9,8},{10,11... | collective-permute-start | bytes 1572872 | tf_op jit(solution)/shard_map/ppermute | solution.py:87
  207.2 28.7 %collective-permute-start.22 = (bf16[32,16,512]{2,1,0:T(8,128)(2,1)S(1)}, bf16[32,16,512]{2,1,0:T(8,128)(2,1)S(1)}, u32[]{:S(2)}, u32[]{:S(2)}) collective-permute-start(bf16[32,16,512]{2,1,0:T(8,128)(2,1)S(1)} %get-tuple-element.108), channel_id=1, source_target_pairs={{0,1},{1,0},{2,3},{3,2},{4,5},{5,4},{6,7},{7,6},{8,9},{9,8},{10,11... | collective-permute-start | bytes 1572872 | tf_op jit(solution)/shard_map/ppermute | solution.py:87
  207.5 30.2 %collective-permute-start.21 = (bf16[40,16,512]{2,1,0:T(8,128)(2,1)}, bf16[40,16,512]{2,1,0:T(8,128)(2,1)S(1)}, u32[]{:S(2)}, u32[]{:S(2)}) collective-permute-start(bf16[40,16,512]{2,1,0:T(8,128)(2,1)} %get-tuple-element.106), channel_id=1, source_target_pairs={{0,1},{1,0},{2,3},{3,2},{4,5},{5,4},{6,7},{7,6},{8,9},{9,8},{10,11... | collective-permute-start | bytes 1966088 | tf_op jit(solution)/shard_map/ppermute | solution.py:87
  231.0 71.6 %collective-permute-start.20 = (f32[2,3,512]{2,1,0:T(4,128)S(1)}, f32[2,3,512]{2,1,0:T(4,128)S(1)}, u32[]{:S(2)}, u32[]{:S(2)}) collective-permute-start(f32[2,3,512]{2,1,0:T(4,128)S(1)} %slice_bitcast_fusion.1), channel_id=1, source_target_pairs={{1,0},{2,1},{3,2},{5,4},{6,5},{7,6},{9,8},{10,9},{11,10},{13,12},{... | collective-permute-start | bytes 36872 | tf_op jit(solution)/shard_map/ppermute | solution.py:97
  232.5 45.2 %collective-permute-start.19 = (f32[2,3,512]{2,1,0:T(4,128)S(1)}, f32[2,3,512]{2,1,0:T(4,128)S(1)}, u32[]{:S(2)}, u32[]{:S(2)}) collective-permute-start(f32[2,3,512]{2,1,0:T(4,128)S(1)} %slice_bitcast_fusion), channel_id=1, source_target_pairs={{0,1},{1,2},{2,3},{4,5},{5,6},{6,7},{8,9},{9,10},{10,11},{12,13},{... | collective-permute-start | bytes 36872 | tf_op jit(solution)/shard_map/ppermute | solution.py:97
  235.9 8.7 %collective-permute-start.28 = (bf16[32,8,512]{2,1,0:T(8,128)(2,1)S(1)}, bf16[32,8,512]{2,1,0:T(8,128)(2,1)S(1)}, u32[]{:S(2)}, u32[]{:S(2)}) collective-permute-start(bf16[32,8,512]{2,1,0:T(8,128)(2,1)S(1)} %constant_dynamic-slice_fusion.1), channel_id=1, source_target_pairs={{0,2},{1,3},{2,0},{3,1},{4,6},{5,7},{6,4},{7,5},{8,10},{9,11},{10,... | collective-permute-start | bytes 786440 | tf_op jit(solution)/shard_map/ppermute | solution.py:87
  237.7 12.5 %collective-permute-start.27 = (bf16[32,8,512]{2,1,0:T(8,128)(2,1)S(1)}, bf16[32,8,512]{2,1,0:T(8,128)(2,1)S(1)}, u32[]{:S(2)}, u32[]{:S(2)}) collective-permute-start(bf16[32,8,512]{2,1,0:T(8,128)(2,1)S(1)} %constant_dynamic-slice_fusion.2), channel_id=1, source_target_pairs={{0,2},{1,3},{2,0},{3,1},{4,6},{5,7},{6,4},{7,5},{8,10},{9,11},{10,... | collective-permute-start | bytes 786440 | tf_op jit(solution)/shard_map/ppermute | solution.py:87
  238.7 39.2 %copy-start.24 = (f32[32,512]{1,0:T(8,128)S(1)}, f32[32,512]{1,0:T(8,128)}, u32[]{:S(2)}) copy-start(f32[32,512]{1,0:T(8,128)} %get-tuple-element.121) | copy-start | bytes 196612
  244.6 11.2 %collective-permute-start.26 = (bf16[32,8,512]{2,1,0:T(8,128)(2,1)S(1)}, bf16[32,8,512]{2,1,0:T(8,128)(2,1)S(1)}, u32[]{:S(2)}, u32[]{:S(2)}) collective-permute-start(bf16[32,8,512]{2,1,0:T(8,128)(2,1)S(1)} %constant_dynamic-slice_fusion.3), channel_id=1, source_target_pairs={{0,2},{1,3},{2,0},{3,1},{4,6},{5,7},{6,4},{7,5},{8,10},{9,11},{10,... | collective-permute-start | bytes 786440 | tf_op jit(solution)/shard_map/ppermute | solution.py:87
  250.2 12.6 %collective-permute-start.25 = (bf16[40,8,512]{2,1,0:T(8,128)(2,1)S(1)}, bf16[40,8,512]{2,1,0:T(8,128)(2,1)S(1)}, u32[]{:S(2)}, u32[]{:S(2)}) collective-permute-start(bf16[40,8,512]{2,1,0:T(8,128)(2,1)S(1)} %get-tuple-element.144), channel_id=1, source_target_pairs={{0,2},{1,3},{2,0},{3,1},{4,6},{5,7},{6,4},{7,5},{8,10},{9,11},{10,... | collective-permute-start | bytes 983048 | tf_op jit(solution)/shard_map/ppermute | solution.py:87
  255.9 59.4 %collective-permute-start.18 = (f32[2,8,384]{2,1,0:T(8,128)S(1)}, f32[2,8,384]{2,1,0:T(8,128)}, u32[]{:S(2)}, u32[]{:S(2)}) collective-permute-start(f32[2,8,384]{2,1,0:T(8,128)S(1)} %get-tuple-element.85), channel_id=1, source_target_pairs={{0,1},{1,2},{2,3},{4,5},{5,6},{6,7},{8,9},{9,10},{10,11},{12,13},{... | collective-permute-start | bytes 73736 | tf_op jit(solution)/shard_map/ppermute | solution.py:97
  275.1 7.9 %collective-permute-start.29 = (bf16[27,8,512]{2,1,0:T(8,128)(2,1)S(1)}, bf16[27,8,512]{2,1,0:T(8,128)(2,1)S(1)}, u32[]{:S(2)}, u32[]{:S(2)}) collective-permute-start(bf16[27,8,512]{2,1,0:T(8,128)(2,1)S(1)} %get-tuple-element.114), channel_id=1, source_target_pairs={{0,8},{1,9},{2,10},{3,11},{8,16},{9,17},{10,18},{11,19},{16,24},{1... | collective-permute-start | bytes 663560 | tf_op jit(solution)/shard_map/ppermute | solution.py:899
  277.9 21.0 %collective-permute-start.39 = (f32[32,512]{1,0:T(8,128)S(1)}, f32[32,512]{1,0:T(8,128)S(1)}, u32[]{:S(2)}, u32[]{:S(2)}) collective-permute-start(f32[32,512]{1,0:T(8,128)S(1)} %add.306), channel_id=1, source_target_pairs={{0,2},{1,3},{2,0},{3,1},{4,6},{5,7},{6,4},{7,5},{8,10},{9,11},{10,... | collective-permute-start | bytes 196616 | tf_op jit(solution)/shard_map/ppermute | solution.py:87
  279.1 6.3 %collective-permute-start.33 = (bf16[27,8,512]{2,1,0:T(8,128)(2,1)S(1)}, bf16[27,8,512]{2,1,0:T(8,128)(2,1)S(1)}, u32[]{:S(2)}, u32[]{:S(2)}) collective-permute-start(bf16[27,8,512]{2,1,0:T(8,128)(2,1)S(1)} %get-tuple-element.118), channel_id=1, source_target_pairs={{0,4},{1,5},{2,6},{3,7},{8,0},{9,1},{10,2},{11,3},{16,8},{17,9},{1... | collective-permute-start | bytes 663560 | tf_op jit(solution)/shard_map/ppermute | solution.py:904
  283.1 7.0 %collective-permute-start.30 = (bf16[27,8,512]{2,1,0:T(8,128)(2,1)S(1)}, bf16[27,8,512]{2,1,0:T(8,128)(2,1)S(1)}, u32[]{:S(2)}, u32[]{:S(2)}) collective-permute-start(bf16[27,8,512]{2,1,0:T(8,128)(2,1)S(1)} %add_convert_fusion.9), channel_id=1, source_target_pairs={{0,8},{1,9},{2,10},{3,11},{8,16},{9,17},{10,18},{11,19},{16,24},{1... | collective-permute-start | bytes 663560 | tf_op jit(solution)/shard_map/ppermute | solution.py:899
  285.5 6.6 %collective-permute-start.34 = (bf16[27,8,512]{2,1,0:T(8,128)(2,1)S(1)}, bf16[27,8,512]{2,1,0:T(8,128)(2,1)S(1)}, u32[]{:S(2)}, u32[]{:S(2)}) collective-permute-start(bf16[27,8,512]{2,1,0:T(8,128)(2,1)S(1)} %add_convert_fusion.6), channel_id=1, source_target_pairs={{0,4},{1,5},{2,6},{3,7},{8,0},{9,1},{10,2},{11,3},{16,8},{17,9},{1... | collective-permute-start | bytes 663560 | tf_op jit(solution)/shard_map/ppermute | solution.py:904
  290.2 6.1 %collective-permute-start.31 = (bf16[27,8,512]{2,1,0:T(8,128)(2,1)S(1)}, bf16[27,8,512]{2,1,0:T(8,128)(2,1)S(1)}, u32[]{:S(2)}, u32[]{:S(2)}) collective-permute-start(bf16[27,8,512]{2,1,0:T(8,128)(2,1)S(1)} %add_convert_fusion.8), channel_id=1, source_target_pairs={{0,8},{1,9},{2,10},{3,11},{8,16},{9,17},{10,18},{11,19},{16,24},{1... | collective-permute-start | bytes 663560 | tf_op jit(solution)/shard_map/ppermute | solution.py:899
  292.1 7.2 %collective-permute-start.35 = (bf16[27,8,512]{2,1,0:T(8,128)(2,1)S(1)}, bf16[27,8,512]{2,1,0:T(8,128)(2,1)S(1)}, u32[]{:S(2)}, u32[]{:S(2)}) collective-permute-start(bf16[27,8,512]{2,1,0:T(8,128)(2,1)S(1)} %add_convert_fusion.5), channel_id=1, source_target_pairs={{0,4},{1,5},{2,6},{3,7},{8,0},{9,1},{10,2},{11,3},{16,8},{17,9},{1... | collective-permute-start | bytes 663560 | tf_op jit(solution)/shard_map/ppermute | solution.py:904
  296.4 6.0 %collective-permute-start.32 = (bf16[27,8,512]{2,1,0:T(8,128)(2,1)S(1)}, bf16[27,8,512]{2,1,0:T(8,128)(2,1)S(1)}, u32[]{:S(2)}, u32[]{:S(2)}) collective-permute-start(bf16[27,8,512]{2,1,0:T(8,128)(2,1)S(1)} %add_convert_fusion.7), channel_id=1, source_target_pairs={{0,8},{1,9},{2,10},{3,11},{8,16},{9,17},{10,18},{11,19},{16,24},{1... | collective-permute-start | bytes 663560 | tf_op jit(solution)/shard_map/ppermute | solution.py:899
  298.9 5.2 %collective-permute-start.40 = (f32[32,512]{1,0:T(8,128)S(1)}, f32[32,512]{1,0:T(8,128)}, u32[]{:S(2)}, u32[]{:S(2)}) collective-permute-start(f32[32,512]{1,0:T(8,128)S(1)} %add.307), channel_id=1, source_target_pairs={{0,4},{4,0},{8,12},{12,8},{16,20},{20,16},{24,28},{28,24},{1,5},{5... | collective-permute-start | bytes 196616 | tf_op jit(solution)/shard_map/ppermute | solution.py:92
  302.4 6.1 %collective-permute-start.36 = (bf16[27,8,512]{2,1,0:T(8,128)(2,1)S(1)}, bf16[27,8,512]{2,1,0:T(8,128)(2,1)}, u32[]{:S(2)}, u32[]{:S(2)}) collective-permute-start(bf16[27,8,512]{2,1,0:T(8,128)(2,1)S(1)} %add_convert_fusion.4), channel_id=1, source_target_pairs={{0,2},{1,3},{2,0},{3,1},{4,6},{5,7},{6,4},{7,5},{8,10},{9,11},{10,... | collective-permute-start | bytes 663560 | tf_op jit(solution)/shard_map/ppermute | solution.py:87
  305.0 7.7 %collective-permute-start.41 = (f32[32,512]{1,0:T(8,128)S(1)}, f32[32,512]{1,0:T(8,128)S(1)}, u32[]{:S(2)}, u32[]{:S(2)}) collective-permute-start(f32[32,512]{1,0:T(8,128)S(1)} %add.308), channel_id=1, source_target_pairs={{0,8},{4,12},{8,0},{12,4},{16,24},{20,28},{24,16},{28,20},{1,9},{5... | collective-permute-start | bytes 196616 | tf_op jit(solution)/shard_map/ppermute | solution.py:92
  310.5 9.9 %collective-permute-start.37 = (bf16[27,16,512]{2,1,0:T(8,128)(2,1)}, bf16[27,16,512]{2,1,0:T(8,128)(2,1)}, u32[]{:S(2)}, u32[]{:S(2)}) collective-permute-start(bf16[27,16,512]{2,1,0:T(8,128)(2,1)} %maximum_select_fusion.1), channel_id=1, source_target_pairs={{0,1},{1,0},{2,3},{3,2},{4,5},{5,4},{6,7},{7,6},{8,9},{9,8},{10,11... | collective-permute-start | bytes 1327112 | tf_op jit(solution)/shard_map/ppermute | solution.py:87
  312.7 7.7 %collective-permute-start.42 = (f32[32,512]{1,0:T(8,128)S(1)}, f32[32,512]{1,0:T(8,128)S(1)}, u32[]{:S(2)}, u32[]{:S(2)}) collective-permute-start(f32[32,512]{1,0:T(8,128)S(1)} %add.309), channel_id=1, source_target_pairs={{0,16},{4,20},{8,24},{12,28},{16,0},{20,4},{24,8},{28,12},{1,17},{... | collective-permute-start | bytes 196616 | tf_op jit(solution)/shard_map/ppermute | solution.py:92
  (32 other events, 284.6 us)

commit v2 on v0

v2 whole, which is shorter than its diff:
```python
import functools
import math

import jax
import jax.numpy as jnp
import numpy as np
from jax import lax
from jax.experimental import pallas as pl
from jax.experimental.pallas import tpu as pltpu
from jax.sharding import PartitionSpec as P

FF = 1536
NFFT = 1280
HOP = 320
NBW = 4
KW = 7
UTT = 4
BR = 32
STEP_COUNT = 6
BINS = 641
NOUT = 1282
VROWS = 20
IN_ROWS = 3
HEAD_ROWS = 3
NB = 137

NORM_EPS = 1e-06
ENV_FLOOR = 0.5
BETA_ONE = 0.8
BETA_TWO = 0.9
LEARN_RATE = 0.04
WEIGHT_DECAY = 0.01
ADAM_EPS = 1e-08

LAPS = NFFT // HOP
RIM = (KW - 1) // 2
LAP_PAD = 384
BIN_PAD = 768
HALF = BR // 2
QUART = BR // 4
EDGE = 16
TILE = 256
CHUNK = 512
LANE = 128
AXES = ("rows", "seq")

F32 = jnp.float32
BF16 = jnp.bfloat16
MIB = 1 << 20
VMEM_BYTES = 60 * MIB


def synthesis_table():
    k = np.arange(BINS)[:, None]
    n = np.arange(NFFT)[None, :]
    angle = (k * n % NFFT) * (2.0 * math.pi / NFFT)
    factor = np.where((k == 0) | (k == NFFT // 2), 1.0, 2.0) / NFFT
    out = np.zeros((2, BIN_PAD, LAPS, LAP_PAD), np.float32)
    out[0, :BINS, :, :HOP] = (factor * np.cos(angle)).reshape(BINS, LAPS, HOP)
    out[1, :BINS, :, :HOP] = (-factor * np.sin(angle)).reshape(BINS, LAPS, HOP)
    return out.reshape(2 * BIN_PAD, LAPS * LAP_PAD).astype(jnp.bfloat16)


def window_tables():
    window = 0.5 - 0.5 * np.cos(np.arange(NFFT) * (2.0 * math.pi / NFFT))
    rows = np.zeros((LAPS, LAP_PAD), np.float64)
    rows[:, :HOP] = window.reshape(LAPS, HOP)
    envelope = np.cumsum(rows**2, axis=0)
    return np.concatenate([rows, 1.0 / np.maximum(envelope, ENV_FLOOR)], axis=0).astype(np.float32)


def ring_of(count):
    if count != 8:
        return None
    return [0, 2, 4, 6, 7, 5, 3, 1]


def ring_step(ring, shift, seq_count):
    where = {r: i for i, r in enumerate(ring)}
    pairs = []
    for r in ring:
        target = ring[(where[r] + shift) % len(ring)]
        pairs += [(r * seq_count + s, target * seq_count + s) for s in range(seq_count)]
    return pairs


def seq_swap(value, bit):
    count = lax.axis_size("seq")
    return lax.ppermute(value, "seq", [(s, s ^ bit) for s in range(count)])


def rows_swap(value, bit):
    count = lax.axis_size("rows")
    return lax.ppermute(value, "rows", [(r, r ^ bit) for r in range(count)])


def shifted(value, distance):
    devices = range(lax.axis_size("seq"))
    return lax.ppermute(
        value, "seq", [(i - distance, i) for i in devices if i - distance in devices]
    )


def dot(a, b, dims):
    return lax.dot_general(a, b, (dims, ((), ())), preferred_element_type=F32)


NN = ((1,), (0,))
NT = ((1,), (1,))
TN = ((0,), (0,))


def frame_reach(meta, row, first, count, utts):
    index = first + lax.broadcasted_iota(jnp.int32, (count, 128), 0)
    start = jnp.zeros_like(index)
    end = jnp.zeros_like(index) + meta[row, 1]
    for u in range(1, utts):
        inside = index >= meta[row, u]
        start = jnp.where(inside, meta[row, u], start)
        end = jnp.where(inside, meta[row, u + 1], end)
    return index - start, end - 1 - index


def spans(count, size):
    return [(at, min(size, count - at)) for at in range(0, count, size)]


def over(table, base, reach, lane_tile, width=LANE):
    cut = slice(lane_tile * LANE, lane_tile * LANE + width)
    picked = jnp.broadcast_to(table[base + LAPS - 1 : base + LAPS, cut], (reach.shape[0], width))
    for j in range(LAPS - 2, -1, -1):
        picked = jnp.where(reach[:, :width] == j, table[base + j : base + j + 1, cut], picked)
    return picked


def keep_within(values, reach, left, offset):
    if offset < 0:
        return jnp.where(reach >= -offset, values, 0.0)
    if offset > 0:
        return jnp.where(left >= offset, values, 0.0)
    return values


def row_mean(values):
    return jnp.mean(values, axis=1, keepdims=True)


def fold(values):
    rows, columns = values.shape
    return jnp.sum(values.reshape(rows // 8, 8, columns), axis=0)


def sincos(angle):
    turns = jnp.round(angle * (1.0 / math.pi))
    rest = angle - turns * 3.140625
    rest = rest - turns * 9.670257568359375e-4
    rest = rest - turns * 6.2771141529083251953e-7
    rest = rest - turns * 1.2154201256553420e-10
    half = turns * 0.5
    sign = 1.0 - 4.0 * (half - jnp.floor(half))
    sq = rest * rest
    sine = rest + rest * sq * (
        -1.6666667163e-01
        + sq * (8.3333337680e-03 + sq * (-1.9841270114e-04 + sq * (2.7557314297e-06 - sq * 2.5050759689e-08)))
    )
    cosine = 1.0 + sq * (
        -0.5
        + sq
        * (
            4.1666667908e-02
            + sq
            * (-1.3888889225e-03 + sq * (2.4801587642e-05 + sq * (-2.7557314297e-07 + sq * 2.0875723372e-09)))
        )
    )
    return sine * sign, cosine * sign


ANGLE_LIMIT = 8192.0


def params():
    return pltpu.CompilerParams(vmem_limit_bytes=VMEM_BYTES)


def cost(flops, bytes_accessed, transcendentals=0):
    return pl.CostEstimate(
        flops=int(flops), bytes_accessed=int(bytes_accessed), transcendentals=int(transcendentals)
    )


WHOLE = pl.BlockSpec(memory_space=pltpu.VMEM)
SCALARS = pl.BlockSpec(memory_space=pltpu.SMEM)
ANYWHERE = pl.BlockSpec(memory_space=pl.ANY)
shape_of = jax.ShapeDtypeStruct


def pre_body(meta, wave_ref, halo_ref, synth_ref, win_ref, *rest, row, tiles, utts):
    out_ref, scaled, signal = rest[-3:]
    step = pl.program_id(0)
    first = pl.multiple_of(step * TILE, TILE)
    base = meta[row, 2 * utts + 1] + first
    reach, left = frame_reach(meta, row, base, TILE + EDGE, utts)

    @pl.when(step == 0)
    def _():
        scaled[...] = jnp.zeros_like(scaled)

    def scale(block, at, size):
        block = block.astype(F32)
        for c, width in ((0, LANE), (1, LANE), (2, HOP - 2 * LANE)):
            value = block[:, c * LANE : c * LANE + width]
            scaled[c, at : at + size, 0:width] = value * over(win_ref, LAPS, reach[at : at + size], c, width)

    for at, size in spans(TILE, 64):
        scale(wave_ref[row, pl.ds(pl.multiple_of(first + at, 64), size), :], at, size)

    @pl.when(step == tiles - 1)
    def _():
        scale(halo_ref[row], TILE, EDGE)

    @pl.when(step < tiles - 1)
    def _():
        scale(wave_ref[row, pl.ds(pl.multiple_of(first + TILE, TILE), EDGE), :], TILE, EDGE)

    for j in range(LAPS):
        for c in range(LAP_PAD // LANE):
            weight = win_ref[j : j + 1, c * LANE : (c + 1) * LANE]
            for at, size in spans(TILE, 64):
                part = scaled[c, at + j : at + j + size, :] * weight
                part = keep_within(part, None, left[at : at + size], j)
                column = j * LAP_PAD + c * LANE
                signal[at : at + size, column : column + LANE] = part.astype(BF16)
    for c in range(0, 2 * BIN_PAD, 512):
        out_ref[:, c : c + 512] = dot(signal[...], synth_ref[c : c + 512, :], NT).astype(BF16)


def spectrum_cotangent(row, before, meta, wave, halo, synth, win, utts):
    rows, frames, _ = wave.shape
    tiles = frames // TILE
    more = [] if before is None else [before]
    return pl.pallas_call(
        functools.partial(pre_body, row=row, tiles=tiles, utts=utts),
        grid=(tiles,),
        in_specs=[SCALARS, WHOLE, WHOLE, WHOLE, WHOLE] + [ANYWHERE] * len(more),
        out_specs=pl.BlockSpec((TILE, 2 * BIN_PAD), lambda i: (row * tiles + i, 0)),
        out_shape=shape_of((rows * frames, 2 * BIN_PAD), BF16),
        input_output_aliases={5: 0} if more else {},
        scratch_shapes=[
            pltpu.VMEM((LAP_PAD // LANE, TILE + EDGE, LANE), F32),
            pltpu.VMEM((TILE, LAPS * LAP_PAD), BF16),
        ],
        compiler_params=params(),
        cost_estimate=cost(2 * frames * 1536 * 1536, frames * 1536 * 2 + 8 * MIB),
        name=f"spectrum_cotangent_{row}",
    )(meta, wave, halo, synth, win, *more)


def fill_frames(xs, x_ref, low_ref, high_ref, row, tile, tiles, channels):
    first = pl.multiple_of(tile * TILE, TILE)

    def put(at, block):
        block = block.astype(F32)
        for c in range(channels // LANE):
            xs[c, at : at + block.shape[0], :] = block[:, c * LANE : (c + 1) * LANE]

    for at, size in spans(TILE, 64):
        put(EDGE + at, x_ref[row, pl.ds(pl.multiple_of(first + at, 64), size), :])

    @pl.when(tile == 0)
    def _():
        put(0, low_ref[row])

    @pl.when(tile > 0)
    def _():
        put(0, x_ref[row, pl.ds(pl.multiple_of(first - EDGE, EDGE), EDGE), :])

    @pl.when(tile == tiles - 1)
    def _():
        put(EDGE + TILE, high_ref[row])

    @pl.when(tile < tiles - 1)
    def _():
        put(EDGE + TILE, x_ref[row, pl.ds(pl.multiple_of(first + TILE, EDGE), EDGE), :])


def by_utterance(meta, row, utts, index, rows_of):
    value = jnp.broadcast_to(rows_of(0), (index.shape[0], LANE))
    for u in range(1, utts):
        value = jnp.where(index >= meta[row, u], rows_of(u), value)
    return value


def pick_rows(meta, row, utts, vec, out, channels):
    for u in range(utts):
        wanted = meta[row, utts + 1 + u]
        for at, offset in ((u, KW + 1), (utts + u, KW + 1 + NBW)):
            value = vec(offset)
            for b in range(1, NBW):
                value = jnp.where(wanted == b, vec(offset + b), value)
            out[at : at + 1, :] = value


def forward_body(meta, places, x_ref, low_ref, high_ref, cot_ref, *rest, parts, tiles, utts):
    sources = rest[:parts]
    (
        table,
        spec_ref,
        act_ref,
        der_ref,
        ada_ref,
        lowg_ref,
        resg_ref,
        xc_ref,
        rc_ref,
        send_ref,
        keep_ref,
        tail_ref,
        sums_ref,
        bsum_ref,
        xs,
        w_head,
        b_head,
        vecs,
        picks,
        grad,
        hg,
        wide,
        wide2,
        slim,
        xn_ref,
        normed,
        branch_ref,
        rn_ref,
        sem,
    ) = rest[parts:]
    step = pl.program_id(0)
    steps = pl.num_programs(0)
    core = meta[0, 2 * utts + 2]
    channels = x_ref.shape[2]
    lane_tiles = channels // LANE
    row, tile = step // tiles, step % tiles
    vec = lambda v: vecs[2 + v : 3 + v, :]
    vec_at = KW + 1 + 2 * NBW

    @pl.when(step == 0)
    def _():
        def go(start):
            base = 0
            for index, ref in enumerate(sources):
                slots = ref.shape[0]
                side = core if index % 2 == 0 else 1 - core

                def one(s, carry, ref=ref, base=base, side=side):
                    bucket = places[0, base + s]

                    @pl.when(bucket < NB)
                    def _():
                        at = pl.multiple_of(bucket * BR + side * HALF, HALF)
                        copy = pltpu.make_async_copy(ref.at[s], table.at[pl.ds(at, HALF), :], sem)
                        if start:
                            copy.start()
                        else:
                            copy.wait()

                    return carry

                lax.fori_loop(0, slots, one, 0)
                if index % 2 == 1:
                    base = base + slots

        go(True)
        grad[...] = jnp.zeros_like(grad)
        sums_ref[...] = jnp.zeros_like(sums_ref)
        bsum_ref[...] = jnp.zeros_like(bsum_ref)
        go(False)
        head_at = 2 * FF
        w_head[0:640, :] = table[head_at : head_at + 640, :]
        edge = table[head_at + 640 : head_at + 640 + 656, :].astype(F32)
        inside = lax.broadcasted_iota(jnp.int32, (128, channels), 0)
        w_head[640:768, :] = jnp.where(inside < 1, edge[0:128], 0.0).astype(BF16)
        w_head[768:1408, :] = edge[1:641].astype(BF16)
        w_head[1408:1536, :] = jnp.where(inside < 1, edge[641:642], 0.0).astype(BF16)
        last = table[2 * FF + 1280 : 2 * FF + 1280 + BR, :].astype(F32)
        vecs[...] = last
        line = jnp.concatenate([last[25:26], last[26:27], last[27:28]], axis=1)
        line = jnp.broadcast_to(line, (8, 3 * channels))
        column = lax.broadcasted_iota(jnp.int32, (8, BIN_PAD), 1)
        b_head[:, 0:BIN_PAD] = jnp.where(column < BINS, line[:, 0:BIN_PAD], 0.0)
        moved = pltpu.roll(line, 3 * channels - BINS, 1)
        b_head[:, BIN_PAD:] = jnp.where(column < BINS, moved[:, 0:BIN_PAD], 0.0)

    @pl.when(tile == 0)
    def _():
        pick_rows(meta, row, utts, vec, picks, channels)

    base = meta[row, 2 * utts + 1] + tile * TILE
    fill_frames(xs, x_ref, low_ref, high_ref, row, tile, tiles, channels)
    for at, size in spans(TILE, 32):
        reach, left = frame_reach(meta, row, base + at, size, utts)
        index = base + at + lax.broadcasted_iota(jnp.int32, (size, LANE), 0)
        conv = []
        for c in range(lane_tiles):
            cut = slice(c * LANE, (c + 1) * LANE)
            total = vecs[2 + KW : 3 + KW, cut]
            for k in range(KW):
                offset = k - RIM
                moved = xs[c, EDGE + offset + at : EDGE + offset + at + size, :]
                total = total + keep_within(moved, reach, left, offset) * vecs[2 + k : 3 + k, cut]
            conv.append(total)
        mean = jnp.sum(sum(conv), axis=1, keepdims=True) * (1.0 / channels)
        conv = [v - mean for v in conv]
        square = jnp.sum(sum([v * v for v in conv]), axis=1, keepdims=True) * (1.0 / channels)
        rc = jnp.broadcast_to(lax.rsqrt(square + NORM_EPS), (size, LANE))
        rc_ref[at : at + size, :] = rc
        for c in range(lane_tiles):
            cut = slice(c * LANE, (c + 1) * LANE)
            xc = conv[c] * rc
            xc_ref[at : at + size, cut] = xc
            scale = by_utterance(meta, row, utts, index, lambda u: picks[u : u + 1, cut])
            shift = by_utterance(meta, row, utts, index, lambda u: picks[utts + u : utts + u + 1, cut])
            ada_ref[at : at + size, cut] = (xc * scale + shift).astype(BF16)
    for c in range(IN_ROWS):
        pre_ref = (wide, wide2)[c % 2]
        pre_ref[...] = dot(ada_ref[...], table[c * CHUNK : (c + 1) * CHUNK, :], NT)
        for at, size in spans(TILE, 32):
            for d in range(0, CHUNK, 256):
                bias = vecs[2 + VROWS + c : 3 + VROWS + c, d : d + 256]
                pre = pre_ref[at : at + size, d : d + 256] + bias
                phi = 0.5 + 0.5 * lax.erf(pre * math.sqrt(0.5))
                bell = jnp.exp(-0.5 * pre * pre) * (1.0 / math.sqrt(2.0 * math.pi))
                cut = slice(c * CHUNK + d, c * CHUNK + d + 256)
                act_ref[at : at + size, cut] = (pre * phi).astype(BF16)
                der_ref[at : at + size, cut] = (phi + pre * bell).astype(BF16)
    slim[...] = dot(act_ref[...], table[FF : 2 * FF, :], NN)
    for at, size in spans(TILE, 16):
        span = slice(at, at + size)
        branch = slim[span, :] + vec(vec_at)
        branch_ref[span, :] = branch
        x = jnp.concatenate([xs[c, EDGE + at : EDGE + at + size, :] for c in range(lane_tiles)], axis=1)
        residual = x + vec(vec_at + 1) * branch
        residual = residual - row_mean(residual)
        rn = lax.rsqrt(row_mean(residual * residual) + NORM_EPS)
        rn_ref[span, :] = jnp.broadcast_to(rn, (size, LANE))
        xn = residual * rn
        xn_ref[span, :] = xn
        normed[span, :] = (xn * vec(vec_at + 2) + vec(vec_at + 3)).astype(BF16)

    def head(c, turn):
        logs_ref, angle_ref = wide, wide2
        half = slice((c // 256 % 2) * 256, (c // 256 % 2) * 256 + 256)
        logs_ref[:, half] = dot(normed[...], w_head[c : c + 256, :], NT)
        angle_ref[:, half] = dot(normed[...], w_head[BIN_PAD + c : BIN_PAD + c + 256, :], NT)
        widest = jnp.zeros((8, 256), F32)
        for at, size in spans(TILE, 16):
            span = slice(at, at + size)
            one, two = slice(c, c + 256), slice(BIN_PAD + c, BIN_PAD + c + 256)
            angle = angle_ref[span, half] + b_head[0:1, two]
            scale = jnp.exp(logs_ref[span, half] + b_head[0:1, one])
            sine, cosine = turn(angle)
            real, imag = scale * cosine, scale * sine
            spec_ref[span, one] = real.astype(BF16)
            spec_ref[span, two] = imag.astype(BF16)
            dre = cot_ref[span, one].astype(F32)
            dim = cot_ref[span, two].astype(F32)
            hg[span, one] = (dre * real + dim * imag).astype(BF16)
            hg[span, two] = (dim * real - dre * imag).astype(BF16)
            widest = jnp.maximum(widest, jnp.max(jnp.abs(angle).reshape(size // 8, 8, 256), axis=0))
        return widest

    widest = head(0, sincos)
    for c in range(256, BIN_PAD, 256):
        widest = jnp.maximum(widest, head(c, sincos))

    @pl.when(jnp.max(widest) > ANGLE_LIMIT)
    def _():
        for c in range(0, BIN_PAD, 256):
            head(c, lambda angle: (jnp.sin(angle), jnp.cos(angle)))

    slim[...] = dot(hg[...], w_head[...], NN)
    grad[...] += dot(hg[...], normed[...], TN)
    for c in range(0, 2 * BIN_PAD, 512):
        total = bsum_ref[:, c : c + 512]
        for at, size in spans(TILE, 32):
            total = total + fold(hg[at : at + size, c : c + 512].astype(F32))
        bsum_ref[:, c : c + 512] = total
    sums = [sums_ref[v] for v in range(4)]
    for at, size in spans(TILE, 16):
        span = slice(at, at + size)
        ngrad = slim[span, :]
        xn = xn_ref[span, :]
        e = ngrad * vec(vec_at + 2)
        resg = rn_ref[span, 0:1] * (e - row_mean(e) - xn * row_mean(e * xn))
        resg_ref[span, :] = resg
        low = (vec(vec_at + 1) * resg).astype(BF16)
        lowg_ref[span, :] = low
        sums[0] = sums[0] + fold(low.astype(F32))
        sums[1] = sums[1] + fold(resg * branch_ref[span, :])
        sums[2] = sums[2] + fold(ngrad * xn)
        sums[3] = sums[3] + fold(ngrad)
    for v in range(4):
        sums_ref[v] = sums[v]

    @pl.when(step == steps - 1)
    def _():
        grad[767:768, :] = grad[640:641, :]
        for b in range(40):
            at = b * BR if b < 20 else b * BR + 127
            low_half = grad[at : at + HALF, :].astype(BF16)
            high_half = grad[at + HALF : at + BR, :].astype(BF16)
            keep_ref[b] = jnp.where(core == 0, low_half, high_half)
            send_ref[b] = jnp.where(core == 0, high_half, low_half)
        tail_ref[...] = grad[1407:1415, :]


def forward(meta, places, x, low, high, cot, sources, utts):
    rows, frames, channels = x.shape
    tiles = frames // TILE
    count = rows * frames
    wide = pl.BlockSpec((TILE, FF), lambda i: (i, 0))
    slim = pl.BlockSpec((TILE, channels), lambda i: (i, 0))
    return pl.pallas_call(
        functools.partial(forward_body, parts=len(sources), tiles=tiles, utts=utts),
        grid=(rows * tiles,),
        in_specs=[SCALARS, SCALARS, WHOLE, WHOLE, WHOLE, wide] + [ANYWHERE] * len(sources),
        out_specs=[WHOLE, wide, wide, wide, slim, slim, slim, slim]
        + [pl.BlockSpec((TILE, LANE), lambda i: (i, 0))]
        + [WHOLE] * 5,
        out_shape=[
            shape_of((NB * BR, channels), BF16),
            shape_of((count, FF), BF16),
            shape_of((count, FF), BF16),
            shape_of((count, FF), BF16),
            shape_of((count, channels), BF16),
            shape_of((count, channels), BF16),
            shape_of((count, channels), F32),
            shape_of((count, channels), F32),
            shape_of((count, LANE), F32),
            shape_of((40, HALF, channels), BF16),
            shape_of((40, HALF, channels), BF16),
            shape_of((8, channels), F32),
            shape_of((4, 8, channels), F32),
            shape_of((8, 2 * BIN_PAD), F32),
        ],
        scratch_shapes=[
            pltpu.VMEM((channels // LANE, TILE + 2 * EDGE, LANE), F32),
            pltpu.VMEM((2 * BIN_PAD, channels), BF16),
            pltpu.VMEM((8, 2 * BIN_PAD), F32),
            pltpu.VMEM((BR, channels), F32),
            pltpu.VMEM((2 * utts, channels), F32),
            pltpu.VMEM((2 * BIN_PAD, channels), F32),
            pltpu.VMEM((TILE, 2 * BIN_PAD), BF16),
            pltpu.VMEM((TILE, CHUNK), F32),
            pltpu.VMEM((TILE, CHUNK), F32),
            pltpu.VMEM((TILE, channels), F32),
            pltpu.VMEM((TILE, channels), F32),
            pltpu.VMEM((TILE, channels), BF16),
            pltpu.VMEM((TILE, channels), F32),
            pltpu.VMEM((TILE, LANE), F32),
            pltpu.SemaphoreType.DMA,
        ],
        compiler_params=params(),
        cost_estimate=cost(10 * count * 1536 * 512, 40 * MIB, count * 4096),
        name="forward",
    )(meta, places, x, low, high, cot, *sources)


def mlp_body(meta, low_ref, act_ref, der_ref, ada_ref, wout_ref, *rest, utts):
    pre_ref, send_ref, keep_ref, bsum_ref, gout, gin, agrad = rest[-7:]
    step = pl.program_id(0)
    core = meta[0, 2 * utts + 2]
    tile = low_ref.shape[0]

    @pl.when(step == 0)
    def _():
        gout[...] = jnp.zeros_like(gout)
        gin[...] = jnp.zeros_like(gin)
        bsum_ref[...] = jnp.zeros_like(bsum_ref)

    agrad[...] = dot(low_ref[...], wout_ref[...], NT)
    gout[...] += dot(act_ref[...], low_ref[...], TN)
    total = bsum_ref[...]
    for at, size in spans(tile, 16):
        span = slice(at, at + size)
        pre = (agrad[span, :] * der_ref[span, :].astype(F32)).astype(BF16)
        pre_ref[span, :] = pre
        total = total + fold(pre.astype(F32))
    bsum_ref[...] = total
    gin[...] += dot(pre_ref[...], ada_ref[...], TN)

    @pl.when(step == pl.num_programs(0) - 1)
    def _():
        buckets = CHUNK // BR
        for at, ref in ((0, gin), (buckets, gout)):
            for b in range(buckets):
                low_half = ref[b * BR : b * BR + HALF, :].astype(BF16)
                high_half = ref[b * BR + HALF : b * BR + BR, :].astype(BF16)
                keep_ref[at + b] = jnp.where(core == 0, low_half, high_half)
                send_ref[at + b] = jnp.where(core == 0, high_half, low_half)


def mlp_backward(chunk, before, meta, low, act, der, ada, table, utts):
    count, channels = low.shape
    tile = 512
    slim = pl.BlockSpec((tile, channels), lambda i: (i, 0))
    part = pl.BlockSpec((tile, CHUNK), lambda i: (i, chunk))
    buckets = 2 * CHUNK // BR
    more = [] if before is None else [before]
    return pl.pallas_call(
        functools.partial(mlp_body, utts=utts),
        grid=(count // tile,),
        in_specs=[
            SCALARS,
            slim,
            part,
            part,
            slim,
            pl.BlockSpec((CHUNK, channels), lambda i: (FF // CHUNK + chunk, 0)),
        ]
        + [ANYWHERE] * len(more),
        out_specs=[part, WHOLE, WHOLE, WHOLE],
        out_shape=[
            shape_of((count, FF), BF16),
            shape_of((buckets, HALF, channels), BF16),
            shape_of((buckets, HALF, channels), BF16),
            shape_of((8, CHUNK), F32),
        ],
        input_output_aliases={6: 0} if more else {},
        scratch_shapes=[
            pltpu.VMEM((CHUNK, channels), F32),
            pltpu.VMEM((CHUNK, channels), F32),
            pltpu.VMEM((tile, CHUNK), F32),
        ],
        compiler_params=params(),
        cost_estimate=cost(6 * count * CHUNK * 512, 12 * MIB),
        name=f"mlp_backward_{chunk}",
    )(meta, low, act, der, ada, table, *more)


def norm_body(
    meta, x_ref, low_ref, high_ref, pre_ref, w_in, last_ref, xc_ref, rc_ref, *rest, row, tiles, utts, closing
):
    more = rest[: 7 if closing else 0]
    outs = rest[len(more) :]
    cg_ref, edge_ref, part_ref = outs[:3]
    xs, vecs, picks, agrad, cg, reaches = outs[-6:]
    tile = pl.program_id(0)
    channels = x_ref.shape[2]
    lane_tiles = channels // LANE
    base = meta[row, 2 * utts + 1] + tile * TILE
    vec = lambda v: vecs[2 + v : 3 + v, :]

    @pl.when(tile == 0)
    def _():
        vecs[...] = last_ref[...].astype(F32)
        part_ref[...] = more[0][...] if closing else jnp.zeros_like(part_ref)
        pick_rows(meta, row, utts, vec, picks, channels)

    agrad[...] = dot(pre_ref[...], w_in[...], NN)
    fill_frames(xs, x_ref, low_ref, high_ref, row, tile, tiles, channels)
    for at, size in spans(TILE, 32):
        span = slice(at, at + size)
        reach, left = frame_reach(meta, row, base + at, size, utts)
        reaches[0, span, :] = reach
        reaches[1, span, :] = left
        index = base + at + lax.broadcasted_iota(jnp.int32, (size, LANE), 0)
        ecs, xcs = [], []
        for c in range(lane_tiles):
            cut = slice(c * LANE, (c + 1) * LANE)
            scale = by_utterance(meta, row, utts, index, lambda u: picks[u : u + 1, cut])
            ecs.append(agrad[span, cut] * scale)
            xcs.append(xc_ref[span, cut])
        m_one = jnp.sum(sum(ecs), axis=1, keepdims=True) * (1.0 / channels)
        m_two = jnp.sum(sum([e * v for e, v in zip(ecs, xcs)]), axis=1, keepdims=True) * (1.0 / channels)
        rc = rc_ref[span, :]
        for c in range(lane_tiles):
            cut = slice(c * LANE, (c + 1) * LANE)
            value = rc * (ecs[c] - m_one - xcs[c] * m_two)
            cg[c, span, :] = value
            cg_ref[span, cut] = value
    for u in range(utts):
        begin, end = meta[row, u], meta[row, u + 1]

        @pl.when((begin < base + TILE) & (end > base))
        def _(u=u, begin=begin, end=end):
            wanted = meta[row, utts + 1 + u]
            for c in range(lane_tiles):
                cut = slice(c * LANE, (c + 1) * LANE)
                one = jnp.zeros((8, LANE), F32)
                two = jnp.zeros((8, LANE), F32)
                for at, size in spans(TILE, 64):
                    span = slice(at, at + size)
                    index = base + at + lax.broadcasted_iota(jnp.int32, (size, LANE), 0)
                    value = jnp.where((index >= begin) & (index < end), agrad[span, cut], 0.0)
                    one = one + fold(value * xc_ref[span, cut])
                    two = two + fold(value)
                part_ref[KW + 1 + wanted, :, cut] += one
                part_ref[KW + 1 + NBW + wanted, :, cut] += two

    for c in range(lane_tiles):
        cut = slice(c * LANE, (c + 1) * LANE)
        sums = [part_ref[k, :, cut] for k in range(KW + 1)]
        for at, size in spans(TILE, 32):
            span = slice(at, at + size)
            reach, left = reaches[0, span, :], reaches[1, span, :]
            value = cg[c, span, :]
            for k in range(KW):
                offset = k - RIM
                moved = xs[c, EDGE + offset + at : EDGE + offset + at + size, :] * value
                sums[k] = sums[k] + fold(keep_within(moved, reach, left, offset))
            sums[KW] = sums[KW] + fold(value)
        for k in range(KW + 1):
            part_ref[k, :, cut] = sums[k]

    @pl.when(tile == 0)
    def _():
        edge_ref[0] = cg_ref[0:8, :]

    @pl.when(tile == tiles - 1)
    def _():
        edge_ref[1] = cg_ref[TILE - 8 : TILE, :]

    if closing:
        _, tail_ref, sums_ref, hsum_ref, bsum0, bsum1, bsum2 = more
        vec_ref = outs[3]

        @pl.when(tile == tiles - 1)
        def _():
            vec_ref[0:8, :] = jnp.zeros((8, channels), F32)
            vec_ref[0:2, :] = tail_ref[0:2, :]
            for v in range(VROWS):
                at = v - (KW + 1 + 2 * NBW)
                rows_of = part_ref[v] if at < 0 else sums_ref[at]
                vec_ref[2 + v : 3 + v, :] = jnp.sum(rows_of, axis=0, keepdims=True)
            for c, ref in enumerate((bsum0, bsum1, bsum2)):
                vec_ref[2 + VROWS + c : 3 + VROWS + c, :] = jnp.sum(ref[...], axis=0, keepdims=True)
            flat = jnp.broadcast_to(jnp.sum(hsum_ref[...], axis=0, keepdims=True), (8, 2 * BIN_PAD))
            column = lax.broadcasted_iota(jnp.int32, (8, 3 * channels), 1)
            moved = pltpu.roll(flat, 2 * BIN_PAD - (BIN_PAD - BINS), 1)
            joined = jnp.where(column < BINS, flat, moved)
            joined = jnp.where(column < NOUT, joined, 0.0)
            for c in range(HEAD_ROWS):
                at = 2 + VROWS + IN_ROWS + c
                vec_ref[at : at + 1, :] = joined[0:1, c * channels : (c + 1) * channels]
            vec_ref[28:32, :] = jnp.zeros((4, channels), F32)


def norm_backward(row, closing, meta, x, low, high, pre, table, xc, rc, utts):
    rows, frames, channels = x.shape
    tiles = frames // TILE
    block = lambda width: pl.BlockSpec((TILE, width), lambda i: (row * tiles + i, 0))
    sums = KW + 1 + 2 * NBW
    out_specs = [pl.BlockSpec((TILE, channels), lambda i: (i, 0)), WHOLE, WHOLE]
    out_shape = [
        shape_of((frames, channels), F32),
        shape_of((2, 8, channels), F32),
        shape_of((sums, 8, channels), F32),
    ]
    if closing:
        out_specs.append(WHOLE)
        out_shape.append(shape_of((BR, channels), F32))
    return pl.pallas_call(
        functools.partial(norm_body, row=row, tiles=tiles, utts=utts, closing=bool(closing)),
        grid=(tiles,),
        in_specs=[SCALARS, WHOLE, WHOLE, WHOLE, block(FF)]
        + [
            pl.BlockSpec((FF, channels), lambda i: (0, 0)),
            pl.BlockSpec((BR, channels), lambda i: (NB - 1, 0)),
            block(channels),
            block(LANE),
        ]
        + [WHOLE] * len(closing),
        out_specs=out_specs,
        out_shape=out_shape,
        scratch_shapes=[
            pltpu.VMEM((channels // LANE, TILE + 2 * EDGE, LANE), F32),
            pltpu.VMEM((BR, channels), F32),
            pltpu.VMEM((2 * utts, channels), F32),
            pltpu.VMEM((TILE, channels), F32),
            pltpu.VMEM((channels // LANE, TILE, LANE), F32),
            pltpu.VMEM((2, TILE, LANE), jnp.int32),
        ],
        compiler_params=params(),
        cost_estimate=cost(2 * frames * 1536 * 512, 12 * MIB),
        name=f"norm_backward_{row}",
    )(meta, x, low, high, pre, table, table, xc, rc, *closing)


def conv_body(meta, cg_ref, before_ref, after_ref, low_ref, high_ref, resg_ref, last_ref, *rest, row, tiles, utts):
    out_ref, cs, vecs = rest[-3:]
    tile = pl.program_id(0)
    channels = cg_ref.shape[1]
    base = meta[row, 2 * utts + 1] + tile * TILE

    @pl.when(tile == 0)
    def _():
        vecs[...] = last_ref[...].astype(F32)

    for c in range(channels // LANE):
        cut = slice(c * LANE, (c + 1) * LANE)
        cs[c, 8 : 8 + TILE, :] = cg_ref[:, cut]
        cs[c, 0:8, :] = jnp.where(tile == 0, low_ref[row, :, cut], before_ref[:, cut])
        cs[c, 8 + TILE :, :] = jnp.where(tile == tiles - 1, high_ref[row, :, cut], after_ref[:, cut])
    for at, size in spans(TILE, 32):
        span = slice(at, at + size)
        reach, left = frame_reach(meta, row, base + at, size, utts)
        for c in range(channels // LANE):
            cut = slice(c * LANE, (c + 1) * LANE)
            total = resg_ref[span, cut]
            for k in range(KW):
                offset = RIM - k
                moved = cs[c, 8 + offset + at : 8 + offset + at + size, :]
                total = total + keep_within(moved, reach, left, offset) * vecs[2 + k : 3 + k, cut]
            out_ref[0, span, cut] = total


def conv_backward(row, before, meta, cg, low, high, resg, table, rows, utts):
    frames, channels = cg.shape
    tiles = frames // TILE
    per = TILE // 8
    more = [] if before is None else [before]
    return pl.pallas_call(
        functools.partial(conv_body, row=row, tiles=tiles, utts=utts),
        grid=(tiles,),
        in_specs=[
            SCALARS,
            pl.BlockSpec((TILE, channels), lambda i: (i, 0)),
            pl.BlockSpec((8, channels), lambda i: (jnp.maximum(i * per - 1, 0), 0)),
            pl.BlockSpec((8, channels), lambda i: (jnp.minimum((i + 1) * per, tiles * per - 1), 0)),
            WHOLE,
            WHOLE,
            pl.BlockSpec((TILE, channels), lambda i: (row * tiles + i, 0)),
            pl.BlockSpec((BR, channels), lambda i: (NB - 1, 0)),
        ]
        + [ANYWHERE] * len(more),
        out_specs=pl.BlockSpec((1, TILE, channels), lambda i: (row, i, 0)),
        out_shape=shape_of((rows, frames, channels), F32),
        input_output_aliases={8: 0} if more else {},
        scratch_shapes=[
            pltpu.VMEM((channels // LANE, TILE + 16, LANE), F32),
            pltpu.VMEM((BR, channels), F32),
        ],
        compiler_params=params(),
        cost_estimate=cost(16 * frames * 512, 6 * MIB),
        name=f"conv_backward_{row}",
    )(meta, cg, cg, cg, low, high, resg, table, *more)


def wave_body(meta, spec_ref, prev_ref, halo_ref, synth_ref, win_ref, *rest, row, tiles, utts):
    out_ref, spec, held = rest[-3:]
    tile = pl.program_id(0)
    base = meta[row, 2 * utts + 1] + tile * TILE
    spec[EDGE:, :] = spec_ref[...]
    spec[0:EDGE, :] = jnp.where(tile == 0, halo_ref[row], prev_ref[...])
    for j in range(LAPS):
        piece = dot(spec[...], synth_ref[:, j * LAP_PAD : (j + 1) * LAP_PAD], NN)
        for c in range(LAP_PAD // LANE):
            held[j, c] = piece[:, c * LANE : (c + 1) * LANE]
    for at, size in spans(TILE, 32):
        reach, _ = frame_reach(meta, row, base + at, size, utts)
        for c, width in ((0, LANE), (1, LANE), (2, HOP - 2 * LANE)):
            cut = slice(c * LANE, c * LANE + width)
            total = held[0, c, EDGE + at : EDGE + at + size, :] * win_ref[0:1, c * LANE : (c + 1) * LANE]
            for j in range(1, LAPS):
                moved = held[j, c, EDGE + at - j : EDGE + at - j + size, :]
                moved = moved * win_ref[j : j + 1, c * LANE : (c + 1) * LANE]
                total = total + jnp.where(reach >= j, moved, 0.0)
            out_ref[0, at : at + size, cut] = total[:, 0:width] * over(win_ref, LAPS, reach, c, width)


def wave_forward(row, before, meta, spec, halo, synth, win, rows, utts):
    frames = spec.shape[0] // rows
    tiles = frames // TILE
    per = TILE // EDGE
    more = [] if before is None else [before]
    return pl.pallas_call(
        functools.partial(wave_body, row=row, tiles=tiles, utts=utts),
        grid=(tiles,),
        in_specs=[
            SCALARS,
            pl.BlockSpec((TILE, 2 * BIN_PAD), lambda i: (row * tiles + i, 0)),
            pl.BlockSpec((EDGE, 2 * BIN_PAD), lambda i: (jnp.maximum((row * tiles + i) * per - 1, 0), 0)),
            WHOLE,
            WHOLE,
            WHOLE,
        ]
        + [ANYWHERE] * len(more),
        out_specs=pl.BlockSpec((1, TILE, HOP), lambda i: (row, i, 0)),
        out_shape=shape_of((rows, frames, HOP), F32),
        input_output_aliases={6: 0} if more else {},
        scratch_shapes=[
            pltpu.VMEM((TILE + EDGE, 2 * BIN_PAD), BF16),
            pltpu.VMEM((LAPS, LAP_PAD // LANE, TILE + EDGE, LANE), F32),
        ],
        compiler_params=params(),
        cost_estimate=cost(2 * frames * 1536 * 1536, 12 * MIB),
        name=f"wave_forward_{row}",
    )(meta, spec, spec, halo, synth, win, *more)


def slot_body(slot_of, *refs, bounds):
    count = len(bounds)
    out = refs[-1]
    for (start, stop), keep, came in zip(bounds, refs[:count], refs[count : 2 * count]):

        def one(b, carry, start=start, keep=keep, came=came):
            value = keep[b].astype(F32) + came[b].astype(F32)
            out[slot_of[0, start + b]] = value.astype(BF16)
            return carry

        lax.fori_loop(0, stop - start, one, 0)


def to_slots(slot_of, keeps, cames, bounds, total):
    channels = keeps[0].shape[2]
    return pl.pallas_call(
        functools.partial(slot_body, bounds=bounds),
        in_specs=[SCALARS] + [WHOLE] * (2 * len(bounds)),
        out_specs=WHOLE,
        out_shape=shape_of((total, QUART, channels), BF16),
        compiler_params=params(),
        cost_estimate=cost(0, 6 * MIB),
        name="to_slots",
    )(slot_of, *keeps, *cames)


def adam_body(places, spot, own, near, far, cross, last_ref, master, first, second, *outs, block):
    out_master, out_first, out_second = outs
    core, plane = spot[0], spot[1]
    one_fix = 1.0 / (1.0 - BETA_ONE**STEP_COUNT)
    two_fix = 1.0 / (1.0 - BETA_TWO**STEP_COUNT)
    for s in range(block):
        bucket = places[0, pl.program_id(0) * block + s]
        for ref, c, p in (
            (own, core, plane),
            (near, 1 - core, plane),
            (far, core, 1 - plane),
            (cross, 1 - core, 1 - plane),
        ):
            rows = pl.ds(pl.multiple_of(c * HALF + p * QUART, QUART), QUART)
            grad = ref[s].astype(F32)
            grad = jnp.where(bucket == NB - 1, last_ref[rows, :], grad)
            grad = jnp.where(bucket < NB, grad, 0.0)
            old = master[s, rows, :]
            one = BETA_ONE * first[s, rows, :] + (1.0 - BETA_ONE) * grad
            two = BETA_TWO * second[s, rows, :] + (1.0 - BETA_TWO) * grad * grad
            out_first[s, rows, :] = one
            out_second[s, rows, :] = two
            step = one * one_fix / (jnp.sqrt(two * two_fix) + ADAM_EPS)
            out_master[s, rows, :] = old - LEARN_RATE * (step + WEIGHT_DECAY * old)


def adam(places, spot, quarters, last, master, first, second):
    slots, depth, channels = master.shape
    block = max(b for b in range(1, 10) if slots % b == 0)
    full = pl.BlockSpec((block, depth, channels), lambda i: (i, 0, 0))
    part = pl.BlockSpec((block, QUART, channels), lambda i: (i, 0, 0))
    return pl.pallas_call(
        functools.partial(adam_body, block=block),
        grid=(slots // block,),
        in_specs=[SCALARS, SCALARS] + [part] * 4 + [WHOLE, full, full, full],
        out_specs=[full] * 3,
        out_shape=[shape_of(master.shape, F32)] * 3,
        compiler_params=params(),
        cost_estimate=cost(0, 12 * MIB),
        name="adam",
    )(places, spot, *quarters, last, master, first, second)


def tie(*values):
    return lax.optimization_barrier(values)


def plus(*values):
    return sum([v.astype(F32) for v in values]).astype(BF16)


def local(frames_in, lengths, bw_ids, owner_list, master, moment1, moment2, wave_grad):
    rows, frames, channels = frames_in.shape
    slots = master.shape[0]
    utts = lengths.shape[1]
    owners = lax.axis_size("rows")
    seqs = lax.axis_size("seq")
    row_at = lax.axis_index("rows")
    seq_at = lax.axis_index("seq")
    core, plane = seq_at % 2, seq_at // 2
    ring = ring_of(owners)
    half_ring = owners // 2

    mine = lax.dynamic_slice_in_dim(master, core * HALF, HALF, axis=1).astype(BF16)

    starts = [jnp.zeros((rows, 1), jnp.int32)]
    for u in range(utts):
        starts.append(starts[-1] + lengths[:, u : u + 1])
    spot = jnp.broadcast_to(jnp.stack([seq_at * frames, core])[None, :], (rows, 2)).astype(jnp.int32)
    meta = jnp.concatenate(starts + [bw_ids, spot], axis=1)
    blocks = wave_grad.reshape(rows, frames, HOP)
    synth = jnp.asarray(synthesis_table())
    win = jnp.asarray(window_tables())

    low = shifted(frames_in[:, frames - EDGE :], 1)
    high = shifted(frames_in[:, :EDGE], -1)
    later = shifted(blocks[:, :EDGE], -1)
    if ring:
        offsets = [0]
        sources = [mine, seq_swap(mine, 1)]
        ahead = back = mine
        cot = None
        for hop in range(half_ring):
            source = (ahead, back)
            ahead = lax.ppermute(ahead, AXES, ring_step(ring, 1, seqs))
            if hop < half_ring - 1:
                back = lax.ppermute(back, AXES, ring_step(ring, -1, seqs))
            if hop in (1, 2):
                feed = tie(blocks, *source)[0]
                cot = spectrum_cotangent(hop - 1, cot, meta, feed, later, synth, win, utts)
                ahead, back, cot = tie(ahead, back, cot)
            sources += [ahead, seq_swap(ahead, 1)]
            offsets.append(-(hop + 1))
            if hop < half_ring - 1:
                sources += [back, seq_swap(back, 1)]
                offsets.append(hop + 1)
        order = jnp.asarray(ring, jnp.int32)
        ids = jnp.arange(owners, dtype=jnp.int32)
        where = jnp.sum(jnp.where(order == row_at, ids, 0))
        at = (where + jnp.asarray(offsets, jnp.int32)) % owners
        owner_ids = jnp.sum(jnp.where(at[:, None] == ids[None, :], order[None, :], 0), axis=1)
    else:
        gathered = lax.all_gather(mine, "rows", axis=0, tiled=True)
        sources = [gathered, seq_swap(gathered, 1)]
        owner_ids = jnp.arange(owners, dtype=jnp.int32)
        cot = None
        for r in range(rows):
            cot = spectrum_cotangent(r, cot, meta, blocks, later, synth, win, utts)

    bucket_index = jnp.arange(NB, dtype=jnp.int32)
    same = owner_list[None, :] == owner_list[:, None]
    rank = jnp.sum((same & (bucket_index[None, :] < bucket_index[:, None])).astype(jnp.int32), axis=1)

    def held_by(ids):
        targets = (ids[:, None] * slots + jnp.arange(slots, dtype=jnp.int32)[None, :]).reshape(-1)
        match = (owner_list * slots + rank)[None, :] == targets[:, None]
        return (NB + jnp.sum(match.astype(jnp.int32) * (bucket_index[None, :] - NB), axis=1))[None, :]

    places = held_by(owner_ids)
    held = held_by(row_at[None].astype(jnp.int32))
    place_at = jnp.arange(owners, dtype=jnp.int32)
    rel = jnp.sum(jnp.where(owner_list[:, None] == owner_ids[None, :], place_at[None, :], 0), axis=1)
    slot_of = (rel * slots + rank)[None, :]
    places, held, slot_of, meta = tie(places, held, slot_of, meta)

    (table, spec, act, der, ada, low_grad, resg, xc, rc, send, keep, tail, sums, hsum) = forward(
        meta, places, frames_in, low, high, cot, sources, utts
    )
    halo = shifted(spec.reshape(rows, frames, 2 * BIN_PAD)[:, frames - EDGE :], 1)

    keeps, cames, bounds = [], [], []

    def split(keep, came):
        both = plus(keep, came)
        stay = lax.dynamic_slice_in_dim(both, plane * QUART, QUART, axis=1)
        leave = lax.dynamic_slice_in_dim(both, (1 - plane) * QUART, QUART, axis=1)
        return stay, leave

    def record(stay, came, begins, per):
        for at, begin in enumerate(begins):
            keeps.append(stay[at * per : (at + 1) * per])
            cames.append(came[at * per : (at + 1) * per])
            bounds.append((begin, begin + per))

    per = CHUNK // BR
    pre, bsums = None, []
    begins, count = (2 * FF // BR,), 40
    for chunk in range(FF // CHUNK):
        near = seq_swap(send, 1)
        pre, next_send, next_keep, bsum = mlp_backward(chunk, pre, meta, low_grad, act, der, ada, table, utts)
        near, pre, next_send, next_keep = tie(near, pre, next_send, next_keep)
        bsums.append(bsum)
        stay, leave = split(keep, near)
        record(stay, seq_swap(leave, 2), begins, count)
        send, keep = next_send, next_keep
        begins, count = (chunk * per, FF // BR + chunk * per), per

    near = seq_swap(send, 1)
    cg0, edge0, parts = norm_backward(0, (), meta, frames_in, low, high, pre, table, xc, rc, utts)
    near, cg0, edge0, parts, pre = tie(near, cg0, edge0, parts, pre)
    stay, leave = split(keep, near)
    came = seq_swap(leave, 2)
    closing = (parts, tail, sums, hsum, *bsums)
    cg1, edge1, _, last = norm_backward(1, closing, meta, frames_in, low, high, pre, table, xc, rc, utts)
    came, cg1, edge1, last, spec = tie(came, cg1, edge1, last, spec)
    record(stay, came, begins, count)
    chunks = to_slots(slot_of, keeps, cames, tuple(bounds), owners * slots)
    edges = jnp.stack([edge0, edge1])

    state = {}

    def work(stage, *ready):
        if stage == 0:
            feed = tie(spec, *ready)[0]
            state["low"] = shifted(edges[:, 1], 1)
            state["high"] = shifted(edges[:, 0], -1)
            state["wave"] = wave_forward(0, None, meta, feed, halo, synth, win, rows, utts)
            return state["wave"]
        if stage == 1:
            feed = tie(cg0, *ready)[0]
            state["grad"] = conv_backward(
                0, None, meta, feed, state["low"], state["high"], resg, table, rows, utts
            )
            return state["grad"]
        if stage == 2:
            feed = tie(cg1, *ready)[0]
            state["grad"] = conv_backward(
                1, state["grad"], meta, feed, state["low"], state["high"], resg, table, rows, utts
            )
            return state["grad"]
        if stage == 3:
            feed = tie(spec, *ready)[0]
            state["wave"] = wave_forward(1, state["wave"], meta, feed, halo, synth, win, rows, utts)
            return state["wave"]
        return state["wave"]

    if ring:
        cut = {o: chunks[i * slots : (i + 1) * slots] for i, o in enumerate(offsets)}
        up, down = cut[-half_ring], cut[1 - half_ring]
        for hop in range(half_ring):
            left_over = half_ring - 1 - hop
            source = (up, down, last)
            up = lax.ppermute(up, AXES, ring_step(ring, 1, seqs))
            if hop < half_ring - 1:
                down = lax.ppermute(down, AXES, ring_step(ring, -1, seqs))
            if hop < 2:
                last = last + seq_swap(last, 1 << hop)
            else:
                last = last + rows_swap(last, 1 << (hop - 2))
            done = work(hop, *source)
            if hop in (0, 3):
                up, down, last, state["wave"] = tie(up, down, last, done)
            else:
                up, down, last, state["grad"] = tie(up, down, last, done)
            if left_over:
                up = plus(up, cut[left_over])
                if hop < half_ring - 2:
                    down = plus(down, cut[1 - left_over])
        own = plus(cut[0], up, down)
    else:
        own = lax.psum_scatter(chunks, "rows", scatter_dimension=0, tiled=True)
        last = lax.psum(last, AXES)
        for hop in range(4):
            work(hop, own)
    far = seq_swap(own, 2)
    near = seq_swap(own, 1)
    if ring:
        last = last + rows_swap(last, 4)
    waveform = state["wave"].reshape(rows, frames * HOP)
    far, waveform = tie(far, waveform)
    cross = seq_swap(far, 1)
    where_at = jnp.stack([core, plane]).astype(jnp.int32)
    new_master, new_first, new_second = adam(
        held, where_at, (own, near, far, cross), last, master, moment1, moment2
    )
    return waveform, state["grad"], new_master, new_first, new_second


def solution(mesh):
    in_specs = (
        P("rows", "seq", None),
        P("rows", None),
        P("rows", None),
        P(),
        P("rows", None, None),
        P("rows", None, None),
        P("rows", None, None),
        P("rows", "seq"),
    )
    out_specs = (
        P("rows", "seq"),
        P("rows", "seq", None),
        P("rows", None, None),
        P("rows", None, None),
        P("rows", None, None),
    )
    return jax.shard_map(local, mesh=mesh, in_specs=in_specs, out_specs=out_specs, check_vma=False)
```

time: 556 us -> 261 us (0.47); the launches traced: 546 us -> 260 us
  Pallas kernels: 0 us -> 166 us
  other arithmetic: 136 us -> 6.37 us
  matrix products: 119 us -> 0 us
  waiting for transfers between devices: 130 us -> 14.4 us
  local copies, waits for them, and re-layouts: 133 us -> 24.7 us
  starting transfers between devices: 12.2 us -> 47.1 us
  between operations: 15.7 us -> 1.51 us
    pallas_call x0 -> x14, Pallas kernels: none -> 166 us  [the longest x1 56.5 us: forward(): pl.pallas_call(functools.partial(forward_body, parts=len(sources), tiles=...]
    dot_general x15 -> x0, matrix products: 119 us -> none  [the longest x11 109 us: contract(): lax.dot_general(left_side, right_side, (((left_dim,), (right_dim,)), ((),...]
    psum x1 -> x0, waiting for transfers between devices: 104 us -> none  [local(): summed = lax.psum(grad_buckets, ('rows', 'seq'))]
    another operation x6 -> x2, other arithmetic: 50.9 us -> 0.65 us  [the longest x1 0.58 us: local(): where_at = jnp.stack([core, plane]).astype(jnp.int32)]
    concatenate x3 -> x1, local copies, waits for them, and re-layouts: 45.7 us -> 0.68 us  [local(): meta = jnp.concatenate(starts + [bw_ids, spot], axis=1)]
    ppermute x6 -> x44, starting transfers between devices: 12.1 us -> 47.1 us  [the longest x21 15.1 us: seq_swap(): return lax.ppermute(value, 'seq', [(s, s ^ bit) for s in range(count)])]
    all_gather x1 -> x0, waiting for transfers between devices: 25.9 us -> none  [local(): lax.all_gather(master.astype(jnp.bfloat16), 'rows', axis=0, tiled=True)]
    reduce_sum x14 -> x6, other arithmetic: 24.1 us -> 1.39 us  [the longest x1 0.63 us: local(): where = jnp.sum(jnp.where(order == row_at, ids, 0))]
  transfers between devices with their start and end apart: 8 -> 44, of which waited for: 2 -> 7; matrix products, arithmetic and copies ran while one was open for 28% -> 9% of each run, Pallas kernels for 0% -> 39%
where the time goes in v2:
time: 261 us; the launch traced here: 260 us
  Pallas kernels  166 us (64%)
  starting transfers between devices  47.1 us (18%)
  local copies, waits for them, and re-layouts  24.7 us (9%)
  waiting for transfers between devices  14.4 us (6%)
  other arithmetic  6.37 us (2%)
    pallas_call x1, Pallas kernels, forward(): pl.pallas_call(functools.partial(forward_body, parts=len(sources), tiles=...  56.5 us
    pallas_call x3, Pallas kernels, mlp_backward(): pl.pallas_call(functools.partial(mlp_body, utts=utts), grid=(count // til...  25.1 us
    pallas_call x2, Pallas kernels, wave_forward(): pl.pallas_call(functools.partial(wave_body, row=row, tiles=tiles, utts=ut...  22.7 us
    pallas_call x2, Pallas kernels, spectrum_cotangent(): pl.pallas_call(functools.partial(pre_body, row=row, tiles=tiles, utts=utt...  20.7 us
    pallas_call x2, Pallas kernels, norm_backward(): pl.pallas_call(functools.partial(norm_body, row=row, tiles=tiles, utts=ut...  19.9 us
    ppermute x21, starting transfers between devices, seq_swap(): return lax.ppermute(value, 'seq', [(s, s ^ bit) for s in range(count)])  15.1 us
    ppermute x6, starting transfers between devices, shifted(): lax.ppermute(value, 'seq', [(i - distance, i) for i in devices if i - dis...  10.5 us
    pallas_call x2, Pallas kernels, conv_backward(): pl.pallas_call(functools.partial(conv_body, row=row, tiles=tiles, utts=ut...  10.2 us
  transfers between devices with their start and end apart: 44, of which 7 were waited for; matrix products, arithmetic and copies ran while one was open for 9% of the time, Pallas kernels for 39%

profile of v2, /device:TPU:0, one launch (start us, length us, event | category | flops | bytes accessed | tf_op | source)
XLA Modules:
  0.0 260.0 jit_solution(4119127313147831835)
XLA Ops:
  0.6 1.2 dynamic-slice_convert_fusion.rest_0_
  1.9 3.1 %collective-permute-start.2 = (bf16[27,16,512]{2,1,0:T(8,128)(2,1)S(1)}, bf16[27,16,512]{2,1,0:T(8,128)(2,1)}, u32[]{:S(2)}, u32[]{:S(2)}) collective-permute-start(bf16[27,16,512]{2,1,0:T(8,128)(2,1)S(1)} %dynamic-slice_convert_fusion.rest_0_), channel_id=1, source_target_pairs={{0,8},{1,9},{2,10},{3,11},{8,16},{9,17},{10,18},{11,19},{16,24},{1... | collective-permute-start | bytes 1327112 | tf_op jit(solution)/shard_map/ppermute | solution.py:1010
  5.8 2.4 collective-permute-start
  8.2 2.3 reshape.98
  10.5 1.4 reshape.95.wave_ref
  12.0 1.3 collective-permute-start.6
  16.7 1.8 collective-permute-start.3
  18.7 1.4 collective-permute-start.10
  20.2 10.3 %spectrum_cotangent_0.1.rest_0_ = bf16[2048,1536]{1,0:T(8,128)(2,1)} custom-call(s32[2,11]{1,0:T(2,128)} %concatenate.3.meta, bf16[2,1024,320]{2,1,0:T(8,128)(2,1)} %copy-done.1, bf16[2,16,320]{2,1,0:T(8,128)(2,1)} %copy-done.20, bf16[1536,1536]{1,0:T(8,128)(2,1)} %constant.77.clone.synth_ref, f32[8,384]{1,0:T(8,128)} %constant.78.clone.win_ref), custom_call_target="tpu_custom_call" | custom-call | flops 4831838208 | bytes 11534336 | tf_op jit(solution)/shard_map/spectrum_cotangent_0/pallas_call | solution.py:241
  31.3 1.6 collective-permute-start.7
  33.4 10.3 %spectrum_cotangent_1.1.cot_ref = bf16[2048,1536]{1,0:T(8,128)(2,1)} custom-call(s32[2,11]{1,0:T(2,128)} %concatenate.3.meta, bf16[2,1024,320]{2,1,0:T(8,128)(2,1)} %copy-done.1, bf16[2,16,320]{2,1,0:T(8,128)(2,1)} %copy-done.20, bf16[1536,1536]{1,0:T(8,128)(2,1)} %constant.77.clone.synth_ref, ...), custom_call_target="tpu_custom_call", output_to_operand_aliasing={{}: (5, {})} | custom-call | flops 4831838208 | bytes 11534336 | tf_op jit(solution)/shard_map/spectrum_cotangent_1/pallas_call | solution.py:241
  43.8 1.2 collective-permute-done.8.rest_12_
  45.0 1.6 collective-permute-start.16
  46.8 1.5 collective-permute-start.1
  48.5 1.4 collective-permute-done.1.high_ref
  50.0 2.6 collective-permute-start.12
  53.1 3.3 %collective-permute-done.16.rest_14_ = bf16[27,16,512]{2,1,0:T(8,128)(2,1)} collective-permute-done((bf16[27,16,512]{2,1,0:T(8,128)(2,1)S(1)}, bf16[27,16,512]{2,1,0:T(8,128)(2,1)}, u32[]{:S(2)}, u32[]{:S(2)}) %collective-permute-start.16) | collective-permute-done | bytes 442400 | tf_op jit(solution)/shard_map/ppermute | solution.py:1010
  59.2 56.5 %forward.1 = (bf16[4384,512]{1,0:T(8,128)(2,1)}, bf16[2048,1536]{1,0:T(8,128)(2,1)}, bf16[2048,1536]{1,0:T(8,128)(2,1)}, bf16[2048,1536]{1,0:T(8,128)(2,1)}, bf1...) custom-call(s32[2,11]{1,0:T(2,128)} %concatenate.3.meta, ...), custom_call_target="tpu_custom_call" | custom-call | flops 16106127360 | bytes 41943040 | tf_op jit(solution)/shard_map/forward/pallas_call | solution.py:521
  116.3 0.9 slice.128
  117.2 2.2 collective-permute-start.29
  119.4 8.4 %mlp_backward_0.1 = (bf16[2048,1536]{1,0:T(8,128)(2,1)}, bf16[32,16,512]{2,1,0:T(8,128)(2,1)}, bf16[32,16,512]{2,1,0:T(8,128)(2,1)}, f32[8,512]{1,0:T(8,128)}) custom-call(s32[2,11]{1,0:T(2,128)} %concatenate.3.meta, bf16[2048,512]{1,0:T(8,128)(2,1)} %get-tuple-element.109.low_ref, bf16[2048,1536]{1,0:T(8,128)(2,1)} %get-tuple-element.110.act_ref, ...), custom_call_target="tpu_custom_call" | custom-call | flops 3221225472 | bytes 12582912 | tf_op jit(solution)/shard_map/mlp_backward_0/pallas_call | solution.py:608
  127.9 2.1 collective-permute-start.19
  131.0 8.4 %mlp_backward_1.1 = (bf16[2048,1536]{1,0:T(8,128)(2,1)}, bf16[32,16,512]{2,1,0:T(8,128)(2,1)}, bf16[32,16,512]{2,1,0:T(8,128)(2,1)}, f32[8,512]{1,0:T(8,128)}) custom-call(s32[2,11]{1,0:T(2,128)} %concatenate.3.meta, bf16[2048,512]{1,0:T(8,128)(2,1)} %get-tuple-element.109.low_ref, ...), custom_call_target="tpu_custom_call", output_to_operand_aliasing={{0}: (6, {})} | custom-call | flops 3221225472 | bytes 12582912 | tf_op jit(solution)/shard_map/mlp_backward_1/pallas_call | solution.py:608
  140.6 1.8 collective-permute-start.23
  142.4 8.3 %mlp_backward_2.1 = (bf16[2048,1536]{1,0:T(8,128)(2,1)}, bf16[32,16,512]{2,1,0:T(8,128)(2,1)}, bf16[32,16,512]{2,1,0:T(8,128)(2,1)}, f32[8,512]{1,0:T(8,128)}) custom-call(s32[2,11]{1,0:T(2,128)} %concatenate.3.meta, bf16[2048,512]{1,0:T(8,128)(2,1)} %get-tuple-element.109.low_ref, ...), custom_call_target="tpu_custom_call", output_to_operand_aliasing={{0}: (6, {})} | custom-call | flops 3221225472 | bytes 12582912 | tf_op jit(solution)/shard_map/mlp_backward_2/pallas_call | solution.py:608
  153.0 9.8 %norm_backward_0.1 = (f32[1024,512]{1,0:T(8,128)}, f32[2,8,512]{2,1,0:T(8,128)}, f32[16,8,512]{2,1,0:T(8,128)}) custom-call(s32[2,11]{1,0:T(2,128)} %concatenate.3.meta, bf16[2,1024,512]{2,1,0:T(8,128)(2,1)} %x_ref.5, bf16[2,16,512]{2,1,0:T(8,128)(2,1)} %copy-done.13, bf16[2,16,512]{2,1,0:T(8,128)(2,1)} %copy-done.14, ...), custom_call_target="tpu_custom_call" | custom-call | flops 1610612736 | bytes 12582912 | tf_op jit(solution)/shard_map/norm_backward_0/pallas_call | solution.py:761
  163.8 1.8 collective-permute-start.25
  165.6 10.1 %norm_backward_1.1 = (f32[1024,512]{1,0:T(8,128)}, f32[2,8,512]{2,1,0:T(8,128)}, f32[16,8,512]{2,1,0:T(8,128)}, f32[32,512]{1,0:T(8,128)}) custom-call(s32[2,11]{1,0:T(2,128)} %concatenate.3.meta, bf16[2,1024,512]{2,1,0:T(8,128)(2,1)} %x_ref.5, bf16[2,16,512]{2,1,0:T(8,128)(2,1)} %copy-done.13, bf16[2,16,512]{2,1,0:T(8,128)(2,1)} %copy-done.14, ...), custom_call_target="tpu_custom_call" | custom-call | flops 1610612736 | bytes 12582912 | tf_op jit(solution)/shard_map/norm_backward_1/pallas_call | solution.py:761
  177.9 3.8 %to_slots.1 = bf16[216,8,512]{2,1,0:T(8,128)(2,1)} custom-call(s32[1,137]{1,0:T(1,128)} %bitcast.17, bf16[40,8,512]{2,1,0:T(8,128)(2,1)} %get-tuple-element.199.refs_0_, bf16[16,8,512]{2,1,0:T(8,128)(2,1)} %get-tuple-element.205.refs_1_, bf16[16,8,512]{2,1,0:T(8,128)(2,1)} %get-tuple-element.204.refs_2_, bf16[16,8,512]{2,1,0:T(8,128)(2,1)} %get-tuple-element.203.refs_3_, ...), custom_call_target="tpu_custom_call" | custom-call | bytes 6291456 | tf_op jit(solution)/shard_map/to_slots/pallas_call | solution.py:915
  181.6 1.1 fusion.7
  182.7 1.8 collective-permute-start.26
  185.5 11.3 %wave_forward_0.1.rest_0_ = f32[2,1024,320]{2,1,0:T(8,128)} custom-call(s32[2,11]{1,0:T(2,128)} %concatenate.3.meta, bf16[2048,1536]{1,0:T(8,128)(2,1)} %get-tuple-element.174.spec_ref.prev_ref, bf16[2048,1536]{1,0:T(8,128)(2,1)} %get-tuple-element.174.spec_ref.prev_ref, bf16[2,16,1536]{2,1,0:T(8,128)(2,1)} %copy-done.8, ...), custom_call_target="tpu_custom_call" | custom-call | flops 4831838208 | bytes 12582912 | tf_op jit(solution)/shard_map/wave_forward_0/pallas_call | solution.py:875
  197.0 1.8 collective-permute-start.30
  199.4 1.7 collective-permute-start.33
  201.1 1.6 collective-permute-start.34
  202.6 3.1 %collective-permute-done.34.high_ref = f32[2,8,512]{2,1,0:T(8,128)S(1)} collective-permute-done((f32[2,8,512]{2,1,0:T(8,128)S(1)}, f32[2,8,512]{2,1,0:T(8,128)S(1)}, u32[]{:S(2)}, u32[]{:S(2)}) %collective-permute-start.34) | collective-permute-done | bytes 32800 | tf_op jit(solution)/shard_map/ppermute | solution.py:99
  206.3 5.1 %conv_backward_0.1.rest_0_ = f32[2,1024,512]{2,1,0:T(8,128)} custom-call(s32[2,11]{1,0:T(2,128)} %concatenate.3.meta, f32[1024,512]{1,0:T(8,128)} %get-tuple-element.161.cg_ref.before_ref.after_ref, f32[1024,512]{1,0:T(8,128)} %get-tuple-element.161.cg_ref.before_ref.after_ref, f32[1024,512]{1,0:T(8,128)} %get-tuple-element.161.cg_ref.before_ref.after_ref, ...), custom_call_target="tpu_custom_call" | custom-call | flops 8388608 | bytes 6291456 | tf_op jit(solution)/shard_map/conv_backward_0/pallas_call | solution.py:821
  211.6 1.8 collective-permute-start.35
  213.7 1.6 collective-permute-start.37
  215.4 5.1 %conv_backward_1.1 = f32[2,1024,512]{2,1,0:T(8,128)} custom-call(s32[2,11]{1,0:T(2,128)} %concatenate.3.meta, f32[1024,512]{1,0:T(8,128)} %get-tuple-element.169.cg_ref.before_ref.after_ref, f32[1024,512]{1,0:T(8,128)} %get-tuple-element.169.cg_ref.before_ref.after_ref, ...), custom_call_target="tpu_custom_call", output_to_operand_aliasing={{}: (8, {})} | custom-call | flops 8388608 | bytes 6291456 | tf_op jit(solution)/shard_map/conv_backward_1/pallas_call | solution.py:821
  220.6 1.6 collective-permute-start.38
  222.2 1.6 collective-permute-start.39
  223.8 11.3 %wave_forward_1.1 = f32[2,1024,320]{2,1,0:T(8,128)} custom-call(s32[2,11]{1,0:T(2,128)} %concatenate.3.meta, bf16[2048,1536]{1,0:T(8,128)(2,1)} %get-tuple-element.174.spec_ref.prev_ref, bf16[2048,1536]{1,0:T(8,128)(2,1)} %get-tuple-element.174.spec_ref.prev_ref, bf16[2,16,1536]{2,1,0:T(8,128)(2,1)} %copy-done.8, ...), custom_call_target="tpu_custom_call", output_to_operand_aliasing={{}: (6, {})} | custom-call | flops 4831838208 | bytes 12582912 | tf_op jit(solution)/shard_map/wave_forward_1/pallas_call | solution.py:875
  235.2 2.6 collective-permute-start.40
  237.8 6.0 %reshape.97 = f32[2,327680]{1,0:T(2,128)} reshape(f32[2,1024,320]{2,1,0:T(8,128)} %wave_forward_1.1) | data formatting | bytes 5242880 | tf_op jit(solution)/shard_map/reshape | solution.py:1154
  244.4 1.7 collective-permute-start.43
  246.7 4.1 %collective-permute-done.43 = f32[32,512]{1,0:T(8,128)S(1)} collective-permute-done((f32[32,512]{1,0:T(8,128)S(1)}, f32[32,512]{1,0:T(8,128)S(1)}, u32[]{:S(2)}, u32[]{:S(2)}) %collective-permute-start.43) | collective-permute-done | bytes 65568 | tf_op jit(solution)/shard_map/ppermute | solution.py:94
  252.8 7.0 %adam.1 = (f32[27,32,512]{2,1,0:T(8,128)}, f32[27,32,512]{2,1,0:T(8,128)}, f32[27,32,512]{2,1,0:T(8,128)}) custom-call(s32[1,27]{1,0:T(1,128)} %add_bitcast_fusion.places, s32[2]{0:T(128)} %pad_add_fusion.1.spot, bf16[27,8,512]{2,1,0:T(8,128)(2,1)} %copy-done.2, bf16[27,8,512]{2,1,0:T(8,128)(2,1)} %copy-done.11, bf16[27,8,512]{2,1,0:T(8,128)(2,1)} %copy-done.10, ...), custom_call_target="tpu_custom_call" | custom-call | bytes 12582912 | tf_op jit(solution)/shard_map/adam/pallas_call | solution.py:957
  (178 shorter events, 23.8 us)
Async XLA Ops:
  1.9 14.6 %collective-permute-start.2 = (bf16[27,16,512]{2,1,0:T(8,128)(2,1)S(1)}, bf16[27,16,512]{2,1,0:T(8,128)(2,1)}, u32[]{:S(2)}, u32[]{:S(2)}) collective-permute-start(bf16[27,16,512]{2,1,0:T(8,128)(2,1)S(1)} %dynamic-slice_convert_fusion.rest_0_), channel_id=1, source_target_pairs={{0,8},{1,9},{2,10},{3,11},{8,16},{9,17},{10,18},{11,19},{16,24},{1... | collective-permute-start | bytes 1327112 | tf_op jit(solution)/shard_map/ppermute | solution.py:1010
  5.0 11.7 %collective-permute-start.4 = (bf16[27,16,512]{2,1,0:T(8,128)(2,1)S(1)}, bf16[27,16,512]{2,1,0:T(8,128)(2,1)}, u32[]{:S(2)}, u32[]{:S(2)}) collective-permute-start(bf16[27,16,512]{2,1,0:T(8,128)(2,1)S(1)} %dynamic-slice_convert_fusion.rest_0_), channel_id=1, source_target_pairs={{0,4},{1,5},{2,6},{3,7},{8,0},{9,1},{10,2},{11,3},{16,8},{17,9},{1... | collective-permute-start | bytes 1327112 | tf_op jit(solution)/shard_map/ppermute | solution.py:1012
  5.0 47.6 %collective-permute-start.9 = (bf16[27,16,512]{2,1,0:T(8,128)(2,1)S(1)}, bf16[27,16,512]{2,1,0:T(8,128)(2,1)}, u32[]{:S(2)}, u32[]{:S(2)}) collective-permute-start(bf16[27,16,512]{2,1,0:T(8,128)(2,1)S(1)} %dynamic-slice_convert_fusion.rest_0_), channel_id=1, source_target_pairs={{0,1},{1,0},{2,3},{3,2},{4,5},{5,4},{6,7},{7,6},{8,9},{9,8},{10,11... | collective-permute-start | bytes 1327112 | tf_op jit(solution)/shard_map/ppermute | solution.py:89
  5.8 41.1 %collective-permute-start = (bf16[2,16,512]{2,1,0:T(8,128)(2,1)S(1)}, bf16[2,16,512]{2,1,0:T(8,128)(2,1)S(1)}, u32[]{:S(2)}, u32[]{:S(2)}) collective-permute-start(bf16[2,16,512]{2,1,0:T(8,128)(2,1)S(1)} %get-tuple-element.191), channel_id=1, source_target_pairs={{0,1},{1,2},{2,3},{4,5},{5,6},{6,7},{8,9},{9,10},{10,11},{12,13},{... | collective-permute-start | bytes 98312 | tf_op jit(solution)/shard_map/ppermute | solution.py:99
  12.0 6.8 %collective-permute-start.6 = (bf16[2,16,320]{2,1,0:T(8,128)(2,1)S(1)}, bf16[2,16,320]{2,1,0:T(8,128)(2,1)S(1)}, u32[]{:S(2)}, u32[]{:S(2)}) collective-permute-start(bf16[2,16,320]{2,1,0:T(8,128)(2,1)S(1)} %slice.120), channel_id=1, source_target_pairs={{1,0},{2,1},{3,2},{5,4},{6,5},{7,6},{9,8},{10,9},{11,10},{13,12},{... | collective-permute-start | bytes 61448 | tf_op jit(solution)/shard_map/ppermute | solution.py:99
  16.7 13.8 %collective-permute-start.3 = (bf16[27,16,512]{2,1,0:T(8,128)(2,1)}, bf16[27,16,512]{2,1,0:T(8,128)(2,1)S(1)}, u32[]{:S(2)}, u32[]{:S(2)}) collective-permute-start(bf16[27,16,512]{2,1,0:T(8,128)(2,1)} %collective-permute-done.2.rest_2_), channel_id=1, source_target_pairs={{0,8},{1,9},{2,10},{3,11},{8,16},{9,17},{10,18},{11,19},{16,24},{1... | collective-permute-start | bytes 1327112 | tf_op jit(solution)/shard_map/ppermute | solution.py:1010
  18.5 12.8 %collective-permute-start.5 = (bf16[27,16,512]{2,1,0:T(8,128)(2,1)}, bf16[27,16,512]{2,1,0:T(8,128)(2,1)S(1)}, u32[]{:S(2)}, u32[]{:S(2)}) collective-permute-start(bf16[27,16,512]{2,1,0:T(8,128)(2,1)} %collective-permute-done.4.rest_4_), channel_id=1, source_target_pairs={{0,4},{1,5},{2,6},{3,7},{8,0},{9,1},{10,2},{11,3},{16,8},{17,9},{1... | collective-permute-start | bytes 1327112 | tf_op jit(solution)/shard_map/ppermute | solution.py:1012
  18.7 33.9 %collective-permute-start.10 = (bf16[27,16,512]{2,1,0:T(8,128)(2,1)}, bf16[27,16,512]{2,1,0:T(8,128)(2,1)}, u32[]{:S(2)}, u32[]{:S(2)}) collective-permute-start(bf16[27,16,512]{2,1,0:T(8,128)(2,1)} %collective-permute-done.2.rest_2_), channel_id=1, source_target_pairs={{0,1},{1,0},{2,3},{3,2},{4,5},{5,4},{6,7},{7,6},{8,9},{9,8},{10,11... | collective-permute-start | bytes 1327112 | tf_op jit(solution)/shard_map/ppermute | solution.py:89
  30.5 19.5 %copy-start.25 = (bf16[27,16,512]{2,1,0:T(8,128)(2,1)}, bf16[27,16,512]{2,1,0:T(8,128)(2,1)S(1)}, u32[]{:S(2)}) copy-start(bf16[27,16,512]{2,1,0:T(8,128)(2,1)S(1)} %collective-permute-done.3.rest_6_) | copy-start | bytes 1327108
  31.3 12.4 %collective-permute-start.7 = (bf16[27,16,512]{2,1,0:T(8,128)(2,1)S(1)}, bf16[27,16,512]{2,1,0:T(8,128)(2,1)S(1)}, u32[]{:S(2)}, u32[]{:S(2)}) collective-permute-start(bf16[27,16,512]{2,1,0:T(8,128)(2,1)S(1)} %collective-permute-done.3.rest_6_), channel_id=1, source_target_pairs={{0,8},{1,9},{2,10},{3,11},{8,16},{9,17},{10,18},{11,19},{16,24},{1... | collective-permute-start | bytes 1327112 | tf_op jit(solution)/shard_map/ppermute | solution.py:1010
  32.9 12.1 %collective-permute-start.8 = (bf16[27,16,512]{2,1,0:T(8,128)(2,1)S(1)}, bf16[27,16,512]{2,1,0:T(8,128)(2,1)S(1)}, u32[]{:S(2)}, u32[]{:S(2)}) collective-permute-start(bf16[27,16,512]{2,1,0:T(8,128)(2,1)S(1)} %collective-permute-done.5.rest_8_), channel_id=1, source_target_pairs={{0,4},{1,5},{2,6},{3,7},{8,0},{9,1},{10,2},{11,3},{16,8},{17,9},{1... | collective-permute-start | bytes 1327112 | tf_op jit(solution)/shard_map/ppermute | solution.py:1012
  43.7 15.5 %copy-start.27 = (bf16[27,16,512]{2,1,0:T(8,128)(2,1)}, bf16[27,16,512]{2,1,0:T(8,128)(2,1)S(1)}, u32[]{:S(2)}) copy-start(bf16[27,16,512]{2,1,0:T(8,128)(2,1)S(1)} %collective-permute-done.7.rest_10_) | copy-start | bytes 1327108
  43.7 9.3 %collective-permute-start.11 = (bf16[27,16,512]{2,1,0:T(8,128)(2,1)}, bf16[27,16,512]{2,1,0:T(8,128)(2,1)S(1)}, u32[]{:S(2)}, u32[]{:S(2)}) collective-permute-start(bf16[27,16,512]{2,1,0:T(8,128)(2,1)} %collective-permute-done.4.rest_4_), channel_id=1, source_target_pairs={{0,1},{1,0},{2,3},{3,2},{4,5},{5,4},{6,7},{7,6},{8,9},{9,8},{10,11... | collective-permute-start | bytes 1327112 | tf_op jit(solution)/shard_map/ppermute | solution.py:89
  45.0 11.5 %collective-permute-start.16 = (bf16[27,16,512]{2,1,0:T(8,128)(2,1)S(1)}, bf16[27,16,512]{2,1,0:T(8,128)(2,1)}, u32[]{:S(2)}, u32[]{:S(2)}) collective-permute-start(bf16[27,16,512]{2,1,0:T(8,128)(2,1)S(1)} %collective-permute-done.7.rest_10_), channel_id=1, source_target_pairs={{0,8},{1,9},{2,10},{3,11},{8,16},{9,17},{10,18},{11,19},{16,24},{1... | collective-permute-start | bytes 1327112 | tf_op jit(solution)/shard_map/ppermute | solution.py:1010
  46.8 3.1 %collective-permute-start.1 = (bf16[2,16,512]{2,1,0:T(8,128)(2,1)S(1)}, bf16[2,16,512]{2,1,0:T(8,128)(2,1)S(1)}, u32[]{:S(2)}, u32[]{:S(2)}) collective-permute-start(bf16[2,16,512]{2,1,0:T(8,128)(2,1)S(1)} %get-tuple-element.190), channel_id=1, source_target_pairs={{1,0},{2,1},{3,2},{5,4},{6,5},{7,6},{9,8},{10,9},{11,10},{13,12},{... | collective-permute-start | bytes 98312 | tf_op jit(solution)/shard_map/ppermute | solution.py:99
  50.0 7.6 %collective-permute-start.12 = (bf16[27,16,512]{2,1,0:T(8,128)(2,1)S(1)}, bf16[27,16,512]{2,1,0:T(8,128)(2,1)S(1)}, u32[]{:S(2)}, u32[]{:S(2)}) collective-permute-start(bf16[27,16,512]{2,1,0:T(8,128)(2,1)S(1)} %collective-permute-done.3.rest_6_), channel_id=1, source_target_pairs={{0,1},{1,0},{2,3},{3,2},{4,5},{5,4},{6,7},{7,6},{8,9},{9,8},{10,11... | collective-permute-start | bytes 1327112 | tf_op jit(solution)/shard_map/ppermute | solution.py:89
  52.5 5.0 %collective-permute-start.13 = (bf16[27,16,512]{2,1,0:T(8,128)(2,1)}, bf16[27,16,512]{2,1,0:T(8,128)(2,1)S(1)}, u32[]{:S(2)}, u32[]{:S(2)}) collective-permute-start(bf16[27,16,512]{2,1,0:T(8,128)(2,1)} %copy-done.26), channel_id=1, source_target_pairs={{0,1},{1,0},{2,3},{3,2},{4,5},{5,4},{6,7},{7,6},{8,9},{9,8},{10,11... | collective-permute-start | bytes 1327112 | tf_op jit(solution)/shard_map/ppermute | solution.py:89
  52.6 5.0 %collective-permute-start.14 = (bf16[27,16,512]{2,1,0:T(8,128)(2,1)S(1)}, bf16[27,16,512]{2,1,0:T(8,128)(2,1)S(1)}, u32[]{:S(2)}, u32[]{:S(2)}) collective-permute-start(bf16[27,16,512]{2,1,0:T(8,128)(2,1)S(1)} %collective-permute-done.7.rest_10_), channel_id=1, source_target_pairs={{0,1},{1,0},{2,3},{3,2},{4,5},{5,4},{6,7},{7,6},{8,9},{9,8},{10,11... | collective-permute-start | bytes 1327112 | tf_op jit(solution)/shard_map/ppermute | solution.py:89
  53.1 4.6 %collective-permute-start.15 = (bf16[27,16,512]{2,1,0:T(8,128)(2,1)S(1)}, bf16[27,16,512]{2,1,0:T(8,128)(2,1)S(1)}, u32[]{:S(2)}, u32[]{:S(2)}) collective-permute-start(bf16[27,16,512]{2,1,0:T(8,128)(2,1)S(1)} %collective-permute-done.8.rest_12_), channel_id=1, source_target_pairs={{0,1},{1,0},{2,3},{3,2},{4,5},{5,4},{6,7},{7,6},{8,9},{9,8},{10,11... | collective-permute-start | bytes 1327112 | tf_op jit(solution)/shard_map/ppermute | solution.py:89
  56.5 2.7 %collective-permute-start.17 = (bf16[27,16,512]{2,1,0:T(8,128)(2,1)}, bf16[27,16,512]{2,1,0:T(8,128)(2,1)}, u32[]{:S(2)}, u32[]{:S(2)}) collective-permute-start(bf16[27,16,512]{2,1,0:T(8,128)(2,1)} %collective-permute-done.16.rest_14_), channel_id=1, source_target_pairs={{0,1},{1,0},{2,3},{3,2},{4,5},{5,4},{6,7},{7,6},{8,9},{9,8},{10,11... | collective-permute-start | bytes 1327112 | tf_op jit(solution)/shard_map/ppermute | solution.py:89
  115.8 12.1 %collective-permute-start.18 = (bf16[40,16,512]{2,1,0:T(8,128)(2,1)}, bf16[40,16,512]{2,1,0:T(8,128)(2,1)S(1)}, u32[]{:S(2)}, u32[]{:S(2)}) collective-permute-start(bf16[40,16,512]{2,1,0:T(8,128)(2,1)} %get-tuple-element.108), channel_id=1, source_target_pairs={{0,1},{1,0},{2,3},{3,2},{4,5},{5,4},{6,7},{7,6},{8,9},{9,8},{10,11... | collective-permute-start | bytes 1966088 | tf_op jit(solution)/shard_map/ppermute | solution.py:89
  117.2 67.6 %collective-permute-start.29 = (bf16[2,16,1536]{2,1,0:T(8,128)(2,1)S(1)}, bf16[2,16,1536]{2,1,0:T(8,128)(2,1)S(1)}, u32[]{:S(2)}, u32[]{:S(2)}) collective-permute-start(bf16[2,16,1536]{2,1,0:T(8,128)(2,1)S(1)} %slice.128), channel_id=1, source_target_pairs={{0,1},{1,2},{2,3},{4,5},{5,6},{6,7},{8,9},{9,10},{10,11},{12,13},{... | collective-permute-start | bytes 294920 | tf_op jit(solution)/shard_map/ppermute | solution.py:99
  127.9 11.6 %collective-permute-start.19 = (bf16[32,16,512]{2,1,0:T(8,128)(2,1)}, bf16[32,16,512]{2,1,0:T(8,128)(2,1)S(1)}, u32[]{:S(2)}, u32[]{:S(2)}) collective-permute-start(bf16[32,16,512]{2,1,0:T(8,128)(2,1)} %get-tuple-element.119), channel_id=1, source_target_pairs={{0,1},{1,0},{2,3},{3,2},{4,5},{5,4},{6,7},{7,6},{8,9},{9,8},{10,11... | collective-permute-start | bytes 1572872 | tf_op jit(solution)/shard_map/ppermute | solution.py:89
  131.0 46.1 %collective-permute-start.22 = (bf16[40,8,512]{2,1,0:T(8,128)(2,1)S(1)}, bf16[40,8,512]{2,1,0:T(8,128)(2,1)S(1)}, u32[]{:S(2)}, u32[]{:S(2)}) collective-permute-start(bf16[40,8,512]{2,1,0:T(8,128)(2,1)S(1)} %get-tuple-element.198), channel_id=1, source_target_pairs={{0,2},{1,3},{2,0},{3,1},{4,6},{5,7},{6,4},{7,5},{8,10},{9,11},{10,... | collective-permute-start | bytes 983048 | tf_op jit(solution)/shard_map/ppermute | solution.py:89
  140.5 11.0 %collective-permute-start.20 = (bf16[32,16,512]{2,1,0:T(8,128)(2,1)S(1)}, bf16[32,16,512]{2,1,0:T(8,128)(2,1)S(1)}, u32[]{:S(2)}, u32[]{:S(2)}) collective-permute-start(bf16[32,16,512]{2,1,0:T(8,128)(2,1)S(1)} %copy-done.24), channel_id=1, source_target_pairs={{0,1},{1,0},{2,3},{3,2},{4,5},{5,4},{6,7},{7,6},{8,9},{9,8},{10,11... | collective-permute-start | bytes 1572872 | tf_op jit(solution)/shard_map/ppermute | solution.py:89
  140.6 10.2 %collective-permute-start.23 = (bf16[32,8,512]{2,1,0:T(8,128)(2,1)S(1)}, bf16[32,8,512]{2,1,0:T(8,128)(2,1)S(1)}, u32[]{:S(2)}, u32[]{:S(2)}) collective-permute-start(bf16[32,8,512]{2,1,0:T(8,128)(2,1)S(1)} %constant_dynamic-slice_fusion.3), channel_id=1, source_target_pairs={{0,2},{1,3},{2,0},{3,1},{4,6},{5,7},{6,4},{7,5},{8,10},{9,11},{10,... | collective-permute-start | bytes 786440 | tf_op jit(solution)/shard_map/ppermute | solution.py:89
  151.5 12.1 %collective-permute-start.21 = (bf16[32,16,512]{2,1,0:T(8,128)(2,1)}, bf16[32,16,512]{2,1,0:T(8,128)(2,1)S(1)}, u32[]{:S(2)}, u32[]{:S(2)}) collective-permute-start(bf16[32,16,512]{2,1,0:T(8,128)(2,1)} %get-tuple-element.133), channel_id=1, source_target_pairs={{0,1},{1,0},{2,3},{3,2},{4,5},{5,4},{6,7},{7,6},{8,9},{9,8},{10,11... | collective-permute-start | bytes 1572872 | tf_op jit(solution)/shard_map/ppermute | solution.py:89
  151.9 10.9 %collective-permute-start.24 = (bf16[32,8,512]{2,1,0:T(8,128)(2,1)S(1)}, bf16[32,8,512]{2,1,0:T(8,128)(2,1)S(1)}, u32[]{:S(2)}, u32[]{:S(2)}) collective-permute-start(bf16[32,8,512]{2,1,0:T(8,128)(2,1)S(1)} %constant_dynamic-slice_fusion.2), channel_id=1, source_target_pairs={{0,2},{1,3},{2,0},{3,1},{4,6},{5,7},{6,4},{7,5},{8,10},{9,11},{10,... | collective-permute-start | bytes 786440 | tf_op jit(solution)/shard_map/ppermute | solution.py:89
  163.8 12.6 %collective-permute-start.25 = (bf16[32,8,512]{2,1,0:T(8,128)(2,1)S(1)}, bf16[32,8,512]{2,1,0:T(8,128)(2,1)S(1)}, u32[]{:S(2)}, u32[]{:S(2)}) collective-permute-start(bf16[32,8,512]{2,1,0:T(8,128)(2,1)S(1)} %constant_dynamic-slice_fusion.1), channel_id=1, source_target_pairs={{0,2},{1,3},{2,0},{3,1},{4,6},{5,7},{6,4},{7,5},{8,10},{9,11},{10,... | collective-permute-start | bytes 786440 | tf_op jit(solution)/shard_map/ppermute | solution.py:89
  182.7 14.1 %collective-permute-start.26 = (bf16[27,8,512]{2,1,0:T(8,128)(2,1)S(1)}, bf16[27,8,512]{2,1,0:T(8,128)(2,1)S(1)}, u32[]{:S(2)}, u32[]{:S(2)}) collective-permute-start(bf16[27,8,512]{2,1,0:T(8,128)(2,1)S(1)} %get-tuple-element.197), channel_id=1, source_target_pairs={{0,8},{1,9},{2,10},{3,11},{8,16},{9,17},{10,18},{11,19},{16,24},{1... | collective-permute-start | bytes 663560 | tf_op jit(solution)/shard_map/ppermute | solution.py:1128
  184.5 14.9 %copy-start.18 = (f32[2,8,512]{2,1,0:T(8,128)S(1)}, f32[2,8,512]{2,1,0:T(8,128)}, u32[]{:S(2)}) copy-start(f32[2,8,512]{2,1,0:T(8,128)} %get-tuple-element.162) | copy-start | bytes 98308
  184.5 14.9 %copy-start.19 = (f32[2,8,512]{2,1,0:T(8,128)S(1)}, f32[2,8,512]{2,1,0:T(8,128)}, u32[]{:S(2)}) copy-start(f32[2,8,512]{2,1,0:T(8,128)} %get-tuple-element.163) | copy-start | bytes 98308
  184.5 12.3 %collective-permute-start.27 = (bf16[27,8,512]{2,1,0:T(8,128)(2,1)S(1)}, bf16[27,8,512]{2,1,0:T(8,128)(2,1)S(1)}, u32[]{:S(2)}, u32[]{:S(2)}) collective-permute-start(bf16[27,8,512]{2,1,0:T(8,128)(2,1)S(1)} %get-tuple-element.196), channel_id=1, source_target_pairs={{0,4},{1,5},{2,6},{3,7},{8,0},{9,1},{10,2},{11,3},{16,8},{17,9},{1... | collective-permute-start | bytes 663560 | tf_op jit(solution)/shard_map/ppermute | solution.py:1130
  184.8 12.0 %collective-permute-start.28 = (f32[32,512]{1,0:T(8,128)S(1)}, f32[32,512]{1,0:T(8,128)S(1)}, u32[]{:S(2)}, u32[]{:S(2)}) collective-permute-start(f32[32,512]{1,0:T(8,128)S(1)} %copy-done.17), channel_id=1, source_target_pairs={{0,1},{1,0},{2,3},{3,2},{4,5},{5,4},{6,7},{7,6},{8,9},{9,8},{10,11... | collective-permute-start | bytes 196616 | tf_op jit(solution)/shard_map/ppermute | solution.py:89
  197.0 14.5 %collective-permute-start.30 = (bf16[27,8,512]{2,1,0:T(8,128)(2,1)S(1)}, bf16[27,8,512]{2,1,0:T(8,128)(2,1)S(1)}, u32[]{:S(2)}, u32[]{:S(2)}) collective-permute-start(bf16[27,8,512]{2,1,0:T(8,128)(2,1)S(1)} %get-tuple-element.195), channel_id=1, source_target_pairs={{0,8},{1,9},{2,10},{3,11},{8,16},{9,17},{10,18},{11,19},{16,24},{1... | collective-permute-start | bytes 663560 | tf_op jit(solution)/shard_map/ppermute | solution.py:1128
  198.7 12.8 %collective-permute-start.31 = (bf16[27,8,512]{2,1,0:T(8,128)(2,1)S(1)}, bf16[27,8,512]{2,1,0:T(8,128)(2,1)S(1)}, u32[]{:S(2)}, u32[]{:S(2)}) collective-permute-start(bf16[27,8,512]{2,1,0:T(8,128)(2,1)S(1)} %get-tuple-element.194), channel_id=1, source_target_pairs={{0,4},{1,5},{2,6},{3,7},{8,0},{9,1},{10,2},{11,3},{16,8},{17,9},{1... | collective-permute-start | bytes 663560 | tf_op jit(solution)/shard_map/ppermute | solution.py:1130
  199.1 12.4 %collective-permute-start.32 = (f32[32,512]{1,0:T(8,128)S(1)}, f32[32,512]{1,0:T(8,128)S(1)}, u32[]{:S(2)}, u32[]{:S(2)}) collective-permute-start(f32[32,512]{1,0:T(8,128)S(1)} %add.203), channel_id=1, source_target_pairs={{0,2},{1,3},{2,0},{3,1},{4,6},{5,7},{6,4},{7,5},{8,10},{9,11},{10,... | collective-permute-start | bytes 196616 | tf_op jit(solution)/shard_map/ppermute | solution.py:89
  199.4 3.2 %collective-permute-start.33 = (f32[2,8,512]{2,1,0:T(8,128)S(1)}, f32[2,8,512]{2,1,0:T(8,128)S(1)}, u32[]{:S(2)}, u32[]{:S(2)}) collective-permute-start(f32[2,8,512]{2,1,0:T(8,128)S(1)} %get-tuple-element.213), channel_id=1, source_target_pairs={{0,1},{1,2},{2,3},{4,5},{5,6},{6,7},{8,9},{9,10},{10,11},{12,13},{... | collective-permute-start | bytes 98312 | tf_op jit(solution)/shard_map/ppermute | solution.py:99
  201.1 4.7 %collective-permute-start.34 = (f32[2,8,512]{2,1,0:T(8,128)S(1)}, f32[2,8,512]{2,1,0:T(8,128)S(1)}, u32[]{:S(2)}, u32[]{:S(2)}) collective-permute-start(f32[2,8,512]{2,1,0:T(8,128)S(1)} %get-tuple-element.212), channel_id=1, source_target_pairs={{1,0},{2,1},{3,2},{5,4},{6,5},{7,6},{9,8},{10,9},{11,10},{13,12},{... | collective-permute-start | bytes 98312 | tf_op jit(solution)/shard_map/ppermute | solution.py:99
  211.6 8.9 %collective-permute-start.35 = (bf16[27,8,512]{2,1,0:T(8,128)(2,1)S(1)}, bf16[27,8,512]{2,1,0:T(8,128)(2,1)S(1)}, u32[]{:S(2)}, u32[]{:S(2)}) collective-permute-start(bf16[27,8,512]{2,1,0:T(8,128)(2,1)S(1)} %get-tuple-element.193), channel_id=1, source_target_pairs={{0,8},{1,9},{2,10},{3,11},{8,16},{9,17},{10,18},{11,19},{16,24},{1... | collective-permute-start | bytes 663560 | tf_op jit(solution)/shard_map/ppermute | solution.py:1128
  213.4 7.1 %collective-permute-start.36 = (bf16[27,8,512]{2,1,0:T(8,128)(2,1)S(1)}, bf16[27,8,512]{2,1,0:T(8,128)(2,1)S(1)}, u32[]{:S(2)}, u32[]{:S(2)}) collective-permute-start(bf16[27,8,512]{2,1,0:T(8,128)(2,1)S(1)} %get-tuple-element.192), channel_id=1, source_target_pairs={{0,4},{1,5},{2,6},{3,7},{8,0},{9,1},{10,2},{11,3},{16,8},{17,9},{1... | collective-permute-start | bytes 663560 | tf_op jit(solution)/shard_map/ppermute | solution.py:1130
  213.7 6.8 %collective-permute-start.37 = (f32[32,512]{1,0:T(8,128)S(1)}, f32[32,512]{1,0:T(8,128)S(1)}, u32[]{:S(2)}, u32[]{:S(2)}) collective-permute-start(f32[32,512]{1,0:T(8,128)S(1)} %add.206), channel_id=1, source_target_pairs={{0,4},{4,0},{8,12},{12,8},{16,20},{20,16},{24,28},{28,24},{1,5},{5... | collective-permute-start | bytes 196616 | tf_op jit(solution)/shard_map/ppermute | solution.py:94
  220.6 14.6 %collective-permute-start.38 = (bf16[27,8,512]{2,1,0:T(8,128)(2,1)S(1)}, bf16[27,8,512]{2,1,0:T(8,128)(2,1)S(1)}, u32[]{:S(2)}, u32[]{:S(2)}) collective-permute-start(bf16[27,8,512]{2,1,0:T(8,128)(2,1)S(1)} %add_convert_fusion.5), channel_id=1, source_target_pairs={{0,8},{1,9},{2,10},{3,11},{8,16},{9,17},{10,18},{11,19},{16,24},{1... | collective-permute-start | bytes 663560 | tf_op jit(solution)/shard_map/ppermute | solution.py:1128
  222.2 12.9 %collective-permute-start.39 = (f32[32,512]{1,0:T(8,128)S(1)}, f32[32,512]{1,0:T(8,128)S(1)}, u32[]{:S(2)}, u32[]{:S(2)}) collective-permute-start(f32[32,512]{1,0:T(8,128)S(1)} %add.209), channel_id=1, source_target_pairs={{0,8},{4,12},{8,0},{12,4},{16,24},{20,28},{24,16},{28,20},{1,9},{5... | collective-permute-start | bytes 196616 | tf_op jit(solution)/shard_map/ppermute | solution.py:94
  235.2 8.6 %collective-permute-start.40 = (bf16[27,8,512]{2,1,0:T(8,128)(2,1)S(1)}, bf16[27,8,512]{2,1,0:T(8,128)(2,1)S(1)}, u32[]{:S(2)}, u32[]{:S(2)}) collective-permute-start(bf16[27,8,512]{2,1,0:T(8,128)(2,1)S(1)} %add_convert_fusion.4.own), channel_id=1, source_target_pairs={{0,2},{1,3},{2,0},{3,1},{4,6},{5,7},{6,4},{7,5},{8,10},{9,11},{10,... | collective-permute-start | bytes 663560 | tf_op jit(solution)/shard_map/ppermute | solution.py:89
  237.8 13.6 %collective-permute-start.41 = (bf16[27,8,512]{2,1,0:T(8,128)(2,1)S(1)}, bf16[27,8,512]{2,1,0:T(8,128)(2,1)S(1)}, u32[]{:S(2)}, u32[]{:S(2)}) collective-permute-start(bf16[27,8,512]{2,1,0:T(8,128)(2,1)S(1)} %add_convert_fusion.4.own), channel_id=1, source_target_pairs={{0,1},{1,0},{2,3},{3,2},{4,5},{5,4},{6,7},{7,6},{8,9},{9,8},{10,11... | collective-permute-start | bytes 663560 | tf_op jit(solution)/shard_map/ppermute | solution.py:89
  243.9 7.5 %collective-permute-start.42 = (bf16[27,8,512]{2,1,0:T(8,128)(2,1)S(1)}, bf16[27,8,512]{2,1,0:T(8,128)(2,1)S(1)}, u32[]{:S(2)}, u32[]{:S(2)}) collective-permute-start(bf16[27,8,512]{2,1,0:T(8,128)(2,1)S(1)} %collective-permute-done.40.far), channel_id=1, source_target_pairs={{0,1},{1,0},{2,3},{3,2},{4,5},{5,4},{6,7},{7,6},{8,9},{9,8},{10,11... | collective-permute-start | bytes 663560 | tf_op jit(solution)/shard_map/ppermute | solution.py:89
  244.4 6.4 %collective-permute-start.43 = (f32[32,512]{1,0:T(8,128)S(1)}, f32[32,512]{1,0:T(8,128)S(1)}, u32[]{:S(2)}, u32[]{:S(2)}) collective-permute-start(f32[32,512]{1,0:T(8,128)S(1)} %add.211), channel_id=1, source_target_pairs={{0,16},{4,20},{8,24},{12,28},{16,0},{20,4},{24,8},{28,12},{1,17},{... | collective-permute-start | bytes 196616 | tf_op jit(solution)/shard_map/ppermute | solution.py:94
  (32 other events, 181.9 us)

commit v3 on v2

--- a/solution.py
+++ b/solution.py
@@ -40,7 +40,9 @@
 QUART = BR // 4
 EDGE = 16
 TILE = 256
-CHUNK = 512
+CHUNK = 768
+HALF_BIN = 384
+PAIR = 5
 LANE = 128
 AXES = ("rows", "seq")
 
@@ -50,15 +52,29 @@
 VMEM_BYTES = 60 * MIB
 
 
+def bin_order():
+    order = np.full(BIN_PAD, -1)
+    order[: (BINS + 1) // 2] = np.arange(0, BINS, 2)
+    order[HALF_BIN : HALF_BIN + BINS // 2] = np.arange(1, BINS, 2)
+    return order
+
+
+def order_table():
+    return (np.arange(BIN_PAD)[:, None] == bin_order()[None, :]).astype(jnp.bfloat16)
+
+
 def synthesis_table():
-    k = np.arange(BINS)[:, None]
-    n = np.arange(NFFT)[None, :]
-    angle = (k * n % NFFT) * (2.0 * math.pi / NFFT)
-    factor = np.where((k == 0) | (k == NFFT // 2), 1.0, 2.0) / NFFT
-    out = np.zeros((2, BIN_PAD, LAPS, LAP_PAD), np.float32)
-    out[0, :BINS, :, :HOP] = (factor * np.cos(angle)).reshape(BINS, LAPS, HOP)
-    out[1, :BINS, :, :HOP] = (-factor * np.sin(angle)).reshape(BINS, LAPS, HOP)
-    return out.reshape(2 * BIN_PAD, LAPS * LAP_PAD).astype(jnp.bfloat16)
+    n = np.arange(2 * HOP)[None, :]
+    order = bin_order()
+    out = np.zeros((2, 2, HALF_BIN, 2, LAP_PAD), np.float32)
+    for parity in range(2):
+        k = order[parity * HALF_BIN : (parity + 1) * HALF_BIN]
+        k = k[k >= 0][:, None]
+        angle = (k * n % NFFT) * (2.0 * math.pi / NFFT)
+        factor = np.where((k == 0) | (k == NFFT // 2), 1.0, 2.0) / NFFT
+        out[parity, 0, : len(k), :, :HOP] = (factor * np.cos(angle)).reshape(-1, 2, HOP)
+        out[parity, 1, : len(k), :, :HOP] = (-factor * np.sin(angle)).reshape(-1, 2, HOP)
+    return out.reshape(2, BIN_PAD, 2 * LAP_PAD).astype(jnp.bfloat16)
 
 
 def window_tables():
@@ -151,31 +167,24 @@
 
 
 def sincos(angle):
-    turns = jnp.round(angle * (1.0 / math.pi))
-    rest = angle - turns * 3.140625
-    rest = rest - turns * 9.670257568359375e-4
-    rest = rest - turns * 6.2771141529083251953e-7
-    rest = rest - turns * 1.2154201256553420e-10
-    half = turns * 0.5
-    sign = 1.0 - 4.0 * (half - jnp.floor(half))
+    turns = jnp.round(angle * (0.5 / math.pi))
+    rest = angle * 0.5 - turns * 3.1416015625
+    rest = rest + turns * 8.908910206761537e-06
     sq = rest * rest
-    sine = rest + rest * sq * (
-        -1.6666667163e-01
-        + sq * (8.3333337680e-03 + sq * (-1.9841270114e-04 + sq * (2.7557314297e-06 - sq * 2.5050759689e-08)))
+    sine = 1.0 + sq * (
+        -0.16666656732559204
+        + sq * (0.008333033882081509 + sq * (-0.00019807791977655143 + sq * 2.6022808015113696e-06))
     )
     cosine = 1.0 + sq * (
-        -0.5
-        + sq
-        * (
-            4.1666667908e-02
-            + sq
-            * (-1.3888889225e-03 + sq * (2.4801587642e-05 + sq * (-2.7557314297e-07 + sq * 2.0875723372e-09)))
-        )
+        -0.4999992549419403
+        + sq * (0.04166382923722267 + sq * (-0.001385461655445397 + sq * 2.3163083824329078e-05))
     )
-    return sine * sign, cosine * sign
-
-
-ANGLE_LIMIT = 8192.0
+    sine = rest * sine
+    double = sine + sine
+    return double * cosine, 1.0 - double * sine
+
+
+ANGLE_LIMIT = 1024.0
 
 
 def params():
@@ -194,65 +203,148 @@
 shape_of = jax.ShapeDtypeStruct
 
 
-def pre_body(meta, wave_ref, halo_ref, synth_ref, win_ref, *rest, row, tiles, utts):
-    out_ref, scaled, signal = rest[-3:]
+def pre_body(meta, wave_ref, halo_ref, synth_ref, win_ref, *rest, start, tiles, rows, utts):
+    out_ref, flat, scaled_all, even_all, odd_all = rest[-5:]
     step = pl.program_id(0)
-    first = pl.multiple_of(step * TILE, TILE)
-    base = meta[row, 2 * utts + 1] + first
-    reach, left = frame_reach(meta, row, base, TILE + EDGE, utts)
-
-    @pl.when(step == 0)
-    def _():
-        scaled[...] = jnp.zeros_like(scaled)
-
-    def scale(block, at, size):
-        block = block.astype(F32)
-        for c, width in ((0, LANE), (1, LANE), (2, HOP - 2 * LANE)):
-            value = block[:, c * LANE : c * LANE + width]
-            scaled[c, at : at + size, 0:width] = value * over(win_ref, LAPS, reach[at : at + size], c, width)
-
-    for at, size in spans(TILE, 64):
-        scale(wave_ref[row, pl.ds(pl.multiple_of(first + at, 64), size), :], at, size)
-
-    @pl.when(step == tiles - 1)
-    def _():
-        scale(halo_ref[row], TILE, EDGE)
-
-    @pl.when(step < tiles - 1)
-    def _():
-        scale(wave_ref[row, pl.ds(pl.multiple_of(first + TILE, TILE), EDGE), :], TILE, EDGE)
-
-    for j in range(LAPS):
-        for c in range(LAP_PAD // LANE):
-            weight = win_ref[j : j + 1, c * LANE : (c + 1) * LANE]
-            for at, size in spans(TILE, 64):
-                part = scaled[c, at + j : at + j + size, :] * weight
-                part = keep_within(part, None, left[at : at + size], j)
-                column = j * LAP_PAD + c * LANE
-                signal[at : at + size, column : column + LANE] = part.astype(BF16)
-    for c in range(0, 2 * BIN_PAD, 512):
-        out_ref[:, c : c + 512] = dot(signal[...], synth_ref[c : c + 512, :], NT).astype(BF16)
-
-
-def spectrum_cotangent(row, before, meta, wave, halo, synth, win, utts):
-    rows, frames, _ = wave.shape
-    tiles = frames // TILE
+    tile = start + step
+    lines = PAIR * TILE
+    extra = PAIR * EDGE
+    count = TILE + EDGE
+    lane = lax.broadcasted_iota(jnp.int32, (count // 2, LANE), 1)
+    for at, size in spans(lines, 320):
+        rows_at = pl.ds(pl.multiple_of(tile * lines + at, 16), size)
+        flat[at : at + size, :] = wave_ref[rows_at, :].astype(F32)
+    after = jnp.minimum((tile + 1) * lines, tiles * lines - extra)
+    following = wave_ref[pl.ds(pl.multiple_of(after, 16), extra), :]
+    flat[lines:, :] = jnp.where(tile == tiles - 1, halo_ref[...], following).astype(F32)
+    for r in range(rows):
+        scaled, even, odd = scaled_all.at[r], even_all.at[r], odd_all.at[r]
+        base = meta[r, 2 * utts + 1] + tile * TILE
+        part = [flat[pl.ds(2 * k + r, count // 2, stride=2 * PAIR), :] for k in range(PAIR)]
+        turned = [pltpu.roll(v, LANE // 2, 1) for v in part[2:]]
+        front = lane < LANE // 2
+        frame = (
+            part[0],
+            part[1],
+            jnp.where(front, part[2], 0.0),
+            jnp.where(front, turned[0], turned[1]),
+            jnp.where(front, turned[1], turned[2]),
+            jnp.where(front, turned[2], 0.0),
+        )
+        for c in range(3):
+            scaled[c, pl.ds(0, count // 2, stride=2), :] = frame[c]
+            scaled[c, pl.ds(1, count // 2, stride=2), :] = frame[3 + c]
+        for at, size in spans(count, 32):
+            reach, _ = frame_reach(meta, r, base + at, size, utts)
+            for c in range(3):
+                scaled[c, at : at + size, :] = scaled[c, at : at + size, :] * over(win_ref, LAPS, reach, c)
+        for at, size in spans(TILE, 32):
+            _, left = frame_reach(meta, r, base + at, size, utts)
+            for j in range(2):
+                for c in range(3):
+                    span = slice(c * LANE, (c + 1) * LANE)
+
+                    def lap(i):
+                        value = scaled[c, at + i : at + i + size, :] * win_ref[i : i + 1, span]
+                        return keep_within(value, None, left, i).astype(BF16).astype(F32)
+
+                    one, two = lap(j), lap(j + 2)
+                    column = slice(j * LAP_PAD + c * LANE, j * LAP_PAD + (c + 1) * LANE)
+                    even[at : at + size, column] = (one + two).astype(BF16)
+                    odd[at : at + size, column] = (one - two).astype(BF16)
+        out_ref[r, :, 0:BIN_PAD] = dot(even[...], synth_ref[0], NT).astype(BF16)
+        out_ref[r, :, BIN_PAD:] = dot(odd[...], synth_ref[1], NT).astype(BF16)
+
+
+def spectrum_cotangent(start, stop, before, meta, wave, halo, synth, win, rows, utts):
+    tiles = wave.shape[0] // (PAIR * TILE)
+    frames = tiles * TILE
     more = [] if before is None else [before]
+    steps = stop - start
     return pl.pallas_call(
-        functools.partial(pre_body, row=row, tiles=tiles, utts=utts),
-        grid=(tiles,),
+        functools.partial(pre_body, start=start, tiles=tiles, rows=rows, utts=utts),
+        grid=(steps,),
         in_specs=[SCALARS, WHOLE, WHOLE, WHOLE, WHOLE] + [ANYWHERE] * len(more),
-        out_specs=pl.BlockSpec((TILE, 2 * BIN_PAD), lambda i: (row * tiles + i, 0)),
-        out_shape=shape_of((rows * frames, 2 * BIN_PAD), BF16),
+        out_specs=pl.BlockSpec((rows, TILE, 2 * BIN_PAD), lambda i: (0, start + i, 0)),
+        out_shape=shape_of((rows, frames, 2 * BIN_PAD), BF16),
         input_output_aliases={5: 0} if more else {},
         scratch_shapes=[
-            pltpu.VMEM((LAP_PAD // LANE, TILE + EDGE, LANE), F32),
-            pltpu.VMEM((TILE, LAPS * LAP_PAD), BF16),
+            pltpu.VMEM((PAIR * (TILE + EDGE), LANE), F32),
+            pltpu.VMEM((rows, LAP_PAD // LANE, TILE + EDGE, LANE), F32),
+            pltpu.VMEM((rows, TILE, BIN_PAD), BF16),
+            pltpu.VMEM((rows, TILE, BIN_PAD), BF16),
         ],
         compiler_params=params(),
-        cost_estimate=cost(2 * frames * 1536 * 1536, frames * 1536 * 2 + 8 * MIB),
-        name=f"spectrum_cotangent_{row}",
+        cost_estimate=cost(4 * rows * steps * TILE * 768 * 768, rows * steps * TILE * 3072 + 4 * MIB),
+        name=f"spectrum_cotangent_{start}",
     )(meta, wave, halo, synth, win, *more)
+
+
+def place_parts(places, counts, core, pieces, table, sem, slots, owners, start):
+    for index, ref in enumerate(pieces):
+        side = core if index % 2 == 0 else 1 - core
+        owner = owners[index // 2]
+
+        def one(s, carry, ref=ref, side=side, owner=owner):
+            bucket = places[0, owner * slots + s]
+            at = pl.multiple_of(bucket * BR + side * HALF, HALF)
+            copy = pltpu.make_async_copy(ref.at[s], table.at[pl.ds(at, HALF), :], sem)
+            if start:
+                copy.start()
+            else:
+                copy.wait()
+            return carry
+
+        lax.fori_loop(0, counts[0, owner], one, 0)
+
+
+def assemble_body(places, counts, core, *refs, slots, owners):
+    pieces, table, sem = refs[: 2 * len(owners)], refs[-2], refs[-1]
+    place_parts(places, counts, core[0], pieces, table, sem, slots, owners, True)
+    place_parts(places, counts, core[0], pieces, table, sem, slots, owners, False)
+
+
+def assemble(owners, places, counts, core, pieces, slots):
+    channels = pieces[0].shape[2]
+    return pl.pallas_call(
+        functools.partial(assemble_body, slots=slots, owners=owners),
+        in_specs=[SCALARS, SCALARS, SCALARS] + [ANYWHERE] * len(pieces),
+        out_specs=WHOLE,
+        out_shape=shape_of((NB * BR, channels), BF16),
+        scratch_shapes=[pltpu.SemaphoreType.DMA],
+        compiler_params=params(),
+        cost_estimate=cost(0, 12 * MIB),
+        name="assemble",
+    )(places, counts, core, *pieces)
+
+
+def take_body(slot_of, ref, out, sem):
+    def copy(b):
+        return pltpu.make_async_copy(ref.at[slot_of[0, b]], out.at[b], sem)
+
+    def start(b, carry):
+        copy(b).start()
+        return carry
+
+    def wait(b, carry):
+        copy(b).wait()
+        return carry
+
+    lax.fori_loop(0, NB, start, 0)
+    lax.fori_loop(0, NB, wait, 0)
+
+
+def take_slots(slot_of, gathered):
+    return pl.pallas_call(
+        take_body,
+        in_specs=[SCALARS, ANYWHERE],
+        out_specs=WHOLE,
+        out_shape=shape_of((NB, *gathered.shape[1:]), BF16),
+        scratch_shapes=[pltpu.SemaphoreType.DMA],
+        compiler_params=params(),
+        cost_estimate=cost(0, 6 * MIB),
+        name="take_slots",
+    )(slot_of, gathered)
 
 
 def fill_frames(xs, x_ref, low_ref, high_ref, row, tile, tiles, channels):
@@ -266,21 +358,11 @@
     for at, size in spans(TILE, 64):
         put(EDGE + at, x_ref[row, pl.ds(pl.multiple_of(first + at, 64), size), :])
 
-    @pl.when(tile == 0)
-    def _():
-        put(0, low_ref[row])
-
-    @pl.when(tile > 0)
-    def _():
-        put(0, x_ref[row, pl.ds(pl.multiple_of(first - EDGE, EDGE), EDGE), :])
-
-    @pl.when(tile == tiles - 1)
-    def _():
-        put(EDGE + TILE, high_ref[row])
-
-    @pl.when(tile < tiles - 1)
-    def _():
-        put(EDGE + TILE, x_ref[row, pl.ds(pl.multiple_of(first + TILE, EDGE), EDGE), :])
+    before = x_ref[row, pl.ds(pl.multiple_of(jnp.maximum(first - EDGE, 0), EDGE), EDGE), :]
+    put(0, jnp.where(tile == 0, low_ref[row], before))
+    end = jnp.minimum(first + TILE, (tiles - 1) * TILE)
+    after = x_ref[row, pl.ds(pl.multiple_of(end, EDGE), EDGE), :]
+    put(EDGE + TILE, jnp.where(tile == tiles - 1, high_ref[row], after))
 
 
 def by_utterance(meta, row, utts, index, rows_of):
@@ -300,13 +382,24 @@
             out[at : at + 1, :] = value
 
 
-def forward_body(meta, places, x_ref, low_ref, high_ref, cot_ref, *rest, parts, tiles, utts):
-    sources = rest[:parts]
+def interleave(ones, others):
+    at = 0
+    for i, one in enumerate(ones):
+        one()
+        until = (i + 1) * len(others) // len(ones)
+        for other in others[at:until]:
+            other()
+        at = until
+
+
+def forward_body(meta, places, counts, x_ref, low_ref, high_ref, order_ref, cot_ref, *rest, owners, slots, tiles, count, utts):
+    pieces = rest[: 2 * len(owners)]
+    table_in = rest[2 * len(owners)]
     (
-        table,
+        table_out,
         spec_ref,
         act_ref,
-        der_ref,
+        pre_ref,
         ada_ref,
         lowg_ref,
         resg_ref,
@@ -317,77 +410,63 @@
         tail_ref,
         sums_ref,
         bsum_ref,
+        table,
         xs,
         w_head,
         b_head,
         vecs,
         picks,
         grad,
+        lines,
         hg,
-        wide,
-        wide2,
+        hg_old,
+        logs_ref,
+        angle_ref,
+        ngrad_ref,
         slim,
         xn_ref,
         normed,
+        normed_old,
         branch_ref,
         rn_ref,
+        slow,
         sem,
-    ) = rest[parts:]
+        sems,
+    ) = rest[2 * len(owners) + 1 :]
     step = pl.program_id(0)
-    steps = pl.num_programs(0)
     core = meta[0, 2 * utts + 2]
     channels = x_ref.shape[2]
     lane_tiles = channels // LANE
-    row, tile = step // tiles, step % tiles
+    now = jnp.minimum(step, count - 1)
+    row, tile = now // tiles, now % tiles
     vec = lambda v: vecs[2 + v : 3 + v, :]
     vec_at = KW + 1 + 2 * NBW
+    head_at = 2 * FF
+
+    def store():
+        return pltpu.make_async_copy(table, table_out, sems.at[1])
 
     @pl.when(step == 0)
     def _():
-        def go(start):
-            base = 0
-            for index, ref in enumerate(sources):
-                slots = ref.shape[0]
-                side = core if index % 2 == 0 else 1 - core
-
-                def one(s, carry, ref=ref, base=base, side=side):
-                    bucket = places[0, base + s]
-
-                    @pl.when(bucket < NB)
-                    def _():
-                        at = pl.multiple_of(bucket * BR + side * HALF, HALF)
-                        copy = pltpu.make_async_copy(ref.at[s], table.at[pl.ds(at, HALF), :], sem)
-                        if start:
-                            copy.start()
-                        else:
-                            copy.wait()
-
-                    return carry
-
-                lax.fori_loop(0, slots, one, 0)
-                if index % 2 == 1:
-                    base = base + slots
-
-        go(True)
-        grad[...] = jnp.zeros_like(grad)
+        whole = pltpu.make_async_copy(table_in, table, sems.at[0])
+        whole.start()
+        normed[...] = jnp.zeros_like(normed)
+        w_head[...] = jnp.zeros_like(w_head)
+        b_head[...] = jnp.zeros_like(b_head)
+        whole.wait()
+        place_parts(places, counts, core, pieces, table, sem, slots, owners, True)
+        place_parts(places, counts, core, pieces, table, sem, slots, owners, False)
+        store().start()
+        vecs[...] = table[head_at + 1280 : head_at + 1280 + BR, :].astype(F32)
+
+    @pl.when(step == 1)
+    def _():
         sums_ref[...] = jnp.zeros_like(sums_ref)
         bsum_ref[...] = jnp.zeros_like(bsum_ref)
-        go(False)
-        head_at = 2 * FF
-        w_head[0:640, :] = table[head_at : head_at + 640, :]
-        edge = table[head_at + 640 : head_at + 640 + 656, :].astype(F32)
-        inside = lax.broadcasted_iota(jnp.int32, (128, channels), 0)
-        w_head[640:768, :] = jnp.where(inside < 1, edge[0:128], 0.0).astype(BF16)
-        w_head[768:1408, :] = edge[1:641].astype(BF16)
-        w_head[1408:1536, :] = jnp.where(inside < 1, edge[641:642], 0.0).astype(BF16)
-        last = table[2 * FF + 1280 : 2 * FF + 1280 + BR, :].astype(F32)
-        vecs[...] = last
-        line = jnp.concatenate([last[25:26], last[26:27], last[27:28]], axis=1)
-        line = jnp.broadcast_to(line, (8, 3 * channels))
-        column = lax.broadcasted_iota(jnp.int32, (8, BIN_PAD), 1)
-        b_head[:, 0:BIN_PAD] = jnp.where(column < BINS, line[:, 0:BIN_PAD], 0.0)
-        moved = pltpu.roll(line, 3 * channels - BINS, 1)
-        b_head[:, BIN_PAD:] = jnp.where(column < BINS, moved[:, 0:BIN_PAD], 0.0)
+
+    @pl.when(step == 2)
+    def _():
+        grad[...] = jnp.zeros_like(grad)
 
     @pl.when(tile == 0)
     def _():
@@ -395,7 +474,8 @@
 
     base = meta[row, 2 * utts + 1] + tile * TILE
     fill_frames(xs, x_ref, low_ref, high_ref, row, tile, tiles, channels)
-    for at, size in spans(TILE, 32):
+
+    def convolve(at, size):
         reach, left = frame_reach(meta, row, base + at, size, utts)
         index = base + at + lax.broadcasted_iota(jnp.int32, (size, LANE), 0)
         conv = []
@@ -419,20 +499,34 @@
             scale = by_utterance(meta, row, utts, index, lambda u: picks[u : u + 1, cut])
             shift = by_utterance(meta, row, utts, index, lambda u: picks[utts + u : utts + u + 1, cut])
             ada_ref[at : at + size, cut] = (xc * scale + shift).astype(BF16)
-    for c in range(IN_ROWS):
-        pre_ref = (wide, wide2)[c % 2]
-        pre_ref[...] = dot(ada_ref[...], table[c * CHUNK : (c + 1) * CHUNK, :], NT)
-        for at, size in spans(TILE, 32):
-            for d in range(0, CHUNK, 256):
-                bias = vecs[2 + VROWS + c : 3 + VROWS + c, d : d + 256]
-                pre = pre_ref[at : at + size, d : d + 256] + bias
-                phi = 0.5 + 0.5 * lax.erf(pre * math.sqrt(0.5))
-                bell = jnp.exp(-0.5 * pre * pre) * (1.0 / math.sqrt(2.0 * math.pi))
-                cut = slice(c * CHUNK + d, c * CHUNK + d + 256)
-                act_ref[at : at + size, cut] = (pre * phi).astype(BF16)
-                der_ref[at : at + size, cut] = (phi + pre * bell).astype(BF16)
-    slim[...] = dot(act_ref[...], table[FF : 2 * FF, :], NN)
-    for at, size in spans(TILE, 16):
+
+    def head(at, size, turn):
+        span = slice(at, at + size)
+        for c in range(0, BIN_PAD, LANE):
+            bins, angles = slice(c, c + LANE), slice(BIN_PAD + c, BIN_PAD + c + LANE)
+            parity, inner = c // HALF_BIN, c % HALF_BIN
+            reals = slice(parity * BIN_PAD + inner, parity * BIN_PAD + inner + LANE)
+            imags = slice(reals.start + HALF_BIN, reals.stop + HALF_BIN)
+            angle = angle_ref[span, bins] + b_head[0:1, angles]
+            scale = jnp.exp(logs_ref[span, bins] + b_head[0:1, bins])
+            sine, cosine = turn(angle)
+            real, imag = scale * cosine, scale * sine
+            spec_ref[span, reals] = real.astype(BF16)
+            spec_ref[span, imags] = imag.astype(BF16)
+            dre = cot_ref[span, reals].astype(F32)
+            dim = cot_ref[span, imags].astype(F32)
+            hg[span, bins] = (dre * real + dim * imag).astype(BF16)
+            hg[span, angles] = (dim * real - dre * imag).astype(BF16)
+
+    def gelu(at, size, c):
+        for d in range(c * 512, (c + 1) * 512, 256):
+            cut = slice(d, d + 256)
+            bias = vecs[2 + VROWS + c : 3 + VROWS + c, d - c * 512 : d - c * 512 + 256]
+            pre = pre_ref[at : at + size, cut] + bias
+            phi = 0.5 + 0.5 * lax.erf(pre * math.sqrt(0.5))
+            act_ref[at : at + size, cut] = (pre * phi).astype(BF16)
+
+    def second_norm(at, size):
         span = slice(at, at + size)
         branch = slim[span, :] + vec(vec_at)
         branch_ref[span, :] = branch
@@ -445,91 +539,170 @@
         xn_ref[span, :] = xn
         normed[span, :] = (xn * vec(vec_at + 2) + vec(vec_at + 3)).astype(BF16)
 
-    def head(c, turn):
-        logs_ref, angle_ref = wide, wide2
-        half = slice((c // 256 % 2) * 256, (c // 256 % 2) * 256 + 256)
-        logs_ref[:, half] = dot(normed[...], w_head[c : c + 256, :], NT)
-        angle_ref[:, half] = dot(normed[...], w_head[BIN_PAD + c : BIN_PAD + c + 256, :], NT)
-        widest = jnp.zeros((8, 256), F32)
-        for at, size in spans(TILE, 16):
-            span = slice(at, at + size)
-            one, two = slice(c, c + 256), slice(BIN_PAD + c, BIN_PAD + c + 256)
-            angle = angle_ref[span, half] + b_head[0:1, two]
-            scale = jnp.exp(logs_ref[span, half] + b_head[0:1, one])
-            sine, cosine = turn(angle)
-            real, imag = scale * cosine, scale * sine
-            spec_ref[span, one] = real.astype(BF16)
-            spec_ref[span, two] = imag.astype(BF16)
-            dre = cot_ref[span, one].astype(F32)
-            dim = cot_ref[span, two].astype(F32)
-            hg[span, one] = (dre * real + dim * imag).astype(BF16)
-            hg[span, two] = (dim * real - dre * imag).astype(BF16)
-            widest = jnp.maximum(widest, jnp.max(jnp.abs(angle).reshape(size // 8, 8, 256), axis=0))
-        return widest
-
-    widest = head(0, sincos)
-    for c in range(256, BIN_PAD, 256):
-        widest = jnp.maximum(widest, head(c, sincos))
-
-    @pl.when(jnp.max(widest) > ANGLE_LIMIT)
-    def _():
-        for c in range(0, BIN_PAD, 256):
-            head(c, lambda angle: (jnp.sin(angle), jnp.cos(angle)))
-
-    slim[...] = dot(hg[...], w_head[...], NN)
-    grad[...] += dot(hg[...], normed[...], TN)
-    for c in range(0, 2 * BIN_PAD, 512):
-        total = bsum_ref[:, c : c + 512]
-        for at, size in spans(TILE, 32):
-            total = total + fold(hg[at : at + size, c : c + 512].astype(F32))
-        bsum_ref[:, c : c + 512] = total
-    sums = [sums_ref[v] for v in range(4)]
-    for at, size in spans(TILE, 16):
+    def second_norm_back(at, size, sums):
         span = slice(at, at + size)
-        ngrad = slim[span, :]
+        ngrad = ngrad_ref[span, :]
         xn = xn_ref[span, :]
         e = ngrad * vec(vec_at + 2)
         resg = rn_ref[span, 0:1] * (e - row_mean(e) - xn * row_mean(e * xn))
         resg_ref[span, :] = resg
         low = (vec(vec_at + 1) * resg).astype(BF16)
         lowg_ref[span, :] = low
-        sums[0] = sums[0] + fold(low.astype(F32))
-        sums[1] = sums[1] + fold(resg * branch_ref[span, :])
-        sums[2] = sums[2] + fold(ngrad * xn)
-        sums[3] = sums[3] + fold(ngrad)
+        return (
+            sums[0] + fold(low.astype(F32)),
+            sums[1] + fold(resg * branch_ref[span, :]),
+            sums[2] + fold(ngrad * xn),
+            sums[3] + fold(ngrad),
+        )
+
+    def head_dots(ref, begin):
+        def one(c):
+            ref[:, c : c + 256] = dot(normed[...], w_head[begin + c : begin + c + 256, :], NT)
+
+        return [functools.partial(one, c) for c in range(0, BIN_PAD, 256)]
+
+    def hidden_dot(c):
+        pre_ref[:, c : c + 256] = dot(ada_ref[...], table[c : c + 256, :], NT)
+
+    def grad_dot(c):
+        grad[c : c + 256, :] += dot(hg_old[:, c : c + 256], normed_old[...], TN)
+
+    interleave(
+        head_dots(logs_ref, 0) + head_dots(angle_ref, BIN_PAD),
+        [functools.partial(convolve, at, size) for at, size in spans(TILE, 32)],
+    )
+    interleave(
+        [functools.partial(hidden_dot, c) for c in range(0, FF, 256)]
+        + [functools.partial(grad_dot, c) for c in range(0, 2 * BIN_PAD, 256)],
+        [functools.partial(head, at, size, sincos) for at, size in spans(TILE, 16)],
+    )
+
+    @pl.when((step > 0) & (slow[0] > 0))
+    def _():
+        def again(i, carry):
+            rows = pl.ds(pl.multiple_of(i * 32, 32), 32)
+            for c in range(0, BIN_PAD, LANE):
+                bins, angles = slice(c, c + LANE), slice(BIN_PAD + c, BIN_PAD + c + LANE)
+                parity, inner = c // HALF_BIN, c % HALF_BIN
+                reals = slice(parity * BIN_PAD + inner, parity * BIN_PAD + inner + LANE)
+                imags = slice(reals.start + HALF_BIN, reals.stop + HALF_BIN)
+                angle = angle_ref[rows, bins] + b_head[0:1, angles]
+                scale = jnp.exp(logs_ref[rows, bins] + b_head[0:1, bins])
+                real, imag = scale * jnp.cos(angle), scale * jnp.sin(angle)
+                spec_ref[rows, reals] = real.astype(BF16)
+                spec_ref[rows, imags] = imag.astype(BF16)
+                dre = cot_ref[rows, reals].astype(F32)
+                dim = cot_ref[rows, imags].astype(F32)
+                hg[rows, bins] = (dre * real + dim * imag).astype(BF16)
+                hg[rows, angles] = (dim * real - dre * imag).astype(BF16)
+            return carry
+
+        lax.fori_loop(0, TILE // 32, again, 0)
+
+    @pl.when(step == 0)
+    def _():
+        last = vecs[...]
+        line = jnp.concatenate([last[25:26], last[26:27], last[27:28]], axis=1)
+        line = jnp.broadcast_to(line, (16, 3 * channels))
+        moved = pltpu.roll(line, 3 * channels - BINS, 1)
+        for at, value in ((0, line), (BIN_PAD, moved)):
+            picked = dot(value[:, 0:BIN_PAD].astype(BF16), order_ref[...], NN)
+            b_head[:, at : at + BIN_PAD] = picked[0:8]
+        inside = lax.broadcasted_iota(jnp.int32, (336, LANE), 0)
+        for c in range(lane_tiles):
+            cut = slice(c * LANE, (c + 1) * LANE)
+            lines[c, 0:1312, :] = table[head_at : head_at + 1312, cut].astype(F32)
+            lines[c, 1312:, :] = jnp.zeros((lines.shape[1] - 1312, LANE), F32)
+            for part, start in ((0, 0), (BIN_PAD, BINS)):
+                evens = lines[c, pl.ds(start, 336, stride=2), :]
+                w_head[part : part + 336, cut] = jnp.where(inside < (BINS + 1) // 2, evens, 0.0).astype(BF16)
+                odds = lines[c, pl.ds(start + 1, 320, stride=2), :]
+                w_head[part + HALF_BIN : part + HALF_BIN + 320, cut] = odds.astype(BF16)
+        longest = jnp.zeros((8, 1), F32)
+        for at, size in spans(BIN_PAD, 64):
+            weights = w_head[BIN_PAD + at : BIN_PAD + at + size, :].astype(F32)
+            length = jnp.sum(weights * weights, axis=1, keepdims=True)
+            longest = jnp.maximum(longest, jnp.max(length.reshape(size // 8, 8, 1), axis=0))
+        gain, shift = jnp.abs(vec(vec_at + 2)), vec(vec_at + 3)
+        normed_length = math.sqrt(channels) * jnp.max(gain) + jnp.sqrt(jnp.sum(shift * shift, keepdims=True))[0, 0]
+        bound = 1.05 * normed_length * jnp.max(jnp.sqrt(longest)) + jnp.max(jnp.abs(b_head[:, BIN_PAD:]))
+        slow[0] = jnp.where(bound < ANGLE_LIMIT, 0, 1)
+
+    def ngrad_dot(c):
+        ngrad_ref[:, c : c + 256] = dot(hg[...], w_head[:, c : c + 256], NN)
+
+    def branch_dot(c):
+        slim[:, c : c + 256] = dot(act_ref[...], table[FF : 2 * FF, c : c + 256], NN)
+
+    interleave(
+        [functools.partial(ngrad_dot, c) for c in range(0, channels, 256)],
+        [functools.partial(gelu, at, size, c) for c in range(IN_ROWS) for at, size in spans(TILE, 32)],
+    )
+    sums = [sums_ref[v] for v in range(4)]
+
+    def back(at, size):
+        sums[:] = second_norm_back(at, size, sums)
+
+    interleave(
+        [functools.partial(branch_dot, c) for c in range(0, channels, 256)],
+        [functools.partial(back, at, size) for at, size in spans(TILE, 16)],
+    )
     for v in range(4):
         sums_ref[v] = sums[v]
-
-    @pl.when(step == steps - 1)
+    for c in range(0, 2 * BIN_PAD, 512):
+        total = bsum_ref[:, c : c + 512]
+        for at, size in spans(TILE, 32):
+            total = total + fold(hg[at : at + size, c : c + 512].astype(F32))
+        bsum_ref[:, c : c + 512] = total
+    hg_old[...] = hg[...]
+    normed_old[...] = normed[...]
+    for at, size in spans(TILE, 16):
+        second_norm(at, size)
+
+    @pl.when(step == count)
     def _():
-        grad[767:768, :] = grad[640:641, :]
-        for b in range(40):
-            at = b * BR if b < 20 else b * BR + 127
-            low_half = grad[at : at + HALF, :].astype(BF16)
-            high_half = grad[at + HALF : at + BR, :].astype(BF16)
-            keep_ref[b] = jnp.where(core == 0, low_half, high_half)
-            send_ref[b] = jnp.where(core == 0, high_half, low_half)
-        tail_ref[...] = grad[1407:1415, :]
-
-
-def forward(meta, places, x, low, high, cot, sources, utts):
+        for c in range(0, 2 * BIN_PAD, 256):
+            grad_dot(c)
+        for c in range(lane_tiles):
+            cut = slice(c * LANE, (c + 1) * LANE)
+            for part, start in ((0, 0), (BIN_PAD, BINS)):
+                lines[c, pl.ds(start + 1, 320, stride=2), :] = grad[part + HALF_BIN : part + HALF_BIN + 320, cut]
+                lines[c, pl.ds(start, 320, stride=2), :] = grad[part : part + 320, cut]
+                lines[c, start + 640 : start + 641, :] = grad[part + 320 : part + 321, cut]
+            for b in range(40):
+                low_half = lines[c, b * BR : b * BR + HALF, :].astype(BF16)
+                high_half = lines[c, b * BR + HALF : b * BR + BR, :].astype(BF16)
+                keep_ref[b, :, cut] = jnp.where(core == 0, low_half, high_half)
+                send_ref[b, :, cut] = jnp.where(core == 0, high_half, low_half)
+            tail_ref[:, cut] = lines[c, 1280:1288, :]
+        store().wait()
+
+
+def forward(owners, meta, places, counts, x, low, high, order, cot, pieces, table, utts):
     rows, frames, channels = x.shape
     tiles = frames // TILE
+    steps = rows * tiles
     count = rows * frames
-    wide = pl.BlockSpec((TILE, FF), lambda i: (i, 0))
-    slim = pl.BlockSpec((TILE, channels), lambda i: (i, 0))
+    slots = pieces[0].shape[0]
+    ahead = lambda i: jnp.minimum(i, steps - 1)
+    behind = lambda i: jnp.maximum(i - 1, 0)
+    wide = pl.BlockSpec((TILE, FF), lambda i: (ahead(i), 0))
+    wide_late = pl.BlockSpec((None, TILE, FF), lambda i: (behind(i) // tiles, behind(i) % tiles, 0))
+    slim = pl.BlockSpec((TILE, channels), lambda i: (ahead(i), 0))
+    slim_late = pl.BlockSpec((TILE, channels), lambda i: (behind(i), 0))
     return pl.pallas_call(
-        functools.partial(forward_body, parts=len(sources), tiles=tiles, utts=utts),
-        grid=(rows * tiles,),
-        in_specs=[SCALARS, SCALARS, WHOLE, WHOLE, WHOLE, wide] + [ANYWHERE] * len(sources),
-        out_specs=[WHOLE, wide, wide, wide, slim, slim, slim, slim]
-        + [pl.BlockSpec((TILE, LANE), lambda i: (i, 0))]
+        functools.partial(forward_body, owners=owners, slots=slots, tiles=tiles, count=steps, utts=utts),
+        grid=(steps + 1,),
+        in_specs=[SCALARS, SCALARS, SCALARS, WHOLE, WHOLE, WHOLE, WHOLE, wide_late]
+        + [ANYWHERE] * (len(pieces) + 1),
+        out_specs=[ANYWHERE, wide_late, wide, wide, slim, slim_late, slim_late, slim]
+        + [pl.BlockSpec((TILE, LANE), lambda i: (ahead(i), 0))]
         + [WHOLE] * 5,
         out_shape=[
             shape_of((NB * BR, channels), BF16),
+            shape_of((rows, frames, 2 * BIN_PAD), BF16),
             shape_of((count, FF), BF16),
-            shape_of((count, FF), BF16),
-            shape_of((count, FF), BF16),
+            shape_of((count, FF), F32),
             shape_of((count, channels), BF16),
             shape_of((count, channels), BF16),
             shape_of((count, channels), F32),
@@ -542,50 +715,78 @@
             shape_of((8, 2 * BIN_PAD), F32),
         ],
         scratch_shapes=[
+            pltpu.VMEM((NB * BR, channels), BF16),
             pltpu.VMEM((channels // LANE, TILE + 2 * EDGE, LANE), F32),
             pltpu.VMEM((2 * BIN_PAD, channels), BF16),
             pltpu.VMEM((8, 2 * BIN_PAD), F32),
             pltpu.VMEM((BR, channels), F32),
             pltpu.VMEM((2 * utts, channels), F32),
             pltpu.VMEM((2 * BIN_PAD, channels), F32),
+            pltpu.VMEM((channels // LANE, 1344, LANE), F32),
             pltpu.VMEM((TILE, 2 * BIN_PAD), BF16),
-            pltpu.VMEM((TILE, CHUNK), F32),
-            pltpu.VMEM((TILE, CHUNK), F32),
+            pltpu.VMEM((TILE, 2 * BIN_PAD), BF16),
+            pltpu.VMEM((TILE, BIN_PAD), F32),
+            pltpu.VMEM((TILE, BIN_PAD), F32),
+            pltpu.VMEM((TILE, channels), F32),
             pltpu.VMEM((TILE, channels), F32),
             pltpu.VMEM((TILE, channels), F32),
             pltpu.VMEM((TILE, channels), BF16),
+            pltpu.VMEM((TILE, channels), BF16),
             pltpu.VMEM((TILE, channels), F32),
             pltpu.VMEM((TILE, LANE), F32),
+            pltpu.SMEM((1,), jnp.int32),
             pltpu.SemaphoreType.DMA,
+            pltpu.SemaphoreType.DMA((2,)),
         ],
         compiler_params=params(),
         cost_estimate=cost(10 * count * 1536 * 512, 40 * MIB, count * 4096),
         name="forward",
-    )(meta, places, x, low, high, cot, *sources)
-
-
-def mlp_body(meta, low_ref, act_ref, der_ref, ada_ref, wout_ref, *rest, utts):
-    pre_ref, send_ref, keep_ref, bsum_ref, gout, gin, agrad = rest[-7:]
+    )(meta, places, counts, x, low, high, order, cot, *pieces, table)
+
+
+def mlp_body(meta, low_ref, act_ref, hidden_ref, ada_ref, wout_ref, last_ref, *rest, chunk, utts):
+    pre_ref, send_ref, keep_ref, bsum_ref, gout, gin, agrad, bias = rest[-8:]
     step = pl.program_id(0)
     core = meta[0, 2 * utts + 2]
-    tile = low_ref.shape[0]
+    tile, channels = low_ref.shape
 
     @pl.when(step == 0)
     def _():
         gout[...] = jnp.zeros_like(gout)
         gin[...] = jnp.zeros_like(gin)
         bsum_ref[...] = jnp.zeros_like(bsum_ref)
-
-    agrad[...] = dot(low_ref[...], wout_ref[...], NT)
-    gout[...] += dot(act_ref[...], low_ref[...], TN)
-    total = bsum_ref[...]
-    for at, size in spans(tile, 16):
-        span = slice(at, at + size)
-        pre = (agrad[span, :] * der_ref[span, :].astype(F32)).astype(BF16)
-        pre_ref[span, :] = pre
-        total = total + fold(pre.astype(F32))
-    bsum_ref[...] = total
-    gin[...] += dot(pre_ref[...], ada_ref[...], TN)
+        last = last_ref[...].astype(F32)
+        line = jnp.concatenate([last[2 + VROWS + c : 3 + VROWS + c] for c in range(IN_ROWS)], axis=1)
+        bias[...] = jnp.broadcast_to(line[:, chunk * CHUNK : (chunk + 1) * CHUNK], (8, CHUNK))
+
+    def agrad_dot(c):
+        agrad[:, c : c + 256] = dot(low_ref[...], wout_ref[c : c + 256, :], NT)
+
+    def gout_dot(c):
+        gout[c : c + 256, :] += dot(act_ref[:, c : c + 256], low_ref[...], TN)
+
+    def gin_dot(c):
+        gin[c : c + 256, :] += dot(pre_ref[:, c : c + 256], ada_ref[...], TN)
+
+    def slope(c):
+        cut = slice(c, c + 256)
+        total = bsum_ref[:, cut]
+        for at, size in spans(tile, 32):
+            span = slice(at, at + size)
+            value = hidden_ref[span, cut] + bias[0:1, cut]
+            phi = 0.5 + 0.5 * lax.erf(value * math.sqrt(0.5))
+            bell = jnp.exp(-0.5 * value * value) * (1.0 / math.sqrt(2.0 * math.pi))
+            pre = (agrad[span, cut] * (phi + value * bell)).astype(BF16)
+            pre_ref[span, cut] = pre
+            total = total + fold(pre.astype(F32))
+        bsum_ref[:, cut] = total
+
+    cuts = range(0, CHUNK, 256)
+    for c in cuts:
+        agrad_dot(c)
+    interleave([functools.partial(gout_dot, c) for c in cuts], [functools.partial(slope, c) for c in cuts])
+    for c in cuts:
+        gin_dot(c)
 
     @pl.when(step == pl.num_programs(0) - 1)
     def _():
@@ -598,7 +799,7 @@
                 send_ref[at + b] = jnp.where(core == 0, high_half, low_half)
 
 
-def mlp_backward(chunk, before, meta, low, act, der, ada, table, utts):
+def mlp_backward(chunk, before, meta, low, act, hidden, ada, table, utts):
     count, channels = low.shape
     tile = 512
     slim = pl.BlockSpec((tile, channels), lambda i: (i, 0))
@@ -606,7 +807,7 @@
     buckets = 2 * CHUNK // BR
     more = [] if before is None else [before]
     return pl.pallas_call(
-        functools.partial(mlp_body, utts=utts),
+        functools.partial(mlp_body, chunk=chunk, utts=utts),
         grid=(count // tile,),
         in_specs=[
             SCALARS,
@@ -615,6 +816,7 @@
             part,
             slim,
             pl.BlockSpec((CHUNK, channels), lambda i: (FF // CHUNK + chunk, 0)),
+            pl.BlockSpec((BR, channels), lambda i: (NB - 1, 0)),
         ]
         + [ANYWHERE] * len(more),
         out_specs=[part, WHOLE, WHOLE, WHOLE],
@@ -624,16 +826,17 @@
             shape_of((buckets, HALF, channels), BF16),
             shape_of((8, CHUNK), F32),
         ],
-        input_output_aliases={6: 0} if more else {},
+        input_output_aliases={7: 0} if more else {},
         scratch_shapes=[
             pltpu.VMEM((CHUNK, channels), F32),
             pltpu.VMEM((CHUNK, channels), F32),
             pltpu.VMEM((tile, CHUNK), F32),
+            pltpu.VMEM((8, CHUNK), F32),
         ],
         compiler_params=params(),
-        cost_estimate=cost(6 * count * CHUNK * 512, 12 * MIB),
+        cost_estimate=cost(6 * count * CHUNK * 512, 16 * MIB),
         name=f"mlp_backward_{chunk}",
-    )(meta, low, act, der, ada, table, *more)
+    )(meta, low, act, hidden, ada, table, table, *more)
 
 
 def norm_body(
@@ -720,7 +923,7 @@
         edge_ref[1] = cg_ref[TILE - 8 : TILE, :]
 
     if closing:
-        _, tail_ref, sums_ref, hsum_ref, bsum0, bsum1, bsum2 = more
+        _, tail_ref, sums_ref, hsum_ref, bsum0, bsum1, order_ref = more
         vec_ref = outs[3]
 
         @pl.when(tile == tiles - 1)
@@ -731,9 +934,23 @@
                 at = v - (KW + 1 + 2 * NBW)
                 rows_of = part_ref[v] if at < 0 else sums_ref[at]
                 vec_ref[2 + v : 3 + v, :] = jnp.sum(rows_of, axis=0, keepdims=True)
-            for c, ref in enumerate((bsum0, bsum1, bsum2)):
-                vec_ref[2 + VROWS + c : 3 + VROWS + c, :] = jnp.sum(ref[...], axis=0, keepdims=True)
-            flat = jnp.broadcast_to(jnp.sum(hsum_ref[...], axis=0, keepdims=True), (8, 2 * BIN_PAD))
+            line = jnp.concatenate([bsum0[...], bsum1[...]], axis=1)
+            for c in range(IN_ROWS):
+                at = 2 + VROWS + c
+                vec_ref[at : at + 1, :] = jnp.sum(
+                    line[:, c * channels : (c + 1) * channels], axis=0, keepdims=True
+                )
+
+            def bins(value):
+                value = jnp.broadcast_to(jnp.sum(value, axis=0, keepdims=True), (16, BIN_PAD))
+                total = jnp.zeros((16, BIN_PAD), F32)
+                for _ in range(3):
+                    part = value.astype(BF16)
+                    value = value - part.astype(F32)
+                    total = total + dot(part, order_ref[...], NT)
+                return total[0:8]
+
+            flat = jnp.concatenate([bins(hsum_ref[:, 0:BIN_PAD]), bins(hsum_ref[:, BIN_PAD:])], axis=1)
             column = lax.broadcasted_iota(jnp.int32, (8, 3 * channels), 1)
             moved = pltpu.roll(flat, 2 * BIN_PAD - (BIN_PAD - BINS), 1)
             joined = jnp.where(column < BINS, flat, moved)
@@ -845,55 +1062,74 @@
     )(meta, cg, cg, cg, low, high, resg, table, *more)
 
 
-def wave_body(meta, spec_ref, prev_ref, halo_ref, synth_ref, win_ref, *rest, row, tiles, utts):
-    out_ref, spec, held = rest[-3:]
-    tile = pl.program_id(0)
-    base = meta[row, 2 * utts + 1] + tile * TILE
-    spec[EDGE:, :] = spec_ref[...]
-    spec[0:EDGE, :] = jnp.where(tile == 0, halo_ref[row], prev_ref[...])
-    for j in range(LAPS):
-        piece = dot(spec[...], synth_ref[:, j * LAP_PAD : (j + 1) * LAP_PAD], NN)
-        for c in range(LAP_PAD // LANE):
-            held[j, c] = piece[:, c * LANE : (c + 1) * LANE]
-    for at, size in spans(TILE, 32):
-        reach, _ = frame_reach(meta, row, base + at, size, utts)
-        for c, width in ((0, LANE), (1, LANE), (2, HOP - 2 * LANE)):
-            cut = slice(c * LANE, c * LANE + width)
-            total = held[0, c, EDGE + at : EDGE + at + size, :] * win_ref[0:1, c * LANE : (c + 1) * LANE]
-            for j in range(1, LAPS):
-                moved = held[j, c, EDGE + at - j : EDGE + at - j + size, :]
-                moved = moved * win_ref[j : j + 1, c * LANE : (c + 1) * LANE]
-                total = total + jnp.where(reach >= j, moved, 0.0)
-            out_ref[0, at : at + size, cut] = total[:, 0:width] * over(win_ref, LAPS, reach, c, width)
-
-
-def wave_forward(row, before, meta, spec, halo, synth, win, rows, utts):
-    frames = spec.shape[0] // rows
+def wave_body(meta, spec_ref, prev_ref, halo_ref, synth_ref, win_ref, *rest, start, rows, utts):
+    out_ref, spec_all, held_all, done_all = rest[-4:]
+    tile = start + pl.program_id(0)
+    lane = lax.broadcasted_iota(jnp.int32, (TILE // 2, LANE), 1)
+    front = lane < LANE // 2
+    for r in range(rows):
+        spec, held, done = spec_all.at[r], held_all.at[r], done_all.at[r]
+        base = meta[r, 2 * utts + 1] + tile * TILE
+        spec[EDGE:, :] = spec_ref[r]
+        spec[0:EDGE, :] = jnp.where(tile == 0, halo_ref[r], prev_ref[r])
+        for parity in range(2):
+            half = slice(parity * BIN_PAD, (parity + 1) * BIN_PAD)
+            piece = dot(spec[:, half], synth_ref[parity], NN)
+            for c in range(BIN_PAD // LANE):
+                held[parity, c] = piece[:, c * LANE : (c + 1) * LANE]
+        for at, size in spans(TILE, 32):
+            reach, _ = frame_reach(meta, r, base + at, size, utts)
+            for c in range(3):
+                cut = slice(c * LANE, (c + 1) * LANE)
+                total = None
+                for j in range(LAPS):
+                    rows_at = slice(EDGE + at - j, EDGE + at - j + size)
+                    of = (j % 2) * 3 + c
+                    one, two = held[0, of, rows_at, :], held[1, of, rows_at, :]
+                    piece = (one + two if j < 2 else one - two) * win_ref[j : j + 1, cut]
+                    total = piece if j == 0 else total + jnp.where(reach >= j, piece, 0.0)
+                done[c, at : at + size, :] = total * over(win_ref, LAPS, reach, c)
+        even = [done[c, pl.ds(0, TILE // 2, stride=2), :] for c in range(3)]
+        odd = [pltpu.roll(done[c, pl.ds(1, TILE // 2, stride=2), :], LANE // 2, 1) for c in range(3)]
+        part = (
+            even[0],
+            even[1],
+            jnp.where(front, even[2], odd[0]),
+            jnp.where(front, odd[0], odd[1]),
+            jnp.where(front, odd[1], odd[2]),
+        )
+        for k in range(PAIR):
+            out_ref[pl.ds(2 * k + r, TILE // 2, stride=2 * PAIR), :] = part[k]
+
+
+def wave_forward(start, stop, before, meta, spec, halo, synth, win, utts):
+    rows, frames, _ = spec.shape
     tiles = frames // TILE
     per = TILE // EDGE
     more = [] if before is None else [before]
     return pl.pallas_call(
-        functools.partial(wave_body, row=row, tiles=tiles, utts=utts),
-        grid=(tiles,),
+        functools.partial(wave_body, start=start, rows=rows, utts=utts),
+        grid=(stop - start,),
         in_specs=[
             SCALARS,
-            pl.BlockSpec((TILE, 2 * BIN_PAD), lambda i: (row * tiles + i, 0)),
-            pl.BlockSpec((EDGE, 2 * BIN_PAD), lambda i: (jnp.maximum((row * tiles + i) * per - 1, 0), 0)),
+            pl.BlockSpec((rows, TILE, 2 * BIN_PAD), lambda i: (0, start + i, 0)),
+            pl.BlockSpec((rows, EDGE, 2 * BIN_PAD), lambda i: (0, jnp.maximum((start + i) * per - 1, 0), 0)),
             WHOLE,
             WHOLE,
             WHOLE,
         ]
         + [ANYWHERE] * len(more),
-        out_specs=pl.BlockSpec((1, TILE, HOP), lambda i: (row, i, 0)),
-        out_shape=shape_of((rows, frames, HOP), F32),
+        out_specs=pl.BlockSpec((PAIR * TILE, LANE), lambda i: (start + i, 0)),
+        out_shape=shape_of((PAIR * TILE * tiles, LANE), F32),
         input_output_aliases={6: 0} if more else {},
         scratch_shapes=[
-            pltpu.VMEM((TILE + EDGE, 2 * BIN_PAD), BF16),
-            pltpu.VMEM((LAPS, LAP_PAD // LANE, TILE + EDGE, LANE), F32),
+            pltpu.VMEM((rows, TILE + EDGE, 2 * BIN_PAD), BF16),
+            pltpu.VMEM((rows, 2, BIN_PAD // LANE, TILE + EDGE, LANE), F32),
+            pltpu.VMEM((rows, LAP_PAD // LANE, TILE, LANE), F32),
         ],
         compiler_params=params(),
-        cost_estimate=cost(2 * frames * 1536 * 1536, 12 * MIB),
-        name=f"wave_forward_{row}",
+        cost_estimate=cost(4 * rows * (stop - start) * TILE * 768 * 768, 10 * MIB),
+        name=f"wave_forward_{start}",
     )(meta, spec, spec, halo, synth, win, *more)
 
 
@@ -993,65 +1229,80 @@
         starts.append(starts[-1] + lengths[:, u : u + 1])
     spot = jnp.broadcast_to(jnp.stack([seq_at * frames, core])[None, :], (rows, 2)).astype(jnp.int32)
     meta = jnp.concatenate(starts + [bw_ids, spot], axis=1)
-    blocks = wave_grad.reshape(rows, frames, HOP)
+    lines = wave_grad.reshape(rows, frames * HOP // LANE, LANE).transpose(1, 0, 2).reshape(-1, LANE)
+    order = jnp.asarray(order_table())
     synth = jnp.asarray(synthesis_table())
     win = jnp.asarray(window_tables())
 
     low = shifted(frames_in[:, frames - EDGE :], 1)
     high = shifted(frames_in[:, :EDGE], -1)
-    later = shifted(blocks[:, :EDGE], -1)
+    later = shifted(lines[: PAIR * EDGE], -1)
+    bucket_index = jnp.arange(NB, dtype=jnp.int32)
+    same = owner_list[None, :] == owner_list[:, None]
+    rank = jnp.sum((same & (bucket_index[None, :] < bucket_index[:, None])).astype(jnp.int32), axis=1)
+    ids = jnp.arange(owners, dtype=jnp.int32)
     if ring:
         offsets = [0]
-        sources = [mine, seq_swap(mine, 1)]
+        for hop in range(1, half_ring):
+            offsets += [-hop, hop]
+        offsets.append(-half_ring)
+        order_ids = jnp.asarray(ring, jnp.int32)
+        where = jnp.sum(jnp.where(order_ids == row_at, ids, 0))
+        at = (where + jnp.asarray(offsets, jnp.int32)) % owners
+        owner_ids = jnp.sum(jnp.where(at[:, None] == ids[None, :], order_ids[None, :], 0), axis=1)
+    else:
+        owner_ids = ids
+
+    def held_by(wanted):
+        targets = (wanted[:, None] * slots + jnp.arange(slots, dtype=jnp.int32)[None, :]).reshape(-1)
+        match = (owner_list * slots + rank)[None, :] == targets[:, None]
+        return (NB + jnp.sum(match.astype(jnp.int32) * (bucket_index[None, :] - NB), axis=1))[None, :]
+
+    places = held_by(jnp.concatenate([owner_ids, row_at[None].astype(jnp.int32)]))
+    places, held = places[:, : owners * slots], places[:, owners * slots :]
+    rel = jnp.sum(jnp.where(owner_list[:, None] == owner_ids[None, :], ids[None, :], 0), axis=1)
+    slot_of = (rel * slots + rank)[None, :]
+    counts = jnp.sum((owner_list[None, :] == owner_ids[:, None]).astype(jnp.int32), axis=1)[None, :]
+    at_core = core[None].astype(jnp.int32)
+
+    cot = None
+    tiles = frames // TILE
+    if ring:
         ahead = back = mine
-        cot = None
+        arrived = [mine, seq_swap(mine, 1)]
         for hop in range(half_ring):
             source = (ahead, back)
             ahead = lax.ppermute(ahead, AXES, ring_step(ring, 1, seqs))
             if hop < half_ring - 1:
                 back = lax.ppermute(back, AXES, ring_step(ring, -1, seqs))
             if hop in (1, 2):
-                feed = tie(blocks, *source)[0]
-                cot = spectrum_cotangent(hop - 1, cot, meta, feed, later, synth, win, utts)
+                feed = tie(lines, *source)[0]
+                begin, end = ((0, tiles // 2), (tiles // 2, tiles))[hop - 1]
+                cot = spectrum_cotangent(begin, end, cot, meta, feed, later, synth, win, rows, utts)
                 ahead, back, cot = tie(ahead, back, cot)
-            sources += [ahead, seq_swap(ahead, 1)]
-            offsets.append(-(hop + 1))
-            if hop < half_ring - 1:
-                sources += [back, seq_swap(back, 1)]
-                offsets.append(hop + 1)
-        order = jnp.asarray(ring, jnp.int32)
-        ids = jnp.arange(owners, dtype=jnp.int32)
-        where = jnp.sum(jnp.where(order == row_at, ids, 0))
-        at = (where + jnp.asarray(offsets, jnp.int32)) % owners
-        owner_ids = jnp.sum(jnp.where(at[:, None] == ids[None, :], order[None, :], 0), axis=1)
+            if hop == half_ring - 1:
+                fed = tie(places, *source)[0]
+                partial_table = assemble(tuple(range(owners - 1)), fed, counts, at_core, arrived, slots)
+                ahead, partial_table = tie(ahead, partial_table)
+            else:
+                arrived += [ahead, seq_swap(ahead, 1), back, seq_swap(back, 1)]
+        arrived = [ahead, seq_swap(ahead, 1)]
+        owned = (owners - 1,)
+        part_places, part_counts = places, counts
     else:
         gathered = lax.all_gather(mine, "rows", axis=0, tiled=True)
-        sources = [gathered, seq_swap(gathered, 1)]
-        owner_ids = jnp.arange(owners, dtype=jnp.int32)
-        cot = None
-        for r in range(rows):
-            cot = spectrum_cotangent(r, cot, meta, blocks, later, synth, win, utts)
-
-    bucket_index = jnp.arange(NB, dtype=jnp.int32)
-    same = owner_list[None, :] == owner_list[:, None]
-    rank = jnp.sum((same & (bucket_index[None, :] < bucket_index[:, None])).astype(jnp.int32), axis=1)
-
-    def held_by(ids):
-        targets = (ids[:, None] * slots + jnp.arange(slots, dtype=jnp.int32)[None, :]).reshape(-1)
-        match = (owner_list * slots + rank)[None, :] == targets[:, None]
-        return (NB + jnp.sum(match.astype(jnp.int32) * (bucket_index[None, :] - NB), axis=1))[None, :]
-
-    places = held_by(owner_ids)
-    held = held_by(row_at[None].astype(jnp.int32))
-    place_at = jnp.arange(owners, dtype=jnp.int32)
-    rel = jnp.sum(jnp.where(owner_list[:, None] == owner_ids[None, :], place_at[None, :], 0), axis=1)
-    slot_of = (rel * slots + rank)[None, :]
-    places, held, slot_of, meta = tie(places, held, slot_of, meta)
-
-    (table, spec, act, der, ada, low_grad, resg, xc, rc, send, keep, tail, sums, hsum) = forward(
-        meta, places, frames_in, low, high, cot, sources, utts
+        arrived = [gathered, seq_swap(gathered, 1)]
+        owned = (0,)
+        arrived = [take_slots(slot_of, a) for a in arrived]
+        part_places = jnp.arange(NB, dtype=jnp.int32)[None, :]
+        part_counts = jnp.full((1, 1), NB, jnp.int32)
+        partial_table = jnp.zeros((NB * BR, channels), BF16)
+        cot = spectrum_cotangent(0, tiles, cot, meta, lines, later, synth, win, rows, utts)
+
+    (table, spec, act, hidden, ada, low_grad, resg, xc, rc, send, keep, tail, sums, hsum) = forward(
+        owned, meta, part_places, part_counts, frames_in, low, high, order, cot, arrived, partial_table, utts
     )
-    halo = shifted(spec.reshape(rows, frames, 2 * BIN_PAD)[:, frames - EDGE :], 1)
+    halo = shifted(spec[:, frames - EDGE :], 1)
 
     keeps, cames, bounds = [], [], []
 
@@ -1072,7 +1323,7 @@
     begins, count = (2 * FF // BR,), 40
     for chunk in range(FF // CHUNK):
         near = seq_swap(send, 1)
-        pre, next_send, next_keep, bsum = mlp_backward(chunk, pre, meta, low_grad, act, der, ada, table, utts)
+        pre, next_send, next_keep, bsum = mlp_backward(chunk, pre, meta, low_grad, act, hidden, ada, table, utts)
         near, pre, next_send, next_keep = tie(near, pre, next_send, next_keep)
         bsums.append(bsum)
         stay, leave = split(keep, near)
@@ -1085,7 +1336,7 @@
     near, cg0, edge0, parts, pre = tie(near, cg0, edge0, parts, pre)
     stay, leave = split(keep, near)
     came = seq_swap(leave, 2)
-    closing = (parts, tail, sums, hsum, *bsums)
+    closing = (parts, tail, sums, hsum, *bsums, order)
     cg1, edge1, _, last = norm_backward(1, closing, meta, frames_in, low, high, pre, table, xc, rc, utts)
     came, cg1, edge1, last, spec = tie(came, cg1, edge1, last, spec)
     record(stay, came, begins, count)
@@ -1099,7 +1350,7 @@
             feed = tie(spec, *ready)[0]
             state["low"] = shifted(edges[:, 1], 1)
             state["high"] = shifted(edges[:, 0], -1)
-            state["wave"] = wave_forward(0, None, meta, feed, halo, synth, win, rows, utts)
+            state["wave"] = wave_forward(0, tiles // 2, None, meta, feed, halo, synth, win, utts)
             return state["wave"]
         if stage == 1:
             feed = tie(cg0, *ready)[0]
@@ -1115,7 +1366,7 @@
             return state["grad"]
         if stage == 3:
             feed = tie(spec, *ready)[0]
-            state["wave"] = wave_forward(1, state["wave"], meta, feed, halo, synth, win, rows, utts)
+            state["wave"] = wave_forward(tiles // 2, tiles, state["wave"], meta, feed, halo, synth, win, utts)
             return state["wave"]
         return state["wave"]
 
@@ -1151,8 +1402,7 @@
     near = seq_swap(own, 1)
     if ring:
         last = last + rows_swap(last, 4)
-    waveform = state["wave"].reshape(rows, frames * HOP)
-    far, waveform = tie(far, waveform)
+    waveform = state["wave"].reshape(-1, rows, LANE).transpose(1, 0, 2).reshape(rows, frames * HOP)
     cross = seq_swap(far, 1)
     where_at = jnp.stack([core, plane]).astype(jnp.int32)
     new_master, new_first, new_second = adam(

time: 261 us -> 256 us (0.981)
  waiting for transfers between devices: 14.4 us -> 28.2 us
  Pallas kernels: 166 us -> 155 us
  starting transfers between devices: 47.1 us -> 39.7 us
  local copies, waits for them, and re-layouts: 24.7 us -> 17.6 us
  other arithmetic: 6.37 us -> 12.8 us
    pallas_call x8, Pallas kernels: 125 us -> 113 us  [the longest x1 53.5 us: forward(): pl.pallas_call(functools.partial(forward_body, owners=owners, slots=slots...]
    ppermute x21 -> x19, waiting for transfers between devices: 0.1 us -> 11.7 us  [seq_swap(): return lax.ppermute(value, 'seq', [(s, s ^ bit) for s in range(count)])]
    reshape x2 -> x0, local copies, waits for them, and re-layouts: 7.38 us -> none  [the longest x1 5.99 us: local(): waveform = state['wave'].reshape(rows, frames * HOP)]
    ppermute x21 -> x19, starting transfers between devices: 15.1 us -> 8.01 us  [seq_swap(): return lax.ppermute(value, 'seq', [(s, s ^ bit) for s in range(count)])]
    reduce_sum x3 -> x4, other arithmetic: 0.9 us -> 4.91 us  [the longest x1 1.44 us: local(): jnp.sum((owner_list[None, :] == owner_ids[:, None]).astype(jnp.int32), ax...]
    unnamed x73 -> x72, local copies, waits for them, and re-layouts: 7.4 us -> 6.92 us
  transfers between devices with their start and end apart: 44 -> 42, of which waited for: 7 -> 12; matrix products, arithmetic and copies ran while one was open for 9% -> 9% of each run, Pallas kernels for 39% -> 37%
where the time goes in v3:
time: 256 us; the launch traced here: 255 us
  Pallas kernels  155 us (61%)
  starting transfers between devices  39.7 us (16%)
  waiting for transfers between devices  28.2 us (11%)
  local copies, waits for them, and re-layouts  17.6 us (7%)
  other arithmetic  12.8 us (5%)
    pallas_call x1, Pallas kernels, forward(): pl.pallas_call(functools.partial(forward_body, owners=owners, slots=slots...  53.5 us
    pallas_call x2, Pallas kernels, mlp_backward(): pl.pallas_call(functools.partial(mlp_body, chunk=chunk, utts=utts), grid=...  24.2 us
    pallas_call x2, Pallas kernels, norm_backward(): pl.pallas_call(functools.partial(norm_body, row=row, tiles=tiles, utts=ut...  21.6 us
    pallas_call x2, Pallas kernels, spectrum_cotangent(): pl.pallas_call(functools.partial(pre_body, start=start, tiles=tiles, rows...  15.1 us
    pallas_call x2, Pallas kernels, wave_forward(): pl.pallas_call(functools.partial(wave_body, start=start, rows=rows, utts=...  14.1 us
    ppermute x19, waiting for transfers between devices, seq_swap(): return lax.ppermute(value, 'seq', [(s, s ^ bit) for s in range(count)])  11.7 us
    ppermute x6, starting transfers between devices, shifted(): lax.ppermute(value, 'seq', [(i - distance, i) for i in devices if i - dis...  10.8 us
    pallas_call x2, Pallas kernels, conv_backward(): pl.pallas_call(functools.partial(conv_body, row=row, tiles=tiles, utts=ut...  10.2 us
  transfers between devices with their start and end apart: 42, of which 12 were waited for; matrix products, arithmetic and copies ran while one was open for 9% of the time, Pallas kernels for 37%

profile of v3, /device:TPU:0, one launch (start us, length us, event | category | flops | bytes accessed | tf_op | source)
XLA Modules:
  0.0 255.1 jit_solution(16058512482814517529)
XLA Ops:
  0.6 1.2 dynamic-slice_convert_fusion.refs_0_
  1.9 3.1 %collective-permute-start.2 = (bf16[27,16,512]{2,1,0:T(8,128)(2,1)S(1)}, bf16[27,16,512]{2,1,0:T(8,128)(2,1)S(1)}, u32[]{:S(2)}, u32[]{:S(2)}) collective-permute-start(bf16[27,16,512]{2,1,0:T(8,128)(2,1)S(1)} %dynamic-slice_convert_fusion.refs_0_), channel_id=1, source_target_pairs={{0,8},{1,9},{2,10},{3,11},{8,16},{9,17},{10,18},{11,19},{16,24},{1... | collective-permute-start | bytes 1327112 | tf_op jit(solution)/shard_map/ppermute | solution.py:1275
  5.7 1.3 collective-permute-start.6
  8.0 1.3 fusion.5
  9.3 1.3 and_select_fusion
  10.6 1.4 select_reduce_fusion.2
  13.7 1.3 collective-permute-done.2.refs_2_
  15.1 1.8 collective-permute-start.3
  18.0 1.3 concatenate.12.meta
  20.0 7.5 %spectrum_cotangent_0.1.rest_0_ = bf16[2,1024,1536]{2,1,0:T(8,128)(2,1)} custom-call(s32[2,11]{1,0:T(2,128)} %concatenate.12.meta, bf16[5120,128]{1,0:T(8,128)(2,1)} %bitcast.27, bf16[80,128]{1,0:T(8,128)(2,1)} %copy-done.27, bf16[2,768,768]{2,1,0:T(8,128)(2,1)} %constant.76.clone.synth_ref, f32[8,384]{1,0:T(8,128)} %constant.77.clone.win_ref), custom_call_target="tpu_custom_call" | custom-call | flops 2415919104 | bytes 7340032 | tf_op jit(solution)/shard_map/spectrum_cotangent_0/pallas_call | solution.py:264
  27.5 1.2 collective-permute-done.5.refs_8_
  28.7 1.6 collective-permute-start.7
  31.3 7.6 %spectrum_cotangent_2.1.cot_ref = bf16[2,1024,1536]{2,1,0:T(8,128)(2,1)} custom-call(s32[2,11]{1,0:T(2,128)} %concatenate.12.meta, bf16[5120,128]{1,0:T(8,128)(2,1)} %bitcast.28, bf16[80,128]{1,0:T(8,128)(2,1)} %copy-done.27, bf16[2,768,768]{2,1,0:T(8,128)(2,1)} %constant.76.clone.synth_ref, ...), custom_call_target="tpu_custom_call", output_to_operand_aliasing={{}: (5, {})} | custom-call | flops 2415919104 | bytes 7340032 | tf_op jit(solution)/shard_map/spectrum_cotangent_2/pallas_call | solution.py:264
  38.9 1.2 collective-permute-done.7.refs_10_
  40.2 1.6 collective-permute-done.8.refs_12_
  41.8 1.6 collective-permute-start.9
  44.0 1.4 convert_reduce_fusion.1
  47.9 6.1 %assemble.1.rest_2_ = bf16[4384,512]{1,0:T(8,128)(2,1)} custom-call(s32[1,216]{1,0:T(1,128)} %bitcast.32, s32[1,8]{1,0:T(1,128)} %bitcast.36, s32[1]{0:T(128)} %bitcast.2.core, bf16[27,16,512]{2,1,0:T(8,128)(2,1)} %copy-done.1, bf16[27,16,512]{2,1,0:T(8,128)(2,1)} %copy-done.8, bf16[27,16,512]{2,1,0:T(8,128)(2,1)} %copy-done.6, ...), custom_call_target="tpu_custom_call" | custom-call | bytes 12582912 | tf_op jit(solution)/shard_map/assemble/pallas_call | solution.py:309
  55.3 2.4 collective-permute-start
  57.7 1.5 collective-permute-start.1
  59.2 2.4 collective-permute-done.1.high_ref
  62.9 53.5 %forward.1 = (bf16[4384,512]{1,0:T(8,128)(2,1)}, bf16[2,1024,1536]{2,1,0:T(8,128)(2,1)}, bf16[2048,1536]{1,0:T(8,128)(2,1)}, f32[2048,1536]{1,0:T(8,128)}, bf16[...) custom-call(s32[2,11]{1,0:T(2,128)} %concatenate.12.meta, ...), custom_call_target="tpu_custom_call" | custom-call | flops 16106127360 | bytes 41943040 | tf_op jit(solution)/shard_map/forward/pallas_call | solution.py:693
  116.4 2.7 %collective-permute-start.18 = (bf16[40,16,512]{2,1,0:T(8,128)(2,1)}, bf16[40,16,512]{2,1,0:T(8,128)(2,1)S(1)}, u32[]{:S(2)}, u32[]{:S(2)}) collective-permute-start(bf16[40,16,512]{2,1,0:T(8,128)(2,1)} %get-tuple-element.97), channel_id=1, source_target_pairs={{0,1},{1,0},{2,3},{3,2},{4,5},{5,4},{6,7},{7,6},{8,9},{9,8},{10,11... | collective-permute-start | bytes 1966088 | tf_op jit(solution)/shard_map/ppermute | solution.py:105
  119.1 12.1 %mlp_backward_0.1 = (bf16[2048,1536]{1,0:T(8,128)(2,1)}, bf16[48,16,512]{2,1,0:T(8,128)(2,1)}, bf16[48,16,512]{2,1,0:T(8,128)(2,1)}, f32[8,768]{1,0:T(8,128)}) custom-call(s32[2,11]{1,0:T(2,128)} %concatenate.12.meta, bf16[2048,512]{1,0:T(8,128)(2,1)} %get-tuple-element.98.low_ref, bf16[2048,1536]{1,0:T(8,128)(2,1)} %get-tuple-element.99.act_ref, ...), custom_call_target="tpu_custom_call" | custom-call | flops 4831838208 | bytes 16777216 | tf_op jit(solution)/shard_map/mlp_backward_0/pallas_call | solution.py:809
  132.2 2.6 %collective-permute-start.27 = (bf16[2,16,1536]{2,1,0:T(8,128)(2,1)S(1)}, bf16[2,16,1536]{2,1,0:T(8,128)(2,1)S(1)}, u32[]{:S(2)}, u32[]{:S(2)}) collective-permute-start(bf16[2,16,1536]{2,1,0:T(8,128)(2,1)S(1)} %slice.106), channel_id=1, source_target_pairs={{0,1},{1,2},{2,3},{4,5},{5,6},{6,7},{8,9},{9,10},{10,11},{12,13},{... | collective-permute-start | bytes 294920 | tf_op jit(solution)/shard_map/ppermute | solution.py:115
  135.1 12.1 %mlp_backward_1.1 = (bf16[2048,1536]{1,0:T(8,128)(2,1)}, bf16[48,16,512]{2,1,0:T(8,128)(2,1)}, bf16[48,16,512]{2,1,0:T(8,128)(2,1)}, f32[8,768]{1,0:T(8,128)}) custom-call(s32[2,11]{1,0:T(2,128)} %concatenate.12.meta, bf16[2048,512]{1,0:T(8,128)(2,1)} %get-tuple-element.98.low_ref, ...), custom_call_target="tpu_custom_call", output_to_operand_aliasing={{0}: (7, {})} | custom-call | flops 4831838208 | bytes 16777216 | tf_op jit(solution)/shard_map/mlp_backward_1/pallas_call | solution.py:809
  148.8 1.7 collective-permute-start.22
  151.2 9.5 %norm_backward_0.1 = (f32[1024,512]{1,0:T(8,128)}, f32[2,8,512]{2,1,0:T(8,128)}, f32[16,8,512]{2,1,0:T(8,128)}) custom-call(s32[2,11]{1,0:T(2,128)} %concatenate.12.meta, bf16[2,1024,512]{2,1,0:T(8,128)(2,1)} %x_ref.5, bf16[2,16,512]{2,1,0:T(8,128)(2,1)} %copy-done.23, bf16[2,16,512]{2,1,0:T(8,128)(2,1)} %copy-done.24, ...), custom_call_target="tpu_custom_call" | custom-call | flops 1610612736 | bytes 12582912 | tf_op jit(solution)/shard_map/norm_backward_0/pallas_call | solution.py:978
  161.5 5.5 %collective-permute-done.22 = bf16[48,8,512]{2,1,0:T(8,128)(2,1)S(1)} collective-permute-done((bf16[48,8,512]{2,1,0:T(8,128)(2,1)S(1)}, bf16[48,8,512]{2,1,0:T(8,128)(2,1)S(1)}, u32[]{:S(2)}, u32[]{:S(2)}) %collective-permute-start.22) | collective-permute-done | bytes 393248 | tf_op jit(solution)/shard_map/ppermute | solution.py:105
  167.7 12.0 %norm_backward_1.1 = (f32[1024,512]{1,0:T(8,128)}, f32[2,8,512]{2,1,0:T(8,128)}, f32[16,8,512]{2,1,0:T(8,128)}, f32[32,512]{1,0:T(8,128)}) custom-call(s32[2,11]{1,0:T(2,128)} %concatenate.12.meta, bf16[2,1024,512]{2,1,0:T(8,128)(2,1)} %x_ref.5, bf16[2,16,512]{2,1,0:T(8,128)(2,1)} %copy-done.23, bf16[2,16,512]{2,1,0:T(8,128)(2,1)} %copy-done.24, ...), custom_call_target="tpu_custom_call" | custom-call | flops 1610612736 | bytes 12582912 | tf_op jit(solution)/shard_map/norm_backward_1/pallas_call | solution.py:978
  182.0 3.8 %to_slots.1 = bf16[216,8,512]{2,1,0:T(8,128)(2,1)} custom-call(s32[1,137]{1,0:T(1,128)} %bitcast.35, bf16[40,8,512]{2,1,0:T(8,128)(2,1)} %get-tuple-element.181.refs_0_, bf16[24,8,512]{2,1,0:T(8,128)(2,1)} %get-tuple-element.179.refs_1_, bf16[24,8,512]{2,1,0:T(8,128)(2,1)} %get-tuple-element.178.refs_2_, bf16[24,8,512]{2,1,0:T(8,128)(2,1)} %get-tuple-element.177.refs_3_, ...), custom_call_target="tpu_custom_call" | custom-call | bytes 6291456 | tf_op jit(solution)/shard_map/to_slots/pallas_call | solution.py:1151
  186.9 1.6 collective-permute-start.24
  189.6 7.1 %wave_forward_0.1.rest_0_ = f32[5120,128]{1,0:T(8,128)} custom-call(s32[2,11]{1,0:T(2,128)} %concatenate.12.meta, bf16[2,1024,1536]{2,1,0:T(8,128)(2,1)} %get-tuple-element.155.spec_ref.prev_ref, bf16[2,1024,1536]{2,1,0:T(8,128)(2,1)} %get-tuple-element.155.spec_ref.prev_ref, bf16[2,16,1536]{2,1,0:T(8,128)(2,1)} %copy-done.18, ...), custom_call_target="tpu_custom_call" | custom-call | flops 2415919104 | bytes 10485760 | tf_op jit(solution)/shard_map/wave_forward_0/pallas_call | solution.py:1110
  196.9 1.6 collective-permute-start.28
  199.1 1.8 collective-permute-start.31
  200.8 1.3 collective-permute-start.32
  202.2 3.5 %collective-permute-done.32.high_ref = f32[2,8,512]{2,1,0:T(8,128)S(1)} collective-permute-done((f32[2,8,512]{2,1,0:T(8,128)S(1)}, f32[2,8,512]{2,1,0:T(8,128)S(1)}, u32[]{:S(2)}, u32[]{:S(2)}) %collective-permute-start.32) | collective-permute-done | bytes 32800 | tf_op jit(solution)/shard_map/ppermute | solution.py:115
  206.3 5.1 %conv_backward_0.1.rest_0_ = f32[2,1024,512]{2,1,0:T(8,128)} custom-call(s32[2,11]{1,0:T(2,128)} %concatenate.12.meta, f32[1024,512]{1,0:T(8,128)} %get-tuple-element.142.cg_ref.before_ref.after_ref, f32[1024,512]{1,0:T(8,128)} %get-tuple-element.142.cg_ref.before_ref.after_ref, f32[1024,512]{1,0:T(8,128)} %get-tuple-element.142.cg_ref.before_ref.after_ref, ...), custom_call_target="tpu_custom_call" | custom-call | flops 8388608 | bytes 6291456 | tf_op jit(solution)/shard_map/conv_backward_0/pallas_call | solution.py:1038
  211.5 1.6 collective-permute-start.33
  214.0 5.1 %conv_backward_1.1 = f32[2,1024,512]{2,1,0:T(8,128)} custom-call(s32[2,11]{1,0:T(2,128)} %concatenate.12.meta, f32[1024,512]{1,0:T(8,128)} %get-tuple-element.150.cg_ref.before_ref.after_ref, f32[1024,512]{1,0:T(8,128)} %get-tuple-element.150.cg_ref.before_ref.after_ref, ...), custom_call_target="tpu_custom_call", output_to_operand_aliasing={{}: (8, {})} | custom-call | flops 8388608 | bytes 6291456 | tf_op jit(solution)/shard_map/conv_backward_1/pallas_call | solution.py:1038
  220.1 1.5 collective-permute-start.36
  221.6 1.6 collective-permute-start.37
  223.2 7.0 %wave_forward_2.1 = f32[5120,128]{1,0:T(8,128)} custom-call(s32[2,11]{1,0:T(2,128)} %concatenate.12.meta, bf16[2,1024,1536]{2,1,0:T(8,128)(2,1)} %get-tuple-element.155.spec_ref.prev_ref, bf16[2,1024,1536]{2,1,0:T(8,128)(2,1)} %get-tuple-element.155.spec_ref.prev_ref, bf16[2,16,1536]{2,1,0:T(8,128)(2,1)} %copy-done.18, ...), custom_call_target="tpu_custom_call", output_to_operand_aliasing={{}: (6, {})} | custom-call | flops 2415919104 | bytes 10485760 | tf_op jit(solution)/shard_map/wave_forward_2/pallas_call | solution.py:1110
  230.4 2.0 collective-permute-start.39
  232.4 6.1 %collective-permute-done.39.far = bf16[27,8,512]{2,1,0:T(8,128)(2,1)S(1)} collective-permute-done((bf16[27,8,512]{2,1,0:T(8,128)(2,1)S(1)}, bf16[27,8,512]{2,1,0:T(8,128)(2,1)S(1)}, u32[]{:S(2)}, u32[]{:S(2)}) %collective-permute-start.39) | collective-permute-done | bytes 221216 | tf_op jit(solution)/shard_map/ppermute | solution.py:105
  239.1 2.3 collective-permute-start.41
  242.1 3.8 %collective-permute-done.41 = f32[32,512]{1,0:T(8,128)S(1)} collective-permute-done((f32[32,512]{1,0:T(8,128)S(1)}, f32[32,512]{1,0:T(8,128)S(1)}, u32[]{:S(2)}, u32[]{:S(2)}) %collective-permute-start.41) | collective-permute-done | bytes 65568 | tf_op jit(solution)/shard_map/ppermute | solution.py:110
  247.9 7.0 %adam.1 = (f32[27,32,512]{2,1,0:T(8,128)}, f32[27,32,512]{2,1,0:T(8,128)}, f32[27,32,512]{2,1,0:T(8,128)}) custom-call(s32[1,27]{1,0:T(1,128)} %slice.129.places, s32[2]{0:T(128)} %pad_add_fusion.1.spot, bf16[27,8,512]{2,1,0:T(8,128)(2,1)} %copy-done.2, bf16[27,8,512]{2,1,0:T(8,128)(2,1)} %copy-done.21, bf16[27,8,512]{2,1,0:T(8,128)(2,1)} %copy-done.20, ...), custom_call_target="tpu_custom_call" | custom-call | bytes 12582912 | tf_op jit(solution)/shard_map/adam/pallas_call | solution.py:1193
  (166 shorter events, 27.8 us)
Async XLA Ops:
  1.9 25.6 %copy-start.1 = (bf16[27,16,512]{2,1,0:T(8,128)(2,1)}, bf16[27,16,512]{2,1,0:T(8,128)(2,1)S(1)}, u32[]{:S(2)}) copy-start(bf16[27,16,512]{2,1,0:T(8,128)(2,1)S(1)} %dynamic-slice_convert_fusion.refs_0_) | copy-start | bytes 1327108
  1.9 13.2 %collective-permute-start.2 = (bf16[27,16,512]{2,1,0:T(8,128)(2,1)S(1)}, bf16[27,16,512]{2,1,0:T(8,128)(2,1)S(1)}, u32[]{:S(2)}, u32[]{:S(2)}) collective-permute-start(bf16[27,16,512]{2,1,0:T(8,128)(2,1)S(1)} %dynamic-slice_convert_fusion.refs_0_), channel_id=1, source_target_pairs={{0,8},{1,9},{2,10},{3,11},{8,16},{9,17},{10,18},{11,19},{16,24},{1... | collective-permute-start | bytes 1327112 | tf_op jit(solution)/shard_map/ppermute | solution.py:1275
  5.0 11.9 %collective-permute-start.4 = (bf16[27,16,512]{2,1,0:T(8,128)(2,1)S(1)}, bf16[27,16,512]{2,1,0:T(8,128)(2,1)S(1)}, u32[]{:S(2)}, u32[]{:S(2)}) collective-permute-start(bf16[27,16,512]{2,1,0:T(8,128)(2,1)S(1)} %dynamic-slice_convert_fusion.refs_0_), channel_id=1, source_target_pairs={{0,4},{1,5},{2,6},{3,7},{8,0},{9,1},{10,2},{11,3},{16,8},{17,9},{1... | collective-permute-start | bytes 1327112 | tf_op jit(solution)/shard_map/ppermute | solution.py:1277
  5.0 36.8 %collective-permute-start.10 = (bf16[27,16,512]{2,1,0:T(8,128)(2,1)S(1)}, bf16[27,16,512]{2,1,0:T(8,128)(2,1)S(1)}, u32[]{:S(2)}, u32[]{:S(2)}) collective-permute-start(bf16[27,16,512]{2,1,0:T(8,128)(2,1)S(1)} %dynamic-slice_convert_fusion.refs_0_), channel_id=1, source_target_pairs={{0,1},{1,0},{2,3},{3,2},{4,5},{5,4},{6,7},{7,6},{8,9},{9,8},{10,11... | collective-permute-start | bytes 1327112 | tf_op jit(solution)/shard_map/ppermute | solution.py:105
  5.7 13.7 %collective-permute-start.6 = (bf16[80,128]{1,0:T(8,128)(2,1)S(1)}, bf16[80,128]{1,0:T(8,128)(2,1)S(1)}, u32[]{:S(2)}, u32[]{:S(2)}) collective-permute-start(bf16[80,128]{1,0:T(8,128)(2,1)S(1)} %bitcast.31), channel_id=1, source_target_pairs={{1,0},{2,1},{3,2},{5,4},{6,5},{7,6},{9,8},{10,9},{11,10},{13,12},{... | collective-permute-start | bytes 61448 | tf_op jit(solution)/shard_map/ppermute | solution.py:115
  15.1 12.4 %collective-permute-start.3 = (bf16[27,16,512]{2,1,0:T(8,128)(2,1)S(1)}, bf16[27,16,512]{2,1,0:T(8,128)(2,1)S(1)}, u32[]{:S(2)}, u32[]{:S(2)}) collective-permute-start(bf16[27,16,512]{2,1,0:T(8,128)(2,1)S(1)} %collective-permute-done.2.refs_2_), channel_id=1, source_target_pairs={{0,8},{1,9},{2,10},{3,11},{8,16},{9,17},{10,18},{11,19},{16,24},{1... | collective-permute-start | bytes 1327112 | tf_op jit(solution)/shard_map/ppermute | solution.py:1275
  16.9 11.8 %collective-permute-start.5 = (bf16[27,16,512]{2,1,0:T(8,128)(2,1)S(1)}, bf16[27,16,512]{2,1,0:T(8,128)(2,1)S(1)}, u32[]{:S(2)}, u32[]{:S(2)}) collective-permute-start(bf16[27,16,512]{2,1,0:T(8,128)(2,1)S(1)} %collective-permute-done.4.refs_4_), channel_id=1, source_target_pairs={{0,4},{1,5},{2,6},{3,7},{8,0},{9,1},{10,2},{11,3},{16,8},{17,9},{1... | collective-permute-start | bytes 1327112 | tf_op jit(solution)/shard_map/ppermute | solution.py:1277
  19.4 24.1 %collective-permute-start.11 = (bf16[27,16,512]{2,1,0:T(8,128)(2,1)S(1)}, bf16[27,16,512]{2,1,0:T(8,128)(2,1)S(1)}, u32[]{:S(2)}, u32[]{:S(2)}) collective-permute-start(bf16[27,16,512]{2,1,0:T(8,128)(2,1)S(1)} %collective-permute-done.2.refs_2_), channel_id=1, source_target_pairs={{0,1},{1,0},{2,3},{3,2},{4,5},{5,4},{6,7},{7,6},{8,9},{9,8},{10,11... | collective-permute-start | bytes 1327112 | tf_op jit(solution)/shard_map/ppermute | solution.py:105
  19.4 24.2 %collective-permute-start.12 = (bf16[27,16,512]{2,1,0:T(8,128)(2,1)S(1)}, bf16[27,16,512]{2,1,0:T(8,128)(2,1)S(1)}, u32[]{:S(2)}, u32[]{:S(2)}) collective-permute-start(bf16[27,16,512]{2,1,0:T(8,128)(2,1)S(1)} %collective-permute-done.4.refs_4_), channel_id=1, source_target_pairs={{0,1},{1,0},{2,3},{3,2},{4,5},{5,4},{6,7},{7,6},{8,9},{9,8},{10,11... | collective-permute-start | bytes 1327112 | tf_op jit(solution)/shard_map/ppermute | solution.py:105
  28.7 11.5 %collective-permute-start.7 = (bf16[27,16,512]{2,1,0:T(8,128)(2,1)S(1)}, bf16[27,16,512]{2,1,0:T(8,128)(2,1)S(1)}, u32[]{:S(2)}, u32[]{:S(2)}) collective-permute-start(bf16[27,16,512]{2,1,0:T(8,128)(2,1)S(1)} %collective-permute-done.3.refs_6_), channel_id=1, source_target_pairs={{0,8},{1,9},{2,10},{3,11},{8,16},{9,17},{10,18},{11,19},{16,24},{1... | collective-permute-start | bytes 1327112 | tf_op jit(solution)/shard_map/ppermute | solution.py:1275
  30.3 11.5 %collective-permute-start.8 = (bf16[27,16,512]{2,1,0:T(8,128)(2,1)S(1)}, bf16[27,16,512]{2,1,0:T(8,128)(2,1)}, u32[]{:S(2)}, u32[]{:S(2)}) collective-permute-start(bf16[27,16,512]{2,1,0:T(8,128)(2,1)S(1)} %collective-permute-done.5.refs_8_), channel_id=1, source_target_pairs={{0,4},{1,5},{2,6},{3,7},{8,0},{9,1},{10,2},{11,3},{16,8},{17,9},{1... | collective-permute-start | bytes 1327112 | tf_op jit(solution)/shard_map/ppermute | solution.py:1277
  31.3 14.1 %copy-start.33 = (s32[137]{0:T(256)S(1)}, s32[137]{0:T(256)}, u32[]{:S(2)}) copy-start(s32[137]{0:T(256)} %get-tuple-element.188) | copy-start | bytes 1648
  31.3 14.1 %copy-start.34 = (s32[137]{0:T(256)S(1)}, s32[137]{0:T(256)}, u32[]{:S(2)}) copy-start(s32[137]{0:T(256)} %get-tuple-element.191) | copy-start | bytes 1648
  40.2 6.0 %collective-permute-start.13 = (bf16[27,16,512]{2,1,0:T(8,128)(2,1)S(1)}, bf16[27,16,512]{2,1,0:T(8,128)(2,1)S(1)}, u32[]{:S(2)}, u32[]{:S(2)}) collective-permute-start(bf16[27,16,512]{2,1,0:T(8,128)(2,1)S(1)} %collective-permute-done.3.refs_6_), channel_id=1, source_target_pairs={{0,1},{1,0},{2,3},{3,2},{4,5},{5,4},{6,7},{7,6},{8,9},{9,8},{10,11... | collective-permute-start | bytes 1327112 | tf_op jit(solution)/shard_map/ppermute | solution.py:105
  41.8 4.3 %collective-permute-start.14 = (bf16[27,16,512]{2,1,0:T(8,128)(2,1)S(1)}, bf16[27,16,512]{2,1,0:T(8,128)(2,1)S(1)}, u32[]{:S(2)}, u32[]{:S(2)}) collective-permute-start(bf16[27,16,512]{2,1,0:T(8,128)(2,1)S(1)} %collective-permute-done.5.refs_8_), channel_id=1, source_target_pairs={{0,1},{1,0},{2,3},{3,2},{4,5},{5,4},{6,7},{7,6},{8,9},{9,8},{10,11... | collective-permute-start | bytes 1327112 | tf_op jit(solution)/shard_map/ppermute | solution.py:105
  41.8 12.7 %collective-permute-start.9 = (bf16[27,16,512]{2,1,0:T(8,128)(2,1)S(1)}, bf16[27,16,512]{2,1,0:T(8,128)(2,1)}, u32[]{:S(2)}, u32[]{:S(2)}) collective-permute-start(bf16[27,16,512]{2,1,0:T(8,128)(2,1)S(1)} %collective-permute-done.7.refs_10_), channel_id=1, source_target_pairs={{0,8},{1,9},{2,10},{3,11},{8,16},{9,17},{10,18},{11,19},{16,24},{1... | collective-permute-start | bytes 1327112 | tf_op jit(solution)/shard_map/ppermute | solution.py:1275
  43.5 2.7 %collective-permute-start.15 = (bf16[27,16,512]{2,1,0:T(8,128)(2,1)S(1)}, bf16[27,16,512]{2,1,0:T(8,128)(2,1)S(1)}, u32[]{:S(2)}, u32[]{:S(2)}) collective-permute-start(bf16[27,16,512]{2,1,0:T(8,128)(2,1)S(1)} %collective-permute-done.7.refs_10_), channel_id=1, source_target_pairs={{0,1},{1,0},{2,3},{3,2},{4,5},{5,4},{6,7},{7,6},{8,9},{9,8},{10,11... | collective-permute-start | bytes 1327112 | tf_op jit(solution)/shard_map/ppermute | solution.py:105
  43.6 3.3 %collective-permute-start.16 = (bf16[27,16,512]{2,1,0:T(8,128)(2,1)}, bf16[27,16,512]{2,1,0:T(8,128)(2,1)S(1)}, u32[]{:S(2)}, u32[]{:S(2)}) collective-permute-start(bf16[27,16,512]{2,1,0:T(8,128)(2,1)} %collective-permute-done.8.refs_12_), channel_id=1, source_target_pairs={{0,1},{1,0},{2,3},{3,2},{4,5},{5,4},{6,7},{7,6},{8,9},{9,8},{10,11... | collective-permute-start | bytes 1327112 | tf_op jit(solution)/shard_map/ppermute | solution.py:105
  54.5 7.0 %collective-permute-start.17 = (bf16[27,16,512]{2,1,0:T(8,128)(2,1)}, bf16[27,16,512]{2,1,0:T(8,128)(2,1)S(1)}, u32[]{:S(2)}, u32[]{:S(2)}) collective-permute-start(bf16[27,16,512]{2,1,0:T(8,128)(2,1)} %collective-permute-done.9.rest_0_), channel_id=1, source_target_pairs={{0,1},{1,0},{2,3},{3,2},{4,5},{5,4},{6,7},{7,6},{8,9},{9,8},{10,11... | collective-permute-start | bytes 1327112 | tf_op jit(solution)/shard_map/ppermute | solution.py:105
  55.3 3.9 %collective-permute-start = (bf16[2,16,512]{2,1,0:T(8,128)(2,1)S(1)}, bf16[2,16,512]{2,1,0:T(8,128)(2,1)S(1)}, u32[]{:S(2)}, u32[]{:S(2)}) collective-permute-start(bf16[2,16,512]{2,1,0:T(8,128)(2,1)S(1)} %get-tuple-element.169), channel_id=1, source_target_pairs={{0,1},{1,2},{2,3},{4,5},{5,6},{6,7},{8,9},{9,10},{10,11},{12,13},{... | collective-permute-start | bytes 98312 | tf_op jit(solution)/shard_map/ppermute | solution.py:115
  57.7 3.9 %collective-permute-start.1 = (bf16[2,16,512]{2,1,0:T(8,128)(2,1)S(1)}, bf16[2,16,512]{2,1,0:T(8,128)(2,1)S(1)}, u32[]{:S(2)}, u32[]{:S(2)}) collective-permute-start(bf16[2,16,512]{2,1,0:T(8,128)(2,1)S(1)} %get-tuple-element.168), channel_id=1, source_target_pairs={{1,0},{2,1},{3,2},{5,4},{6,5},{7,6},{9,8},{10,9},{11,10},{13,12},{... | collective-permute-start | bytes 98312 | tf_op jit(solution)/shard_map/ppermute | solution.py:115
  116.4 14.8 %collective-permute-start.18 = (bf16[40,16,512]{2,1,0:T(8,128)(2,1)}, bf16[40,16,512]{2,1,0:T(8,128)(2,1)S(1)}, u32[]{:S(2)}, u32[]{:S(2)}) collective-permute-start(bf16[40,16,512]{2,1,0:T(8,128)(2,1)} %get-tuple-element.97), channel_id=1, source_target_pairs={{0,1},{1,0},{2,3},{3,2},{4,5},{5,4},{6,7},{7,6},{8,9},{9,8},{10,11... | collective-permute-start | bytes 1966088 | tf_op jit(solution)/shard_map/ppermute | solution.py:105
  119.1 15.7 %copy-start.5 = (bf16[40,16,512]{2,1,0:T(8,128)(2,1)S(1)}, bf16[40,16,512]{2,1,0:T(8,128)(2,1)}, u32[]{:S(2)}) copy-start(bf16[40,16,512]{2,1,0:T(8,128)(2,1)} %get-tuple-element.96) | copy-start | bytes 1966084
  131.2 15.9 %collective-permute-start.19 = (bf16[48,16,512]{2,1,0:T(8,128)(2,1)}, bf16[48,16,512]{2,1,0:T(8,128)(2,1)S(1)}, u32[]{:S(2)}, u32[]{:S(2)}) collective-permute-start(bf16[48,16,512]{2,1,0:T(8,128)(2,1)} %get-tuple-element.108), channel_id=1, source_target_pairs={{0,1},{1,0},{2,3},{3,2},{4,5},{5,4},{6,7},{7,6},{8,9},{9,8},{10,11... | collective-permute-start | bytes 2359304 | tf_op jit(solution)/shard_map/ppermute | solution.py:105
  132.2 56.8 %collective-permute-start.27 = (bf16[2,16,1536]{2,1,0:T(8,128)(2,1)S(1)}, bf16[2,16,1536]{2,1,0:T(8,128)(2,1)S(1)}, u32[]{:S(2)}, u32[]{:S(2)}) collective-permute-start(bf16[2,16,1536]{2,1,0:T(8,128)(2,1)S(1)} %slice.106), channel_id=1, source_target_pairs={{0,1},{1,2},{2,3},{4,5},{5,6},{6,7},{8,9},{9,10},{10,11},{12,13},{... | collective-permute-start | bytes 294920 | tf_op jit(solution)/shard_map/ppermute | solution.py:115
  147.2 13.6 %collective-permute-start.20 = (bf16[48,16,512]{2,1,0:T(8,128)(2,1)}, bf16[48,16,512]{2,1,0:T(8,128)(2,1)S(1)}, u32[]{:S(2)}, u32[]{:S(2)}) collective-permute-start(bf16[48,16,512]{2,1,0:T(8,128)(2,1)} %get-tuple-element.115), channel_id=1, source_target_pairs={{0,1},{1,0},{2,3},{3,2},{4,5},{5,4},{6,7},{7,6},{8,9},{9,8},{10,11... | collective-permute-start | bytes 2359304 | tf_op jit(solution)/shard_map/ppermute | solution.py:105
  148.0 33.3 %collective-permute-start.21 = (bf16[40,8,512]{2,1,0:T(8,128)(2,1)S(1)}, bf16[40,8,512]{2,1,0:T(8,128)(2,1)S(1)}, u32[]{:S(2)}, u32[]{:S(2)}) collective-permute-start(bf16[40,8,512]{2,1,0:T(8,128)(2,1)S(1)} %get-tuple-element.180), channel_id=1, source_target_pairs={{0,2},{1,3},{2,0},{3,1},{4,6},{5,7},{6,4},{7,5},{8,10},{9,11},{10,... | collective-permute-start | bytes 983048 | tf_op jit(solution)/shard_map/ppermute | solution.py:105
  148.8 18.2 %collective-permute-start.22 = (bf16[48,8,512]{2,1,0:T(8,128)(2,1)S(1)}, bf16[48,8,512]{2,1,0:T(8,128)(2,1)S(1)}, u32[]{:S(2)}, u32[]{:S(2)}) collective-permute-start(bf16[48,8,512]{2,1,0:T(8,128)(2,1)S(1)} %constant_dynamic-slice_fusion.2), channel_id=1, source_target_pairs={{0,2},{1,3},{2,0},{3,1},{4,6},{5,7},{6,4},{7,5},{8,10},{9,11},{10,... | collective-permute-start | bytes 1179656 | tf_op jit(solution)/shard_map/ppermute | solution.py:105
  161.2 19.4 %collective-permute-start.23 = (bf16[48,8,512]{2,1,0:T(8,128)(2,1)S(1)}, bf16[48,8,512]{2,1,0:T(8,128)(2,1)S(1)}, u32[]{:S(2)}, u32[]{:S(2)}) collective-permute-start(bf16[48,8,512]{2,1,0:T(8,128)(2,1)S(1)} %constant_dynamic-slice_fusion.1), channel_id=1, source_target_pairs={{0,2},{1,3},{2,0},{3,1},{4,6},{5,7},{6,4},{7,5},{8,10},{9,11},{10,... | collective-permute-start | bytes 1179656 | tf_op jit(solution)/shard_map/ppermute | solution.py:105
  186.9 9.8 %collective-permute-start.24 = (bf16[27,8,512]{2,1,0:T(8,128)(2,1)S(1)}, bf16[27,8,512]{2,1,0:T(8,128)(2,1)S(1)}, u32[]{:S(2)}, u32[]{:S(2)}) collective-permute-start(bf16[27,8,512]{2,1,0:T(8,128)(2,1)S(1)} %get-tuple-element.175), channel_id=1, source_target_pairs={{0,8},{1,9},{2,10},{3,11},{8,16},{9,17},{10,18},{11,19},{16,24},{1... | collective-permute-start | bytes 663560 | tf_op jit(solution)/shard_map/ppermute | solution.py:1379
  188.6 8.2 %collective-permute-start.25 = (bf16[27,8,512]{2,1,0:T(8,128)(2,1)S(1)}, bf16[27,8,512]{2,1,0:T(8,128)(2,1)S(1)}, u32[]{:S(2)}, u32[]{:S(2)}) collective-permute-start(bf16[27,8,512]{2,1,0:T(8,128)(2,1)S(1)} %get-tuple-element.174), channel_id=1, source_target_pairs={{0,4},{1,5},{2,6},{3,7},{8,0},{9,1},{10,2},{11,3},{16,8},{17,9},{1... | collective-permute-start | bytes 663560 | tf_op jit(solution)/shard_map/ppermute | solution.py:1381
  189.0 7.7 %collective-permute-start.26 = (f32[32,512]{1,0:T(8,128)S(1)}, f32[32,512]{1,0:T(8,128)S(1)}, u32[]{:S(2)}, u32[]{:S(2)}) collective-permute-start(f32[32,512]{1,0:T(8,128)S(1)} %copy-done.28), channel_id=1, source_target_pairs={{0,1},{1,0},{2,3},{3,2},{4,5},{5,4},{6,7},{7,6},{8,9},{9,8},{10,11... | collective-permute-start | bytes 196616 | tf_op jit(solution)/shard_map/ppermute | solution.py:105
  196.9 14.5 %collective-permute-start.28 = (bf16[27,8,512]{2,1,0:T(8,128)(2,1)S(1)}, bf16[27,8,512]{2,1,0:T(8,128)(2,1)S(1)}, u32[]{:S(2)}, u32[]{:S(2)}) collective-permute-start(bf16[27,8,512]{2,1,0:T(8,128)(2,1)S(1)} %get-tuple-element.173), channel_id=1, source_target_pairs={{0,8},{1,9},{2,10},{3,11},{8,16},{9,17},{10,18},{11,19},{16,24},{1... | collective-permute-start | bytes 663560 | tf_op jit(solution)/shard_map/ppermute | solution.py:1379
  198.5 12.9 %collective-permute-start.29 = (bf16[27,8,512]{2,1,0:T(8,128)(2,1)S(1)}, bf16[27,8,512]{2,1,0:T(8,128)(2,1)S(1)}, u32[]{:S(2)}, u32[]{:S(2)}) collective-permute-start(bf16[27,8,512]{2,1,0:T(8,128)(2,1)S(1)} %get-tuple-element.172), channel_id=1, source_target_pairs={{0,4},{1,5},{2,6},{3,7},{8,0},{9,1},{10,2},{11,3},{16,8},{17,9},{1... | collective-permute-start | bytes 663560 | tf_op jit(solution)/shard_map/ppermute | solution.py:1381
  199.0 12.4 %collective-permute-start.30 = (f32[32,512]{1,0:T(8,128)S(1)}, f32[32,512]{1,0:T(8,128)S(1)}, u32[]{:S(2)}, u32[]{:S(2)}) collective-permute-start(f32[32,512]{1,0:T(8,128)S(1)} %add.165), channel_id=1, source_target_pairs={{0,2},{1,3},{2,0},{3,1},{4,6},{5,7},{6,4},{7,5},{8,10},{9,11},{10,... | collective-permute-start | bytes 196616 | tf_op jit(solution)/shard_map/ppermute | solution.py:105
  199.1 3.1 %collective-permute-start.31 = (f32[2,8,512]{2,1,0:T(8,128)S(1)}, f32[2,8,512]{2,1,0:T(8,128)S(1)}, u32[]{:S(2)}, u32[]{:S(2)}) collective-permute-start(f32[2,8,512]{2,1,0:T(8,128)S(1)} %get-tuple-element.187), channel_id=1, source_target_pairs={{0,1},{1,2},{2,3},{4,5},{5,6},{6,7},{8,9},{9,10},{10,11},{12,13},{... | collective-permute-start | bytes 98312 | tf_op jit(solution)/shard_map/ppermute | solution.py:115
  200.8 4.8 %collective-permute-start.32 = (f32[2,8,512]{2,1,0:T(8,128)S(1)}, f32[2,8,512]{2,1,0:T(8,128)S(1)}, u32[]{:S(2)}, u32[]{:S(2)}) collective-permute-start(f32[2,8,512]{2,1,0:T(8,128)S(1)} %get-tuple-element.186), channel_id=1, source_target_pairs={{1,0},{2,1},{3,2},{5,4},{6,5},{7,6},{9,8},{10,9},{11,10},{13,12},{... | collective-permute-start | bytes 98312 | tf_op jit(solution)/shard_map/ppermute | solution.py:115
  211.5 8.0 %collective-permute-start.33 = (bf16[27,8,512]{2,1,0:T(8,128)(2,1)S(1)}, bf16[27,8,512]{2,1,0:T(8,128)(2,1)S(1)}, u32[]{:S(2)}, u32[]{:S(2)}) collective-permute-start(bf16[27,8,512]{2,1,0:T(8,128)(2,1)S(1)} %get-tuple-element.171), channel_id=1, source_target_pairs={{0,8},{1,9},{2,10},{3,11},{8,16},{9,17},{10,18},{11,19},{16,24},{1... | collective-permute-start | bytes 663560 | tf_op jit(solution)/shard_map/ppermute | solution.py:1379
  213.2 6.9 %collective-permute-start.34 = (bf16[27,8,512]{2,1,0:T(8,128)(2,1)S(1)}, bf16[27,8,512]{2,1,0:T(8,128)(2,1)S(1)}, u32[]{:S(2)}, u32[]{:S(2)}) collective-permute-start(bf16[27,8,512]{2,1,0:T(8,128)(2,1)S(1)} %get-tuple-element.170), channel_id=1, source_target_pairs={{0,4},{1,5},{2,6},{3,7},{8,0},{9,1},{10,2},{11,3},{16,8},{17,9},{1... | collective-permute-start | bytes 663560 | tf_op jit(solution)/shard_map/ppermute | solution.py:1381
  213.6 6.0 %collective-permute-start.35 = (f32[32,512]{1,0:T(8,128)S(1)}, f32[32,512]{1,0:T(8,128)S(1)}, u32[]{:S(2)}, u32[]{:S(2)}) collective-permute-start(f32[32,512]{1,0:T(8,128)S(1)} %add.168), channel_id=1, source_target_pairs={{0,4},{4,0},{8,12},{12,8},{16,20},{20,16},{24,28},{28,24},{1,5},{5... | collective-permute-start | bytes 196616 | tf_op jit(solution)/shard_map/ppermute | solution.py:110
  220.1 18.4 %copy-start.32 = (s32[243]{0:T(256)S(1)}, s32[243]{0:T(256)}, u32[]{:S(2)}) copy-start(s32[243]{0:T(256)} %broadcast_add_fusion) | copy-start | bytes 2920
  220.1 10.2 %collective-permute-start.36 = (bf16[27,8,512]{2,1,0:T(8,128)(2,1)S(1)}, bf16[27,8,512]{2,1,0:T(8,128)(2,1)S(1)}, u32[]{:S(2)}, u32[]{:S(2)}) collective-permute-start(bf16[27,8,512]{2,1,0:T(8,128)(2,1)S(1)} %add_convert_fusion.4), channel_id=1, source_target_pairs={{0,8},{1,9},{2,10},{3,11},{8,16},{9,17},{10,18},{11,19},{16,24},{1... | collective-permute-start | bytes 663560 | tf_op jit(solution)/shard_map/ppermute | solution.py:1379
  221.6 8.7 %collective-permute-start.37 = (f32[32,512]{1,0:T(8,128)S(1)}, f32[32,512]{1,0:T(8,128)S(1)}, u32[]{:S(2)}, u32[]{:S(2)}) collective-permute-start(f32[32,512]{1,0:T(8,128)S(1)} %add.171), channel_id=1, source_target_pairs={{0,8},{4,12},{8,0},{12,4},{16,24},{20,28},{24,16},{28,20},{1,9},{5... | collective-permute-start | bytes 196616 | tf_op jit(solution)/shard_map/ppermute | solution.py:110
  230.4 16.2 %copy-start.2 = (bf16[27,8,512]{2,1,0:T(8,128)(2,1)}, bf16[27,8,512]{2,1,0:T(8,128)(2,1)S(1)}, u32[]{:S(2)}) copy-start(bf16[27,8,512]{2,1,0:T(8,128)(2,1)S(1)} %add_convert_fusion.3.own) | copy-start | bytes 663556
  230.4 8.1 %collective-permute-start.39 = (bf16[27,8,512]{2,1,0:T(8,128)(2,1)S(1)}, bf16[27,8,512]{2,1,0:T(8,128)(2,1)S(1)}, u32[]{:S(2)}, u32[]{:S(2)}) collective-permute-start(bf16[27,8,512]{2,1,0:T(8,128)(2,1)S(1)} %add_convert_fusion.3.own), channel_id=1, source_target_pairs={{0,2},{1,3},{2,0},{3,1},{4,6},{5,7},{6,4},{7,5},{8,10},{9,11},{10,... | collective-permute-start | bytes 663560 | tf_op jit(solution)/shard_map/ppermute | solution.py:105
  232.4 14.1 %collective-permute-start.38 = (bf16[27,8,512]{2,1,0:T(8,128)(2,1)S(1)}, bf16[27,8,512]{2,1,0:T(8,128)(2,1)S(1)}, u32[]{:S(2)}, u32[]{:S(2)}) collective-permute-start(bf16[27,8,512]{2,1,0:T(8,128)(2,1)S(1)} %add_convert_fusion.3.own), channel_id=1, source_target_pairs={{0,1},{1,0},{2,3},{3,2},{4,5},{5,4},{6,7},{7,6},{8,9},{9,8},{10,11... | collective-permute-start | bytes 663560 | tf_op jit(solution)/shard_map/ppermute | solution.py:105
  238.5 8.0 %collective-permute-start.40 = (bf16[27,8,512]{2,1,0:T(8,128)(2,1)S(1)}, bf16[27,8,512]{2,1,0:T(8,128)(2,1)S(1)}, u32[]{:S(2)}, u32[]{:S(2)}) collective-permute-start(bf16[27,8,512]{2,1,0:T(8,128)(2,1)S(1)} %collective-permute-done.39.far), channel_id=1, source_target_pairs={{0,1},{1,0},{2,3},{3,2},{4,5},{5,4},{6,7},{7,6},{8,9},{9,8},{10,11... | collective-permute-start | bytes 663560 | tf_op jit(solution)/shard_map/ppermute | solution.py:105
  239.1 6.8 %collective-permute-start.41 = (f32[32,512]{1,0:T(8,128)S(1)}, f32[32,512]{1,0:T(8,128)S(1)}, u32[]{:S(2)}, u32[]{:S(2)}) collective-permute-start(f32[32,512]{1,0:T(8,128)S(1)} %add.173), channel_id=1, source_target_pairs={{0,16},{4,20},{8,24},{12,28},{16,0},{20,4},{24,8},{28,12},{1,17},{... | collective-permute-start | bytes 196616 | tf_op jit(solution)/shard_map/ppermute | solution.py:110
  (30 other events, 148.9 us)

commit v4 on v3

--- a/solution.py
+++ b/solution.py
@@ -399,7 +399,7 @@
         table_out,
         spec_ref,
         act_ref,
-        pre_ref,
+        der_ref,
         ada_ref,
         lowg_ref,
         resg_ref,
@@ -420,6 +420,7 @@
         lines,
         hg,
         hg_old,
+        pre_ref,
         logs_ref,
         angle_ref,
         ngrad_ref,
@@ -495,7 +496,7 @@
         for c in range(lane_tiles):
             cut = slice(c * LANE, (c + 1) * LANE)
             xc = conv[c] * rc
-            xc_ref[at : at + size, cut] = xc
+            xc_ref[at : at + size, cut] = xc.astype(BF16)
             scale = by_utterance(meta, row, utts, index, lambda u: picks[u : u + 1, cut])
             shift = by_utterance(meta, row, utts, index, lambda u: picks[utts + u : utts + u + 1, cut])
             ada_ref[at : at + size, cut] = (xc * scale + shift).astype(BF16)
@@ -524,7 +525,9 @@
             bias = vecs[2 + VROWS + c : 3 + VROWS + c, d - c * 512 : d - c * 512 + 256]
             pre = pre_ref[at : at + size, cut] + bias
             phi = 0.5 + 0.5 * lax.erf(pre * math.sqrt(0.5))
+            bell = jnp.exp(-0.5 * pre * pre) * (1.0 / math.sqrt(2.0 * math.pi))
             act_ref[at : at + size, cut] = (pre * phi).astype(BF16)
+            der_ref[at : at + size, cut] = (phi + pre * bell).astype(BF16)
 
     def second_norm(at, size):
         span = slice(at, at + size)
@@ -545,7 +548,7 @@
         xn = xn_ref[span, :]
         e = ngrad * vec(vec_at + 2)
         resg = rn_ref[span, 0:1] * (e - row_mean(e) - xn * row_mean(e * xn))
-        resg_ref[span, :] = resg
+        resg_ref[span, :] = resg.astype(BF16)
         low = (vec(vec_at + 1) * resg).astype(BF16)
         lowg_ref[span, :] = low
         return (
@@ -702,11 +705,11 @@
             shape_of((NB * BR, channels), BF16),
             shape_of((rows, frames, 2 * BIN_PAD), BF16),
             shape_of((count, FF), BF16),
-            shape_of((count, FF), F32),
+            shape_of((count, FF), BF16),
             shape_of((count, channels), BF16),
             shape_of((count, channels), BF16),
-            shape_of((count, channels), F32),
-            shape_of((count, channels), F32),
+            shape_of((count, channels), BF16),
+            shape_of((count, channels), BF16),
             shape_of((count, LANE), F32),
             shape_of((40, HALF, channels), BF16),
             shape_of((40, HALF, channels), BF16),
@@ -725,6 +728,7 @@
             pltpu.VMEM((channels // LANE, 1344, LANE), F32),
             pltpu.VMEM((TILE, 2 * BIN_PAD), BF16),
             pltpu.VMEM((TILE, 2 * BIN_PAD), BF16),
+            pltpu.VMEM((TILE, FF), F32),
             pltpu.VMEM((TILE, BIN_PAD), F32),
             pltpu.VMEM((TILE, BIN_PAD), F32),
             pltpu.VMEM((TILE, channels), F32),
@@ -744,20 +748,17 @@
     )(meta, places, counts, x, low, high, order, cot, *pieces, table)
 
 
-def mlp_body(meta, low_ref, act_ref, hidden_ref, ada_ref, wout_ref, last_ref, *rest, chunk, utts):
-    pre_ref, send_ref, keep_ref, bsum_ref, gout, gin, agrad, bias = rest[-8:]
+def mlp_body(meta, low_ref, act_ref, der_ref, ada_ref, wout_ref, *rest, utts):
+    pre_ref, send_ref, keep_ref, bsum_ref, gout, gin, agrad = rest[-7:]
     step = pl.program_id(0)
     core = meta[0, 2 * utts + 2]
-    tile, channels = low_ref.shape
+    tile = low_ref.shape[0]
 
     @pl.when(step == 0)
     def _():
         gout[...] = jnp.zeros_like(gout)
         gin[...] = jnp.zeros_like(gin)
         bsum_ref[...] = jnp.zeros_like(bsum_ref)
-        last = last_ref[...].astype(F32)
-        line = jnp.concatenate([last[2 + VROWS + c : 3 + VROWS + c] for c in range(IN_ROWS)], axis=1)
-        bias[...] = jnp.broadcast_to(line[:, chunk * CHUNK : (chunk + 1) * CHUNK], (8, CHUNK))
 
     def agrad_dot(c):
         agrad[:, c : c + 256] = dot(low_ref[...], wout_ref[c : c + 256, :], NT)
@@ -773,10 +774,7 @@
         total = bsum_ref[:, cut]
         for at, size in spans(tile, 32):
             span = slice(at, at + size)
-            value = hidden_ref[span, cut] + bias[0:1, cut]
-            phi = 0.5 + 0.5 * lax.erf(value * math.sqrt(0.5))
-            bell = jnp.exp(-0.5 * value * value) * (1.0 / math.sqrt(2.0 * math.pi))
-            pre = (agrad[span, cut] * (phi + value * bell)).astype(BF16)
+            pre = (agrad[span, cut] * der_ref[span, cut].astype(F32)).astype(BF16)
             pre_ref[span, cut] = pre
             total = total + fold(pre.astype(F32))
         bsum_ref[:, cut] = total
@@ -799,7 +797,7 @@
                 send_ref[at + b] = jnp.where(core == 0, high_half, low_half)
 
 
-def mlp_backward(chunk, before, meta, low, act, hidden, ada, table, utts):
+def mlp_backward(chunk, before, meta, low, act, der, ada, table, utts):
     count, channels = low.shape
     tile = 512
     slim = pl.BlockSpec((tile, channels), lambda i: (i, 0))
@@ -807,7 +805,7 @@
     buckets = 2 * CHUNK // BR
     more = [] if before is None else [before]
     return pl.pallas_call(
-        functools.partial(mlp_body, chunk=chunk, utts=utts),
+        functools.partial(mlp_body, utts=utts),
         grid=(count // tile,),
         in_specs=[
             SCALARS,
@@ -816,7 +814,6 @@
             part,
             slim,
             pl.BlockSpec((CHUNK, channels), lambda i: (FF // CHUNK + chunk, 0)),
-            pl.BlockSpec((BR, channels), lambda i: (NB - 1, 0)),
         ]
         + [ANYWHERE] * len(more),
         out_specs=[part, WHOLE, WHOLE, WHOLE],
@@ -826,17 +823,16 @@
             shape_of((buckets, HALF, channels), BF16),
             shape_of((8, CHUNK), F32),
         ],
-        input_output_aliases={7: 0} if more else {},
+        input_output_aliases={6: 0} if more else {},
         scratch_shapes=[
             pltpu.VMEM((CHUNK, channels), F32),
             pltpu.VMEM((CHUNK, channels), F32),
             pltpu.VMEM((tile, CHUNK), F32),
-            pltpu.VMEM((8, CHUNK), F32),
         ],
         compiler_params=params(),
         cost_estimate=cost(6 * count * CHUNK * 512, 16 * MIB),
         name=f"mlp_backward_{chunk}",
-    )(meta, low, act, hidden, ada, table, table, *more)
+    )(meta, low, act, der, ada, table, *more)
 
 
 def norm_body(
@@ -859,7 +855,7 @@
         pick_rows(meta, row, utts, vec, picks, channels)
 
     agrad[...] = dot(pre_ref[...], w_in[...], NN)
-    fill_frames(xs, x_ref, low_ref, high_ref, row, tile, tiles, channels)
+    fill_frames(xs, x_ref, low_ref, high_ref, 0, tile, tiles, channels)
     for at, size in spans(TILE, 32):
         span = slice(at, at + size)
         reach, left = frame_reach(meta, row, base + at, size, utts)
@@ -871,7 +867,7 @@
             cut = slice(c * LANE, (c + 1) * LANE)
             scale = by_utterance(meta, row, utts, index, lambda u: picks[u : u + 1, cut])
             ecs.append(agrad[span, cut] * scale)
-            xcs.append(xc_ref[span, cut])
+            xcs.append(xc_ref[span, cut].astype(F32))
         m_one = jnp.sum(sum(ecs), axis=1, keepdims=True) * (1.0 / channels)
         m_two = jnp.sum(sum([e * v for e, v in zip(ecs, xcs)]), axis=1, keepdims=True) * (1.0 / channels)
         rc = rc_ref[span, :]
@@ -879,7 +875,7 @@
             cut = slice(c * LANE, (c + 1) * LANE)
             value = rc * (ecs[c] - m_one - xcs[c] * m_two)
             cg[c, span, :] = value
-            cg_ref[span, cut] = value
+            cg_ref[span, cut] = value.astype(BF16)
     for u in range(utts):
         begin, end = meta[row, u], meta[row, u + 1]
 
@@ -894,7 +890,7 @@
                     span = slice(at, at + size)
                     index = base + at + lax.broadcasted_iota(jnp.int32, (size, LANE), 0)
                     value = jnp.where((index >= begin) & (index < end), agrad[span, cut], 0.0)
-                    one = one + fold(value * xc_ref[span, cut])
+                    one = one + fold(value * xc_ref[span, cut].astype(F32))
                     two = two + fold(value)
                 part_ref[KW + 1 + wanted, :, cut] += one
                 part_ref[KW + 1 + NBW + wanted, :, cut] += two
@@ -916,15 +912,16 @@
 
     @pl.when(tile == 0)
     def _():
-        edge_ref[0] = cg_ref[0:8, :]
+        edge_ref[0] = cg_ref[0:EDGE, :]
 
     @pl.when(tile == tiles - 1)
     def _():
-        edge_ref[1] = cg_ref[TILE - 8 : TILE, :]
+        edge_ref[1] = cg_ref[TILE - EDGE : TILE, :]
 
     if closing:
         _, tail_ref, sums_ref, hsum_ref, bsum0, bsum1, order_ref = more
-        vec_ref = outs[3]
+        vec_ref, quarter_refs = outs[-7], outs[3:7]
+        core, plane = meta[0, 2 * utts + 2], meta[0, 2 * utts + 3]
 
         @pl.when(tile == tiles - 1)
         def _():
@@ -959,6 +956,12 @@
                 at = 2 + VROWS + IN_ROWS + c
                 vec_ref[at : at + 1, :] = joined[0:1, c * channels : (c + 1) * channels]
             vec_ref[28:32, :] = jnp.zeros((4, channels), F32)
+            for ref, c, p in zip(
+                quarter_refs,
+                (core, 1 - core, core, 1 - core),
+                (plane, plane, 1 - plane, 1 - plane),
+            ):
+                ref[...] = vec_ref[pl.ds(pl.multiple_of(c * HALF + p * QUART, QUART), QUART), :]
 
 
 def norm_backward(row, closing, meta, x, low, high, pre, table, xc, rc, utts):
@@ -968,17 +971,20 @@
     sums = KW + 1 + 2 * NBW
     out_specs = [pl.BlockSpec((TILE, channels), lambda i: (i, 0)), WHOLE, WHOLE]
     out_shape = [
-        shape_of((frames, channels), F32),
-        shape_of((2, 8, channels), F32),
+        shape_of((frames, channels), BF16),
+        shape_of((2, EDGE, channels), BF16),
         shape_of((sums, 8, channels), F32),
     ]
     if closing:
-        out_specs.append(WHOLE)
-        out_shape.append(shape_of((BR, channels), F32))
+        out_specs += [WHOLE] * 4
+        out_shape += [shape_of((QUART, channels), F32)] * 4
     return pl.pallas_call(
         functools.partial(norm_body, row=row, tiles=tiles, utts=utts, closing=bool(closing)),
         grid=(tiles,),
-        in_specs=[SCALARS, WHOLE, WHOLE, WHOLE, block(FF)]
+        in_specs=[SCALARS]
+        + [pl.BlockSpec((1, frames, channels), lambda i: (row, 0, 0))]
+        + [pl.BlockSpec((1, EDGE, channels), lambda i: (row, 0, 0))] * 2
+        + [block(FF)]
         + [
             pl.BlockSpec((FF, channels), lambda i: (0, 0)),
             pl.BlockSpec((BR, channels), lambda i: (NB - 1, 0)),
@@ -988,7 +994,8 @@
         + [WHOLE] * len(closing),
         out_specs=out_specs,
         out_shape=out_shape,
-        scratch_shapes=[
+        scratch_shapes=([pltpu.VMEM((BR, channels), F32)] if closing else [])
+        + [
             pltpu.VMEM((channels // LANE, TILE + 2 * EDGE, LANE), F32),
             pltpu.VMEM((BR, channels), F32),
             pltpu.VMEM((2 * utts, channels), F32),
@@ -1014,18 +1021,19 @@
 
     for c in range(channels // LANE):
         cut = slice(c * LANE, (c + 1) * LANE)
-        cs[c, 8 : 8 + TILE, :] = cg_ref[:, cut]
-        cs[c, 0:8, :] = jnp.where(tile == 0, low_ref[row, :, cut], before_ref[:, cut])
-        cs[c, 8 + TILE :, :] = jnp.where(tile == tiles - 1, high_ref[row, :, cut], after_ref[:, cut])
+        cs[c, EDGE : EDGE + TILE, :] = cg_ref[:, cut].astype(F32)
+        cs[c, 0:EDGE, :] = jnp.where(tile == 0, low_ref[row, :, cut], before_ref[:, cut]).astype(F32)
+        after = jnp.where(tile == tiles - 1, high_ref[row, :, cut], after_ref[:, cut])
+        cs[c, EDGE + TILE :, :] = after.astype(F32)
     for at, size in spans(TILE, 32):
         span = slice(at, at + size)
         reach, left = frame_reach(meta, row, base + at, size, utts)
         for c in range(channels // LANE):
             cut = slice(c * LANE, (c + 1) * LANE)
-            total = resg_ref[span, cut]
+            total = resg_ref[span, cut].astype(F32)
             for k in range(KW):
                 offset = RIM - k
-                moved = cs[c, 8 + offset + at : 8 + offset + at + size, :]
+                moved = cs[c, EDGE + offset + at : EDGE + offset + at + size, :]
                 total = total + keep_within(moved, reach, left, offset) * vecs[2 + k : 3 + k, cut]
             out_ref[0, span, cut] = total
 
@@ -1033,7 +1041,7 @@
 def conv_backward(row, before, meta, cg, low, high, resg, table, rows, utts):
     frames, channels = cg.shape
     tiles = frames // TILE
-    per = TILE // 8
+    per = TILE // EDGE
     more = [] if before is None else [before]
     return pl.pallas_call(
         functools.partial(conv_body, row=row, tiles=tiles, utts=utts),
@@ -1041,8 +1049,8 @@
         in_specs=[
             SCALARS,
             pl.BlockSpec((TILE, channels), lambda i: (i, 0)),
-            pl.BlockSpec((8, channels), lambda i: (jnp.maximum(i * per - 1, 0), 0)),
-            pl.BlockSpec((8, channels), lambda i: (jnp.minimum((i + 1) * per, tiles * per - 1), 0)),
+            pl.BlockSpec((EDGE, channels), lambda i: (jnp.maximum(i * per - 1, 0), 0)),
+            pl.BlockSpec((EDGE, channels), lambda i: (jnp.minimum((i + 1) * per, tiles * per - 1), 0)),
             WHOLE,
             WHOLE,
             pl.BlockSpec((TILE, channels), lambda i: (row * tiles + i, 0)),
@@ -1053,7 +1061,7 @@
         out_shape=shape_of((rows, frames, channels), F32),
         input_output_aliases={8: 0} if more else {},
         scratch_shapes=[
-            pltpu.VMEM((channels // LANE, TILE + 16, LANE), F32),
+            pltpu.VMEM((channels // LANE, TILE + 2 * EDGE, LANE), F32),
             pltpu.VMEM((BR, channels), F32),
         ],
         compiler_params=params(),
@@ -1136,6 +1144,7 @@
 def slot_body(slot_of, *refs, bounds):
     count = len(bounds)
     out = refs[-1]
+    lasts = refs[2 * count : -1]
     for (start, stop), keep, came in zip(bounds, refs[:count], refs[count : 2 * count]):
 
         def one(b, carry, start=start, keep=keep, came=came):
@@ -1144,62 +1153,61 @@
             return carry
 
         lax.fori_loop(0, stop - start, one, 0)
-
-
-def to_slots(slot_of, keeps, cames, bounds, total):
+    out[slot_of[0, NB - 1]] = sum([ref[...] for ref in lasts]).astype(BF16)
+
+
+def to_slots(slot_of, keeps, cames, lasts, bounds, total):
     channels = keeps[0].shape[2]
     return pl.pallas_call(
         functools.partial(slot_body, bounds=bounds),
-        in_specs=[SCALARS] + [WHOLE] * (2 * len(bounds)),
+        in_specs=[SCALARS] + [WHOLE] * (2 * len(bounds) + len(lasts)),
         out_specs=WHOLE,
         out_shape=shape_of((total, QUART, channels), BF16),
         compiler_params=params(),
         cost_estimate=cost(0, 6 * MIB),
         name="to_slots",
-    )(slot_of, *keeps, *cames)
-
-
-def adam_body(places, spot, own, near, far, cross, last_ref, master, first, second, *outs, block):
-    out_master, out_first, out_second = outs
-    core, plane = spot[0], spot[1]
+    )(slot_of, *keeps, *cames, *lasts)
+
+
+def adam_body(places, spot, low_ref, high_ref, master, first, second, *rest, block):
+    out_master, out_first, out_second = rest[-3:]
     one_fix = 1.0 / (1.0 - BETA_ONE**STEP_COUNT)
     two_fix = 1.0 / (1.0 - BETA_TWO**STEP_COUNT)
     for s in range(block):
         bucket = places[0, pl.program_id(0) * block + s]
-        for ref, c, p in (
-            (own, core, plane),
-            (near, 1 - core, plane),
-            (far, core, 1 - plane),
-            (cross, 1 - core, 1 - plane),
-        ):
-            rows = pl.ds(pl.multiple_of(c * HALF + p * QUART, QUART), QUART)
-            grad = ref[s].astype(F32)
-            grad = jnp.where(bucket == NB - 1, last_ref[rows, :], grad)
-            grad = jnp.where(bucket < NB, grad, 0.0)
-            old = master[s, rows, :]
-            one = BETA_ONE * first[s, rows, :] + (1.0 - BETA_ONE) * grad
-            two = BETA_TWO * second[s, rows, :] + (1.0 - BETA_TWO) * grad * grad
-            out_first[s, rows, :] = one
-            out_second[s, rows, :] = two
+        for half, ref in enumerate((low_ref, high_ref)):
+            grad = jnp.where(bucket < NB, ref[s].astype(F32), 0.0)
+            old = master[s, half, 0]
+            one = BETA_ONE * first[s, half, 0] + (1.0 - BETA_ONE) * grad
+            two = BETA_TWO * second[s, half, 0] + (1.0 - BETA_TWO) * grad * grad
+            out_first[s, half, 0] = one
+            out_second[s, half, 0] = two
             step = one * one_fix / (jnp.sqrt(two * two_fix) + ADAM_EPS)
-            out_master[s, rows, :] = old - LEARN_RATE * (step + WEIGHT_DECAY * old)
-
-
-def adam(places, spot, quarters, last, master, first, second):
+            out_master[s, half, 0] = old - LEARN_RATE * (step + WEIGHT_DECAY * old)
+
+
+def adam(places, spot, low, high, master, first, second, before):
     slots, depth, channels = master.shape
     block = max(b for b in range(1, 10) if slots % b == 0)
-    full = pl.BlockSpec((block, depth, channels), lambda i: (i, 0, 0))
-    part = pl.BlockSpec((block, QUART, channels), lambda i: (i, 0, 0))
-    return pl.pallas_call(
+    cut = lambda v: v.reshape(slots, 2, 2, QUART, channels)
+    full = pl.BlockSpec((block, 2, 1, QUART, channels), lambda i, places, spot: (i, 0, spot[0], 0, 0))
+    part = pl.BlockSpec((block, QUART, channels), lambda i, places, spot: (i, 0, 0))
+    more = [cut(v) for v in before]
+    outs = pl.pallas_call(
         functools.partial(adam_body, block=block),
-        grid=(slots // block,),
-        in_specs=[SCALARS, SCALARS] + [part] * 4 + [WHOLE, full, full, full],
-        out_specs=[full] * 3,
-        out_shape=[shape_of(master.shape, F32)] * 3,
+        grid_spec=pltpu.PrefetchScalarGridSpec(
+            num_scalar_prefetch=2,
+            grid=(slots // block,),
+            in_specs=[part] * 2 + [full] * 3 + [ANYWHERE] * len(more),
+            out_specs=[full] * 3,
+        ),
+        out_shape=[shape_of((slots, 2, 2, QUART, channels), F32)] * 3,
+        input_output_aliases={7 + v: v for v in range(len(more))},
         compiler_params=params(),
-        cost_estimate=cost(0, 12 * MIB),
-        name="adam",
-    )(places, spot, *quarters, last, master, first, second)
+        cost_estimate=cost(0, 6 * MIB),
+        name="adam_second" if more else "adam_first",
+    )(places, spot, low, high, cut(master), cut(first), cut(second), *more)
+    return [v.reshape(slots, depth, channels) for v in outs]
 
 
 def tie(*values):
@@ -1227,7 +1235,7 @@
     starts = [jnp.zeros((rows, 1), jnp.int32)]
     for u in range(utts):
         starts.append(starts[-1] + lengths[:, u : u + 1])
-    spot = jnp.broadcast_to(jnp.stack([seq_at * frames, core])[None, :], (rows, 2)).astype(jnp.int32)
+    spot = jnp.broadcast_to(jnp.stack([seq_at * frames, core, plane])[None, :], (rows, 3)).astype(jnp.int32)
     meta = jnp.concatenate(starts + [bw_ids, spot], axis=1)
     lines = wave_grad.reshape(rows, frames * HOP // LANE, LANE).transpose(1, 0, 2).reshape(-1, LANE)
     order = jnp.asarray(order_table())
@@ -1276,7 +1284,7 @@
             if hop < half_ring - 1:
                 back = lax.ppermute(back, AXES, ring_step(ring, -1, seqs))
             if hop in (1, 2):
-                feed = tie(lines, *source)[0]
+                feed, low, high = tie(lines, low, high, *source)[:3]
                 begin, end = ((0, tiles // 2), (tiles // 2, tiles))[hop - 1]
                 cot = spectrum_cotangent(begin, end, cot, meta, feed, later, synth, win, rows, utts)
                 ahead, back, cot = tie(ahead, back, cot)
@@ -1299,7 +1307,7 @@
         partial_table = jnp.zeros((NB * BR, channels), BF16)
         cot = spectrum_cotangent(0, tiles, cot, meta, lines, later, synth, win, rows, utts)
 
-    (table, spec, act, hidden, ada, low_grad, resg, xc, rc, send, keep, tail, sums, hsum) = forward(
+    (table, spec, act, der, ada, low_grad, resg, xc, rc, send, keep, tail, sums, hsum) = forward(
         owned, meta, part_places, part_counts, frames_in, low, high, order, cot, arrived, partial_table, utts
     )
     halo = shifted(spec[:, frames - EDGE :], 1)
@@ -1321,73 +1329,67 @@
     per = CHUNK // BR
     pre, bsums = None, []
     begins, count = (2 * FF // BR,), 40
+    waiting = []
     for chunk in range(FF // CHUNK):
         near = seq_swap(send, 1)
-        pre, next_send, next_keep, bsum = mlp_backward(chunk, pre, meta, low_grad, act, hidden, ada, table, utts)
+        pre, next_send, next_keep, bsum = mlp_backward(chunk, pre, meta, low_grad, act, der, ada, table, utts)
         near, pre, next_send, next_keep = tie(near, pre, next_send, next_keep)
         bsums.append(bsum)
         stay, leave = split(keep, near)
-        record(stay, seq_swap(leave, 2), begins, count)
+        waiting.append((stay, seq_swap(leave, 2), begins, count))
         send, keep = next_send, next_keep
         begins, count = (chunk * per, FF // BR + chunk * per), per
 
     near = seq_swap(send, 1)
+    for stay, came, *where_from in waiting[:-1]:
+        pre, came = tie(pre, came)
+        record(stay, came, *where_from)
     cg0, edge0, parts = norm_backward(0, (), meta, frames_in, low, high, pre, table, xc, rc, utts)
-    near, cg0, edge0, parts, pre = tie(near, cg0, edge0, parts, pre)
+    kept, came, *where_from = waiting[-1]
+    near, cg0, edge0, parts, pre, came = tie(near, cg0, edge0, parts, pre, came)
+    record(kept, came, *where_from)
     stay, leave = split(keep, near)
     came = seq_swap(leave, 2)
     closing = (parts, tail, sums, hsum, *bsums, order)
-    cg1, edge1, _, last = norm_backward(1, closing, meta, frames_in, low, high, pre, table, xc, rc, utts)
-    came, cg1, edge1, last, spec = tie(came, cg1, edge1, last, spec)
+    cg1, edge1, _, own, to_near, to_far, to_cross = norm_backward(
+        1, closing, meta, frames_in, low, high, pre, table, xc, rc, utts
+    )
+    lasts = (own, seq_swap(to_near, 1), seq_swap(to_far, 2), seq_swap(to_cross, 3))
+    edges = jnp.stack([edge0, edge1])
+    edge_low, edge_high = shifted(edges[:, 1], 1), shifted(edges[:, 0], -1)
+    came, spec, edge_low, edge_high, *lasts = tie(came, spec, edge_low, edge_high, *lasts)
     record(stay, came, begins, count)
-    chunks = to_slots(slot_of, keeps, cames, tuple(bounds), owners * slots)
-    edges = jnp.stack([edge0, edge1])
+    chunks = to_slots(slot_of, keeps, cames, lasts, tuple(bounds), owners * slots)
 
     state = {}
 
     def work(stage, *ready):
-        if stage == 0:
+        if stage in (0, 3):
             feed = tie(spec, *ready)[0]
-            state["low"] = shifted(edges[:, 1], 1)
-            state["high"] = shifted(edges[:, 0], -1)
-            state["wave"] = wave_forward(0, tiles // 2, None, meta, feed, halo, synth, win, utts)
-            return state["wave"]
-        if stage == 1:
-            feed = tie(cg0, *ready)[0]
+            begin, end, before = ((0, tiles // 2, None), (tiles // 2, tiles, state.get("wave")))[stage // 3]
+            state["wave"] = wave_forward(begin, end, before, meta, feed, halo, synth, win, utts)
+            return "wave"
+        if stage in (1, 4):
+            row = stage // 4
+            feed = tie((cg0, cg1)[row], *ready)[0]
             state["grad"] = conv_backward(
-                0, None, meta, feed, state["low"], state["high"], resg, table, rows, utts
+                row, state.get("grad"), meta, feed, edge_low, edge_high, resg, table, rows, utts
             )
-            return state["grad"]
-        if stage == 2:
-            feed = tie(cg1, *ready)[0]
-            state["grad"] = conv_backward(
-                1, state["grad"], meta, feed, state["low"], state["high"], resg, table, rows, utts
-            )
-            return state["grad"]
-        if stage == 3:
-            feed = tie(spec, *ready)[0]
-            state["wave"] = wave_forward(tiles // 2, tiles, state["wave"], meta, feed, halo, synth, win, utts)
-            return state["wave"]
-        return state["wave"]
+            return "grad"
+        return None
 
     if ring:
         cut = {o: chunks[i * slots : (i + 1) * slots] for i, o in enumerate(offsets)}
         up, down = cut[-half_ring], cut[1 - half_ring]
         for hop in range(half_ring):
             left_over = half_ring - 1 - hop
-            source = (up, down, last)
+            source = (up, down)
             up = lax.ppermute(up, AXES, ring_step(ring, 1, seqs))
             if hop < half_ring - 1:
                 down = lax.ppermute(down, AXES, ring_step(ring, -1, seqs))
-            if hop < 2:
-                last = last + seq_swap(last, 1 << hop)
-            else:
-                last = last + rows_swap(last, 1 << (hop - 2))
             done = work(hop, *source)
-            if hop in (0, 3):
-                up, down, last, state["wave"] = tie(up, down, last, done)
-            else:
-                up, down, last, state["grad"] = tie(up, down, last, done)
+            if done:
+                up, down, state[done] = tie(up, down, state[done])
             if left_over:
                 up = plus(up, cut[left_over])
                 if hop < half_ring - 2:
@@ -1395,19 +1397,21 @@
         own = plus(cut[0], up, down)
     else:
         own = lax.psum_scatter(chunks, "rows", scatter_dimension=0, tiled=True)
-        last = lax.psum(last, AXES)
-        for hop in range(4):
+        for hop in (0, 1, 3):
             work(hop, own)
-    far = seq_swap(own, 2)
-    near = seq_swap(own, 1)
-    if ring:
-        last = last + rows_swap(last, 4)
+    near, far = seq_swap(own, 1), seq_swap(own, 2)
+    work(4, own)
+    near, far, state["grad"] = tie(near, far, state["grad"])
+    cross = seq_swap(far, 1)
     waveform = state["wave"].reshape(-1, rows, LANE).transpose(1, 0, 2).reshape(rows, frames * HOP)
-    cross = seq_swap(far, 1)
-    where_at = jnp.stack([core, plane]).astype(jnp.int32)
-    new_master, new_first, new_second = adam(
-        held, where_at, (own, near, far, cross), last, master, moment1, moment2
-    )
+
+    def ordered(mine, other):
+        return jnp.where(core == 0, mine, other), jnp.where(core == 0, other, mine)
+
+    here, there = plane[None].astype(jnp.int32), (1 - plane)[None].astype(jnp.int32)
+    first = adam(held, here, *ordered(own, near), master, moment1, moment2, ())
+    cross, *first = tie(cross, *first)
+    new_master, new_first, new_second = adam(held, there, *ordered(far, cross), master, moment1, moment2, first)
     return waveform, state["grad"], new_master, new_first, new_second
 
 

time: 256 us -> 250 us (0.977)
  waiting for transfers between devices: 28.2 us -> 23.4 us
    ppermute x4, waiting for transfers between devices: 0.01 us -> 7.65 us  [local(): up = lax.ppermute(up, AXES, ring_step(ring, 1, seqs))]
    ppermute x6, waiting for transfers between devices: 5.83 us -> 0.02 us  [shifted(): lax.ppermute(value, 'seq', [(i - distance, i) for i in devices if i - dis...]
    ppermute x19 -> x20, waiting for transfers between devices: 11.7 us -> 6.01 us  [seq_swap(): return lax.ppermute(value, 'seq', [(s, s ^ bit) for s in range(count)])]
    ppermute x3, waiting for transfers between devices: 0.47 us -> 5.93 us  [local(): down = lax.ppermute(down, AXES, ring_step(ring, -1, seqs))]
    ppermute x19 -> x20, starting transfers between devices: 8.01 us -> 12.4 us  [seq_swap(): return lax.ppermute(value, 'seq', [(s, s ^ bit) for s in range(count)])]
    ppermute x3 -> x0, starting transfers between devices: 4.36 us -> none  [rows_swap(): return lax.ppermute(value, 'rows', [(r, r ^ bit) for r in range(count)])]
    ppermute x3 -> x0, waiting for transfers between devices: 4.24 us -> none  [rows_swap(): return lax.ppermute(value, 'rows', [(r, r ^ bit) for r in range(count)])]
    pallas_call x1, Pallas kernels: 53.5 us -> 56.1 us  [forward(): pl.pallas_call(functools.partial(forward_body, owners=owners, slots=slots...]
  transfers between devices with their start and end apart: 42 -> 40, of which waited for: 12 -> 11; matrix products, arithmetic and copies ran while one was open for 9% -> 9% of each run, Pallas kernels for 37% -> 38%
where the time goes in v4:
time: 250 us; the launch traced here: 248 us
  Pallas kernels  157 us (63%)
  starting transfers between devices  38.3 us (15%)
  waiting for transfers between devices  23.4 us (9%)
  local copies, waits for them, and re-layouts  15.3 us (6%)
  other arithmetic  13.6 us (5%)
    pallas_call x1, Pallas kernels, forward(): pl.pallas_call(functools.partial(forward_body, owners=owners, slots=slots...  56.1 us
    pallas_call x2, Pallas kernels, mlp_backward(): pl.pallas_call(functools.partial(mlp_body, utts=utts), grid=(count // til...  21 us
    pallas_call x2, Pallas kernels, norm_backward(): pl.pallas_call(functools.partial(norm_body, row=row, tiles=tiles, utts=ut...  20.7 us
    pallas_call x2, Pallas kernels, spectrum_cotangent(): pl.pallas_call(functools.partial(pre_body, start=start, tiles=tiles, rows...  15.1 us
    pallas_call x2, Pallas kernels, wave_forward(): pl.pallas_call(functools.partial(wave_body, start=start, rows=rows, utts=...  14.1 us
    ppermute x20, starting transfers between devices, seq_swap(): return lax.ppermute(value, 'seq', [(s, s ^ bit) for s in range(count)])  12.4 us
    pallas_call x2, Pallas kernels, adam(): pl.pallas_call(functools.partial(adam_body, block=block), grid_spec=pltpu...  9.97 us
    pallas_call x2, Pallas kernels, conv_backward(): pl.pallas_call(functools.partial(conv_body, row=row, tiles=tiles, utts=ut...  9.58 us
  transfers between devices with their start and end apart: 40, of which 11 were waited for; matrix products, arithmetic and copies ran while one was open for 9% of the time, Pallas kernels for 38%

profile of v4, /device:TPU:0, one launch (start us, length us, event | category | flops | bytes accessed | tf_op | source)
XLA Modules:
  0.0 248.2 jit_solution(4109185352599408545)
XLA Ops:
  0.6 1.2 dynamic-slice_convert_fusion.refs_0_
  1.9 3.1 %collective-permute-start.2 = (bf16[27,16,512]{2,1,0:T(8,128)(2,1)S(1)}, bf16[27,16,512]{2,1,0:T(8,128)(2,1)S(1)}, u32[]{:S(2)}, u32[]{:S(2)}) collective-permute-start(bf16[27,16,512]{2,1,0:T(8,128)(2,1)S(1)} %dynamic-slice_convert_fusion.refs_0_), channel_id=1, source_target_pairs={{0,8},{1,9},{2,10},{3,11},{8,16},{9,17},{10,18},{11,19},{16,24},{1... | collective-permute-start | bytes 1327112 | tf_op jit(solution)/shard_map/ppermute | solution.py:1283
  5.8 1.4 collective-permute-start
  7.2 1.3 collective-permute-start.1
  9.3 1.3 collective-permute-start.6
  11.5 1.3 fusion.5
  12.8 1.3 and_select_fusion
  14.1 1.4 select_reduce_fusion.2
  17.2 1.9 collective-permute-start.4
  20.2 1.3 concatenate.12.meta
  21.5 3.2 %collective-permute-start.10 = (bf16[27,16,512]{2,1,0:T(8,128)(2,1)S(1)}, bf16[27,16,512]{2,1,0:T(8,128)(2,1)S(1)}, u32[]{:S(2)}, u32[]{:S(2)}) collective-permute-start(bf16[27,16,512]{2,1,0:T(8,128)(2,1)S(1)} %dynamic-slice_convert_fusion.refs_0_), channel_id=1, source_target_pairs={{0,1},{1,0},{2,3},{3,2},{4,5},{5,4},{6,7},{7,6},{8,9},{9,8},{10,11... | collective-permute-start | bytes 1327112 | tf_op jit(solution)/shard_map/ppermute | solution.py:105
  26.5 7.5 %spectrum_cotangent_0.1.rest_0_ = bf16[2,1024,1536]{2,1,0:T(8,128)(2,1)} custom-call(s32[2,12]{1,0:T(2,128)} %concatenate.12.meta, bf16[5120,128]{1,0:T(8,128)(2,1)} %bitcast.46, bf16[80,128]{1,0:T(8,128)(2,1)} %copy-done.23, bf16[2,768,768]{2,1,0:T(8,128)(2,1)} %constant.76.clone.synth_ref, f32[8,384]{1,0:T(8,128)} %constant.77.clone.win_ref), custom_call_target="tpu_custom_call" | custom-call | flops 2415919104 | bytes 7340032 | tf_op jit(solution)/shard_map/spectrum_cotangent_0/pallas_call | solution.py:264
  34.1 1.6 collective-permute-start.7
  36.7 7.7 %spectrum_cotangent_2.1.cot_ref = bf16[2,1024,1536]{2,1,0:T(8,128)(2,1)} custom-call(s32[2,12]{1,0:T(2,128)} %concatenate.12.meta, bf16[5120,128]{1,0:T(8,128)(2,1)} %bitcast.47, bf16[80,128]{1,0:T(8,128)(2,1)} %copy-done.23, bf16[2,768,768]{2,1,0:T(8,128)(2,1)} %constant.76.clone.synth_ref, ...), custom_call_target="tpu_custom_call", output_to_operand_aliasing={{}: (5, {})} | custom-call | flops 2415919104 | bytes 7340032 | tf_op jit(solution)/shard_map/spectrum_cotangent_2/pallas_call | solution.py:264
  44.4 1.8 collective-permute-done.7.refs_10_
  46.2 1.4 collective-permute-done.8.refs_12_
  47.6 1.6 collective-permute-start.9
  49.8 1.3 convert_reduce_fusion.1
  53.6 6.2 %assemble.1.rest_2_ = bf16[4384,512]{1,0:T(8,128)(2,1)} custom-call(s32[1,216]{1,0:T(1,128)} %bitcast.54, s32[1,8]{1,0:T(1,128)} %bitcast.58, s32[1]{0:T(128)} %bitcast.2.core, bf16[27,16,512]{2,1,0:T(8,128)(2,1)} %copy-done.1, bf16[27,16,512]{2,1,0:T(8,128)(2,1)} %copy-done.9, bf16[27,16,512]{2,1,0:T(8,128)(2,1)} %copy-done.5, ...), custom_call_target="tpu_custom_call" | custom-call | bytes 12582912 | tf_op jit(solution)/shard_map/assemble/pallas_call | solution.py:309
  60.3 2.0 collective-permute-done.17.rest_1_
  63.1 56.1 %forward.1 = (bf16[4384,512]{1,0:T(8,128)(2,1)}, bf16[2,1024,1536]{2,1,0:T(8,128)(2,1)}, bf16[2048,1536]{1,0:T(8,128)(2,1)}, bf16[2048,1536]{1,0:T(8,128)(2,1)},...) custom-call(s32[2,12]{1,0:T(2,128)} %concatenate.12.meta, ...), custom_call_target="tpu_custom_call" | custom-call | flops 16106127360 | bytes 41943040 | tf_op jit(solution)/shard_map/forward/pallas_call | solution.py:696
  119.4 10.5 %mlp_backward_0.1 = (bf16[2048,1536]{1,0:T(8,128)(2,1)}, bf16[48,16,512]{2,1,0:T(8,128)(2,1)}, bf16[48,16,512]{2,1,0:T(8,128)(2,1)}, f32[8,768]{1,0:T(8,128)}) custom-call(s32[2,12]{1,0:T(2,128)} %concatenate.12.meta, bf16[2048,512]{1,0:T(8,128)(2,1)} %get-tuple-element.118.low_ref, bf16[2048,1536]{1,0:T(8,128)(2,1)} %get-tuple-element.119.act_ref, ...), custom_call_target="tpu_custom_call" | custom-call | flops 4831838208 | bytes 16777216 | tf_op jit(solution)/shard_map/mlp_backward_0/pallas_call | solution.py:807
  131.6 2.7 %collective-permute-start.21 = (bf16[40,8,512]{2,1,0:T(8,128)(2,1)}, bf16[40,8,512]{2,1,0:T(8,128)(2,1)S(1)}, u32[]{:S(2)}, u32[]{:S(2)}) collective-permute-start(bf16[40,8,512]{2,1,0:T(8,128)(2,1)} %get-tuple-element.212), channel_id=1, source_target_pairs={{0,2},{1,3},{2,0},{3,1},{4,6},{5,7},{6,4},{7,5},{8,10},{9,11},{10,... | collective-permute-start | bytes 983048 | tf_op jit(solution)/shard_map/ppermute | solution.py:105
  134.2 10.5 %mlp_backward_1.1 = (bf16[2048,1536]{1,0:T(8,128)(2,1)}, bf16[48,16,512]{2,1,0:T(8,128)(2,1)}, bf16[48,16,512]{2,1,0:T(8,128)(2,1)}, f32[8,768]{1,0:T(8,128)}) custom-call(s32[2,12]{1,0:T(2,128)} %concatenate.12.meta, bf16[2048,512]{1,0:T(8,128)(2,1)} %get-tuple-element.118.low_ref, ...), custom_call_target="tpu_custom_call", output_to_operand_aliasing={{0}: (6, {})} | custom-call | flops 4831838208 | bytes 16777216 | tf_op jit(solution)/shard_map/mlp_backward_1/pallas_call | solution.py:807
  147.2 9.0 %norm_backward_0.1 = (bf16[1024,512]{1,0:T(8,128)(2,1)}, bf16[2,16,512]{2,1,0:T(8,128)(2,1)}, f32[16,8,512]{2,1,0:T(8,128)}) custom-call(s32[2,12]{1,0:T(2,128)} %concatenate.12.meta, bf16[2,1024,512]{2,1,0:T(8,128)(2,1)} %x_ref.5, bf16[2,16,512]{2,1,0:T(8,128)(2,1)} %copy-done.19, bf16[2,16,512]{2,1,0:T(8,128)(2,1)} %copy-done.20, ...), custom_call_target="tpu_custom_call" | custom-call | flops 1610612736 | bytes 12582912 | tf_op jit(solution)/shard_map/norm_backward_0/pallas_call | solution.py:981
  157.1 1.6 collective-permute-start.23
  158.6 11.6 %norm_backward_1.1 = (bf16[1024,512]{1,0:T(8,128)(2,1)}, bf16[2,16,512]{2,1,0:T(8,128)(2,1)}, f32[16,8,512]{2,1,0:T(8,128)}, f32[8,512]{1,0:T(8,128)}, f32[8,512...) custom-call(s32[2,12]{1,0:T(2,128)} %concatenate.12.meta, bf16[2,1024,512]{2,1,0:T(8,128)(2,1)} %x_ref.5, ...), custom_call_target="tpu_custom_call" | custom-call | flops 1610612736 | bytes 12582912 | tf_op jit(solution)/shard_map/norm_backward_1/pallas_call | solution.py:981
  171.8 2.4 collective-permute-start.24
  174.2 1.3 collective-permute-start.25
  175.5 2.3 collective-permute-start.27
  178.9 1.2 collective-permute-done.27.refs_12_
  180.0 1.9 collective-permute-start.31
  182.8 3.8 %to_slots.1 = bf16[216,8,512]{2,1,0:T(8,128)(2,1)} custom-call(s32[1,137]{1,0:T(1,128)} %bitcast.57, bf16[40,8,512]{2,1,0:T(8,128)(2,1)} %get-tuple-element.213.refs_0_, bf16[24,8,512]{2,1,0:T(8,128)(2,1)} %get-tuple-element.211.refs_1_, bf16[24,8,512]{2,1,0:T(8,128)(2,1)} %get-tuple-element.210.refs_2_, bf16[24,8,512]{2,1,0:T(8,128)(2,1)} %get-tuple-element.209.refs_3_, ...), custom_call_target="tpu_custom_call" | custom-call | bytes 6291456 | tf_op jit(solution)/shard_map/to_slots/pallas_call | solution.py:1161
  187.7 1.3 collective-permute-start.29
  190.4 7.1 %wave_forward_0.1.rest_0_ = f32[5120,128]{1,0:T(8,128)} custom-call(s32[2,12]{1,0:T(2,128)} %concatenate.12.meta, bf16[2,1024,1536]{2,1,0:T(8,128)(2,1)} %get-tuple-element.176.spec_ref.prev_ref, bf16[2,1024,1536]{2,1,0:T(8,128)(2,1)} %get-tuple-element.176.spec_ref.prev_ref, bf16[2,16,1536]{2,1,0:T(8,128)(2,1)} %copy-done.17, ...), custom_call_target="tpu_custom_call" | custom-call | flops 2415919104 | bytes 10485760 | tf_op jit(solution)/shard_map/wave_forward_0/pallas_call | solution.py:1118
  197.6 1.3 collective-permute-start.32
  199.7 4.8 %conv_backward_0.1.rest_0_ = f32[2,1024,512]{2,1,0:T(8,128)} custom-call(s32[2,12]{1,0:T(2,128)} %concatenate.12.meta, bf16[1024,512]{1,0:T(8,128)(2,1)} %get-tuple-element.170.cg_ref.before_ref.after_ref, bf16[1024,512]{1,0:T(8,128)(2,1)} %get-tuple-element.170.cg_ref.before_ref.after_ref, bf16[1024,512]{1,0:T(8,128)(2,1)} %get-tuple-element.170.cg_ref.before_ref.after_ref, ...), custom_call_target="tpu_custom_call" | custom-call | flops 8388608 | bytes 6291456 | tf_op jit(solution)/shard_map/conv_backward_0/pallas_call | solution.py:1046
  204.5 1.1 collective-permute-done.32
  205.6 1.1 collective-permute-done.33
  206.8 1.2 collective-permute-start.34
  208.0 6.5 %collective-permute-done.34 = bf16[27,8,512]{2,1,0:T(8,128)(2,1)S(1)} collective-permute-done((bf16[27,8,512]{2,1,0:T(8,128)(2,1)S(1)}, bf16[27,8,512]{2,1,0:T(8,128)(2,1)S(1)}, u32[]{:S(2)}, u32[]{:S(2)}) %collective-permute-start.34) | collective-permute-done | bytes 221216 | tf_op jit(solution)/shard_map/ppermute | solution.py:1387
  215.6 1.1 collective-permute-start.35
  216.7 4.8 %collective-permute-done.36 = bf16[27,8,512]{2,1,0:T(8,128)(2,1)S(1)} collective-permute-done((bf16[27,8,512]{2,1,0:T(8,128)(2,1)S(1)}, bf16[27,8,512]{2,1,0:T(8,128)(2,1)S(1)}, u32[]{:S(2)}, u32[]{:S(2)}) %collective-permute-start.36) | collective-permute-done | bytes 221216 | tf_op jit(solution)/shard_map/ppermute | solution.py:1389
  221.5 7.0 %wave_forward_2.1 = f32[5120,128]{1,0:T(8,128)} custom-call(s32[2,12]{1,0:T(2,128)} %concatenate.12.meta, bf16[2,1024,1536]{2,1,0:T(8,128)(2,1)} %get-tuple-element.176.spec_ref.prev_ref, bf16[2,1024,1536]{2,1,0:T(8,128)(2,1)} %get-tuple-element.176.spec_ref.prev_ref, bf16[2,16,1536]{2,1,0:T(8,128)(2,1)} %copy-done.17, ...), custom_call_target="tpu_custom_call", output_to_operand_aliasing={{}: (6, {})} | custom-call | flops 2415919104 | bytes 10485760 | tf_op jit(solution)/shard_map/wave_forward_2/pallas_call | solution.py:1118
  229.4 4.8 %conv_backward_1.1 = f32[2,1024,512]{2,1,0:T(8,128)} custom-call(s32[2,12]{1,0:T(2,128)} %concatenate.12.meta, bf16[1024,512]{1,0:T(8,128)(2,1)} %get-tuple-element.182.cg_ref.before_ref.after_ref, bf16[1024,512]{1,0:T(8,128)(2,1)} %get-tuple-element.182.cg_ref.before_ref.after_ref, ...), custom_call_target="tpu_custom_call", output_to_operand_aliasing={{}: (8, {})} | custom-call | flops 8388608 | bytes 6291456 | tf_op jit(solution)/shard_map/conv_backward_1/pallas_call | solution.py:1046
  234.2 2.4 collective-permute-done.38
  237.4 5.0 %adam_first.1 = (f32[27,2,2,8,512]{4,3,2,1,0:T(8,128)}, f32[27,2,2,8,512]{4,3,2,1,0:T(8,128)}, f32[27,2,2,8,512]{4,3,2,1,0:T(8,128)}) custom-call(s32[1,27]{1,0:T(1,128)} %slice.128.places, s32[1]{0:T(128)} %bitcast.3.spot, bf16[27,8,512]{2,1,0:T(8,128)(2,1)} %get-tuple-element.217.low_ref, bf16[27,8,512]{2,1,0:T(8,128)(2,1)} %get-tuple-element.216.high_ref, ...), custom_call_target="tpu_custom_call" | custom-call | bytes 6291456 | tf_op jit(solution)/shard_map/adam_first/pallas_call | solution.py:1196
  243.2 5.0 %adam_second.1 = (f32[27,2,2,8,512]{4,3,2,1,0:T(8,128)}, f32[27,2,2,8,512]{4,3,2,1,0:T(8,128)}, f32[27,2,2,8,512]{4,3,2,1,0:T(8,128)}) custom-call(s32[1,27]{1,0:T(1,128)} %slice.128.places, s32[1]{0:T(128)} %bitcast.20.spot, bf16[27,8,512]{2,1,0:T(8,128)(2,1)} %get-tuple-element.215.low_ref, ...), custom_call_target="tpu_custom_call", output_to_operand_aliasing={{0}: (7, {}), {1}: (8, {}), {2}: (9, {})} | custom-call | bytes 6291456 | tf_op jit(solution)/shard_map/adam_second/pallas_call | solution.py:1196
  (153 shorter events, 27.8 us)
Async XLA Ops:
  1.9 32.1 %copy-start.1 = (bf16[27,16,512]{2,1,0:T(8,128)(2,1)}, bf16[27,16,512]{2,1,0:T(8,128)(2,1)S(1)}, u32[]{:S(2)}) copy-start(bf16[27,16,512]{2,1,0:T(8,128)(2,1)S(1)} %dynamic-slice_convert_fusion.refs_0_) | copy-start | bytes 1327108
  1.9 15.3 %collective-permute-start.2 = (bf16[27,16,512]{2,1,0:T(8,128)(2,1)S(1)}, bf16[27,16,512]{2,1,0:T(8,128)(2,1)S(1)}, u32[]{:S(2)}, u32[]{:S(2)}) collective-permute-start(bf16[27,16,512]{2,1,0:T(8,128)(2,1)S(1)} %dynamic-slice_convert_fusion.refs_0_), channel_id=1, source_target_pairs={{0,8},{1,9},{2,10},{3,11},{8,16},{9,17},{10,18},{11,19},{16,24},{1... | collective-permute-start | bytes 1327112 | tf_op jit(solution)/shard_map/ppermute | solution.py:1283
  5.0 14.1 %collective-permute-start.3 = (bf16[27,16,512]{2,1,0:T(8,128)(2,1)S(1)}, bf16[27,16,512]{2,1,0:T(8,128)(2,1)S(1)}, u32[]{:S(2)}, u32[]{:S(2)}) collective-permute-start(bf16[27,16,512]{2,1,0:T(8,128)(2,1)S(1)} %dynamic-slice_convert_fusion.refs_0_), channel_id=1, source_target_pairs={{0,4},{1,5},{2,6},{3,7},{8,0},{9,1},{10,2},{11,3},{16,8},{17,9},{1... | collective-permute-start | bytes 1327112 | tf_op jit(solution)/shard_map/ppermute | solution.py:1285
  5.8 15.7 %collective-permute-start = (bf16[2,16,512]{2,1,0:T(8,128)(2,1)S(1)}, bf16[2,16,512]{2,1,0:T(8,128)(2,1)S(1)}, u32[]{:S(2)}, u32[]{:S(2)}) collective-permute-start(bf16[2,16,512]{2,1,0:T(8,128)(2,1)S(1)} %get-tuple-element.201), channel_id=1, source_target_pairs={{0,1},{1,2},{2,3},{4,5},{5,6},{6,7},{8,9},{9,10},{10,11},{12,13},{... | collective-permute-start | bytes 98312 | tf_op jit(solution)/shard_map/ppermute | solution.py:115
  7.2 17.5 %collective-permute-start.1 = (bf16[2,16,512]{2,1,0:T(8,128)(2,1)S(1)}, bf16[2,16,512]{2,1,0:T(8,128)(2,1)S(1)}, u32[]{:S(2)}, u32[]{:S(2)}) collective-permute-start(bf16[2,16,512]{2,1,0:T(8,128)(2,1)S(1)} %get-tuple-element.200), channel_id=1, source_target_pairs={{1,0},{2,1},{3,2},{5,4},{6,5},{7,6},{9,8},{10,9},{11,10},{13,12},{... | collective-permute-start | bytes 98312 | tf_op jit(solution)/shard_map/ppermute | solution.py:115
  9.3 16.6 %collective-permute-start.6 = (bf16[80,128]{1,0:T(8,128)(2,1)S(1)}, bf16[80,128]{1,0:T(8,128)(2,1)S(1)}, u32[]{:S(2)}, u32[]{:S(2)}) collective-permute-start(bf16[80,128]{1,0:T(8,128)(2,1)S(1)} %bitcast.53), channel_id=1, source_target_pairs={{1,0},{2,1},{3,2},{5,4},{6,5},{7,6},{9,8},{10,9},{11,10},{13,12},{... | collective-permute-start | bytes 61448 | tf_op jit(solution)/shard_map/ppermute | solution.py:115
  17.2 16.8 %copy-start.5 = (bf16[27,16,512]{2,1,0:T(8,128)(2,1)}, bf16[27,16,512]{2,1,0:T(8,128)(2,1)S(1)}, u32[]{:S(2)}) copy-start(bf16[27,16,512]{2,1,0:T(8,128)(2,1)S(1)} %collective-permute-done.2.refs_2_) | copy-start | bytes 1327108
  17.2 16.9 %collective-permute-start.4 = (bf16[27,16,512]{2,1,0:T(8,128)(2,1)S(1)}, bf16[27,16,512]{2,1,0:T(8,128)(2,1)S(1)}, u32[]{:S(2)}, u32[]{:S(2)}) collective-permute-start(bf16[27,16,512]{2,1,0:T(8,128)(2,1)S(1)} %collective-permute-done.2.refs_2_), channel_id=1, source_target_pairs={{0,8},{1,9},{2,10},{3,11},{8,16},{9,17},{10,18},{11,19},{16,24},{1... | collective-permute-start | bytes 1327112 | tf_op jit(solution)/shard_map/ppermute | solution.py:1283
  19.1 15.0 %copy-start.6 = (bf16[27,16,512]{2,1,0:T(8,128)(2,1)}, bf16[27,16,512]{2,1,0:T(8,128)(2,1)S(1)}, u32[]{:S(2)}) copy-start(bf16[27,16,512]{2,1,0:T(8,128)(2,1)S(1)} %collective-permute-done.3.refs_4_) | copy-start | bytes 1327108
  19.1 15.0 %collective-permute-start.5 = (bf16[27,16,512]{2,1,0:T(8,128)(2,1)S(1)}, bf16[27,16,512]{2,1,0:T(8,128)(2,1)S(1)}, u32[]{:S(2)}, u32[]{:S(2)}) collective-permute-start(bf16[27,16,512]{2,1,0:T(8,128)(2,1)S(1)} %collective-permute-done.3.refs_4_), channel_id=1, source_target_pairs={{0,4},{1,5},{2,6},{3,7},{8,0},{9,1},{10,2},{11,3},{16,8},{17,9},{1... | collective-permute-start | bytes 1327112 | tf_op jit(solution)/shard_map/ppermute | solution.py:1285
  21.5 26.1 %collective-permute-start.10 = (bf16[27,16,512]{2,1,0:T(8,128)(2,1)S(1)}, bf16[27,16,512]{2,1,0:T(8,128)(2,1)S(1)}, u32[]{:S(2)}, u32[]{:S(2)}) collective-permute-start(bf16[27,16,512]{2,1,0:T(8,128)(2,1)S(1)} %dynamic-slice_convert_fusion.refs_0_), channel_id=1, source_target_pairs={{0,1},{1,0},{2,3},{3,2},{4,5},{5,4},{6,7},{7,6},{8,9},{9,8},{10,11... | collective-permute-start | bytes 1327112 | tf_op jit(solution)/shard_map/ppermute | solution.py:105
  25.3 24.0 %collective-permute-start.11 = (bf16[27,16,512]{2,1,0:T(8,128)(2,1)S(1)}, bf16[27,16,512]{2,1,0:T(8,128)(2,1)S(1)}, u32[]{:S(2)}, u32[]{:S(2)}) collective-permute-start(bf16[27,16,512]{2,1,0:T(8,128)(2,1)S(1)} %collective-permute-done.2.refs_2_), channel_id=1, source_target_pairs={{0,1},{1,0},{2,3},{3,2},{4,5},{5,4},{6,7},{7,6},{8,9},{9,8},{10,11... | collective-permute-start | bytes 1327112 | tf_op jit(solution)/shard_map/ppermute | solution.py:105
  25.9 23.5 %collective-permute-start.12 = (bf16[27,16,512]{2,1,0:T(8,128)(2,1)S(1)}, bf16[27,16,512]{2,1,0:T(8,128)(2,1)S(1)}, u32[]{:S(2)}, u32[]{:S(2)}) collective-permute-start(bf16[27,16,512]{2,1,0:T(8,128)(2,1)S(1)} %collective-permute-done.3.refs_4_), channel_id=1, source_target_pairs={{0,1},{1,0},{2,3},{3,2},{4,5},{5,4},{6,7},{7,6},{8,9},{9,8},{10,11... | collective-permute-start | bytes 1327112 | tf_op jit(solution)/shard_map/ppermute | solution.py:105
  34.1 13.5 %copy-start.8 = (bf16[27,16,512]{2,1,0:T(8,128)(2,1)}, bf16[27,16,512]{2,1,0:T(8,128)(2,1)S(1)}, u32[]{:S(2)}) copy-start(bf16[27,16,512]{2,1,0:T(8,128)(2,1)S(1)} %collective-permute-done.5.refs_8_) | copy-start | bytes 1327108
  34.1 12.1 %collective-permute-start.7 = (bf16[27,16,512]{2,1,0:T(8,128)(2,1)S(1)}, bf16[27,16,512]{2,1,0:T(8,128)(2,1)S(1)}, u32[]{:S(2)}, u32[]{:S(2)}) collective-permute-start(bf16[27,16,512]{2,1,0:T(8,128)(2,1)S(1)} %collective-permute-done.4.refs_6_), channel_id=1, source_target_pairs={{0,8},{1,9},{2,10},{3,11},{8,16},{9,17},{10,18},{11,19},{16,24},{1... | collective-permute-start | bytes 1327112 | tf_op jit(solution)/shard_map/ppermute | solution.py:1283
  35.7 11.9 %collective-permute-start.8 = (bf16[27,16,512]{2,1,0:T(8,128)(2,1)S(1)}, bf16[27,16,512]{2,1,0:T(8,128)(2,1)}, u32[]{:S(2)}, u32[]{:S(2)}) collective-permute-start(bf16[27,16,512]{2,1,0:T(8,128)(2,1)S(1)} %collective-permute-done.5.refs_8_), channel_id=1, source_target_pairs={{0,4},{1,5},{2,6},{3,7},{8,0},{9,1},{10,2},{11,3},{16,8},{17,9},{1... | collective-permute-start | bytes 1327112 | tf_op jit(solution)/shard_map/ppermute | solution.py:1285
  36.7 14.4 %copy-start.30 = (s32[137]{0:T(256)S(1)}, s32[137]{0:T(256)}, u32[]{:S(2)}) copy-start(s32[137]{0:T(256)} %get-tuple-element.224) | copy-start | bytes 1648
  36.7 14.4 %copy-start.31 = (s32[137]{0:T(256)S(1)}, s32[137]{0:T(256)}, u32[]{:S(2)}) copy-start(s32[137]{0:T(256)} %get-tuple-element.227) | copy-start | bytes 1648
  46.2 5.6 %collective-permute-start.13 = (bf16[27,16,512]{2,1,0:T(8,128)(2,1)S(1)}, bf16[27,16,512]{2,1,0:T(8,128)(2,1)S(1)}, u32[]{:S(2)}, u32[]{:S(2)}) collective-permute-start(bf16[27,16,512]{2,1,0:T(8,128)(2,1)S(1)} %collective-permute-done.4.refs_6_), channel_id=1, source_target_pairs={{0,1},{1,0},{2,3},{3,2},{4,5},{5,4},{6,7},{7,6},{8,9},{9,8},{10,11... | collective-permute-start | bytes 1327112 | tf_op jit(solution)/shard_map/ppermute | solution.py:105
  47.6 4.2 %collective-permute-start.14 = (bf16[27,16,512]{2,1,0:T(8,128)(2,1)S(1)}, bf16[27,16,512]{2,1,0:T(8,128)(2,1)S(1)}, u32[]{:S(2)}, u32[]{:S(2)}) collective-permute-start(bf16[27,16,512]{2,1,0:T(8,128)(2,1)S(1)} %collective-permute-done.5.refs_8_), channel_id=1, source_target_pairs={{0,1},{1,0},{2,3},{3,2},{4,5},{5,4},{6,7},{7,6},{8,9},{9,8},{10,11... | collective-permute-start | bytes 1327112 | tf_op jit(solution)/shard_map/ppermute | solution.py:105
  47.6 12.7 %collective-permute-start.9 = (bf16[27,16,512]{2,1,0:T(8,128)(2,1)S(1)}, bf16[27,16,512]{2,1,0:T(8,128)(2,1)}, u32[]{:S(2)}, u32[]{:S(2)}) collective-permute-start(bf16[27,16,512]{2,1,0:T(8,128)(2,1)S(1)} %collective-permute-done.7.refs_10_), channel_id=1, source_target_pairs={{0,8},{1,9},{2,10},{3,11},{8,16},{9,17},{10,18},{11,19},{16,24},{1... | collective-permute-start | bytes 1327112 | tf_op jit(solution)/shard_map/ppermute | solution.py:1283
  49.3 2.6 %collective-permute-start.15 = (bf16[27,16,512]{2,1,0:T(8,128)(2,1)S(1)}, bf16[27,16,512]{2,1,0:T(8,128)(2,1)S(1)}, u32[]{:S(2)}, u32[]{:S(2)}) collective-permute-start(bf16[27,16,512]{2,1,0:T(8,128)(2,1)S(1)} %collective-permute-done.7.refs_10_), channel_id=1, source_target_pairs={{0,1},{1,0},{2,3},{3,2},{4,5},{5,4},{6,7},{7,6},{8,9},{9,8},{10,11... | collective-permute-start | bytes 1327112 | tf_op jit(solution)/shard_map/ppermute | solution.py:105
  49.4 3.1 %collective-permute-start.16 = (bf16[27,16,512]{2,1,0:T(8,128)(2,1)}, bf16[27,16,512]{2,1,0:T(8,128)(2,1)S(1)}, u32[]{:S(2)}, u32[]{:S(2)}) collective-permute-start(bf16[27,16,512]{2,1,0:T(8,128)(2,1)} %collective-permute-done.8.refs_12_), channel_id=1, source_target_pairs={{0,1},{1,0},{2,3},{3,2},{4,5},{5,4},{6,7},{7,6},{8,9},{9,8},{10,11... | collective-permute-start | bytes 1327112 | tf_op jit(solution)/shard_map/ppermute | solution.py:105
  60.3 2.0 collective-permute-start.17
  119.2 10.7 %collective-permute-start.18 = (bf16[40,16,512]{2,1,0:T(8,128)(2,1)}, bf16[40,16,512]{2,1,0:T(8,128)(2,1)S(1)}, u32[]{:S(2)}, u32[]{:S(2)}) collective-permute-start(bf16[40,16,512]{2,1,0:T(8,128)(2,1)} %get-tuple-element.117), channel_id=1, source_target_pairs={{0,1},{1,0},{2,3},{3,2},{4,5},{5,4},{6,7},{7,6},{8,9},{9,8},{10,11... | collective-permute-start | bytes 1966088 | tf_op jit(solution)/shard_map/ppermute | solution.py:105
  130.0 14.7 %collective-permute-start.19 = (bf16[48,16,512]{2,1,0:T(8,128)(2,1)}, bf16[48,16,512]{2,1,0:T(8,128)(2,1)S(1)}, u32[]{:S(2)}, u32[]{:S(2)}) collective-permute-start(bf16[48,16,512]{2,1,0:T(8,128)(2,1)} %get-tuple-element.128), channel_id=1, source_target_pairs={{0,1},{1,0},{2,3},{3,2},{4,5},{5,4},{6,7},{7,6},{8,9},{9,8},{10,11... | collective-permute-start | bytes 2359304 | tf_op jit(solution)/shard_map/ppermute | solution.py:105
  131.6 13.2 %copy-start.3 = (bf16[48,16,512]{2,1,0:T(8,128)(2,1)S(1)}, bf16[48,16,512]{2,1,0:T(8,128)(2,1)}, u32[]{:S(2)}) copy-start(bf16[48,16,512]{2,1,0:T(8,128)(2,1)} %get-tuple-element.127) | copy-start | bytes 2359300
  131.6 14.8 %collective-permute-start.21 = (bf16[40,8,512]{2,1,0:T(8,128)(2,1)}, bf16[40,8,512]{2,1,0:T(8,128)(2,1)S(1)}, u32[]{:S(2)}, u32[]{:S(2)}) collective-permute-start(bf16[40,8,512]{2,1,0:T(8,128)(2,1)} %get-tuple-element.212), channel_id=1, source_target_pairs={{0,2},{1,3},{2,0},{3,1},{4,6},{5,7},{6,4},{7,5},{8,10},{9,11},{10,... | collective-permute-start | bytes 983048 | tf_op jit(solution)/shard_map/ppermute | solution.py:105
  144.7 12.0 %collective-permute-start.20 = (bf16[48,16,512]{2,1,0:T(8,128)(2,1)}, bf16[48,16,512]{2,1,0:T(8,128)(2,1)S(1)}, u32[]{:S(2)}, u32[]{:S(2)}) collective-permute-start(bf16[48,16,512]{2,1,0:T(8,128)(2,1)} %get-tuple-element.135), channel_id=1, source_target_pairs={{0,1},{1,0},{2,3},{3,2},{4,5},{5,4},{6,7},{7,6},{8,9},{9,8},{10,11... | collective-permute-start | bytes 2359304 | tf_op jit(solution)/shard_map/ppermute | solution.py:105
  145.1 11.6 %collective-permute-start.22 = (bf16[48,8,512]{2,1,0:T(8,128)(2,1)S(1)}, bf16[48,8,512]{2,1,0:T(8,128)(2,1)S(1)}, u32[]{:S(2)}, u32[]{:S(2)}) collective-permute-start(bf16[48,8,512]{2,1,0:T(8,128)(2,1)S(1)} %constant_dynamic-slice_fusion.3), channel_id=1, source_target_pairs={{0,2},{1,3},{2,0},{3,1},{4,6},{5,7},{6,4},{7,5},{8,10},{9,11},{10,... | collective-permute-start | bytes 1179656 | tf_op jit(solution)/shard_map/ppermute | solution.py:105
  157.1 24.9 %collective-permute-start.23 = (bf16[48,8,512]{2,1,0:T(8,128)(2,1)S(1)}, bf16[48,8,512]{2,1,0:T(8,128)(2,1)S(1)}, u32[]{:S(2)}, u32[]{:S(2)}) collective-permute-start(bf16[48,8,512]{2,1,0:T(8,128)(2,1)S(1)} %constant_dynamic-slice_fusion.1), channel_id=1, source_target_pairs={{0,2},{1,3},{2,0},{3,1},{4,6},{5,7},{6,4},{7,5},{8,10},{9,11},{10,... | collective-permute-start | bytes 1179656 | tf_op jit(solution)/shard_map/ppermute | solution.py:105
  170.2 7.6 %collective-permute-start.26 = (f32[8,512]{1,0:T(8,128)}, f32[8,512]{1,0:T(8,128)S(1)}, u32[]{:S(2)}, u32[]{:S(2)}) collective-permute-start(f32[8,512]{1,0:T(8,128)} %get-tuple-element.157), channel_id=1, source_target_pairs={{0,1},{1,0},{2,3},{3,2},{4,5},{5,4},{6,7},{7,6},{8,9},{9,8},{10,11... | collective-permute-start | bytes 49160 | tf_op jit(solution)/shard_map/ppermute | solution.py:105
  171.8 10.1 %collective-permute-start.24 = (bf16[2,16,512]{2,1,0:T(8,128)(2,1)S(1)}, bf16[2,16,512]{2,1,0:T(8,128)(2,1)S(1)}, u32[]{:S(2)}, u32[]{:S(2)}) collective-permute-start(bf16[2,16,512]{2,1,0:T(8,128)(2,1)S(1)} %get-tuple-element.223), channel_id=1, source_target_pairs={{0,1},{1,2},{2,3},{4,5},{5,6},{6,7},{8,9},{9,10},{10,11},{12,13},{... | collective-permute-start | bytes 98312 | tf_op jit(solution)/shard_map/ppermute | solution.py:115
  174.2 7.7 %collective-permute-start.25 = (bf16[2,16,512]{2,1,0:T(8,128)(2,1)S(1)}, bf16[2,16,512]{2,1,0:T(8,128)(2,1)S(1)}, u32[]{:S(2)}, u32[]{:S(2)}) collective-permute-start(bf16[2,16,512]{2,1,0:T(8,128)(2,1)S(1)} %get-tuple-element.222), channel_id=1, source_target_pairs={{1,0},{2,1},{3,2},{5,4},{6,5},{7,6},{9,8},{10,9},{11,10},{13,12},{... | collective-permute-start | bytes 98312 | tf_op jit(solution)/shard_map/ppermute | solution.py:115
  175.5 4.5 %collective-permute-start.27 = (f32[8,512]{1,0:T(8,128)}, f32[8,512]{1,0:T(8,128)S(1)}, u32[]{:S(2)}, u32[]{:S(2)}) collective-permute-start(f32[8,512]{1,0:T(8,128)} %get-tuple-element.158), channel_id=1, source_target_pairs={{0,2},{1,3},{2,0},{3,1},{4,6},{5,7},{6,4},{7,5},{8,10},{9,11},{10,... | collective-permute-start | bytes 49160 | tf_op jit(solution)/shard_map/ppermute | solution.py:105
  177.9 4.0 %collective-permute-start.28 = (f32[8,512]{1,0:T(8,128)}, f32[8,512]{1,0:T(8,128)S(1)}, u32[]{:S(2)}, u32[]{:S(2)}) collective-permute-start(f32[8,512]{1,0:T(8,128)} %get-tuple-element.159), channel_id=1, source_target_pairs={{0,3},{1,2},{2,1},{3,0},{4,7},{5,6},{6,5},{7,4},{8,11},{9,10},{10,... | collective-permute-start | bytes 49160 | tf_op jit(solution)/shard_map/ppermute | solution.py:105
  180.0 9.7 %collective-permute-start.31 = (bf16[2,16,1536]{2,1,0:T(8,128)(2,1)S(1)}, bf16[2,16,1536]{2,1,0:T(8,128)(2,1)S(1)}, u32[]{:S(2)}, u32[]{:S(2)}) collective-permute-start(bf16[2,16,1536]{2,1,0:T(8,128)(2,1)S(1)} %slice.108), channel_id=1, source_target_pairs={{0,1},{1,2},{2,3},{4,5},{5,6},{6,7},{8,9},{9,10},{10,11},{12,13},{... | collective-permute-start | bytes 294920 | tf_op jit(solution)/shard_map/ppermute | solution.py:115
  187.7 9.8 %collective-permute-start.29 = (bf16[27,8,512]{2,1,0:T(8,128)(2,1)S(1)}, bf16[27,8,512]{2,1,0:T(8,128)(2,1)S(1)}, u32[]{:S(2)}, u32[]{:S(2)}) collective-permute-start(bf16[27,8,512]{2,1,0:T(8,128)(2,1)S(1)} %get-tuple-element.207), channel_id=1, source_target_pairs={{0,8},{1,9},{2,10},{3,11},{8,16},{9,17},{10,18},{11,19},{16,24},{1... | collective-permute-start | bytes 663560 | tf_op jit(solution)/shard_map/ppermute | solution.py:1387
  189.0 8.5 %collective-permute-start.30 = (bf16[27,8,512]{2,1,0:T(8,128)(2,1)S(1)}, bf16[27,8,512]{2,1,0:T(8,128)(2,1)S(1)}, u32[]{:S(2)}, u32[]{:S(2)}) collective-permute-start(bf16[27,8,512]{2,1,0:T(8,128)(2,1)S(1)} %get-tuple-element.206), channel_id=1, source_target_pairs={{0,4},{1,5},{2,6},{3,7},{8,0},{9,1},{10,2},{11,3},{16,8},{17,9},{1... | collective-permute-start | bytes 663560 | tf_op jit(solution)/shard_map/ppermute | solution.py:1389
  197.6 8.0 %collective-permute-start.32 = (bf16[27,8,512]{2,1,0:T(8,128)(2,1)S(1)}, bf16[27,8,512]{2,1,0:T(8,128)(2,1)S(1)}, u32[]{:S(2)}, u32[]{:S(2)}) collective-permute-start(bf16[27,8,512]{2,1,0:T(8,128)(2,1)S(1)} %get-tuple-element.205), channel_id=1, source_target_pairs={{0,8},{1,9},{2,10},{3,11},{8,16},{9,17},{10,18},{11,19},{16,24},{1... | collective-permute-start | bytes 663560 | tf_op jit(solution)/shard_map/ppermute | solution.py:1387
  198.9 7.8 %collective-permute-start.33 = (bf16[27,8,512]{2,1,0:T(8,128)(2,1)S(1)}, bf16[27,8,512]{2,1,0:T(8,128)(2,1)S(1)}, u32[]{:S(2)}, u32[]{:S(2)}) collective-permute-start(bf16[27,8,512]{2,1,0:T(8,128)(2,1)S(1)} %get-tuple-element.204), channel_id=1, source_target_pairs={{0,4},{1,5},{2,6},{3,7},{8,0},{9,1},{10,2},{11,3},{16,8},{17,9},{1... | collective-permute-start | bytes 663560 | tf_op jit(solution)/shard_map/ppermute | solution.py:1389
  206.8 7.7 %collective-permute-start.34 = (bf16[27,8,512]{2,1,0:T(8,128)(2,1)S(1)}, bf16[27,8,512]{2,1,0:T(8,128)(2,1)S(1)}, u32[]{:S(2)}, u32[]{:S(2)}) collective-permute-start(bf16[27,8,512]{2,1,0:T(8,128)(2,1)S(1)} %add_convert_fusion.6), channel_id=1, source_target_pairs={{0,8},{1,9},{2,10},{3,11},{8,16},{9,17},{10,18},{11,19},{16,24},{1... | collective-permute-start | bytes 663560 | tf_op jit(solution)/shard_map/ppermute | solution.py:1387
  214.6 6.9 %collective-permute-start.36 = (bf16[27,8,512]{2,1,0:T(8,128)(2,1)S(1)}, bf16[27,8,512]{2,1,0:T(8,128)(2,1)S(1)}, u32[]{:S(2)}, u32[]{:S(2)}) collective-permute-start(bf16[27,8,512]{2,1,0:T(8,128)(2,1)S(1)} %get-tuple-element.202), channel_id=1, source_target_pairs={{0,4},{1,5},{2,6},{3,7},{8,0},{9,1},{10,2},{11,3},{16,8},{17,9},{1... | collective-permute-start | bytes 663560 | tf_op jit(solution)/shard_map/ppermute | solution.py:1389
  215.6 13.2 %copy-start.29 = (s32[243]{0:T(256)S(1)}, s32[243]{0:T(256)}, u32[]{:S(2)}) copy-start(s32[243]{0:T(256)} %broadcast_add_fusion) | copy-start | bytes 2920
  215.6 13.0 %collective-permute-start.35 = (bf16[27,8,512]{2,1,0:T(8,128)(2,1)S(1)}, bf16[27,8,512]{2,1,0:T(8,128)(2,1)S(1)}, u32[]{:S(2)}, u32[]{:S(2)}) collective-permute-start(bf16[27,8,512]{2,1,0:T(8,128)(2,1)S(1)} %get-tuple-element.203), channel_id=1, source_target_pairs={{0,8},{1,9},{2,10},{3,11},{8,16},{9,17},{10,18},{11,19},{16,24},{1... | collective-permute-start | bytes 663560 | tf_op jit(solution)/shard_map/ppermute | solution.py:1387
  228.6 5.6 %collective-permute-start.37 = (bf16[27,8,512]{2,1,0:T(8,128)(2,1)S(1)}, bf16[27,8,512]{2,1,0:T(8,128)(2,1)S(1)}, u32[]{:S(2)}, u32[]{:S(2)}) collective-permute-start(bf16[27,8,512]{2,1,0:T(8,128)(2,1)S(1)} %add_convert_fusion.3), channel_id=1, source_target_pairs={{0,1},{1,0},{2,3},{3,2},{4,5},{5,4},{6,7},{7,6},{8,9},{9,8},{10,11... | collective-permute-start | bytes 663560 | tf_op jit(solution)/shard_map/ppermute | solution.py:105
  228.7 7.8 %collective-permute-start.38 = (bf16[27,8,512]{2,1,0:T(8,128)(2,1)S(1)}, bf16[27,8,512]{2,1,0:T(8,128)(2,1)S(1)}, u32[]{:S(2)}, u32[]{:S(2)}) collective-permute-start(bf16[27,8,512]{2,1,0:T(8,128)(2,1)S(1)} %add_convert_fusion.3), channel_id=1, source_target_pairs={{0,2},{1,3},{2,0},{3,1},{4,6},{5,7},{6,4},{7,5},{8,10},{9,11},{10,... | collective-permute-start | bytes 663560 | tf_op jit(solution)/shard_map/ppermute | solution.py:105
  236.6 5.8 %collective-permute-start.39 = (bf16[27,8,512]{2,1,0:T(8,128)(2,1)S(1)}, bf16[27,8,512]{2,1,0:T(8,128)(2,1)S(1)}, u32[]{:S(2)}, u32[]{:S(2)}) collective-permute-start(bf16[27,8,512]{2,1,0:T(8,128)(2,1)S(1)} %collective-permute-done.38), channel_id=1, source_target_pairs={{0,1},{1,0},{2,3},{3,2},{4,5},{5,4},{6,7},{7,6},{8,9},{9,8},{10,11... | collective-permute-start | bytes 663560 | tf_op jit(solution)/shard_map/ppermute | solution.py:105
  (25 other events, 119.8 us)

commit v5 on v4

--- a/solution.py
+++ b/solution.py
@@ -43,6 +43,7 @@
 CHUNK = 768
 HALF_BIN = 384
 PAIR = 5
+ADAM_BLOCK = 9
 LANE = 128
 AXES = ("rows", "seq")
 
@@ -201,6 +202,70 @@
 SCALARS = pl.BlockSpec(memory_space=pltpu.SMEM)
 ANYWHERE = pl.BlockSpec(memory_space=pl.ANY)
 shape_of = jax.ShapeDtypeStruct
+
+
+def plan_body(ids, lengths, bw_ids, owner_list, order, offsets, meta, places, held, slot_of, counts, rel, *, frames, ring):
+    rows, utts = lengths.shape
+    owners, slots = order.shape[0], held.shape[1]
+    row_at, seq_at = ids[0], ids[1]
+    for r in range(rows):
+        start = jnp.int32(0)
+        meta[r, 0] = start
+        for u in range(utts):
+            start = start + lengths[r, u]
+            meta[r, u + 1] = start
+            meta[r, utts + 1 + u] = bw_ids[r, u]
+        meta[r, 2 * utts + 1] = seq_at * frames
+        meta[r, 2 * utts + 2] = lax.rem(seq_at, 2)
+        meta[r, 2 * utts + 3] = lax.div(seq_at, 2)
+    where = jnp.int32(0)
+    if ring:
+        for i in range(owners):
+            where = jnp.where(order[i] == row_at, i, where)
+
+    def name(i, carry):
+        rel[order[lax.rem(where + offsets[i] + owners, owners)]] = i
+        counts[0, i] = 0
+        return carry
+
+    def clear(i, carry):
+        places[0, i] = NB
+        return carry
+
+    def place(b, carry):
+        i = rel[owner_list[b]]
+        n = counts[0, i]
+        counts[0, i] = n + 1
+        places[0, i * slots + n] = b
+        slot_of[0, b] = i * slots + n
+        return carry
+
+    lax.fori_loop(0, owners, name, 0)
+    lax.fori_loop(0, owners * slots, clear, 0)
+    lax.fori_loop(0, NB, place, 0)
+    own = rel[row_at]
+
+    def keep(n, carry):
+        held[0, n] = places[0, own * slots + n]
+        return carry
+
+    lax.fori_loop(0, slots, keep, 0)
+
+
+def plan(ids, lengths, bw_ids, owner_list, order, offsets, slots, frames, ring):
+    rows, utts = lengths.shape
+    owners = order.shape[0]
+    shapes = ((rows, 2 * utts + 4), (1, owners * slots), (1, slots), (1, NB), (1, owners))
+    return pl.pallas_call(
+        functools.partial(plan_body, frames=frames, ring=ring),
+        in_specs=[SCALARS] * 6,
+        out_specs=[SCALARS] * 5,
+        out_shape=[shape_of(shape, jnp.int32) for shape in shapes],
+        scratch_shapes=[pltpu.SMEM((owners,), jnp.int32)],
+        compiler_params=params(),
+        cost_estimate=cost(8000, 8 * 1024),
+        name="plan",
+    )(ids, lengths, bw_ids, owner_list, order, offsets)
 
 
 def pre_body(meta, wave_ref, halo_ref, synth_ref, win_ref, *rest, start, tiles, rows, utts):
@@ -298,13 +363,14 @@
         lax.fori_loop(0, counts[0, owner], one, 0)
 
 
-def assemble_body(places, counts, core, *refs, slots, owners):
+def assemble_body(meta, places, counts, *refs, slots, owners):
     pieces, table, sem = refs[: 2 * len(owners)], refs[-2], refs[-1]
-    place_parts(places, counts, core[0], pieces, table, sem, slots, owners, True)
-    place_parts(places, counts, core[0], pieces, table, sem, slots, owners, False)
-
-
-def assemble(owners, places, counts, core, pieces, slots):
+    core = meta[0, meta.shape[1] - 2]
+    place_parts(places, counts, core, pieces, table, sem, slots, owners, True)
+    place_parts(places, counts, core, pieces, table, sem, slots, owners, False)
+
+
+def assemble(owners, meta, places, counts, pieces, slots):
     channels = pieces[0].shape[2]
     return pl.pallas_call(
         functools.partial(assemble_body, slots=slots, owners=owners),
@@ -315,7 +381,7 @@
         compiler_params=params(),
         cost_estimate=cost(0, 12 * MIB),
         name="assemble",
-    )(places, counts, core, *pieces)
+    )(meta, places, counts, *pieces)
 
 
 def take_body(slot_of, ref, out, sem):
@@ -838,7 +904,7 @@
 def norm_body(
     meta, x_ref, low_ref, high_ref, pre_ref, w_in, last_ref, xc_ref, rc_ref, *rest, row, tiles, utts, closing
 ):
-    more = rest[: 7 if closing else 0]
+    more = rest[: 8 if closing else 0]
     outs = rest[len(more) :]
     cg_ref, edge_ref, part_ref = outs[:3]
     xs, vecs, picks, agrad, cg, reaches = outs[-6:]
@@ -910,16 +976,20 @@
         for k in range(KW + 1):
             part_ref[k, :, cut] = sums[k]
 
+    def edge(side, begin):
+        for c in range(lane_tiles):
+            edge_ref[side, :, c * LANE : (c + 1) * LANE] = cg[c, begin : begin + 8, :]
+
     @pl.when(tile == 0)
     def _():
-        edge_ref[0] = cg_ref[0:EDGE, :]
+        edge(0, 0)
 
     @pl.when(tile == tiles - 1)
     def _():
-        edge_ref[1] = cg_ref[TILE - EDGE : TILE, :]
+        edge(1, TILE - 8)
 
     if closing:
-        _, tail_ref, sums_ref, hsum_ref, bsum0, bsum1, order_ref = more
+        _, other_edge, tail_ref, sums_ref, hsum_ref, bsum0, bsum1, order_ref = more
         vec_ref, quarter_refs = outs[-7], outs[3:7]
         core, plane = meta[0, 2 * utts + 2], meta[0, 2 * utts + 3]
 
@@ -961,7 +1031,10 @@
                 (core, 1 - core, core, 1 - core),
                 (plane, plane, 1 - plane, 1 - plane),
             ):
-                ref[...] = vec_ref[pl.ds(pl.multiple_of(c * HALF + p * QUART, QUART), QUART), :]
+                ref[0:8, :] = vec_ref[pl.ds(pl.multiple_of(c * HALF + p * QUART, QUART), QUART), :]
+            for at, ref in ((8, other_edge), (16, edge_ref)):
+                quarter_refs[1][at : at + 8, :] = jnp.where(core == 0, ref[1], ref[0])
+                quarter_refs[3][at : at + 8, :] = jnp.where(core == 0, ref[0], ref[1])
 
 
 def norm_backward(row, closing, meta, x, low, high, pre, table, xc, rc, utts):
@@ -972,12 +1045,12 @@
     out_specs = [pl.BlockSpec((TILE, channels), lambda i: (i, 0)), WHOLE, WHOLE]
     out_shape = [
         shape_of((frames, channels), BF16),
-        shape_of((2, EDGE, channels), BF16),
+        shape_of((2, 8, channels), F32),
         shape_of((sums, 8, channels), F32),
     ]
     if closing:
         out_specs += [WHOLE] * 4
-        out_shape += [shape_of((QUART, channels), F32)] * 4
+        out_shape += [shape_of((8 * n, channels), F32) for n in (1, 3, 1, 3)]
     return pl.pallas_call(
         functools.partial(norm_body, row=row, tiles=tiles, utts=utts, closing=bool(closing)),
         grid=(tiles,),
@@ -1009,10 +1082,11 @@
     )(meta, x, low, high, pre, table, table, xc, rc, *closing)
 
 
-def conv_body(meta, cg_ref, before_ref, after_ref, low_ref, high_ref, resg_ref, last_ref, *rest, row, tiles, utts):
+def conv_body(meta, cg_ref, before_ref, after_ref, near_ref, cross_ref, resg_ref, last_ref, *rest, row, tiles, utts):
     out_ref, cs, vecs = rest[-3:]
     tile = pl.program_id(0)
     channels = cg_ref.shape[1]
+    core = meta[0, 2 * utts + 2]
     base = meta[row, 2 * utts + 1] + tile * TILE
 
     @pl.when(tile == 0)
@@ -1022,9 +1096,11 @@
     for c in range(channels // LANE):
         cut = slice(c * LANE, (c + 1) * LANE)
         cs[c, EDGE : EDGE + TILE, :] = cg_ref[:, cut].astype(F32)
-        cs[c, 0:EDGE, :] = jnp.where(tile == 0, low_ref[row, :, cut], before_ref[:, cut]).astype(F32)
-        after = jnp.where(tile == tiles - 1, high_ref[row, :, cut], after_ref[:, cut])
-        cs[c, EDGE + TILE :, :] = after.astype(F32)
+        near, cross = near_ref[8 + 8 * row : 16 + 8 * row, cut], cross_ref[8 + 8 * row : 16 + 8 * row, cut]
+        before, after = before_ref[:, cut].astype(F32)[EDGE - 8 :], after_ref[:, cut].astype(F32)[:8]
+        cs[c, EDGE - 8 : EDGE, :] = jnp.where(tile == 0, jnp.where(core == 0, cross, near), before)
+        after = jnp.where(tile == tiles - 1, jnp.where(core == 0, near, cross), after)
+        cs[c, EDGE + TILE : EDGE + TILE + 8, :] = after
     for at, size in spans(TILE, 32):
         span = slice(at, at + size)
         reach, left = frame_reach(meta, row, base + at, size, utts)
@@ -1038,7 +1114,7 @@
             out_ref[0, span, cut] = total
 
 
-def conv_backward(row, before, meta, cg, low, high, resg, table, rows, utts):
+def conv_backward(row, before, meta, cg, near, cross, resg, table, rows, utts):
     frames, channels = cg.shape
     tiles = frames // TILE
     per = TILE // EDGE
@@ -1067,7 +1143,7 @@
         compiler_params=params(),
         cost_estimate=cost(16 * frames * 512, 6 * MIB),
         name=f"conv_backward_{row}",
-    )(meta, cg, cg, cg, low, high, resg, table, *more)
+    )(meta, cg, cg, cg, near, cross, resg, table, *more)
 
 
 def wave_body(meta, spec_ref, prev_ref, halo_ref, synth_ref, win_ref, *rest, start, rows, utts):
@@ -1141,42 +1217,50 @@
     )(meta, spec, spec, halo, synth, win, *more)
 
 
-def slot_body(slot_of, *refs, bounds):
-    count = len(bounds)
-    out = refs[-1]
-    lasts = refs[2 * count : -1]
-    for (start, stop), keep, came in zip(bounds, refs[:count], refs[count : 2 * count]):
-
-        def one(b, carry, start=start, keep=keep, came=came):
-            value = keep[b].astype(F32) + came[b].astype(F32)
+def slot_body(slot_of, *refs, groups, lasts, copies, slots):
+    count = max(g[0] for g in groups) + 1
+    keeps, cames, last_refs = refs[:count], refs[count : 2 * count], refs[2 * count : 2 * count + lasts]
+    out, *more = refs[2 * count + lasts :]
+    for index, offset, start, stop in groups:
+
+        def one(b, carry, keep=keeps[index], came=cames[index], offset=offset, start=start):
+            value = keep[offset + b].astype(F32) + came[offset + b].astype(F32)
             out[slot_of[0, start + b]] = value.astype(BF16)
             return carry
 
         lax.fori_loop(0, stop - start, one, 0)
-    out[slot_of[0, NB - 1]] = sum([ref[...] for ref in lasts]).astype(BF16)
-
-
-def to_slots(slot_of, keeps, cames, lasts, bounds, total):
+    total = last_refs[0][0:QUART, :]
+    for ref in last_refs[1:]:
+        total = total + ref[0:QUART, :]
+    out[slot_of[0, NB - 1]] = total.astype(BF16)
+    for ref, at in zip(more, copies):
+        ref[...] = out[at * slots : (at + 1) * slots]
+
+
+def to_slots(slot_of, keeps, cames, lasts, groups, owners, slots, copies):
     channels = keeps[0].shape[2]
     return pl.pallas_call(
-        functools.partial(slot_body, bounds=bounds),
-        in_specs=[SCALARS] + [WHOLE] * (2 * len(bounds) + len(lasts)),
-        out_specs=WHOLE,
-        out_shape=shape_of((total, QUART, channels), BF16),
+        functools.partial(slot_body, groups=groups, lasts=len(lasts), copies=copies, slots=slots),
+        in_specs=[SCALARS] + [WHOLE] * (2 * len(keeps) + len(lasts)),
+        out_specs=[WHOLE] * (1 + len(copies)),
+        out_shape=[shape_of((owners * slots, QUART, channels), BF16)]
+        + [shape_of((slots, QUART, channels), BF16)] * len(copies),
         compiler_params=params(),
         cost_estimate=cost(0, 6 * MIB),
         name="to_slots",
     )(slot_of, *keeps, *cames, *lasts)
 
 
-def adam_body(places, spot, low_ref, high_ref, master, first, second, *rest, block):
+def adam_body(places, meta, mine_ref, other_ref, master, first, second, *rest, block):
     out_master, out_first, out_second = rest[-3:]
     one_fix = 1.0 / (1.0 - BETA_ONE**STEP_COUNT)
     two_fix = 1.0 / (1.0 - BETA_TWO**STEP_COUNT)
+    core = meta[0, meta.shape[1] - 2]
     for s in range(block):
         bucket = places[0, pl.program_id(0) * block + s]
-        for half, ref in enumerate((low_ref, high_ref)):
-            grad = jnp.where(bucket < NB, ref[s].astype(F32), 0.0)
+        mine, other = mine_ref[s].astype(F32), other_ref[s].astype(F32)
+        for half in range(2):
+            grad = jnp.where(bucket < NB, jnp.where(core == half, mine, other), 0.0)
             old = master[s, half, 0]
             one = BETA_ONE * first[s, half, 0] + (1.0 - BETA_ONE) * grad
             two = BETA_TWO * second[s, half, 0] + (1.0 - BETA_TWO) * grad * grad
@@ -1186,12 +1270,17 @@
             out_master[s, half, 0] = old - LEARN_RATE * (step + WEIGHT_DECAY * old)
 
 
-def adam(places, spot, low, high, master, first, second, before):
+def adam(places, meta, mine, other, master, first, second, before):
     slots, depth, channels = master.shape
-    block = max(b for b in range(1, 10) if slots % b == 0)
+    block = max(b for b in range(1, ADAM_BLOCK + 1) if slots % b == 0)
+    plane_at = meta.shape[1] - 1
     cut = lambda v: v.reshape(slots, 2, 2, QUART, channels)
-    full = pl.BlockSpec((block, 2, 1, QUART, channels), lambda i, places, spot: (i, 0, spot[0], 0, 0))
-    part = pl.BlockSpec((block, QUART, channels), lambda i, places, spot: (i, 0, 0))
+    def at_plane(i, places, meta):
+        plane = meta[0, plane_at]
+        return i, 0, 1 - plane if before else plane, 0, 0
+
+    full = pl.BlockSpec((block, 2, 1, QUART, channels), at_plane)
+    part = pl.BlockSpec((block, QUART, channels), lambda i, places, meta: (i, 0, 0))
     more = [cut(v) for v in before]
     outs = pl.pallas_call(
         functools.partial(adam_body, block=block),
@@ -1206,7 +1295,7 @@
         compiler_params=params(),
         cost_estimate=cost(0, 6 * MIB),
         name="adam_second" if more else "adam_first",
-    )(places, spot, low, high, cut(master), cut(first), cut(second), *more)
+    )(places, meta, mine, other, cut(master), cut(first), cut(second), *more)
     return [v.reshape(slots, depth, channels) for v in outs]
 
 
@@ -1232,11 +1321,6 @@
 
     mine = lax.dynamic_slice_in_dim(master, core * HALF, HALF, axis=1).astype(BF16)
 
-    starts = [jnp.zeros((rows, 1), jnp.int32)]
-    for u in range(utts):
-        starts.append(starts[-1] + lengths[:, u : u + 1])
-    spot = jnp.broadcast_to(jnp.stack([seq_at * frames, core, plane])[None, :], (rows, 3)).astype(jnp.int32)
-    meta = jnp.concatenate(starts + [bw_ids, spot], axis=1)
     lines = wave_grad.reshape(rows, frames * HOP // LANE, LANE).transpose(1, 0, 2).reshape(-1, LANE)
     order = jnp.asarray(order_table())
     synth = jnp.asarray(synthesis_table())
@@ -1245,33 +1329,23 @@
     low = shifted(frames_in[:, frames - EDGE :], 1)
     high = shifted(frames_in[:, :EDGE], -1)
     later = shifted(lines[: PAIR * EDGE], -1)
-    bucket_index = jnp.arange(NB, dtype=jnp.int32)
-    same = owner_list[None, :] == owner_list[:, None]
-    rank = jnp.sum((same & (bucket_index[None, :] < bucket_index[:, None])).astype(jnp.int32), axis=1)
-    ids = jnp.arange(owners, dtype=jnp.int32)
-    if ring:
-        offsets = [0]
-        for hop in range(1, half_ring):
-            offsets += [-hop, hop]
-        offsets.append(-half_ring)
-        order_ids = jnp.asarray(ring, jnp.int32)
-        where = jnp.sum(jnp.where(order_ids == row_at, ids, 0))
-        at = (where + jnp.asarray(offsets, jnp.int32)) % owners
-        owner_ids = jnp.sum(jnp.where(at[:, None] == ids[None, :], order_ids[None, :], 0), axis=1)
-    else:
-        owner_ids = ids
-
-    def held_by(wanted):
-        targets = (wanted[:, None] * slots + jnp.arange(slots, dtype=jnp.int32)[None, :]).reshape(-1)
-        match = (owner_list * slots + rank)[None, :] == targets[:, None]
-        return (NB + jnp.sum(match.astype(jnp.int32) * (bucket_index[None, :] - NB), axis=1))[None, :]
-
-    places = held_by(jnp.concatenate([owner_ids, row_at[None].astype(jnp.int32)]))
-    places, held = places[:, : owners * slots], places[:, owners * slots :]
-    rel = jnp.sum(jnp.where(owner_list[:, None] == owner_ids[None, :], ids[None, :], 0), axis=1)
-    slot_of = (rel * slots + rank)[None, :]
-    counts = jnp.sum((owner_list[None, :] == owner_ids[:, None]).astype(jnp.int32), axis=1)[None, :]
-    at_core = core[None].astype(jnp.int32)
+    offsets = [0]
+    for hop in range(1, half_ring):
+        offsets += [-hop, hop]
+    offsets.append(-half_ring)
+    names = np.arange(owners, dtype=np.int32)
+    ids = jnp.stack([row_at, seq_at]).astype(jnp.int32)
+    meta, places, held, slot_of, counts = plan(
+        ids,
+        lengths,
+        bw_ids,
+        owner_list,
+        jnp.asarray(ring if ring else names, jnp.int32),
+        jnp.asarray(offsets if ring else names, jnp.int32),
+        slots,
+        frames,
+        bool(ring),
+    )
 
     cot = None
     tiles = frames // TILE
@@ -1283,14 +1357,16 @@
             ahead = lax.ppermute(ahead, AXES, ring_step(ring, 1, seqs))
             if hop < half_ring - 1:
                 back = lax.ppermute(back, AXES, ring_step(ring, -1, seqs))
+            if hop == 0:
+                ahead, back, low, high, later, meta = tie(ahead, back, low, high, later, meta)
             if hop in (1, 2):
-                feed, low, high = tie(lines, low, high, *source)[:3]
+                feed = tie(lines, *source)[0]
                 begin, end = ((0, tiles // 2), (tiles // 2, tiles))[hop - 1]
                 cot = spectrum_cotangent(begin, end, cot, meta, feed, later, synth, win, rows, utts)
                 ahead, back, cot = tie(ahead, back, cot)
             if hop == half_ring - 1:
                 fed = tie(places, *source)[0]
-                partial_table = assemble(tuple(range(owners - 1)), fed, counts, at_core, arrived, slots)
+                partial_table = assemble(tuple(range(owners - 1)), meta, fed, counts, arrived, slots)
                 ahead, partial_table = tie(ahead, partial_table)
             else:
                 arrived += [ahead, seq_swap(ahead, 1), back, seq_swap(back, 1)]
@@ -1312,7 +1388,7 @@
     )
     halo = shifted(spec[:, frames - EDGE :], 1)
 
-    keeps, cames, bounds = [], [], []
+    keeps, cames, groups = [], [], []
 
     def split(keep, came):
         both = plus(keep, came)
@@ -1322,9 +1398,9 @@
 
     def record(stay, came, begins, per):
         for at, begin in enumerate(begins):
-            keeps.append(stay[at * per : (at + 1) * per])
-            cames.append(came[at * per : (at + 1) * per])
-            bounds.append((begin, begin + per))
+            groups.append((len(keeps), at * per, begin, begin + per))
+        keeps.append(stay)
+        cames.append(came)
 
     per = CHUNK // BR
     pre, bsums = None, []
@@ -1350,37 +1426,35 @@
     record(kept, came, *where_from)
     stay, leave = split(keep, near)
     came = seq_swap(leave, 2)
-    closing = (parts, tail, sums, hsum, *bsums, order)
-    cg1, edge1, _, own, to_near, to_far, to_cross = norm_backward(
+    closing = (parts, edge0, tail, sums, hsum, *bsums, order)
+    cg1, _, _, own, to_near, to_far, to_cross = norm_backward(
         1, closing, meta, frames_in, low, high, pre, table, xc, rc, utts
     )
     lasts = (own, seq_swap(to_near, 1), seq_swap(to_far, 2), seq_swap(to_cross, 3))
-    edges = jnp.stack([edge0, edge1])
-    edge_low, edge_high = shifted(edges[:, 1], 1), shifted(edges[:, 0], -1)
-    came, spec, edge_low, edge_high, *lasts = tie(came, spec, edge_low, edge_high, *lasts)
+    came, spec, *lasts = tie(came, spec, *lasts)
     record(stay, came, begins, count)
-    chunks = to_slots(slot_of, keeps, cames, lasts, tuple(bounds), owners * slots)
+    first_sent = (owners - 1, owners - 3) if ring else ()
+    chunks, *sent = to_slots(slot_of, keeps, cames, lasts, tuple(groups), owners, slots, first_sent)
 
     state = {}
 
     def work(stage, *ready):
-        if stage in (0, 3):
+        if stage in (0, 2):
             feed = tie(spec, *ready)[0]
-            begin, end, before = ((0, tiles // 2, None), (tiles // 2, tiles, state.get("wave")))[stage // 3]
+            begin, end, before = ((0, tiles // 2, None), (tiles // 2, tiles, state.get("wave")))[stage // 2]
             state["wave"] = wave_forward(begin, end, before, meta, feed, halo, synth, win, utts)
             return "wave"
-        if stage in (1, 4):
-            row = stage // 4
+        if stage in (1, 3):
+            row = stage // 2
             feed = tie((cg0, cg1)[row], *ready)[0]
             state["grad"] = conv_backward(
-                row, state.get("grad"), meta, feed, edge_low, edge_high, resg, table, rows, utts
+                row, state.get("grad"), meta, feed, lasts[1], lasts[3], resg, table, rows, utts
             )
             return "grad"
-        return None
 
     if ring:
         cut = {o: chunks[i * slots : (i + 1) * slots] for i, o in enumerate(offsets)}
-        up, down = cut[-half_ring], cut[1 - half_ring]
+        up, down = sent
         for hop in range(half_ring):
             left_over = half_ring - 1 - hop
             source = (up, down)
@@ -1388,8 +1462,7 @@
             if hop < half_ring - 1:
                 down = lax.ppermute(down, AXES, ring_step(ring, -1, seqs))
             done = work(hop, *source)
-            if done:
-                up, down, state[done] = tie(up, down, state[done])
+            up, down, state[done] = tie(up, down, state[done])
             if left_over:
                 up = plus(up, cut[left_over])
                 if hop < half_ring - 2:
@@ -1397,21 +1470,15 @@
         own = plus(cut[0], up, down)
     else:
         own = lax.psum_scatter(chunks, "rows", scatter_dimension=0, tiled=True)
-        for hop in (0, 1, 3):
+        for hop in range(4):
             work(hop, own)
     near, far = seq_swap(own, 1), seq_swap(own, 2)
-    work(4, own)
-    near, far, state["grad"] = tie(near, far, state["grad"])
     cross = seq_swap(far, 1)
     waveform = state["wave"].reshape(-1, rows, LANE).transpose(1, 0, 2).reshape(rows, frames * HOP)
 
-    def ordered(mine, other):
-        return jnp.where(core == 0, mine, other), jnp.where(core == 0, other, mine)
-
-    here, there = plane[None].astype(jnp.int32), (1 - plane)[None].astype(jnp.int32)
-    first = adam(held, here, *ordered(own, near), master, moment1, moment2, ())
+    first = adam(held, meta, own, near, master, moment1, moment2, ())
     cross, *first = tie(cross, *first)
-    new_master, new_first, new_second = adam(held, there, *ordered(far, cross), master, moment1, moment2, first)
+    new_master, new_first, new_second = adam(held, meta, far, cross, master, moment1, moment2, first)
     return waveform, state["grad"], new_master, new_first, new_second
 
 

time: 250 us -> 236 us (0.944)
  other arithmetic: 13.6 us -> 1.78 us
  Pallas kernels: 157 us -> 162 us
  local copies, waits for them, and re-layouts: 15.3 us -> 11.3 us
  waiting for transfers between devices: 23.4 us -> 19.7 us
    ppermute x4, waiting for transfers between devices: 7.65 us -> 0.01 us  [local(): up = lax.ppermute(up, AXES, ring_step(ring, 1, seqs))]
    ppermute x20, waiting for transfers between devices: 6.01 us -> 12.4 us  [seq_swap(): return lax.ppermute(value, 'seq', [(s, s ^ bit) for s in range(count)])]
    reduce_sum x6 -> x0, other arithmetic: 5.84 us -> none  [the longest x1 1.37 us: local(): jnp.sum(jnp.where(at[:, None] == ids[None, :], order_ids[None, :], 0), ax...]
    pallas_call x1 -> x2, Pallas kernels: 3.8 us -> 9.13 us  [the longest x1 5.27 us: plan(): pl.pallas_call(functools.partial(plan_body, frames=frames, ring=ring), in...]
    ppermute x3, waiting for transfers between devices: 5.93 us -> 0.88 us  [local(): down = lax.ppermute(down, AXES, ring_step(ring, -1, seqs))]
    slice x6 -> x0, local copies, waits for them, and re-layouts: 4.9 us -> none  [the longest x2 1.65 us: record(): keeps.append(stay[at * per:(at + 1) * per])]
    ppermute x6 -> x4, starting transfers between devices: 9.57 us -> 5.51 us  [shifted(): lax.ppermute(value, 'seq', [(i - distance, i) for i in devices if i - dis...]
    ppermute x20, starting transfers between devices: 12.4 us -> 16.3 us  [seq_swap(): return lax.ppermute(value, 'seq', [(s, s ^ bit) for s in range(count)])]
  transfers between devices with their start and end apart: 40 -> 38, of which waited for: 11 -> 12; matrix products, arithmetic and copies ran while one was open for 9% -> 2% of each run, Pallas kernels for 38% -> 43%
where the time goes in v5:
time: 236 us; the launch traced here: 235 us
  Pallas kernels  162 us (69%)
  starting transfers between devices  38.3 us (16%)
  waiting for transfers between devices  19.7 us (8%)
  local copies, waits for them, and re-layouts  11.3 us (5%)
    pallas_call x1, Pallas kernels, forward(): pl.pallas_call(functools.partial(forward_body, owners=owners, slots=slots...  56.1 us
    pallas_call x2, Pallas kernels, mlp_backward(): pl.pallas_call(functools.partial(mlp_body, utts=utts), grid=(count // til...  21.1 us
    pallas_call x2, Pallas kernels, norm_backward(): pl.pallas_call(functools.partial(norm_body, row=row, tiles=tiles, utts=ut...  20.8 us
    ppermute x20, starting transfers between devices, seq_swap(): return lax.ppermute(value, 'seq', [(s, s ^ bit) for s in range(count)])  16.3 us
    pallas_call x2, Pallas kernels, spectrum_cotangent(): pl.pallas_call(functools.partial(pre_body, start=start, tiles=tiles, rows...  15.1 us
    pallas_call x2, Pallas kernels, wave_forward(): pl.pallas_call(functools.partial(wave_body, start=start, rows=rows, utts=...  14.1 us
    ppermute x20, waiting for transfers between devices, seq_swap(): return lax.ppermute(value, 'seq', [(s, s ^ bit) for s in range(count)])  12.4 us
    pallas_call x2, Pallas kernels, adam(): pl.pallas_call(functools.partial(adam_body, block=block), grid_spec=pltpu...  10.1 us
  transfers between devices with their start and end apart: 38, of which 12 were waited for; matrix products, arithmetic and copies ran while one was open for 2% of the time, Pallas kernels for 43%

profile of v5, /device:TPU:0, one launch (start us, length us, event | category | flops | bytes accessed | tf_op | source)
XLA Modules:
  0.0 234.5 jit_solution(13223057862964134609)
XLA Ops:
  0.6 1.2 dynamic-slice_convert_fusion.refs_0_
  1.9 3.1 %collective-permute-start = (bf16[27,16,512]{2,1,0:T(8,128)(2,1)S(1)}, bf16[27,16,512]{2,1,0:T(8,128)(2,1)S(1)}, u32[]{:S(2)}, u32[]{:S(2)}) collective-permute-start(bf16[27,16,512]{2,1,0:T(8,128)(2,1)S(1)} %dynamic-slice_convert_fusion.refs_0_), channel_id=1, source_target_pairs={{0,8},{1,9},{2,10},{3,11},{8,16},{9,17},{10,18},{11,19},{16,24},{1... | collective-permute-start | bytes 1327112 | tf_op jit(solution)/shard_map/ppermute | solution.py:1357
  5.0 0.8 fusion
  5.8 1.4 collective-permute-start.2
  7.2 1.3 collective-permute-start.3
  9.3 1.3 collective-permute-start.4
  11.2 5.3 %plan.1 = (s32[2,12]{1,0:T(2,128)}, s32[1,216]{1,0:T(1,128)}, s32[1,27]{1,0:T(1,128)}, s32[1,137]{1,0:T(1,128)}, s32[1,8]{1,0:T(1,128)}) custom-call(s32[2]{0:T(128)} %pad_add_fusion.ids, s32[2,4]{1,0:T(2,128)} %lengths.1, s32[2,4]{1,0:T(2,128)} %bw_ids.1, s32[137]{0:T(256)} %owner_list.1, s32[8]{0:T(128)} %constant.54.clone.order, s32[8]{0:T(128)} %constant.55.clone.offsets), custom_call_target="tpu_custom_call" | custom-call | flops 8000 | bytes 8192 | tf_op jit(solution)/shard_map/plan/pallas_call | solution.py:259
  17.1 1.9 collective-permute-start.5
  19.1 7.5 %spectrum_cotangent_0.1.rest_0_ = bf16[2,1024,1536]{2,1,0:T(8,128)(2,1)} custom-call(s32[2,12]{1,0:T(2,128)} %get-tuple-element.110.meta, bf16[5120,128]{1,0:T(8,128)(2,1)} %bitcast.33, bf16[80,128]{1,0:T(8,128)(2,1)} %copy-done.29, bf16[2,768,768]{2,1,0:T(8,128)(2,1)} %constant.52.clone.synth_ref, f32[8,384]{1,0:T(8,128)} %constant.53.clone.win_ref), custom_call_target="tpu_custom_call" | custom-call | flops 2415919104 | bytes 7340032 | tf_op jit(solution)/shard_map/spectrum_cotangent_0/pallas_call | solution.py:329
  27.3 2.4 %collective-permute-done.6.refs_8_ = bf16[27,16,512]{2,1,0:T(8,128)(2,1)S(1)} collective-permute-done((bf16[27,16,512]{2,1,0:T(8,128)(2,1)S(1)}, bf16[27,16,512]{2,1,0:T(8,128)(2,1)S(1)}, u32[]{:S(2)}, u32[]{:S(2)}) %collective-permute-start.6) | collective-permute-done | bytes 442400 | tf_op jit(solution)/shard_map/ppermute | solution.py:1359
  29.7 1.6 collective-permute-start.7
  31.7 1.6 collective-permute-start.10
  33.8 7.6 %spectrum_cotangent_2.1.cot_ref = bf16[2,1024,1536]{2,1,0:T(8,128)(2,1)} custom-call(s32[2,12]{1,0:T(2,128)} %get-tuple-element.110.meta, bf16[5120,128]{1,0:T(8,128)(2,1)} %bitcast.34, bf16[80,128]{1,0:T(8,128)(2,1)} %copy-done.29, bf16[2,768,768]{2,1,0:T(8,128)(2,1)} %constant.52.clone.synth_ref, ...), custom_call_target="tpu_custom_call", output_to_operand_aliasing={{}: (5, {})} | custom-call | flops 2415919104 | bytes 7340032 | tf_op jit(solution)/shard_map/spectrum_cotangent_2/pallas_call | solution.py:329
  41.5 1.3 collective-permute-start.13
  44.7 1.6 collective-permute-start.9
  47.9 6.3 %assemble.1.rest_2_ = bf16[4384,512]{1,0:T(8,128)(2,1)} custom-call(s32[2,12]{1,0:T(2,128)} %get-tuple-element.110.meta, s32[1,216]{1,0:T(1,128)} %get-tuple-element.126.places, s32[1,8]{1,0:T(1,128)} %get-tuple-element.112.counts, bf16[27,16,512]{2,1,0:T(8,128)(2,1)} %copy-done, bf16[27,16,512]{2,1,0:T(8,128)(2,1)} %copy-done.14, ...), custom_call_target="tpu_custom_call" | custom-call | bytes 12582912 | tf_op jit(solution)/shard_map/assemble/pallas_call | solution.py:375
  54.2 2.6 %collective-permute-done.9.rest_0_ = bf16[27,16,512]{2,1,0:T(8,128)(2,1)S(1)} collective-permute-done((bf16[27,16,512]{2,1,0:T(8,128)(2,1)S(1)}, bf16[27,16,512]{2,1,0:T(8,128)(2,1)S(1)}, u32[]{:S(2)}, u32[]{:S(2)}) %collective-permute-start.9) | collective-permute-done | bytes 442400 | tf_op jit(solution)/shard_map/ppermute | solution.py:1357
  56.8 1.8 collective-permute-done.17.rest_1_
  58.6 0.8 copy-done.32
  59.4 56.1 %forward.1 = (bf16[4384,512]{1,0:T(8,128)(2,1)}, bf16[2,1024,1536]{2,1,0:T(8,128)(2,1)}, bf16[2048,1536]{1,0:T(8,128)(2,1)}, bf16[2048,1536]{1,0:T(8,128)(2,1)},...) custom-call(s32[2,12]{1,0:T(2,128)} %get-tuple-element.110.meta, ...), custom_call_target="tpu_custom_call" | custom-call | flops 16106127360 | bytes 41943040 | tf_op jit(solution)/shard_map/forward/pallas_call | solution.py:762
  115.7 10.5 %mlp_backward_0.1 = (bf16[2048,1536]{1,0:T(8,128)(2,1)}, bf16[48,16,512]{2,1,0:T(8,128)(2,1)}, bf16[48,16,512]{2,1,0:T(8,128)(2,1)}, f32[8,768]{1,0:T(8,128)}) custom-call(s32[2,12]{1,0:T(2,128)} %get-tuple-element.110.meta, bf16[2048,512]{1,0:T(8,128)(2,1)} %get-tuple-element.131.low_ref, bf16[2048,1536]{1,0:T(8,128)(2,1)} %get-tuple-element.132.act_ref, ...), custom_call_target="tpu_custom_call" | custom-call | flops 4831838208 | bytes 16777216 | tf_op jit(solution)/shard_map/mlp_backward_0/pallas_call | solution.py:873
  127.0 0.8 constant_dynamic-slice_fusion.3
  127.7 5.5 %collective-permute-start.21 = (bf16[40,8,512]{2,1,0:T(8,128)(2,1)S(1)}, bf16[40,8,512]{2,1,0:T(8,128)(2,1)S(1)}, u32[]{:S(2)}, u32[]{:S(2)}) collective-permute-start(bf16[40,8,512]{2,1,0:T(8,128)(2,1)S(1)} %get-tuple-element.221), channel_id=1, source_target_pairs={{0,2},{1,3},{2,0},{3,1},{4,6},{5,7},{6,4},{7,5},{8,10},{9,11},{10,... | collective-permute-start | bytes 983048 | tf_op jit(solution)/shard_map/ppermute | solution.py:106
  133.2 10.6 %mlp_backward_1.1 = (bf16[2048,1536]{1,0:T(8,128)(2,1)}, bf16[48,16,512]{2,1,0:T(8,128)(2,1)}, bf16[48,16,512]{2,1,0:T(8,128)(2,1)}, f32[8,768]{1,0:T(8,128)}) custom-call(s32[2,12]{1,0:T(2,128)} %get-tuple-element.110.meta, bf16[2048,512]{1,0:T(8,128)(2,1)} %get-tuple-element.131.low_ref, ...), custom_call_target="tpu_custom_call", output_to_operand_aliasing={{0}: (6, {})} | custom-call | flops 4831838208 | bytes 16777216 | tf_op jit(solution)/shard_map/mlp_backward_1/pallas_call | solution.py:873
  144.2 0.8 constant_dynamic-slice_fusion.2
  145.2 9.3 %norm_backward_0.1 = (bf16[1024,512]{1,0:T(8,128)(2,1)}, f32[2,8,512]{2,1,0:T(8,128)}, f32[16,8,512]{2,1,0:T(8,128)}) custom-call(s32[2,12]{1,0:T(2,128)} %get-tuple-element.110.meta, bf16[2,1024,512]{2,1,0:T(8,128)(2,1)} %x_ref.5, bf16[2,16,512]{2,1,0:T(8,128)(2,1)} %copy-done.27, bf16[2,16,512]{2,1,0:T(8,128)(2,1)} %copy-done.28, ...), custom_call_target="tpu_custom_call" | custom-call | flops 1610612736 | bytes 12582912 | tf_op jit(solution)/shard_map/norm_backward_0/pallas_call | solution.py:1054
  154.4 2.1 collective-permute-done.22.refs_4_
  156.8 0.8 constant_dynamic-slice_fusion
  157.9 0.9 slice.37
  158.8 1.5 collective-permute-start.29
  160.3 11.6 %norm_backward_1.1 = (bf16[1024,512]{1,0:T(8,128)(2,1)}, f32[2,8,512]{2,1,0:T(8,128)}, f32[16,8,512]{2,1,0:T(8,128)}, f32[8,512]{1,0:T(8,128)}, f32[24,512]{1,0:...) custom-call(s32[2,12]{1,0:T(2,128)} %get-tuple-element.110.meta, bf16[2,1024,512]{2,1,0:T(8,128)(2,1)} %x_ref.5, ...), custom_call_target="tpu_custom_call" | custom-call | flops 1610612736 | bytes 12582912 | tf_op jit(solution)/shard_map/norm_backward_1/pallas_call | solution.py:1054
  171.9 2.4 %collective-permute-start.24 = (f32[24,512]{1,0:T(8,128)}, f32[24,512]{1,0:T(8,128)S(1)}, u32[]{:S(2)}, u32[]{:S(2)}) collective-permute-start(f32[24,512]{1,0:T(8,128)} %get-tuple-element.169), channel_id=1, source_target_pairs={{0,1},{1,0},{2,3},{3,2},{4,5},{5,4},{6,7},{7,6},{8,9},{9,8},{10,11... | collective-permute-start | bytes 147464 | tf_op jit(solution)/shard_map/ppermute | solution.py:106
  174.2 1.7 collective-permute-start.25
  175.9 2.9 %collective-permute-done.25.refs_8_ = f32[8,512]{1,0:T(8,128)S(1)} collective-permute-done((f32[8,512]{1,0:T(8,128)}, f32[8,512]{1,0:T(8,128)S(1)}, u32[]{:S(2)}, u32[]{:S(2)}) %collective-permute-start.25) | collective-permute-done | bytes 16416 | tf_op jit(solution)/shard_map/ppermute | solution.py:106
  179.6 3.9 %to_slots.1 = (bf16[216,8,512]{2,1,0:T(8,128)(2,1)}, bf16[27,8,512]{2,1,0:T(8,128)(2,1)}, bf16[27,8,512]{2,1,0:T(8,128)(2,1)}) custom-call(s32[1,137]{1,0:T(1,128)} %get-tuple-element.108.slot_of, bf16[40,8,512]{2,1,0:T(8,128)(2,1)} %get-tuple-element.222.refs_0_, bf16[48,8,512]{2,1,0:T(8,128)(2,1)} %get-tuple-element.220.refs_1_, ...), custom_call_target="tpu_custom_call" | custom-call | bytes 6291456 | tf_op jit(solution)/shard_map/to_slots/pallas_call | solution.py:1242
  183.5 1.6 collective-permute-start.27
  186.1 7.1 %wave_forward_0.1.rest_0_ = f32[5120,128]{1,0:T(8,128)} custom-call(s32[2,12]{1,0:T(2,128)} %get-tuple-element.110.meta, bf16[2,1024,1536]{2,1,0:T(8,128)(2,1)} %get-tuple-element.189.spec_ref.prev_ref, bf16[2,1024,1536]{2,1,0:T(8,128)(2,1)} %get-tuple-element.189.spec_ref.prev_ref, bf16[2,16,1536]{2,1,0:T(8,128)(2,1)} %copy-done.20, ...), custom_call_target="tpu_custom_call" | custom-call | flops 2415919104 | bytes 10485760 | tf_op jit(solution)/shard_map/wave_forward_0/pallas_call | solution.py:1194
  193.4 1.6 collective-permute-start.30
  195.4 4.8 %conv_backward_0.1.rest_0_ = f32[2,1024,512]{2,1,0:T(8,128)} custom-call(s32[2,12]{1,0:T(2,128)} %get-tuple-element.110.meta, bf16[1024,512]{1,0:T(8,128)(2,1)} %get-tuple-element.185.cg_ref.before_ref.after_ref, bf16[1024,512]{1,0:T(8,128)(2,1)} %get-tuple-element.185.cg_ref.before_ref.after_ref, ...), custom_call_target="tpu_custom_call" | custom-call | flops 8388608 | bytes 6291456 | tf_op jit(solution)/shard_map/conv_backward_0/pallas_call | solution.py:1122
  200.2 0.9 collective-permute-done.31
  201.2 1.6 collective-permute-start.32
  203.3 7.0 %wave_forward_2.1 = f32[5120,128]{1,0:T(8,128)} custom-call(s32[2,12]{1,0:T(2,128)} %get-tuple-element.110.meta, bf16[2,1024,1536]{2,1,0:T(8,128)(2,1)} %get-tuple-element.189.spec_ref.prev_ref, bf16[2,1024,1536]{2,1,0:T(8,128)(2,1)} %get-tuple-element.189.spec_ref.prev_ref, bf16[2,16,1536]{2,1,0:T(8,128)(2,1)} %copy-done.20, ...), custom_call_target="tpu_custom_call", output_to_operand_aliasing={{}: (6, {})} | custom-call | flops 2415919104 | bytes 10485760 | tf_op jit(solution)/shard_map/wave_forward_2/pallas_call | solution.py:1194
  210.4 1.6 collective-permute-start.34
  212.1 4.8 %conv_backward_1.1 = f32[2,1024,512]{2,1,0:T(8,128)} custom-call(s32[2,12]{1,0:T(2,128)} %get-tuple-element.110.meta, bf16[1024,512]{1,0:T(8,128)(2,1)} %get-tuple-element.195.cg_ref.before_ref.after_ref, bf16[1024,512]{1,0:T(8,128)(2,1)} %get-tuple-element.195.cg_ref.before_ref.after_ref, ...), custom_call_target="tpu_custom_call", output_to_operand_aliasing={{}: (8, {})} | custom-call | flops 8388608 | bytes 6291456 | tf_op jit(solution)/shard_map/conv_backward_1/pallas_call | solution.py:1122
  217.0 0.9 collective-permute-start.35
  217.9 5.1 %collective-permute-done.35.mine_ref = bf16[27,8,512]{2,1,0:T(8,128)(2,1)S(1)} collective-permute-done((bf16[27,8,512]{2,1,0:T(8,128)(2,1)S(1)}, bf16[27,8,512]{2,1,0:T(8,128)(2,1)S(1)}, u32[]{:S(2)}, u32[]{:S(2)}) %collective-permute-start.35) | collective-permute-done | bytes 221216 | tf_op jit(solution)/shard_map/ppermute | solution.py:106
  223.7 5.0 %adam_first.1 = (f32[27,2,2,8,512]{4,3,2,1,0:T(8,128)}, f32[27,2,2,8,512]{4,3,2,1,0:T(8,128)}, f32[27,2,2,8,512]{4,3,2,1,0:T(8,128)}) custom-call(s32[1,27]{1,0:T(1,128)} %get-tuple-element.198.places, s32[2,12]{1,0:T(2,128)} %get-tuple-element.110.meta, bf16[27,8,512]{2,1,0:T(8,128)(2,1)} %copy-done.2, bf16[27,8,512]{2,1,0:T(8,128)(2,1)} %copy-done.26, ...), custom_call_target="tpu_custom_call" | custom-call | bytes 6291456 | tf_op jit(solution)/shard_map/adam_first/pallas_call | solution.py:1285
  229.4 5.1 %adam_second.1 = (f32[27,2,2,8,512]{4,3,2,1,0:T(8,128)}, f32[27,2,2,8,512]{4,3,2,1,0:T(8,128)}, f32[27,2,2,8,512]{4,3,2,1,0:T(8,128)}) custom-call(s32[1,27]{1,0:T(1,128)} %get-tuple-element.198.places, s32[2,12]{1,0:T(2,128)} %get-tuple-element.110.meta, bf16[27,8,512]{2,1,0:T(8,128)(2,1)} %copy-done.24, ...), custom_call_target="tpu_custom_call", output_to_operand_aliasing={{0}: (7, {}), {1}: (8, {}), {2}: (9, {})} | custom-call | bytes 6291456 | tf_op jit(solution)/shard_map/adam_second/pallas_call | solution.py:1285
  (125 shorter events, 13.8 us)
Async XLA Ops:
  1.9 29.8 %copy-start = (bf16[27,16,512]{2,1,0:T(8,128)(2,1)}, bf16[27,16,512]{2,1,0:T(8,128)(2,1)S(1)}, u32[]{:S(2)}) copy-start(bf16[27,16,512]{2,1,0:T(8,128)(2,1)S(1)} %dynamic-slice_convert_fusion.refs_0_) | copy-start | bytes 1327108
  1.9 14.6 %collective-permute-start = (bf16[27,16,512]{2,1,0:T(8,128)(2,1)S(1)}, bf16[27,16,512]{2,1,0:T(8,128)(2,1)S(1)}, u32[]{:S(2)}, u32[]{:S(2)}) collective-permute-start(bf16[27,16,512]{2,1,0:T(8,128)(2,1)S(1)} %dynamic-slice_convert_fusion.refs_0_), channel_id=1, source_target_pairs={{0,8},{1,9},{2,10},{3,11},{8,16},{9,17},{10,18},{11,19},{16,24},{1... | collective-permute-start | bytes 1327112 | tf_op jit(solution)/shard_map/ppermute | solution.py:1357
  5.0 11.6 %collective-permute-start.1 = (bf16[27,16,512]{2,1,0:T(8,128)(2,1)S(1)}, bf16[27,16,512]{2,1,0:T(8,128)(2,1)S(1)}, u32[]{:S(2)}, u32[]{:S(2)}) collective-permute-start(bf16[27,16,512]{2,1,0:T(8,128)(2,1)S(1)} %dynamic-slice_convert_fusion.refs_0_), channel_id=1, source_target_pairs={{0,4},{1,5},{2,6},{3,7},{8,0},{9,1},{10,2},{11,3},{16,8},{17,9},{1... | collective-permute-start | bytes 1327112 | tf_op jit(solution)/shard_map/ppermute | solution.py:1359
  5.8 10.7 %collective-permute-start.2 = (bf16[2,16,512]{2,1,0:T(8,128)(2,1)S(1)}, bf16[2,16,512]{2,1,0:T(8,128)(2,1)S(1)}, u32[]{:S(2)}, u32[]{:S(2)}) collective-permute-start(bf16[2,16,512]{2,1,0:T(8,128)(2,1)S(1)} %get-tuple-element.212), channel_id=1, source_target_pairs={{0,1},{1,2},{2,3},{4,5},{5,6},{6,7},{8,9},{9,10},{10,11},{12,13},{... | collective-permute-start | bytes 98312 | tf_op jit(solution)/shard_map/ppermute | solution.py:116
  7.2 9.3 %collective-permute-start.3 = (bf16[2,16,512]{2,1,0:T(8,128)(2,1)S(1)}, bf16[2,16,512]{2,1,0:T(8,128)(2,1)S(1)}, u32[]{:S(2)}, u32[]{:S(2)}) collective-permute-start(bf16[2,16,512]{2,1,0:T(8,128)(2,1)S(1)} %get-tuple-element.211), channel_id=1, source_target_pairs={{1,0},{2,1},{3,2},{5,4},{6,5},{7,6},{9,8},{10,9},{11,10},{13,12},{... | collective-permute-start | bytes 98312 | tf_op jit(solution)/shard_map/ppermute | solution.py:116
  9.3 7.2 %collective-permute-start.4 = (bf16[80,128]{1,0:T(8,128)(2,1)S(1)}, bf16[80,128]{1,0:T(8,128)(2,1)S(1)}, u32[]{:S(2)}, u32[]{:S(2)}) collective-permute-start(bf16[80,128]{1,0:T(8,128)(2,1)S(1)} %bitcast.38), channel_id=1, source_target_pairs={{1,0},{2,1},{3,2},{5,4},{6,5},{7,6},{9,8},{10,9},{11,10},{13,12},{... | collective-permute-start | bytes 61448 | tf_op jit(solution)/shard_map/ppermute | solution.py:116
  16.5 16.8 %copy-start.8 = (bf16[27,16,512]{2,1,0:T(8,128)(2,1)}, bf16[27,16,512]{2,1,0:T(8,128)(2,1)S(1)}, u32[]{:S(2)}) copy-start(bf16[27,16,512]{2,1,0:T(8,128)(2,1)S(1)} %collective-permute-done.refs_2_) | copy-start | bytes 1327108
  16.6 16.8 %copy-start.9 = (bf16[27,16,512]{2,1,0:T(8,128)(2,1)}, bf16[27,16,512]{2,1,0:T(8,128)(2,1)S(1)}, u32[]{:S(2)}) copy-start(bf16[27,16,512]{2,1,0:T(8,128)(2,1)S(1)} %collective-permute-done.1.refs_4_) | copy-start | bytes 1327108
  17.1 10.2 %collective-permute-start.5 = (bf16[27,16,512]{2,1,0:T(8,128)(2,1)S(1)}, bf16[27,16,512]{2,1,0:T(8,128)(2,1)S(1)}, u32[]{:S(2)}, u32[]{:S(2)}) collective-permute-start(bf16[27,16,512]{2,1,0:T(8,128)(2,1)S(1)} %collective-permute-done.refs_2_), channel_id=1, source_target_pairs={{0,8},{1,9},{2,10},{3,11},{8,16},{9,17},{10,18},{11,19},{16,24},{1... | collective-permute-start | bytes 1327112 | tf_op jit(solution)/shard_map/ppermute | solution.py:1357
  19.0 10.7 %collective-permute-start.6 = (bf16[27,16,512]{2,1,0:T(8,128)(2,1)S(1)}, bf16[27,16,512]{2,1,0:T(8,128)(2,1)S(1)}, u32[]{:S(2)}, u32[]{:S(2)}) collective-permute-start(bf16[27,16,512]{2,1,0:T(8,128)(2,1)S(1)} %collective-permute-done.1.refs_4_), channel_id=1, source_target_pairs={{0,4},{1,5},{2,6},{3,7},{8,0},{9,1},{10,2},{11,3},{16,8},{17,9},{1... | collective-permute-start | bytes 1327112 | tf_op jit(solution)/shard_map/ppermute | solution.py:1359
  27.3 14.3 %copy-start.10 = (bf16[27,16,512]{2,1,0:T(8,128)(2,1)}, bf16[27,16,512]{2,1,0:T(8,128)(2,1)S(1)}, u32[]{:S(2)}) copy-start(bf16[27,16,512]{2,1,0:T(8,128)(2,1)S(1)} %collective-permute-done.5.refs_6_) | copy-start | bytes 1327108
  29.7 13.7 %copy-start.11 = (bf16[27,16,512]{2,1,0:T(8,128)(2,1)}, bf16[27,16,512]{2,1,0:T(8,128)(2,1)S(1)}, u32[]{:S(2)}) copy-start(bf16[27,16,512]{2,1,0:T(8,128)(2,1)S(1)} %collective-permute-done.6.refs_8_) | copy-start | bytes 1327108
  29.7 11.8 %collective-permute-start.7 = (bf16[27,16,512]{2,1,0:T(8,128)(2,1)S(1)}, bf16[27,16,512]{2,1,0:T(8,128)(2,1)S(1)}, u32[]{:S(2)}, u32[]{:S(2)}) collective-permute-start(bf16[27,16,512]{2,1,0:T(8,128)(2,1)S(1)} %collective-permute-done.5.refs_6_), channel_id=1, source_target_pairs={{0,8},{1,9},{2,10},{3,11},{8,16},{9,17},{10,18},{11,19},{16,24},{1... | collective-permute-start | bytes 1327112 | tf_op jit(solution)/shard_map/ppermute | solution.py:1357
  31.3 12.2 %collective-permute-start.8 = (bf16[27,16,512]{2,1,0:T(8,128)(2,1)S(1)}, bf16[27,16,512]{2,1,0:T(8,128)(2,1)S(1)}, u32[]{:S(2)}, u32[]{:S(2)}) collective-permute-start(bf16[27,16,512]{2,1,0:T(8,128)(2,1)S(1)} %collective-permute-done.6.refs_8_), channel_id=1, source_target_pairs={{0,4},{1,5},{2,6},{3,7},{8,0},{9,1},{10,2},{11,3},{16,8},{17,9},{1... | collective-permute-start | bytes 1327112 | tf_op jit(solution)/shard_map/ppermute | solution.py:1359
  31.7 12.4 %collective-permute-start.10 = (bf16[27,16,512]{2,1,0:T(8,128)(2,1)S(1)}, bf16[27,16,512]{2,1,0:T(8,128)(2,1)S(1)}, u32[]{:S(2)}, u32[]{:S(2)}) collective-permute-start(bf16[27,16,512]{2,1,0:T(8,128)(2,1)S(1)} %dynamic-slice_convert_fusion.refs_0_), channel_id=1, source_target_pairs={{0,1},{1,0},{2,3},{3,2},{4,5},{5,4},{6,7},{7,6},{8,9},{9,8},{10,11... | collective-permute-start | bytes 1327112 | tf_op jit(solution)/shard_map/ppermute | solution.py:106
  33.3 10.9 %collective-permute-start.11 = (bf16[27,16,512]{2,1,0:T(8,128)(2,1)S(1)}, bf16[27,16,512]{2,1,0:T(8,128)(2,1)S(1)}, u32[]{:S(2)}, u32[]{:S(2)}) collective-permute-start(bf16[27,16,512]{2,1,0:T(8,128)(2,1)S(1)} %collective-permute-done.refs_2_), channel_id=1, source_target_pairs={{0,1},{1,0},{2,3},{3,2},{4,5},{5,4},{6,7},{7,6},{8,9},{9,8},{10,11... | collective-permute-start | bytes 1327112 | tf_op jit(solution)/shard_map/ppermute | solution.py:106
  33.4 11.3 %collective-permute-start.12 = (bf16[27,16,512]{2,1,0:T(8,128)(2,1)S(1)}, bf16[27,16,512]{2,1,0:T(8,128)(2,1)}, u32[]{:S(2)}, u32[]{:S(2)}) collective-permute-start(bf16[27,16,512]{2,1,0:T(8,128)(2,1)S(1)} %collective-permute-done.1.refs_4_), channel_id=1, source_target_pairs={{0,1},{1,0},{2,3},{3,2},{4,5},{5,4},{6,7},{7,6},{8,9},{9,8},{10,11... | collective-permute-start | bytes 1327112 | tf_op jit(solution)/shard_map/ppermute | solution.py:106
  41.5 4.7 %collective-permute-start.13 = (bf16[27,16,512]{2,1,0:T(8,128)(2,1)S(1)}, bf16[27,16,512]{2,1,0:T(8,128)(2,1)S(1)}, u32[]{:S(2)}, u32[]{:S(2)}) collective-permute-start(bf16[27,16,512]{2,1,0:T(8,128)(2,1)S(1)} %collective-permute-done.5.refs_6_), channel_id=1, source_target_pairs={{0,1},{1,0},{2,3},{3,2},{4,5},{5,4},{6,7},{7,6},{8,9},{9,8},{10,11... | collective-permute-start | bytes 1327112 | tf_op jit(solution)/shard_map/ppermute | solution.py:106
  43.4 2.8 %collective-permute-start.14 = (bf16[27,16,512]{2,1,0:T(8,128)(2,1)S(1)}, bf16[27,16,512]{2,1,0:T(8,128)(2,1)S(1)}, u32[]{:S(2)}, u32[]{:S(2)}) collective-permute-start(bf16[27,16,512]{2,1,0:T(8,128)(2,1)S(1)} %collective-permute-done.6.refs_8_), channel_id=1, source_target_pairs={{0,1},{1,0},{2,3},{3,2},{4,5},{5,4},{6,7},{7,6},{8,9},{9,8},{10,11... | collective-permute-start | bytes 1327112 | tf_op jit(solution)/shard_map/ppermute | solution.py:106
  44.1 2.1 collective-permute-start.15
  44.2 2.6 %collective-permute-start.16 = (bf16[27,16,512]{2,1,0:T(8,128)(2,1)S(1)}, bf16[27,16,512]{2,1,0:T(8,128)(2,1)S(1)}, u32[]{:S(2)}, u32[]{:S(2)}) collective-permute-start(bf16[27,16,512]{2,1,0:T(8,128)(2,1)S(1)} %collective-permute-done.8.refs_12_), channel_id=1, source_target_pairs={{0,1},{1,0},{2,3},{3,2},{4,5},{5,4},{6,7},{7,6},{8,9},{9,8},{10,11... | collective-permute-start | bytes 1327112 | tf_op jit(solution)/shard_map/ppermute | solution.py:106
  44.7 12.2 %collective-permute-start.9 = (bf16[27,16,512]{2,1,0:T(8,128)(2,1)S(1)}, bf16[27,16,512]{2,1,0:T(8,128)(2,1)S(1)}, u32[]{:S(2)}, u32[]{:S(2)}) collective-permute-start(bf16[27,16,512]{2,1,0:T(8,128)(2,1)S(1)} %collective-permute-done.7.refs_10_), channel_id=1, source_target_pairs={{0,8},{1,9},{2,10},{3,11},{8,16},{9,17},{10,18},{11,19},{16,24},{1... | collective-permute-start | bytes 1327112 | tf_op jit(solution)/shard_map/ppermute | solution.py:1357
  56.8 1.8 collective-permute-start.17
  115.5 10.7 %collective-permute-start.18 = (bf16[40,16,512]{2,1,0:T(8,128)(2,1)}, bf16[40,16,512]{2,1,0:T(8,128)(2,1)S(1)}, u32[]{:S(2)}, u32[]{:S(2)}) collective-permute-start(bf16[40,16,512]{2,1,0:T(8,128)(2,1)} %get-tuple-element.130), channel_id=1, source_target_pairs={{0,1},{1,0},{2,3},{3,2},{4,5},{5,4},{6,7},{7,6},{8,9},{9,8},{10,11... | collective-permute-start | bytes 1966088 | tf_op jit(solution)/shard_map/ppermute | solution.py:106
  115.7 11.0 %copy-start.5 = (bf16[40,16,512]{2,1,0:T(8,128)(2,1)S(1)}, bf16[40,16,512]{2,1,0:T(8,128)(2,1)}, u32[]{:S(2)}) copy-start(bf16[40,16,512]{2,1,0:T(8,128)(2,1)} %get-tuple-element.129) | copy-start | bytes 1966084
  126.2 17.5 %collective-permute-start.19 = (bf16[48,16,512]{2,1,0:T(8,128)(2,1)}, bf16[48,16,512]{2,1,0:T(8,128)(2,1)S(1)}, u32[]{:S(2)}, u32[]{:S(2)}) collective-permute-start(bf16[48,16,512]{2,1,0:T(8,128)(2,1)} %get-tuple-element.141), channel_id=1, source_target_pairs={{0,1},{1,0},{2,3},{3,2},{4,5},{5,4},{6,7},{7,6},{8,9},{9,8},{10,11... | collective-permute-start | bytes 2359304 | tf_op jit(solution)/shard_map/ppermute | solution.py:106
  127.7 16.1 %copy-start.4 = (bf16[48,16,512]{2,1,0:T(8,128)(2,1)S(1)}, bf16[48,16,512]{2,1,0:T(8,128)(2,1)}, u32[]{:S(2)}) copy-start(bf16[48,16,512]{2,1,0:T(8,128)(2,1)} %get-tuple-element.140) | copy-start | bytes 2359300
  127.7 17.4 %collective-permute-start.21 = (bf16[40,8,512]{2,1,0:T(8,128)(2,1)S(1)}, bf16[40,8,512]{2,1,0:T(8,128)(2,1)S(1)}, u32[]{:S(2)}, u32[]{:S(2)}) collective-permute-start(bf16[40,8,512]{2,1,0:T(8,128)(2,1)S(1)} %get-tuple-element.221), channel_id=1, source_target_pairs={{0,2},{1,3},{2,0},{3,1},{4,6},{5,7},{6,4},{7,5},{8,10},{9,11},{10,... | collective-permute-start | bytes 983048 | tf_op jit(solution)/shard_map/ppermute | solution.py:106
  143.8 12.7 %collective-permute-start.20 = (bf16[48,16,512]{2,1,0:T(8,128)(2,1)}, bf16[48,16,512]{2,1,0:T(8,128)(2,1)S(1)}, u32[]{:S(2)}, u32[]{:S(2)}) collective-permute-start(bf16[48,16,512]{2,1,0:T(8,128)(2,1)} %get-tuple-element.148), channel_id=1, source_target_pairs={{0,1},{1,0},{2,3},{3,2},{4,5},{5,4},{6,7},{7,6},{8,9},{9,8},{10,11... | collective-permute-start | bytes 2359304 | tf_op jit(solution)/shard_map/ppermute | solution.py:106
  145.0 11.5 %collective-permute-start.22 = (bf16[48,8,512]{2,1,0:T(8,128)(2,1)S(1)}, bf16[48,8,512]{2,1,0:T(8,128)(2,1)S(1)}, u32[]{:S(2)}, u32[]{:S(2)}) collective-permute-start(bf16[48,8,512]{2,1,0:T(8,128)(2,1)S(1)} %get-tuple-element.219), channel_id=1, source_target_pairs={{0,2},{1,3},{2,0},{3,1},{4,6},{5,7},{6,4},{7,5},{8,10},{9,11},{10,... | collective-permute-start | bytes 1179656 | tf_op jit(solution)/shard_map/ppermute | solution.py:106
  145.1 9.3 %copy-start.23 = (bf16[40,8,512]{2,1,0:T(8,128)(2,1)}, bf16[40,8,512]{2,1,0:T(8,128)(2,1)S(1)}, u32[]{:S(2)}) copy-start(bf16[40,8,512]{2,1,0:T(8,128)(2,1)S(1)} %collective-permute-done.21.refs_3_) | copy-start | bytes 983044
  145.2 11.4 %copy-start.3 = (bf16[48,16,512]{2,1,0:T(8,128)(2,1)S(1)}, bf16[48,16,512]{2,1,0:T(8,128)(2,1)}, u32[]{:S(2)}) copy-start(bf16[48,16,512]{2,1,0:T(8,128)(2,1)} %get-tuple-element.147) | copy-start | bytes 2359300
  157.6 21.2 %collective-permute-start.23 = (bf16[48,8,512]{2,1,0:T(8,128)(2,1)S(1)}, bf16[48,8,512]{2,1,0:T(8,128)(2,1)S(1)}, u32[]{:S(2)}, u32[]{:S(2)}) collective-permute-start(bf16[48,8,512]{2,1,0:T(8,128)(2,1)S(1)} %get-tuple-element.217), channel_id=1, source_target_pairs={{0,2},{1,3},{2,0},{3,1},{4,6},{5,7},{6,4},{7,5},{8,10},{9,11},{10,... | collective-permute-start | bytes 1179656 | tf_op jit(solution)/shard_map/ppermute | solution.py:106
  158.8 26.7 %collective-permute-start.29 = (bf16[2,16,1536]{2,1,0:T(8,128)(2,1)S(1)}, bf16[2,16,1536]{2,1,0:T(8,128)(2,1)S(1)}, u32[]{:S(2)}, u32[]{:S(2)}) collective-permute-start(bf16[2,16,1536]{2,1,0:T(8,128)(2,1)S(1)} %slice.37), channel_id=1, source_target_pairs={{0,1},{1,2},{2,3},{4,5},{5,6},{6,7},{8,9},{9,10},{10,11},{12,13},{... | collective-permute-start | bytes 294920 | tf_op jit(solution)/shard_map/ppermute | solution.py:116
  171.9 7.0 %collective-permute-start.24 = (f32[24,512]{1,0:T(8,128)}, f32[24,512]{1,0:T(8,128)S(1)}, u32[]{:S(2)}, u32[]{:S(2)}) collective-permute-start(f32[24,512]{1,0:T(8,128)} %get-tuple-element.169), channel_id=1, source_target_pairs={{0,1},{1,0},{2,3},{3,2},{4,5},{5,4},{6,7},{7,6},{8,9},{9,8},{10,11... | collective-permute-start | bytes 147464 | tf_op jit(solution)/shard_map/ppermute | solution.py:106
  174.2 4.6 %collective-permute-start.26 = (f32[24,512]{1,0:T(8,128)}, f32[24,512]{1,0:T(8,128)S(1)}, u32[]{:S(2)}, u32[]{:S(2)}) collective-permute-start(f32[24,512]{1,0:T(8,128)} %get-tuple-element.171), channel_id=1, source_target_pairs={{0,3},{1,2},{2,1},{3,0},{4,7},{5,6},{6,5},{7,4},{8,11},{9,10},{10,... | collective-permute-start | bytes 147464 | tf_op jit(solution)/shard_map/ppermute | solution.py:106
  174.2 4.6 %collective-permute-start.25 = (f32[8,512]{1,0:T(8,128)}, f32[8,512]{1,0:T(8,128)S(1)}, u32[]{:S(2)}, u32[]{:S(2)}) collective-permute-start(f32[8,512]{1,0:T(8,128)} %get-tuple-element.170), channel_id=1, source_target_pairs={{0,2},{1,3},{2,0},{3,1},{4,6},{5,7},{6,4},{7,5},{8,10},{9,11},{10,... | collective-permute-start | bytes 49160 | tf_op jit(solution)/shard_map/ppermute | solution.py:106
  183.5 9.7 %collective-permute-start.27 = (bf16[27,8,512]{2,1,0:T(8,128)(2,1)}, bf16[27,8,512]{2,1,0:T(8,128)(2,1)S(1)}, u32[]{:S(2)}, u32[]{:S(2)}) collective-permute-start(bf16[27,8,512]{2,1,0:T(8,128)(2,1)} %get-tuple-element.177), channel_id=1, source_target_pairs={{0,8},{1,9},{2,10},{3,11},{8,16},{9,17},{10,18},{11,19},{16,24},{1... | collective-permute-start | bytes 663560 | tf_op jit(solution)/shard_map/ppermute | solution.py:1461
  185.1 8.2 %copy-start.1 = (bf16[216,8,512]{2,1,0:T(8,128)(2,1)S(1)}, bf16[216,8,512]{2,1,0:T(8,128)(2,1)}, u32[]{:S(2)}) copy-start(bf16[216,8,512]{2,1,0:T(8,128)(2,1)} %get-tuple-element.182) | copy-start | bytes 5308420
  185.1 8.2 %collective-permute-start.28 = (bf16[27,8,512]{2,1,0:T(8,128)(2,1)}, bf16[27,8,512]{2,1,0:T(8,128)(2,1)S(1)}, u32[]{:S(2)}, u32[]{:S(2)}) collective-permute-start(bf16[27,8,512]{2,1,0:T(8,128)(2,1)} %get-tuple-element.178), channel_id=1, source_target_pairs={{0,4},{1,5},{2,6},{3,7},{8,0},{9,1},{10,2},{11,3},{16,8},{17,9},{1... | collective-permute-start | bytes 663560 | tf_op jit(solution)/shard_map/ppermute | solution.py:1463
  193.4 6.9 %collective-permute-start.30 = (bf16[27,8,512]{2,1,0:T(8,128)(2,1)S(1)}, bf16[27,8,512]{2,1,0:T(8,128)(2,1)S(1)}, u32[]{:S(2)}, u32[]{:S(2)}) collective-permute-start(bf16[27,8,512]{2,1,0:T(8,128)(2,1)S(1)} %get-tuple-element.216), channel_id=1, source_target_pairs={{0,8},{1,9},{2,10},{3,11},{8,16},{9,17},{10,18},{11,19},{16,24},{1... | collective-permute-start | bytes 663560 | tf_op jit(solution)/shard_map/ppermute | solution.py:1461
  195.0 6.1 %collective-permute-start.31 = (bf16[27,8,512]{2,1,0:T(8,128)(2,1)S(1)}, bf16[27,8,512]{2,1,0:T(8,128)(2,1)S(1)}, u32[]{:S(2)}, u32[]{:S(2)}) collective-permute-start(bf16[27,8,512]{2,1,0:T(8,128)(2,1)S(1)} %get-tuple-element.215), channel_id=1, source_target_pairs={{0,4},{1,5},{2,6},{3,7},{8,0},{9,1},{10,2},{11,3},{16,8},{17,9},{1... | collective-permute-start | bytes 663560 | tf_op jit(solution)/shard_map/ppermute | solution.py:1463
  201.2 9.1 %collective-permute-start.32 = (bf16[27,8,512]{2,1,0:T(8,128)(2,1)S(1)}, bf16[27,8,512]{2,1,0:T(8,128)(2,1)S(1)}, u32[]{:S(2)}, u32[]{:S(2)}) collective-permute-start(bf16[27,8,512]{2,1,0:T(8,128)(2,1)S(1)} %get-tuple-element.214), channel_id=1, source_target_pairs={{0,8},{1,9},{2,10},{3,11},{8,16},{9,17},{10,18},{11,19},{16,24},{1... | collective-permute-start | bytes 663560 | tf_op jit(solution)/shard_map/ppermute | solution.py:1461
  202.9 7.5 %collective-permute-start.33 = (bf16[27,8,512]{2,1,0:T(8,128)(2,1)S(1)}, bf16[27,8,512]{2,1,0:T(8,128)(2,1)S(1)}, u32[]{:S(2)}, u32[]{:S(2)}) collective-permute-start(bf16[27,8,512]{2,1,0:T(8,128)(2,1)S(1)} %get-tuple-element.213), channel_id=1, source_target_pairs={{0,4},{1,5},{2,6},{3,7},{8,0},{9,1},{10,2},{11,3},{16,8},{17,9},{1... | collective-permute-start | bytes 663560 | tf_op jit(solution)/shard_map/ppermute | solution.py:1463
  210.4 6.4 %collective-permute-start.34 = (bf16[27,8,512]{2,1,0:T(8,128)(2,1)S(1)}, bf16[27,8,512]{2,1,0:T(8,128)(2,1)S(1)}, u32[]{:S(2)}, u32[]{:S(2)}) collective-permute-start(bf16[27,8,512]{2,1,0:T(8,128)(2,1)S(1)} %add_convert_fusion.4), channel_id=1, source_target_pairs={{0,8},{1,9},{2,10},{3,11},{8,16},{9,17},{10,18},{11,19},{16,24},{1... | collective-permute-start | bytes 663560 | tf_op jit(solution)/shard_map/ppermute | solution.py:1461
  217.0 6.0 %collective-permute-start.35 = (bf16[27,8,512]{2,1,0:T(8,128)(2,1)S(1)}, bf16[27,8,512]{2,1,0:T(8,128)(2,1)S(1)}, u32[]{:S(2)}, u32[]{:S(2)}) collective-permute-start(bf16[27,8,512]{2,1,0:T(8,128)(2,1)S(1)} %add_convert_fusion.3.mine_ref), channel_id=1, source_target_pairs={{0,2},{1,3},{2,0},{3,1},{4,6},{5,7},{6,4},{7,5},{8,10},{9,11},{10,... | collective-permute-start | bytes 663560 | tf_op jit(solution)/shard_map/ppermute | solution.py:106
  217.9 5.1 %collective-permute-start.37 = (bf16[27,8,512]{2,1,0:T(8,128)(2,1)S(1)}, bf16[27,8,512]{2,1,0:T(8,128)(2,1)S(1)}, u32[]{:S(2)}, u32[]{:S(2)}) collective-permute-start(bf16[27,8,512]{2,1,0:T(8,128)(2,1)S(1)} %add_convert_fusion.3.mine_ref), channel_id=1, source_target_pairs={{0,1},{1,0},{2,3},{3,2},{4,5},{5,4},{6,7},{7,6},{8,9},{9,8},{10,11... | collective-permute-start | bytes 663560 | tf_op jit(solution)/shard_map/ppermute | solution.py:106
  223.0 5.8 %collective-permute-start.36 = (bf16[27,8,512]{2,1,0:T(8,128)(2,1)S(1)}, bf16[27,8,512]{2,1,0:T(8,128)(2,1)S(1)}, u32[]{:S(2)}, u32[]{:S(2)}) collective-permute-start(bf16[27,8,512]{2,1,0:T(8,128)(2,1)S(1)} %collective-permute-done.35.mine_ref), channel_id=1, source_target_pairs={{0,1},{1,0},{2,3},{3,2},{4,5},{5,4},{6,7},{7,6},{8,9},{9,8},{10,11... | collective-permute-start | bytes 663560 | tf_op jit(solution)/shard_map/ppermute | solution.py:106
  (23 other events, 42.9 us)

commit v6 on v5

--- a/solution.py
+++ b/solution.py
@@ -43,7 +43,7 @@
 CHUNK = 768
 HALF_BIN = 384
 PAIR = 5
-ADAM_BLOCK = 9
+ADAM_BLOCK = 27
 LANE = 128
 AXES = ("rows", "seq")
 
@@ -241,7 +241,7 @@
         return carry
 
     lax.fori_loop(0, owners, name, 0)
-    lax.fori_loop(0, owners * slots, clear, 0)
+    lax.fori_loop(0, owners * slots, clear, 0, unroll=8)
     lax.fori_loop(0, NB, place, 0)
     own = rel[row_at]
 
@@ -249,7 +249,7 @@
         held[0, n] = places[0, own * slots + n]
         return carry
 
-    lax.fori_loop(0, slots, keep, 0)
+    lax.fori_loop(0, slots, keep, 0, unroll=True)
 
 
 def plan(ids, lengths, bw_ids, owner_list, order, offsets, slots, frames, ring):
@@ -346,12 +346,15 @@
 
 
 def place_parts(places, counts, core, pieces, table, sem, slots, owners, start):
+    done = {}
     for index, ref in enumerate(pieces):
         side = core if index % 2 == 0 else 1 - core
         owner = owners[index // 2]
-
-        def one(s, carry, ref=ref, side=side, owner=owner):
-            bucket = places[0, owner * slots + s]
+        first = done.get((owner, index % 2), 0)
+        done[owner, index % 2] = first + ref.shape[0]
+
+        def one(s, carry, ref=ref, side=side, owner=owner, first=first):
+            bucket = places[0, owner * slots + first + s]
             at = pl.multiple_of(bucket * BR + side * HALF, HALF)
             copy = pltpu.make_async_copy(ref.at[s], table.at[pl.ds(at, HALF), :], sem)
             if start:
@@ -360,7 +363,8 @@
                 copy.wait()
             return carry
 
-        lax.fori_loop(0, counts[0, owner], one, 0)
+        held = jnp.clip(counts[0, owner] - first, 0, ref.shape[0])
+        lax.fori_loop(0, held, one, 0)
 
 
 def assemble_body(meta, places, counts, *refs, slots, owners):
@@ -456,6 +460,8 @@
         for other in others[at:until]:
             other()
         at = until
+    for other in others[at:]:
+        other()
 
 
 def forward_body(meta, places, counts, x_ref, low_ref, high_ref, order_ref, cot_ref, *rest, owners, slots, tiles, count, utts):
@@ -636,18 +642,13 @@
     def grad_dot(c):
         grad[c : c + 256, :] += dot(hg_old[:, c : c + 256], normed_old[...], TN)
 
-    interleave(
-        head_dots(logs_ref, 0) + head_dots(angle_ref, BIN_PAD),
-        [functools.partial(convolve, at, size) for at, size in spans(TILE, 32)],
-    )
-    interleave(
-        [functools.partial(hidden_dot, c) for c in range(0, FF, 256)]
-        + [functools.partial(grad_dot, c) for c in range(0, 2 * BIN_PAD, 256)],
-        [functools.partial(head, at, size, sincos) for at, size in spans(TILE, 16)],
-    )
-
-    @pl.when((step > 0) & (slow[0] > 0))
-    def _():
+    def ngrad_dot(c):
+        ngrad_ref[:, c : c + 256] = dot(hg[...], w_head[:, c : c + 256], NN)
+
+    def branch_dot(c):
+        slim[:, c : c + 256] = dot(act_ref[...], table[FF : 2 * FF, c : c + 256], NN)
+
+    def head_again():
         def again(i, carry):
             rows = pl.ds(pl.multiple_of(i * 32, 32), 32)
             for c in range(0, BIN_PAD, LANE):
@@ -668,8 +669,7 @@
 
         lax.fori_loop(0, TILE // 32, again, 0)
 
-    @pl.when(step == 0)
-    def _():
+    def build_head():
         last = vecs[...]
         line = jnp.concatenate([last[25:26], last[26:27], last[27:28]], axis=1)
         line = jnp.broadcast_to(line, (16, 3 * channels))
@@ -697,36 +697,62 @@
         bound = 1.05 * normed_length * jnp.max(jnp.sqrt(longest)) + jnp.max(jnp.abs(b_head[:, BIN_PAD:]))
         slow[0] = jnp.where(bound < ANGLE_LIMIT, 0, 1)
 
-    def ngrad_dot(c):
-        ngrad_ref[:, c : c + 256] = dot(hg[...], w_head[:, c : c + 256], NN)
-
-    def branch_dot(c):
-        slim[:, c : c + 256] = dot(act_ref[...], table[FF : 2 * FF, c : c + 256], NN)
-
-    interleave(
-        [functools.partial(ngrad_dot, c) for c in range(0, channels, 256)],
-        [functools.partial(gelu, at, size, c) for c in range(IN_ROWS) for at, size in spans(TILE, 32)],
-    )
-    sums = [sums_ref[v] for v in range(4)]
-
-    def back(at, size):
-        sums[:] = second_norm_back(at, size, sums)
-
-    interleave(
-        [functools.partial(branch_dot, c) for c in range(0, channels, 256)],
-        [functools.partial(back, at, size) for at, size in spans(TILE, 16)],
-    )
-    for v in range(4):
-        sums_ref[v] = sums[v]
-    for c in range(0, 2 * BIN_PAD, 512):
-        total = bsum_ref[:, c : c + 512]
-        for at, size in spans(TILE, 32):
-            total = total + fold(hg[at : at + size, c : c + 512].astype(F32))
-        bsum_ref[:, c : c + 512] = total
-    hg_old[...] = hg[...]
-    normed_old[...] = normed[...]
-    for at, size in spans(TILE, 16):
-        second_norm(at, size)
+    def over_all(call, values):
+        return [functools.partial(call, v) for v in values]
+
+    def in_spans(call, size, *more):
+        return [functools.partial(call, at, length, *more) for at, length in spans(TILE, size)]
+
+    def work(first, second):
+        interleave(
+            head_dots(logs_ref, 0) + head_dots(angle_ref, BIN_PAD) if second else [],
+            in_spans(convolve, 32) if first else [],
+        )
+        interleave(
+            (over_all(hidden_dot, range(0, FF, 256)) if first else [])
+            + (over_all(grad_dot, range(0, 2 * BIN_PAD, 256)) if second else []),
+            in_spans(head, 16, sincos) if second else [],
+        )
+        if second:
+            pl.when(slow[0] > 0)(head_again)
+        interleave(
+            over_all(ngrad_dot, range(0, channels, 256)) if second else [],
+            [call for c in range(IN_ROWS) for call in in_spans(gelu, 32, c)] if first else [],
+        )
+        sums = [sums_ref[v] for v in range(4)]
+
+        def back(at, size):
+            sums[:] = second_norm_back(at, size, sums)
+
+        interleave(
+            over_all(branch_dot, range(0, channels, 256)) if first else [],
+            in_spans(back, 16) if second else [],
+        )
+        if second:
+            for v in range(4):
+                sums_ref[v] = sums[v]
+            for c in range(0, 2 * BIN_PAD, 512):
+                total = bsum_ref[:, c : c + 512]
+                for at, size in spans(TILE, 32):
+                    total = total + fold(hg[at : at + size, c : c + 512].astype(F32))
+                bsum_ref[:, c : c + 512] = total
+            hg_old[...] = hg[...]
+            normed_old[...] = normed[...]
+        if first:
+            interleave([], in_spans(second_norm, 16))
+
+    @pl.when(step == 0)
+    def _():
+        work(True, False)
+        build_head()
+
+    @pl.when((step > 0) & (step < count))
+    def _():
+        work(True, True)
+
+    @pl.when(step == count)
+    def _():
+        work(False, True)
 
     @pl.when(step == count)
     def _():
@@ -747,12 +773,11 @@
         store().wait()
 
 
-def forward(owners, meta, places, counts, x, low, high, order, cot, pieces, table, utts):
+def forward(owners, slots, meta, places, counts, x, low, high, order, cot, pieces, table, utts):
     rows, frames, channels = x.shape
     tiles = frames // TILE
     steps = rows * tiles
     count = rows * frames
-    slots = pieces[0].shape[0]
     ahead = lambda i: jnp.minimum(i, steps - 1)
     behind = lambda i: jnp.maximum(i - 1, 0)
     wide = pl.BlockSpec((TILE, FF), lambda i: (ahead(i), 0))
@@ -902,26 +927,58 @@
 
 
 def norm_body(
-    meta, x_ref, low_ref, high_ref, pre_ref, w_in, last_ref, xc_ref, rc_ref, *rest, row, tiles, utts, closing
+    meta,
+    x_ref,
+    low_ref,
+    high_ref,
+    pre_ref,
+    w_in,
+    last_ref,
+    xc_ref,
+    rc_ref,
+    tail_ref,
+    sums_ref,
+    hsum_ref,
+    bsum0,
+    bsum1,
+    order_ref,
+    cg_ref,
+    own_ref,
+    near_ref,
+    far_ref,
+    cross_ref,
+    part_ref,
+    edge_ref,
+    vec_ref,
+    xs,
+    vecs,
+    picks,
+    agrad,
+    cg,
+    reaches,
+    *,
+    tiles,
+    utts,
 ):
-    more = rest[: 8 if closing else 0]
-    outs = rest[len(more) :]
-    cg_ref, edge_ref, part_ref = outs[:3]
-    xs, vecs, picks, agrad, cg, reaches = outs[-6:]
-    tile = pl.program_id(0)
+    step = pl.program_id(0)
+    row, tile = step // tiles, step % tiles
+    rows = x_ref.shape[0]
     channels = x_ref.shape[2]
     lane_tiles = channels // LANE
     base = meta[row, 2 * utts + 1] + tile * TILE
     vec = lambda v: vecs[2 + v : 3 + v, :]
 
+    @pl.when(step == 0)
+    def _():
+        vecs[...] = last_ref[...].astype(F32)
+        part_ref[...] = jnp.zeros_like(part_ref)
+
     @pl.when(tile == 0)
     def _():
-        vecs[...] = last_ref[...].astype(F32)
-        part_ref[...] = more[0][...] if closing else jnp.zeros_like(part_ref)
         pick_rows(meta, row, utts, vec, picks, channels)
 
     agrad[...] = dot(pre_ref[...], w_in[...], NN)
-    fill_frames(xs, x_ref, low_ref, high_ref, 0, tile, tiles, channels)
+    fill_frames(xs, x_ref, low_ref, high_ref, row, tile, tiles, channels)
     for at, size in spans(TILE, 32):
         span = slice(at, at + size)
         reach, left = frame_reach(meta, row, base + at, size, utts)
@@ -978,7 +1035,7 @@
 
     def edge(side, begin):
         for c in range(lane_tiles):
-            edge_ref[side, :, c * LANE : (c + 1) * LANE] = cg[c, begin : begin + 8, :]
+            edge_ref[row, side, :, c * LANE : (c + 1) * LANE] = cg[c, begin : begin + 8, :]
 
     @pl.when(tile == 0)
     def _():
@@ -988,87 +1045,75 @@
     def _():
         edge(1, TILE - 8)
 
-    if closing:
-        _, other_edge, tail_ref, sums_ref, hsum_ref, bsum0, bsum1, order_ref = more
-        vec_ref, quarter_refs = outs[-7], outs[3:7]
-        core, plane = meta[0, 2 * utts + 2], meta[0, 2 * utts + 3]
-
-        @pl.when(tile == tiles - 1)
-        def _():
-            vec_ref[0:8, :] = jnp.zeros((8, channels), F32)
-            vec_ref[0:2, :] = tail_ref[0:2, :]
-            for v in range(VROWS):
-                at = v - (KW + 1 + 2 * NBW)
-                rows_of = part_ref[v] if at < 0 else sums_ref[at]
-                vec_ref[2 + v : 3 + v, :] = jnp.sum(rows_of, axis=0, keepdims=True)
-            line = jnp.concatenate([bsum0[...], bsum1[...]], axis=1)
-            for c in range(IN_ROWS):
-                at = 2 + VROWS + c
-                vec_ref[at : at + 1, :] = jnp.sum(
-                    line[:, c * channels : (c + 1) * channels], axis=0, keepdims=True
-                )
-
-            def bins(value):
-                value = jnp.broadcast_to(jnp.sum(value, axis=0, keepdims=True), (16, BIN_PAD))
-                total = jnp.zeros((16, BIN_PAD), F32)
-                for _ in range(3):
-                    part = value.astype(BF16)
-                    value = value - part.astype(F32)
-                    total = total + dot(part, order_ref[...], NT)
-                return total[0:8]
-
-            flat = jnp.concatenate([bins(hsum_ref[:, 0:BIN_PAD]), bins(hsum_ref[:, BIN_PAD:])], axis=1)
-            column = lax.broadcasted_iota(jnp.int32, (8, 3 * channels), 1)
-            moved = pltpu.roll(flat, 2 * BIN_PAD - (BIN_PAD - BINS), 1)
-            joined = jnp.where(column < BINS, flat, moved)
-            joined = jnp.where(column < NOUT, joined, 0.0)
-            for c in range(HEAD_ROWS):
-                at = 2 + VROWS + IN_ROWS + c
-                vec_ref[at : at + 1, :] = joined[0:1, c * channels : (c + 1) * channels]
-            vec_ref[28:32, :] = jnp.zeros((4, channels), F32)
-            for ref, c, p in zip(
-                quarter_refs,
-                (core, 1 - core, core, 1 - core),
-                (plane, plane, 1 - plane, 1 - plane),
-            ):
-                ref[0:8, :] = vec_ref[pl.ds(pl.multiple_of(c * HALF + p * QUART, QUART), QUART), :]
-            for at, ref in ((8, other_edge), (16, edge_ref)):
-                quarter_refs[1][at : at + 8, :] = jnp.where(core == 0, ref[1], ref[0])
-                quarter_refs[3][at : at + 8, :] = jnp.where(core == 0, ref[0], ref[1])
-
-
-def norm_backward(row, closing, meta, x, low, high, pre, table, xc, rc, utts):
+    core, plane = meta[0, 2 * utts + 2], meta[0, 2 * utts + 3]
+
+    @pl.when(step == rows * tiles - 1)
+    def _():
+        vec_ref[0:8, :] = jnp.zeros((8, channels), F32)
+        vec_ref[0:2, :] = tail_ref[0:2, :]
+        for v in range(VROWS):
+            at = v - (KW + 1 + 2 * NBW)
+            rows_of = part_ref[v] if at < 0 else sums_ref[at]
+            vec_ref[2 + v : 3 + v, :] = jnp.sum(rows_of, axis=0, keepdims=True)
+        line = jnp.concatenate([bsum0[...], bsum1[...]], axis=1)
+        for c in range(IN_ROWS):
+            at = 2 + VROWS + c
+            vec_ref[at : at + 1, :] = jnp.sum(
+                line[:, c * channels : (c + 1) * channels], axis=0, keepdims=True
+            )
+
+        def bins(value):
+            value = jnp.broadcast_to(jnp.sum(value, axis=0, keepdims=True), (16, BIN_PAD))
+            total = jnp.zeros((16, BIN_PAD), F32)
+            for _ in range(3):
+                part = value.astype(BF16)
+                value = value - part.astype(F32)
+                total = total + dot(part, order_ref[...], NT)
+            return total[0:8]
+
+        flat = jnp.concatenate([bins(hsum_ref[:, 0:BIN_PAD]), bins(hsum_ref[:, BIN_PAD:])], axis=1)
+        column = lax.broadcasted_iota(jnp.int32, (8, 3 * channels), 1)
+        moved = pltpu.roll(flat, 2 * BIN_PAD - (BIN_PAD - BINS), 1)
+        joined = jnp.where(column < BINS, flat, moved)
+        joined = jnp.where(column < NOUT, joined, 0.0)
+        for c in range(HEAD_ROWS):
+            at = 2 + VROWS + IN_ROWS + c
+            vec_ref[at : at + 1, :] = joined[0:1, c * channels : (c + 1) * channels]
+        vec_ref[28:32, :] = jnp.zeros((4, channels), F32)
+        for ref, c, p in zip(
+            (own_ref, near_ref, far_ref, cross_ref),
+            (core, 1 - core, core, 1 - core),
+            (plane, plane, 1 - plane, 1 - plane),
+        ):
+            ref[0:8, :] = vec_ref[pl.ds(pl.multiple_of(c * HALF + p * QUART, QUART), QUART), :]
+        for r in range(rows):
+            at = 8 + 8 * r
+            near_ref[at : at + 8, :] = jnp.where(core == 0, edge_ref[r, 1], edge_ref[r, 0])
+            cross_ref[at : at + 8, :] = jnp.where(core == 0, edge_ref[r, 0], edge_ref[r, 1])
+
+
+def norm_backward(meta, x, low, high, pre, table, xc, rc, tail, sums, hsum, bsums, order, utts):
     rows, frames, channels = x.shape
     tiles = frames // TILE
-    block = lambda width: pl.BlockSpec((TILE, width), lambda i: (row * tiles + i, 0))
-    sums = KW + 1 + 2 * NBW
-    out_specs = [pl.BlockSpec((TILE, channels), lambda i: (i, 0)), WHOLE, WHOLE]
-    out_shape = [
-        shape_of((frames, channels), BF16),
-        shape_of((2, 8, channels), F32),
-        shape_of((sums, 8, channels), F32),
-    ]
-    if closing:
-        out_specs += [WHOLE] * 4
-        out_shape += [shape_of((8 * n, channels), F32) for n in (1, 3, 1, 3)]
+    block = lambda width: pl.BlockSpec((TILE, width), lambda i: (i, 0))
     return pl.pallas_call(
-        functools.partial(norm_body, row=row, tiles=tiles, utts=utts, closing=bool(closing)),
-        grid=(tiles,),
-        in_specs=[SCALARS]
-        + [pl.BlockSpec((1, frames, channels), lambda i: (row, 0, 0))]
-        + [pl.BlockSpec((1, EDGE, channels), lambda i: (row, 0, 0))] * 2
-        + [block(FF)]
+        functools.partial(norm_body, tiles=tiles, utts=utts),
+        grid=(rows * tiles,),
+        in_specs=[SCALARS, WHOLE, WHOLE, WHOLE, block(FF)]
         + [
             pl.BlockSpec((FF, channels), lambda i: (0, 0)),
             pl.BlockSpec((BR, channels), lambda i: (NB - 1, 0)),
             block(channels),
             block(LANE),
         ]
-        + [WHOLE] * len(closing),
-        out_specs=out_specs,
-        out_shape=out_shape,
-        scratch_shapes=([pltpu.VMEM((BR, channels), F32)] if closing else [])
-        + [
+        + [WHOLE] * 6,
+        out_specs=[block(channels)] + [WHOLE] * 4,
+        out_shape=[shape_of((rows * frames, channels), BF16)]
+        + [shape_of((8 * n, channels), F32) for n in (1, 1 + rows, 1, 1 + rows)],
+        scratch_shapes=[
+            pltpu.VMEM((KW + 1 + 2 * NBW, 8, channels), F32),
+            pltpu.VMEM((rows, 2, 8, channels), F32),
+            pltpu.VMEM((BR, channels), F32),
             pltpu.VMEM((channels // LANE, TILE + 2 * EDGE, LANE), F32),
             pltpu.VMEM((BR, channels), F32),
             pltpu.VMEM((2 * utts, channels), F32),
@@ -1077,9 +1122,9 @@
             pltpu.VMEM((2, TILE, LANE), jnp.int32),
         ],
         compiler_params=params(),
-        cost_estimate=cost(2 * frames * 1536 * 512, 12 * MIB),
-        name=f"norm_backward_{row}",
-    )(meta, x, low, high, pre, table, table, xc, rc, *closing)
+        cost_estimate=cost(2 * rows * frames * 1536 * 512, 20 * MIB),
+        name="norm_backward",
+    )(meta, x, low, high, pre, table, table, xc, rc, tail, sums, hsum, *bsums, order)
 
 
 def conv_body(meta, cg_ref, before_ref, after_ref, near_ref, cross_ref, resg_ref, last_ref, *rest, row, tiles, utts):
@@ -1115,7 +1160,7 @@
 
 
 def conv_backward(row, before, meta, cg, near, cross, resg, table, rows, utts):
-    frames, channels = cg.shape
+    frames, channels = cg.shape[0] // rows, cg.shape[1]
     tiles = frames // TILE
     per = TILE // EDGE
     more = [] if before is None else [before]
@@ -1124,9 +1169,9 @@
         grid=(tiles,),
         in_specs=[
             SCALARS,
-            pl.BlockSpec((TILE, channels), lambda i: (i, 0)),
-            pl.BlockSpec((EDGE, channels), lambda i: (jnp.maximum(i * per - 1, 0), 0)),
-            pl.BlockSpec((EDGE, channels), lambda i: (jnp.minimum((i + 1) * per, tiles * per - 1), 0)),
+            pl.BlockSpec((TILE, channels), lambda i: (row * tiles + i, 0)),
+            pl.BlockSpec((EDGE, channels), lambda i: (row * tiles * per + jnp.maximum(i * per - 1, 0), 0)),
+            pl.BlockSpec((EDGE, channels), lambda i: (row * tiles * per + jnp.minimum((i + 1) * per, tiles * per - 1), 0)),
             WHOLE,
             WHOLE,
             pl.BlockSpec((TILE, channels), lambda i: (row * tiles + i, 0)),
@@ -1228,7 +1273,7 @@
             out[slot_of[0, start + b]] = value.astype(BF16)
             return carry
 
-        lax.fori_loop(0, stop - start, one, 0)
+        lax.fori_loop(0, stop - start, one, 0, unroll=8)
     total = last_refs[0][0:QUART, :]
     for ref in last_refs[1:]:
         total = total + ref[0:QUART, :]
@@ -1326,8 +1371,6 @@
     synth = jnp.asarray(synthesis_table())
     win = jnp.asarray(window_tables())
 
-    low = shifted(frames_in[:, frames - EDGE :], 1)
-    high = shifted(frames_in[:, :EDGE], -1)
     later = shifted(lines[: PAIR * EDGE], -1)
     offsets = [0]
     for hop in range(1, half_ring):
@@ -1358,7 +1401,12 @@
             if hop < half_ring - 1:
                 back = lax.ppermute(back, AXES, ring_step(ring, -1, seqs))
             if hop == 0:
-                ahead, back, low, high, later, meta = tie(ahead, back, low, high, later, meta)
+                ahead, back, later, meta = tie(ahead, back, later, meta)
+            if hop == 1:
+                edges = tie(frames_in, *source)[0]
+                low = shifted(edges[:, frames - EDGE :], 1)
+                high = shifted(edges[:, :EDGE], -1)
+                ahead, back, low, high = tie(ahead, back, low, high)
             if hop in (1, 2):
                 feed = tie(lines, *source)[0]
                 begin, end = ((0, tiles // 2), (tiles // 2, tiles))[hop - 1]
@@ -1367,24 +1415,26 @@
             if hop == half_ring - 1:
                 fed = tie(places, *source)[0]
                 partial_table = assemble(tuple(range(owners - 1)), meta, fed, counts, arrived, slots)
-                ahead, partial_table = tie(ahead, partial_table)
+                ahead, back, partial_table = tie(ahead, back, partial_table)
             else:
                 arrived += [ahead, seq_swap(ahead, 1), back, seq_swap(back, 1)]
         arrived = [ahead, seq_swap(ahead, 1)]
         owned = (owners - 1,)
-        part_places, part_counts = places, counts
+        part_places, part_counts, part_slots = places, counts, slots
     else:
+        low = shifted(frames_in[:, frames - EDGE :], 1)
+        high = shifted(frames_in[:, :EDGE], -1)
         gathered = lax.all_gather(mine, "rows", axis=0, tiled=True)
         arrived = [gathered, seq_swap(gathered, 1)]
         owned = (0,)
         arrived = [take_slots(slot_of, a) for a in arrived]
         part_places = jnp.arange(NB, dtype=jnp.int32)[None, :]
-        part_counts = jnp.full((1, 1), NB, jnp.int32)
+        part_counts, part_slots = jnp.full((1, 1), NB, jnp.int32), NB
         partial_table = jnp.zeros((NB * BR, channels), BF16)
         cot = spectrum_cotangent(0, tiles, cot, meta, lines, later, synth, win, rows, utts)
 
     (table, spec, act, der, ada, low_grad, resg, xc, rc, send, keep, tail, sums, hsum) = forward(
-        owned, meta, part_places, part_counts, frames_in, low, high, order, cot, arrived, partial_table, utts
+        owned, part_slots, meta, part_places, part_counts, frames_in, low, high, order, cot, arrived, partial_table, utts
     )
     halo = shifted(spec[:, frames - EDGE :], 1)
 
@@ -1416,42 +1466,37 @@
         send, keep = next_send, next_keep
         begins, count = (chunk * per, FF // BR + chunk * per), per
 
+    state = {"wave": None, "grad": None}
+
+    def wave_piece(n, *ready):
+        feed = tie(spec, *ready)[0]
+        begin, end = n * tiles // 2, (n + 1) * tiles // 2
+        state["wave"] = wave_forward(begin, end, state["wave"], meta, feed, halo, synth, win, utts)
+        return "wave"
+
+    def conv_piece(row, *ready):
+        feed = tie(cg, *ready)[0]
+        state["grad"] = conv_backward(row, state["grad"], meta, feed, lasts[1], lasts[3], resg, table, rows, utts)
+        return "grad"
+
     near = seq_swap(send, 1)
     for stay, came, *where_from in waiting[:-1]:
         pre, came = tie(pre, came)
         record(stay, came, *where_from)
-    cg0, edge0, parts = norm_backward(0, (), meta, frames_in, low, high, pre, table, xc, rc, utts)
+    cg, own, to_near, to_far, to_cross = norm_backward(
+        meta, frames_in, low, high, pre, table, xc, rc, tail, sums, hsum, bsums, order, utts
+    )
     kept, came, *where_from = waiting[-1]
-    near, cg0, edge0, parts, pre, came = tie(near, cg0, edge0, parts, pre, came)
+    near, came, cg, own, to_near, to_far, to_cross = tie(near, came, cg, own, to_near, to_far, to_cross)
     record(kept, came, *where_from)
     stay, leave = split(keep, near)
     came = seq_swap(leave, 2)
-    closing = (parts, edge0, tail, sums, hsum, *bsums, order)
-    cg1, _, _, own, to_near, to_far, to_cross = norm_backward(
-        1, closing, meta, frames_in, low, high, pre, table, xc, rc, utts
-    )
-    lasts = (own, seq_swap(to_near, 1), seq_swap(to_far, 2), seq_swap(to_cross, 3))
-    came, spec, *lasts = tie(came, spec, *lasts)
+    lasts = [own, seq_swap(to_near, 1), seq_swap(to_far, 2), seq_swap(to_cross, 3)]
+    wave_piece(0, own)
+    came, state["wave"], *lasts = tie(came, state["wave"], *lasts)
     record(stay, came, begins, count)
     first_sent = (owners - 1, owners - 3) if ring else ()
     chunks, *sent = to_slots(slot_of, keeps, cames, lasts, tuple(groups), owners, slots, first_sent)
-
-    state = {}
-
-    def work(stage, *ready):
-        if stage in (0, 2):
-            feed = tie(spec, *ready)[0]
-            begin, end, before = ((0, tiles // 2, None), (tiles // 2, tiles, state.get("wave")))[stage // 2]
-            state["wave"] = wave_forward(begin, end, before, meta, feed, halo, synth, win, utts)
-            return "wave"
-        if stage in (1, 3):
-            row = stage // 2
-            feed = tie((cg0, cg1)[row], *ready)[0]
-            state["grad"] = conv_backward(
-                row, state.get("grad"), meta, feed, lasts[1], lasts[3], resg, table, rows, utts
-            )
-            return "grad"
-
     if ring:
         cut = {o: chunks[i * slots : (i + 1) * slots] for i, o in enumerate(offsets)}
         up, down = sent
@@ -1461,8 +1506,12 @@
             up = lax.ppermute(up, AXES, ring_step(ring, 1, seqs))
             if hop < half_ring - 1:
                 down = lax.ppermute(down, AXES, ring_step(ring, -1, seqs))
-            done = work(hop, *source)
-            up, down, state[done] = tie(up, down, state[done])
+            if hop < 2:
+                done = conv_piece(hop, *source)
+                up, down, state[done] = tie(up, down, state[done])
+            elif hop == 2:
+                done = wave_piece(1, *source)
+                up, down, state[done] = tie(up, down, state[done])
             if left_over:
                 up = plus(up, cut[left_over])
                 if hop < half_ring - 2:
@@ -1470,8 +1519,9 @@
         own = plus(cut[0], up, down)
     else:
         own = lax.psum_scatter(chunks, "rows", scatter_dimension=0, tiled=True)
-        for hop in range(4):
-            work(hop, own)
+        conv_piece(0, own)
+        conv_piece(1, own)
+        wave_piece(1, own)
     near, far = seq_swap(own, 1), seq_swap(own, 2)
     cross = seq_swap(far, 1)
     waveform = state["wave"].reshape(-1, rows, LANE).transpose(1, 0, 2).reshape(rows, frames * HOP)

time: 236 us -> 230 us (0.975)
  Pallas kernels: 162 us -> 152 us
  starting transfers between devices: 38.3 us -> 42.5 us
    ppermute x20, waiting for transfers between devices: 12.4 us -> 6.29 us  [seq_swap(): return lax.ppermute(value, 'seq', [(s, s ^ bit) for s in range(count)])]
    ppermute x4, waiting for transfers between devices: 0.01 us -> 5.29 us  [local(): up = lax.ppermute(up, AXES, ring_step(ring, 1, seqs))]
    pallas_call x1, Pallas kernels: 56.1 us -> 51.5 us  [forward(): pl.pallas_call(functools.partial(forward_body, owners=owners, slots=slots...]
    ppermute x20, starting transfers between devices: 16.3 us -> 20.8 us  [seq_swap(): return lax.ppermute(value, 'seq', [(s, s ^ bit) for s in range(count)])]
    ppermute x4, waiting for transfers between devices: 3.31 us -> 6.26 us  [local(): ahead = lax.ppermute(ahead, AXES, ring_step(ring, 1, seqs))]
    pallas_call x2 -> x1, Pallas kernels: 20.8 us -> 18.2 us  [norm_backward(): pl.pallas_call(functools.partial(norm_body, tiles=tiles, utts=utts), grid...]
    unnamed x66 -> x72, local copies, waits for them, and re-layouts: 5.23 us -> 4.74 us
  transfers between devices with their start and end apart: 38 -> 38, of which waited for: 12 -> 9; matrix products, arithmetic and copies ran while one was open for 2% -> 2% of each run, Pallas kernels for 43% -> 41%
where the time goes in v6:
time: 230 us; the launch traced here: 229 us
  Pallas kernels  152 us (66%)
  starting transfers between devices  42.5 us (18%)
  waiting for transfers between devices  20.7 us (9%)
  local copies, waits for them, and re-layouts  10.8 us (5%)
    pallas_call x1, Pallas kernels, forward(): pl.pallas_call(functools.partial(forward_body, owners=owners, slots=slots...  51.5 us
    pallas_call x2, Pallas kernels, mlp_backward(): pl.pallas_call(functools.partial(mlp_body, utts=utts), grid=(count // til...  21.1 us
    ppermute x20, starting transfers between devices, seq_swap(): return lax.ppermute(value, 'seq', [(s, s ^ bit) for s in range(count)])  20.8 us
    pallas_call x1, Pallas kernels, norm_backward(): pl.pallas_call(functools.partial(norm_body, tiles=tiles, utts=utts), grid...  18.2 us
    pallas_call x2, Pallas kernels, spectrum_cotangent(): pl.pallas_call(functools.partial(pre_body, start=start, tiles=tiles, rows...  15.1 us
    pallas_call x2, Pallas kernels, wave_forward(): pl.pallas_call(functools.partial(wave_body, start=start, rows=rows, utts=...  14.1 us
    pallas_call x2, Pallas kernels, conv_backward(): pl.pallas_call(functools.partial(conv_body, row=row, tiles=tiles, utts=ut...  9.72 us
    pallas_call x2, Pallas kernels, adam(): pl.pallas_call(functools.partial(adam_body, block=block), grid_spec=pltpu...  9.2 us
  transfers between devices with their start and end apart: 38, of which 9 were waited for; matrix products, arithmetic and copies ran while one was open for 2% of the time, Pallas kernels for 41%

profile of v6, /device:TPU:0, one launch (start us, length us, event | category | flops | bytes accessed | tf_op | source)
XLA Modules:
  0.0 229.2 jit_solution(2826672894216508146)
XLA Ops:
  0.6 1.2 dynamic-slice_convert_fusion.refs_0_
  1.9 3.1 %collective-permute-start = (bf16[27,16,512]{2,1,0:T(8,128)(2,1)S(1)}, bf16[27,16,512]{2,1,0:T(8,128)(2,1)S(1)}, u32[]{:S(2)}, u32[]{:S(2)}) collective-permute-start(bf16[27,16,512]{2,1,0:T(8,128)(2,1)S(1)} %dynamic-slice_convert_fusion.refs_0_), channel_id=1, source_target_pairs={{0,8},{1,9},{2,10},{3,11},{8,16},{9,17},{10,18},{11,19},{16,24},{1... | collective-permute-start | bytes 1327112 | tf_op jit(solution)/shard_map/ppermute | solution.py:1400
  5.0 0.7 slice.44
  5.7 1.3 collective-permute-start.2
  7.6 4.0 %plan.1 = (s32[2,12]{1,0:T(2,128)}, s32[1,216]{1,0:T(1,128)}, s32[1,27]{1,0:T(1,128)}, s32[1,137]{1,0:T(1,128)}, s32[1,8]{1,0:T(1,128)}) custom-call(s32[2]{0:T(128)} %pad_add_fusion.ids, s32[2,4]{1,0:T(2,128)} %lengths.1, s32[2,4]{1,0:T(2,128)} %bw_ids.1, s32[137]{0:T(256)} %owner_list.1, s32[8]{0:T(128)} %constant.54.clone.order, s32[8]{0:T(128)} %constant.55.clone.offsets), custom_call_target="tpu_custom_call" | custom-call | flops 8000 | bytes 8192 | tf_op jit(solution)/shard_map/plan/pallas_call | solution.py:259
  11.6 3.4 %collective-permute-done.refs_2_ = bf16[27,16,512]{2,1,0:T(8,128)(2,1)S(1)} collective-permute-done((bf16[27,16,512]{2,1,0:T(8,128)(2,1)S(1)}, bf16[27,16,512]{2,1,0:T(8,128)(2,1)S(1)}, u32[]{:S(2)}, u32[]{:S(2)}) %collective-permute-start) | collective-permute-done | bytes 442400 | tf_op jit(solution)/shard_map/ppermute | solution.py:1400
  15.1 1.5 collective-permute-done.1.refs_4_
  16.6 1.6 collective-permute-start.3
  18.6 0.8 fusion
  19.4 1.3 collective-permute-start.5
  20.7 1.3 collective-permute-start.6
  22.0 7.5 %spectrum_cotangent_0.1.rest_0_ = bf16[2,1024,1536]{2,1,0:T(8,128)(2,1)} custom-call(s32[2,12]{1,0:T(2,128)} %get-tuple-element.108.meta, bf16[5120,128]{1,0:T(8,128)(2,1)} %bitcast.33, bf16[80,128]{1,0:T(8,128)(2,1)} %copy-done.27, bf16[2,768,768]{2,1,0:T(8,128)(2,1)} %constant.52.clone.synth_ref, f32[8,384]{1,0:T(8,128)} %constant.53.clone.win_ref), custom_call_target="tpu_custom_call" | custom-call | flops 2415919104 | bytes 7340032 | tf_op jit(solution)/shard_map/spectrum_cotangent_0/pallas_call | solution.py:329
  29.6 1.6 collective-permute-start.7
  31.7 2.3 %collective-permute-start.10 = (bf16[27,16,512]{2,1,0:T(8,128)(2,1)S(1)}, bf16[27,16,512]{2,1,0:T(8,128)(2,1)S(1)}, u32[]{:S(2)}, u32[]{:S(2)}) collective-permute-start(bf16[27,16,512]{2,1,0:T(8,128)(2,1)S(1)} %dynamic-slice_convert_fusion.refs_0_), channel_id=1, source_target_pairs={{0,1},{1,0},{2,3},{3,2},{4,5},{5,4},{6,7},{7,6},{8,9},{9,8},{10,11... | collective-permute-start | bytes 1327112 | tf_op jit(solution)/shard_map/ppermute | solution.py:106
  34.5 7.6 %spectrum_cotangent_2.1.cot_ref = bf16[2,1024,1536]{2,1,0:T(8,128)(2,1)} custom-call(s32[2,12]{1,0:T(2,128)} %get-tuple-element.108.meta, bf16[5120,128]{1,0:T(8,128)(2,1)} %bitcast.34, bf16[80,128]{1,0:T(8,128)(2,1)} %copy-done.27, bf16[2,768,768]{2,1,0:T(8,128)(2,1)} %constant.52.clone.synth_ref, ...), custom_call_target="tpu_custom_call", output_to_operand_aliasing={{}: (5, {})} | custom-call | flops 2415919104 | bytes 7340032 | tf_op jit(solution)/shard_map/spectrum_cotangent_2/pallas_call | solution.py:329
  42.7 1.4 collective-permute-start.14
  44.6 1.6 collective-permute-start.9
  47.9 6.0 %assemble.1.rest_2_ = bf16[4384,512]{1,0:T(8,128)(2,1)} custom-call(s32[2,12]{1,0:T(2,128)} %get-tuple-element.108.meta, s32[1,216]{1,0:T(1,128)} %get-tuple-element.127.places, s32[1,8]{1,0:T(1,128)} %get-tuple-element.110.counts, bf16[27,16,512]{2,1,0:T(8,128)(2,1)} %copy-done, bf16[27,16,512]{2,1,0:T(8,128)(2,1)} %copy-done.12, ...), custom_call_target="tpu_custom_call" | custom-call | bytes 12582912 | tf_op jit(solution)/shard_map/assemble/pallas_call | solution.py:379
  54.0 2.8 %collective-permute-done.9.rest_0_ = bf16[27,16,512]{2,1,0:T(8,128)(2,1)S(1)} collective-permute-done((bf16[27,16,512]{2,1,0:T(8,128)(2,1)S(1)}, bf16[27,16,512]{2,1,0:T(8,128)(2,1)S(1)}, u32[]{:S(2)}, u32[]{:S(2)}) %collective-permute-start.9) | collective-permute-done | bytes 442400 | tf_op jit(solution)/shard_map/ppermute | solution.py:1400
  56.8 1.8 collective-permute-done.17.rest_1_
  58.6 0.8 copy-done.32
  59.4 51.5 %forward.1 = (bf16[4384,512]{1,0:T(8,128)(2,1)}, bf16[2,1024,1536]{2,1,0:T(8,128)(2,1)}, bf16[2048,1536]{1,0:T(8,128)(2,1)}, bf16[2048,1536]{1,0:T(8,128)(2,1)},...) custom-call(s32[2,12]{1,0:T(2,128)} %get-tuple-element.108.meta, ...), custom_call_target="tpu_custom_call" | custom-call | flops 16106127360 | bytes 41943040 | tf_op jit(solution)/shard_map/forward/pallas_call | solution.py:787
  111.1 10.5 %mlp_backward_0.1 = (bf16[2048,1536]{1,0:T(8,128)(2,1)}, bf16[48,16,512]{2,1,0:T(8,128)(2,1)}, bf16[48,16,512]{2,1,0:T(8,128)(2,1)}, f32[8,768]{1,0:T(8,128)}) custom-call(s32[2,12]{1,0:T(2,128)} %get-tuple-element.108.meta, bf16[2048,512]{1,0:T(8,128)(2,1)} %get-tuple-element.132.low_ref, bf16[2048,1536]{1,0:T(8,128)(2,1)} %get-tuple-element.133.act_ref, ...), custom_call_target="tpu_custom_call" | custom-call | flops 4831838208 | bytes 16777216 | tf_op jit(solution)/shard_map/mlp_backward_0/pallas_call | solution.py:898
  122.3 0.8 constant_dynamic-slice_fusion.2
  123.1 2.6 %collective-permute-start.22 = (bf16[40,8,512]{2,1,0:T(8,128)(2,1)S(1)}, bf16[40,8,512]{2,1,0:T(8,128)(2,1)S(1)}, u32[]{:S(2)}, u32[]{:S(2)}) collective-permute-start(bf16[40,8,512]{2,1,0:T(8,128)(2,1)S(1)} %get-tuple-element.217), channel_id=1, source_target_pairs={{0,2},{1,3},{2,0},{3,1},{4,6},{5,7},{6,4},{7,5},{8,10},{9,11},{10,... | collective-permute-start | bytes 983048 | tf_op jit(solution)/shard_map/ppermute | solution.py:106
  125.7 10.5 %mlp_backward_1.1 = (bf16[2048,1536]{1,0:T(8,128)(2,1)}, bf16[48,16,512]{2,1,0:T(8,128)(2,1)}, bf16[48,16,512]{2,1,0:T(8,128)(2,1)}, f32[8,768]{1,0:T(8,128)}) custom-call(s32[2,12]{1,0:T(2,128)} %get-tuple-element.108.meta, bf16[2048,512]{1,0:T(8,128)(2,1)} %get-tuple-element.132.low_ref, ...), custom_call_target="tpu_custom_call", output_to_operand_aliasing={{0}: (6, {})} | custom-call | flops 4831838208 | bytes 16777216 | tf_op jit(solution)/shard_map/mlp_backward_1/pallas_call | solution.py:898
  136.7 0.8 constant_dynamic-slice_fusion.3
  137.7 18.2 %norm_backward.1 = (bf16[2048,512]{1,0:T(8,128)(2,1)}, f32[8,512]{1,0:T(8,128)}, f32[24,512]{1,0:T(8,128)}, f32[8,512]{1,0:T(8,128)}, f32[24,512]{1,0:T(8,128)}) custom-call(s32[2,12]{1,0:T(2,128)} %get-tuple-element.108.meta, bf16[2,1024,512]{2,1,0:T(8,128)(2,1)} %x_ref.3, bf16[2,16,512]{2,1,0:T(8,128)(2,1)} %copy-done.28, bf16[2,16,512]{2,1,0:T(8,128)(2,1)} %copy-done.29, ...), custom_call_target="tpu_custom_call" | custom-call | flops 3221225472 | bytes 20971520 | tf_op jit(solution)/shard_map/norm_backward/pallas_call | solution.py:1099
  156.3 0.8 constant_dynamic-slice_fusion
  157.1 1.7 collective-permute-start.23
  158.8 0.9 slice.37
  159.7 1.9 collective-permute-start.24
  162.1 1.5 collective-permute-start.27
  164.2 7.1 %wave_forward_0.1.rest_0_ = f32[5120,128]{1,0:T(8,128)} custom-call(s32[2,12]{1,0:T(2,128)} %get-tuple-element.108.meta, bf16[2,1024,1536]{2,1,0:T(8,128)(2,1)} %get-tuple-element.190.spec_ref.prev_ref, bf16[2,1024,1536]{2,1,0:T(8,128)(2,1)} %get-tuple-element.190.spec_ref.prev_ref, bf16[2,16,1536]{2,1,0:T(8,128)(2,1)} %copy-done.20, ...), custom_call_target="tpu_custom_call" | custom-call | flops 2415919104 | bytes 10485760 | tf_op jit(solution)/shard_map/wave_forward_0/pallas_call | solution.py:1239
  172.1 3.2 %to_slots.1 = (bf16[216,8,512]{2,1,0:T(8,128)(2,1)}, bf16[27,8,512]{2,1,0:T(8,128)(2,1)}, bf16[27,8,512]{2,1,0:T(8,128)(2,1)}) custom-call(s32[1,137]{1,0:T(1,128)} %get-tuple-element.106.slot_of, bf16[40,8,512]{2,1,0:T(8,128)(2,1)} %get-tuple-element.218.refs_0_, bf16[48,8,512]{2,1,0:T(8,128)(2,1)} %get-tuple-element.216.refs_1_, ...), custom_call_target="tpu_custom_call" | custom-call | bytes 6291456 | tf_op jit(solution)/shard_map/to_slots/pallas_call | solution.py:1287
  175.3 1.6 collective-permute-start.28
  177.4 4.9 %conv_backward_0.1.rest_0_ = f32[2,1024,512]{2,1,0:T(8,128)} custom-call(s32[2,12]{1,0:T(2,128)} %get-tuple-element.108.meta, bf16[2048,512]{1,0:T(8,128)(2,1)} %get-tuple-element.186.cg_ref.before_ref.after_ref, bf16[2048,512]{1,0:T(8,128)(2,1)} %get-tuple-element.186.cg_ref.before_ref.after_ref, ...), custom_call_target="tpu_custom_call" | custom-call | flops 8388608 | bytes 6291456 | tf_op jit(solution)/shard_map/conv_backward_0/pallas_call | solution.py:1167
  183.1 1.5 collective-permute-start.30
  185.2 4.8 %conv_backward_1.1 = f32[2,1024,512]{2,1,0:T(8,128)} custom-call(s32[2,12]{1,0:T(2,128)} %get-tuple-element.108.meta, bf16[2048,512]{1,0:T(8,128)(2,1)} %get-tuple-element.186.cg_ref.before_ref.after_ref, bf16[2048,512]{1,0:T(8,128)(2,1)} %get-tuple-element.186.cg_ref.before_ref.after_ref, ...), custom_call_target="tpu_custom_call", output_to_operand_aliasing={{}: (8, {})} | custom-call | flops 8388608 | bytes 6291456 | tf_op jit(solution)/shard_map/conv_backward_1/pallas_call | solution.py:1167
  190.7 1.0 collective-permute-start.32
  191.7 1.1 collective-permute-start.33
  192.8 7.0 %wave_forward_2.1 = f32[5120,128]{1,0:T(8,128)} custom-call(s32[2,12]{1,0:T(2,128)} %get-tuple-element.108.meta, bf16[2,1024,1536]{2,1,0:T(8,128)(2,1)} %get-tuple-element.190.spec_ref.prev_ref, bf16[2,1024,1536]{2,1,0:T(8,128)(2,1)} %get-tuple-element.190.spec_ref.prev_ref, bf16[2,16,1536]{2,1,0:T(8,128)(2,1)} %copy-done.20, ...), custom_call_target="tpu_custom_call", output_to_operand_aliasing={{}: (6, {})} | custom-call | flops 2415919104 | bytes 10485760 | tf_op jit(solution)/shard_map/wave_forward_2/pallas_call | solution.py:1239
  199.9 1.0 collective-permute-start.34
  200.9 5.3 %collective-permute-done.34 = bf16[27,8,512]{2,1,0:T(8,128)(2,1)S(1)} collective-permute-done((bf16[27,8,512]{2,1,0:T(8,128)(2,1)S(1)}, bf16[27,8,512]{2,1,0:T(8,128)(2,1)S(1)}, u32[]{:S(2)}, u32[]{:S(2)}) %collective-permute-start.34) | collective-permute-done | bytes 221216 | tf_op jit(solution)/shard_map/ppermute | solution.py:1506
  206.3 8.4 %collective-permute-start.35 = (bf16[27,8,512]{2,1,0:T(8,128)(2,1)S(1)}, bf16[27,8,512]{2,1,0:T(8,128)(2,1)S(1)}, u32[]{:S(2)}, u32[]{:S(2)}) collective-permute-start(bf16[27,8,512]{2,1,0:T(8,128)(2,1)S(1)} %add_convert_fusion.3.mine_ref), channel_id=1, source_target_pairs={{0,2},{1,3},{2,0},{3,1},{4,6},{5,7},{6,4},{7,5},{8,10},{9,11},{10,... | collective-permute-start | bytes 663560 | tf_op jit(solution)/shard_map/ppermute | solution.py:106
  214.6 3.9 %collective-permute-done.35.mine_ref = bf16[27,8,512]{2,1,0:T(8,128)(2,1)S(1)} collective-permute-done((bf16[27,8,512]{2,1,0:T(8,128)(2,1)S(1)}, bf16[27,8,512]{2,1,0:T(8,128)(2,1)S(1)}, u32[]{:S(2)}, u32[]{:S(2)}) %collective-permute-start.35) | collective-permute-done | bytes 221216 | tf_op jit(solution)/shard_map/ppermute | solution.py:106
  219.3 4.6 %adam_first.1 = (f32[27,2,2,8,512]{4,3,2,1,0:T(8,128)}, f32[27,2,2,8,512]{4,3,2,1,0:T(8,128)}, f32[27,2,2,8,512]{4,3,2,1,0:T(8,128)}) custom-call(s32[1,27]{1,0:T(1,128)} %get-tuple-element.194.places, s32[2,12]{1,0:T(2,128)} %get-tuple-element.108.meta, bf16[27,8,512]{2,1,0:T(8,128)(2,1)} %copy-done.2, bf16[27,8,512]{2,1,0:T(8,128)(2,1)} %copy-done.26, ...), custom_call_target="tpu_custom_call" | custom-call | bytes 6291456 | tf_op jit(solution)/shard_map/adam_first/pallas_call | solution.py:1330
  224.6 4.6 %adam_second.1 = (f32[27,2,2,8,512]{4,3,2,1,0:T(8,128)}, f32[27,2,2,8,512]{4,3,2,1,0:T(8,128)}, f32[27,2,2,8,512]{4,3,2,1,0:T(8,128)}) custom-call(s32[1,27]{1,0:T(1,128)} %get-tuple-element.194.places, s32[2,12]{1,0:T(2,128)} %get-tuple-element.108.meta, bf16[27,8,512]{2,1,0:T(8,128)(2,1)} %copy-done.24, ...), custom_call_target="tpu_custom_call", output_to_operand_aliasing={{0}: (7, {}), {1}: (8, {}), {2}: (9, {})} | custom-call | bytes 6291456 | tf_op jit(solution)/shard_map/adam_second/pallas_call | solution.py:1330
  (130 shorter events, 12.6 us)
Async XLA Ops:
  1.9 29.8 %copy-start = (bf16[27,16,512]{2,1,0:T(8,128)(2,1)}, bf16[27,16,512]{2,1,0:T(8,128)(2,1)S(1)}, u32[]{:S(2)}) copy-start(bf16[27,16,512]{2,1,0:T(8,128)(2,1)S(1)} %dynamic-slice_convert_fusion.refs_0_) | copy-start | bytes 1327108
  1.9 13.2 %collective-permute-start = (bf16[27,16,512]{2,1,0:T(8,128)(2,1)S(1)}, bf16[27,16,512]{2,1,0:T(8,128)(2,1)S(1)}, u32[]{:S(2)}, u32[]{:S(2)}) collective-permute-start(bf16[27,16,512]{2,1,0:T(8,128)(2,1)S(1)} %dynamic-slice_convert_fusion.refs_0_), channel_id=1, source_target_pairs={{0,8},{1,9},{2,10},{3,11},{8,16},{9,17},{10,18},{11,19},{16,24},{1... | collective-permute-start | bytes 1327112 | tf_op jit(solution)/shard_map/ppermute | solution.py:1400
  5.0 11.6 %collective-permute-start.1 = (bf16[27,16,512]{2,1,0:T(8,128)(2,1)S(1)}, bf16[27,16,512]{2,1,0:T(8,128)(2,1)S(1)}, u32[]{:S(2)}, u32[]{:S(2)}) collective-permute-start(bf16[27,16,512]{2,1,0:T(8,128)(2,1)S(1)} %dynamic-slice_convert_fusion.refs_0_), channel_id=1, source_target_pairs={{0,4},{1,5},{2,6},{3,7},{8,0},{9,1},{10,2},{11,3},{16,8},{17,9},{1... | collective-permute-start | bytes 1327112 | tf_op jit(solution)/shard_map/ppermute | solution.py:1402
  5.7 5.9 %collective-permute-start.2 = (bf16[80,128]{1,0:T(8,128)(2,1)S(1)}, bf16[80,128]{1,0:T(8,128)(2,1)S(1)}, u32[]{:S(2)}, u32[]{:S(2)}) collective-permute-start(bf16[80,128]{1,0:T(8,128)(2,1)S(1)} %bitcast.38), channel_id=1, source_target_pairs={{1,0},{2,1},{3,2},{5,4},{6,5},{7,6},{9,8},{10,9},{11,10},{13,12},{... | collective-permute-start | bytes 61448 | tf_op jit(solution)/shard_map/ppermute | solution.py:116
  15.1 19.0 %copy-start.6 = (bf16[27,16,512]{2,1,0:T(8,128)(2,1)}, bf16[27,16,512]{2,1,0:T(8,128)(2,1)S(1)}, u32[]{:S(2)}) copy-start(bf16[27,16,512]{2,1,0:T(8,128)(2,1)S(1)} %collective-permute-done.refs_2_) | copy-start | bytes 1327108
  16.6 17.5 %copy-start.7 = (bf16[27,16,512]{2,1,0:T(8,128)(2,1)}, bf16[27,16,512]{2,1,0:T(8,128)(2,1)S(1)}, u32[]{:S(2)}) copy-start(bf16[27,16,512]{2,1,0:T(8,128)(2,1)S(1)} %collective-permute-done.1.refs_4_) | copy-start | bytes 1327108
  16.6 13.0 %collective-permute-start.3 = (bf16[27,16,512]{2,1,0:T(8,128)(2,1)S(1)}, bf16[27,16,512]{2,1,0:T(8,128)(2,1)S(1)}, u32[]{:S(2)}, u32[]{:S(2)}) collective-permute-start(bf16[27,16,512]{2,1,0:T(8,128)(2,1)S(1)} %collective-permute-done.refs_2_), channel_id=1, source_target_pairs={{0,8},{1,9},{2,10},{3,11},{8,16},{9,17},{10,18},{11,19},{16,24},{1... | collective-permute-start | bytes 1327112 | tf_op jit(solution)/shard_map/ppermute | solution.py:1400
  18.2 11.4 %collective-permute-start.4 = (bf16[27,16,512]{2,1,0:T(8,128)(2,1)S(1)}, bf16[27,16,512]{2,1,0:T(8,128)(2,1)S(1)}, u32[]{:S(2)}, u32[]{:S(2)}) collective-permute-start(bf16[27,16,512]{2,1,0:T(8,128)(2,1)S(1)} %collective-permute-done.1.refs_4_), channel_id=1, source_target_pairs={{0,4},{1,5},{2,6},{3,7},{8,0},{9,1},{10,2},{11,3},{16,8},{17,9},{1... | collective-permute-start | bytes 1327112 | tf_op jit(solution)/shard_map/ppermute | solution.py:1402
  19.4 10.1 %collective-permute-start.5 = (bf16[2,16,512]{2,1,0:T(8,128)(2,1)S(1)}, bf16[2,16,512]{2,1,0:T(8,128)(2,1)S(1)}, u32[]{:S(2)}, u32[]{:S(2)}) collective-permute-start(bf16[2,16,512]{2,1,0:T(8,128)(2,1)S(1)} %get-tuple-element.208), channel_id=1, source_target_pairs={{0,1},{1,2},{2,3},{4,5},{5,6},{6,7},{8,9},{9,10},{10,11},{12,13},{... | collective-permute-start | bytes 98312 | tf_op jit(solution)/shard_map/ppermute | solution.py:116
  20.7 8.9 %collective-permute-start.6 = (bf16[2,16,512]{2,1,0:T(8,128)(2,1)S(1)}, bf16[2,16,512]{2,1,0:T(8,128)(2,1)S(1)}, u32[]{:S(2)}, u32[]{:S(2)}) collective-permute-start(bf16[2,16,512]{2,1,0:T(8,128)(2,1)S(1)} %get-tuple-element.207), channel_id=1, source_target_pairs={{1,0},{2,1},{3,2},{5,4},{6,5},{7,6},{9,8},{10,9},{11,10},{13,12},{... | collective-permute-start | bytes 98312 | tf_op jit(solution)/shard_map/ppermute | solution.py:116
  29.6 12.6 %copy-start.28 = (bf16[2,16,512]{2,1,0:T(8,128)(2,1)}, bf16[2,16,512]{2,1,0:T(8,128)(2,1)S(1)}, u32[]{:S(2)}) copy-start(bf16[2,16,512]{2,1,0:T(8,128)(2,1)S(1)} %collective-permute-done.5.low_ref) | copy-start | bytes 98308
  29.6 12.6 %copy-start.29 = (bf16[2,16,512]{2,1,0:T(8,128)(2,1)}, bf16[2,16,512]{2,1,0:T(8,128)(2,1)S(1)}, u32[]{:S(2)}) copy-start(bf16[2,16,512]{2,1,0:T(8,128)(2,1)S(1)} %collective-permute-done.6.high_ref) | copy-start | bytes 98308
  29.6 12.6 %copy-start.8 = (bf16[27,16,512]{2,1,0:T(8,128)(2,1)}, bf16[27,16,512]{2,1,0:T(8,128)(2,1)S(1)}, u32[]{:S(2)}) copy-start(bf16[27,16,512]{2,1,0:T(8,128)(2,1)S(1)} %collective-permute-done.3.refs_6_) | copy-start | bytes 1327108
  29.6 13.1 %copy-start.9 = (bf16[27,16,512]{2,1,0:T(8,128)(2,1)}, bf16[27,16,512]{2,1,0:T(8,128)(2,1)S(1)}, u32[]{:S(2)}) copy-start(bf16[27,16,512]{2,1,0:T(8,128)(2,1)S(1)} %collective-permute-done.4.refs_8_) | copy-start | bytes 1327108
  29.6 12.5 %collective-permute-start.7 = (bf16[27,16,512]{2,1,0:T(8,128)(2,1)S(1)}, bf16[27,16,512]{2,1,0:T(8,128)(2,1)S(1)}, u32[]{:S(2)}, u32[]{:S(2)}) collective-permute-start(bf16[27,16,512]{2,1,0:T(8,128)(2,1)S(1)} %collective-permute-done.3.refs_6_), channel_id=1, source_target_pairs={{0,8},{1,9},{2,10},{3,11},{8,16},{9,17},{10,18},{11,19},{16,24},{1... | collective-permute-start | bytes 1327112 | tf_op jit(solution)/shard_map/ppermute | solution.py:1400
  31.2 11.5 %collective-permute-start.8 = (bf16[27,16,512]{2,1,0:T(8,128)(2,1)S(1)}, bf16[27,16,512]{2,1,0:T(8,128)(2,1)S(1)}, u32[]{:S(2)}, u32[]{:S(2)}) collective-permute-start(bf16[27,16,512]{2,1,0:T(8,128)(2,1)S(1)} %collective-permute-done.4.refs_8_), channel_id=1, source_target_pairs={{0,4},{1,5},{2,6},{3,7},{8,0},{9,1},{10,2},{11,3},{16,8},{17,9},{1... | collective-permute-start | bytes 1327112 | tf_op jit(solution)/shard_map/ppermute | solution.py:1402
  31.7 12.4 %collective-permute-start.10 = (bf16[27,16,512]{2,1,0:T(8,128)(2,1)S(1)}, bf16[27,16,512]{2,1,0:T(8,128)(2,1)S(1)}, u32[]{:S(2)}, u32[]{:S(2)}) collective-permute-start(bf16[27,16,512]{2,1,0:T(8,128)(2,1)S(1)} %dynamic-slice_convert_fusion.refs_0_), channel_id=1, source_target_pairs={{0,1},{1,0},{2,3},{3,2},{4,5},{5,4},{6,7},{7,6},{8,9},{9,8},{10,11... | collective-permute-start | bytes 1327112 | tf_op jit(solution)/shard_map/ppermute | solution.py:106
  34.0 10.2 %collective-permute-start.11 = (bf16[27,16,512]{2,1,0:T(8,128)(2,1)S(1)}, bf16[27,16,512]{2,1,0:T(8,128)(2,1)S(1)}, u32[]{:S(2)}, u32[]{:S(2)}) collective-permute-start(bf16[27,16,512]{2,1,0:T(8,128)(2,1)S(1)} %collective-permute-done.refs_2_), channel_id=1, source_target_pairs={{0,1},{1,0},{2,3},{3,2},{4,5},{5,4},{6,7},{7,6},{8,9},{9,8},{10,11... | collective-permute-start | bytes 1327112 | tf_op jit(solution)/shard_map/ppermute | solution.py:106
  34.1 10.5 %collective-permute-start.12 = (bf16[27,16,512]{2,1,0:T(8,128)(2,1)S(1)}, bf16[27,16,512]{2,1,0:T(8,128)(2,1)}, u32[]{:S(2)}, u32[]{:S(2)}) collective-permute-start(bf16[27,16,512]{2,1,0:T(8,128)(2,1)S(1)} %collective-permute-done.1.refs_4_), channel_id=1, source_target_pairs={{0,1},{1,0},{2,3},{3,2},{4,5},{5,4},{6,7},{7,6},{8,9},{9,8},{10,11... | collective-permute-start | bytes 1327112 | tf_op jit(solution)/shard_map/ppermute | solution.py:106
  42.2 4.0 %collective-permute-start.13 = (bf16[27,16,512]{2,1,0:T(8,128)(2,1)S(1)}, bf16[27,16,512]{2,1,0:T(8,128)(2,1)S(1)}, u32[]{:S(2)}, u32[]{:S(2)}) collective-permute-start(bf16[27,16,512]{2,1,0:T(8,128)(2,1)S(1)} %collective-permute-done.3.refs_6_), channel_id=1, source_target_pairs={{0,1},{1,0},{2,3},{3,2},{4,5},{5,4},{6,7},{7,6},{8,9},{9,8},{10,11... | collective-permute-start | bytes 1327112 | tf_op jit(solution)/shard_map/ppermute | solution.py:106
  42.7 3.5 %collective-permute-start.14 = (bf16[27,16,512]{2,1,0:T(8,128)(2,1)S(1)}, bf16[27,16,512]{2,1,0:T(8,128)(2,1)S(1)}, u32[]{:S(2)}, u32[]{:S(2)}) collective-permute-start(bf16[27,16,512]{2,1,0:T(8,128)(2,1)S(1)} %collective-permute-done.4.refs_8_), channel_id=1, source_target_pairs={{0,1},{1,0},{2,3},{3,2},{4,5},{5,4},{6,7},{7,6},{8,9},{9,8},{10,11... | collective-permute-start | bytes 1327112 | tf_op jit(solution)/shard_map/ppermute | solution.py:106
  44.1 2.1 collective-permute-start.15
  44.2 2.6 %collective-permute-start.16 = (bf16[27,16,512]{2,1,0:T(8,128)(2,1)S(1)}, bf16[27,16,512]{2,1,0:T(8,128)(2,1)S(1)}, u32[]{:S(2)}, u32[]{:S(2)}) collective-permute-start(bf16[27,16,512]{2,1,0:T(8,128)(2,1)S(1)} %collective-permute-done.8.refs_12_), channel_id=1, source_target_pairs={{0,1},{1,0},{2,3},{3,2},{4,5},{5,4},{6,7},{7,6},{8,9},{9,8},{10,11... | collective-permute-start | bytes 1327112 | tf_op jit(solution)/shard_map/ppermute | solution.py:106
  44.6 12.2 %collective-permute-start.9 = (bf16[27,16,512]{2,1,0:T(8,128)(2,1)S(1)}, bf16[27,16,512]{2,1,0:T(8,128)(2,1)S(1)}, u32[]{:S(2)}, u32[]{:S(2)}) collective-permute-start(bf16[27,16,512]{2,1,0:T(8,128)(2,1)S(1)} %collective-permute-done.7.refs_10_), channel_id=1, source_target_pairs={{0,8},{1,9},{2,10},{3,11},{8,16},{9,17},{10,18},{11,19},{16,24},{1... | collective-permute-start | bytes 1327112 | tf_op jit(solution)/shard_map/ppermute | solution.py:1400
  56.8 1.8 collective-permute-start.17
  110.9 10.7 %collective-permute-start.18 = (bf16[40,16,512]{2,1,0:T(8,128)(2,1)}, bf16[40,16,512]{2,1,0:T(8,128)(2,1)S(1)}, u32[]{:S(2)}, u32[]{:S(2)}) collective-permute-start(bf16[40,16,512]{2,1,0:T(8,128)(2,1)} %get-tuple-element.131), channel_id=1, source_target_pairs={{0,1},{1,0},{2,3},{3,2},{4,5},{5,4},{6,7},{7,6},{8,9},{9,8},{10,11... | collective-permute-start | bytes 1966088 | tf_op jit(solution)/shard_map/ppermute | solution.py:106
  121.6 14.6 %collective-permute-start.19 = (bf16[48,16,512]{2,1,0:T(8,128)(2,1)}, bf16[48,16,512]{2,1,0:T(8,128)(2,1)S(1)}, u32[]{:S(2)}, u32[]{:S(2)}) collective-permute-start(bf16[48,16,512]{2,1,0:T(8,128)(2,1)} %get-tuple-element.142), channel_id=1, source_target_pairs={{0,1},{1,0},{2,3},{3,2},{4,5},{5,4},{6,7},{7,6},{8,9},{9,8},{10,11... | collective-permute-start | bytes 2359304 | tf_op jit(solution)/shard_map/ppermute | solution.py:106
  123.1 13.2 %copy-start.4 = (bf16[48,16,512]{2,1,0:T(8,128)(2,1)S(1)}, bf16[48,16,512]{2,1,0:T(8,128)(2,1)}, u32[]{:S(2)}) copy-start(bf16[48,16,512]{2,1,0:T(8,128)(2,1)} %get-tuple-element.141) | copy-start | bytes 2359300
  123.1 14.6 %collective-permute-start.22 = (bf16[40,8,512]{2,1,0:T(8,128)(2,1)S(1)}, bf16[40,8,512]{2,1,0:T(8,128)(2,1)S(1)}, u32[]{:S(2)}, u32[]{:S(2)}) collective-permute-start(bf16[40,8,512]{2,1,0:T(8,128)(2,1)S(1)} %get-tuple-element.217), channel_id=1, source_target_pairs={{0,2},{1,3},{2,0},{3,1},{4,6},{5,7},{6,4},{7,5},{8,10},{9,11},{10,... | collective-permute-start | bytes 983048 | tf_op jit(solution)/shard_map/ppermute | solution.py:106
  136.3 19.6 %collective-permute-start.20 = (bf16[48,16,512]{2,1,0:T(8,128)(2,1)}, bf16[48,16,512]{2,1,0:T(8,128)(2,1)S(1)}, u32[]{:S(2)}, u32[]{:S(2)}) collective-permute-start(bf16[48,16,512]{2,1,0:T(8,128)(2,1)} %get-tuple-element.149), channel_id=1, source_target_pairs={{0,1},{1,0},{2,3},{3,2},{4,5},{5,4},{6,7},{7,6},{8,9},{9,8},{10,11... | collective-permute-start | bytes 2359304 | tf_op jit(solution)/shard_map/ppermute | solution.py:106
  137.5 18.4 %collective-permute-start.21 = (bf16[48,8,512]{2,1,0:T(8,128)(2,1)S(1)}, bf16[48,8,512]{2,1,0:T(8,128)(2,1)S(1)}, u32[]{:S(2)}, u32[]{:S(2)}) collective-permute-start(bf16[48,8,512]{2,1,0:T(8,128)(2,1)S(1)} %get-tuple-element.215), channel_id=1, source_target_pairs={{0,2},{1,3},{2,0},{3,1},{4,6},{5,7},{6,4},{7,5},{8,10},{9,11},{10,... | collective-permute-start | bytes 1179656 | tf_op jit(solution)/shard_map/ppermute | solution.py:106
  137.7 18.2 %copy-start.23 = (bf16[40,8,512]{2,1,0:T(8,128)(2,1)}, bf16[40,8,512]{2,1,0:T(8,128)(2,1)S(1)}, u32[]{:S(2)}) copy-start(bf16[40,8,512]{2,1,0:T(8,128)(2,1)S(1)} %collective-permute-done.22.refs_3_) | copy-start | bytes 983044
  137.7 18.2 %copy-start.3 = (bf16[48,16,512]{2,1,0:T(8,128)(2,1)S(1)}, bf16[48,16,512]{2,1,0:T(8,128)(2,1)}, u32[]{:S(2)}) copy-start(bf16[48,16,512]{2,1,0:T(8,128)(2,1)} %get-tuple-element.148) | copy-start | bytes 2359300
  157.1 14.2 %collective-permute-start.23 = (bf16[48,8,512]{2,1,0:T(8,128)(2,1)S(1)}, bf16[48,8,512]{2,1,0:T(8,128)(2,1)S(1)}, u32[]{:S(2)}, u32[]{:S(2)}) collective-permute-start(bf16[48,8,512]{2,1,0:T(8,128)(2,1)S(1)} %get-tuple-element.213), channel_id=1, source_target_pairs={{0,2},{1,3},{2,0},{3,1},{4,6},{5,7},{6,4},{7,5},{8,10},{9,11},{10,... | collective-permute-start | bytes 1179656 | tf_op jit(solution)/shard_map/ppermute | solution.py:106
  159.7 3.9 %collective-permute-start.24 = (bf16[2,16,1536]{2,1,0:T(8,128)(2,1)S(1)}, bf16[2,16,1536]{2,1,0:T(8,128)(2,1)S(1)}, u32[]{:S(2)}, u32[]{:S(2)}) collective-permute-start(bf16[2,16,1536]{2,1,0:T(8,128)(2,1)S(1)} %slice.37), channel_id=1, source_target_pairs={{0,1},{1,2},{2,3},{4,5},{5,6},{6,7},{8,9},{9,10},{10,11},{12,13},{... | collective-permute-start | bytes 294920 | tf_op jit(solution)/shard_map/ppermute | solution.py:116
  161.6 9.6 %collective-permute-start.25 = (f32[24,512]{1,0:T(8,128)S(1)}, f32[24,512]{1,0:T(8,128)S(1)}, u32[]{:S(2)}, u32[]{:S(2)}) collective-permute-start(f32[24,512]{1,0:T(8,128)S(1)} %copy-done.34), channel_id=1, source_target_pairs={{0,1},{1,0},{2,3},{3,2},{4,5},{5,4},{6,7},{7,6},{8,9},{9,8},{10,11... | collective-permute-start | bytes 147464 | tf_op jit(solution)/shard_map/ppermute | solution.py:106
  162.1 9.2 %collective-permute-start.26 = (f32[8,512]{1,0:T(8,128)S(1)}, f32[8,512]{1,0:T(8,128)S(1)}, u32[]{:S(2)}, u32[]{:S(2)}) collective-permute-start(f32[8,512]{1,0:T(8,128)S(1)} %copy-done.35), channel_id=1, source_target_pairs={{0,2},{1,3},{2,0},{3,1},{4,6},{5,7},{6,4},{7,5},{8,10},{9,11},{10,... | collective-permute-start | bytes 49160 | tf_op jit(solution)/shard_map/ppermute | solution.py:106
  162.1 9.2 %collective-permute-start.27 = (f32[24,512]{1,0:T(8,128)S(1)}, f32[24,512]{1,0:T(8,128)S(1)}, u32[]{:S(2)}, u32[]{:S(2)}) collective-permute-start(f32[24,512]{1,0:T(8,128)S(1)} %copy-done.33), channel_id=1, source_target_pairs={{0,3},{1,2},{2,1},{3,0},{4,7},{5,6},{6,5},{7,4},{8,11},{9,10},{10,... | collective-permute-start | bytes 147464 | tf_op jit(solution)/shard_map/ppermute | solution.py:106
  175.3 7.0 %collective-permute-start.28 = (bf16[27,8,512]{2,1,0:T(8,128)(2,1)}, bf16[27,8,512]{2,1,0:T(8,128)(2,1)S(1)}, u32[]{:S(2)}, u32[]{:S(2)}) collective-permute-start(bf16[27,8,512]{2,1,0:T(8,128)(2,1)} %get-tuple-element.178), channel_id=1, source_target_pairs={{0,8},{1,9},{2,10},{3,11},{8,16},{9,17},{10,18},{11,19},{16,24},{1... | collective-permute-start | bytes 663560 | tf_op jit(solution)/shard_map/ppermute | solution.py:1506
  176.9 6.1 %collective-permute-start.29 = (bf16[27,8,512]{2,1,0:T(8,128)(2,1)}, bf16[27,8,512]{2,1,0:T(8,128)(2,1)S(1)}, u32[]{:S(2)}, u32[]{:S(2)}) collective-permute-start(bf16[27,8,512]{2,1,0:T(8,128)(2,1)} %get-tuple-element.179), channel_id=1, source_target_pairs={{0,4},{1,5},{2,6},{3,7},{8,0},{9,1},{10,2},{11,3},{16,8},{17,9},{1... | collective-permute-start | bytes 663560 | tf_op jit(solution)/shard_map/ppermute | solution.py:1508
  183.1 6.9 %collective-permute-start.30 = (bf16[27,8,512]{2,1,0:T(8,128)(2,1)S(1)}, bf16[27,8,512]{2,1,0:T(8,128)(2,1)S(1)}, u32[]{:S(2)}, u32[]{:S(2)}) collective-permute-start(bf16[27,8,512]{2,1,0:T(8,128)(2,1)S(1)} %get-tuple-element.212), channel_id=1, source_target_pairs={{0,8},{1,9},{2,10},{3,11},{8,16},{9,17},{10,18},{11,19},{16,24},{1... | collective-permute-start | bytes 663560 | tf_op jit(solution)/shard_map/ppermute | solution.py:1506
  184.7 5.9 %collective-permute-start.31 = (bf16[27,8,512]{2,1,0:T(8,128)(2,1)S(1)}, bf16[27,8,512]{2,1,0:T(8,128)(2,1)S(1)}, u32[]{:S(2)}, u32[]{:S(2)}) collective-permute-start(bf16[27,8,512]{2,1,0:T(8,128)(2,1)S(1)} %get-tuple-element.211), channel_id=1, source_target_pairs={{0,4},{1,5},{2,6},{3,7},{8,0},{9,1},{10,2},{11,3},{16,8},{17,9},{1... | collective-permute-start | bytes 663560 | tf_op jit(solution)/shard_map/ppermute | solution.py:1508
  190.7 9.1 %collective-permute-start.32 = (bf16[27,8,512]{2,1,0:T(8,128)(2,1)S(1)}, bf16[27,8,512]{2,1,0:T(8,128)(2,1)S(1)}, u32[]{:S(2)}, u32[]{:S(2)}) collective-permute-start(bf16[27,8,512]{2,1,0:T(8,128)(2,1)S(1)} %get-tuple-element.210), channel_id=1, source_target_pairs={{0,8},{1,9},{2,10},{3,11},{8,16},{9,17},{10,18},{11,19},{16,24},{1... | collective-permute-start | bytes 663560 | tf_op jit(solution)/shard_map/ppermute | solution.py:1506
  191.7 8.2 %collective-permute-start.33 = (bf16[27,8,512]{2,1,0:T(8,128)(2,1)S(1)}, bf16[27,8,512]{2,1,0:T(8,128)(2,1)S(1)}, u32[]{:S(2)}, u32[]{:S(2)}) collective-permute-start(bf16[27,8,512]{2,1,0:T(8,128)(2,1)S(1)} %get-tuple-element.209), channel_id=1, source_target_pairs={{0,4},{1,5},{2,6},{3,7},{8,0},{9,1},{10,2},{11,3},{16,8},{17,9},{1... | collective-permute-start | bytes 663560 | tf_op jit(solution)/shard_map/ppermute | solution.py:1508
  199.9 6.2 %collective-permute-start.34 = (bf16[27,8,512]{2,1,0:T(8,128)(2,1)S(1)}, bf16[27,8,512]{2,1,0:T(8,128)(2,1)S(1)}, u32[]{:S(2)}, u32[]{:S(2)}) collective-permute-start(bf16[27,8,512]{2,1,0:T(8,128)(2,1)S(1)} %add_convert_fusion.4), channel_id=1, source_target_pairs={{0,8},{1,9},{2,10},{3,11},{8,16},{9,17},{10,18},{11,19},{16,24},{1... | collective-permute-start | bytes 663560 | tf_op jit(solution)/shard_map/ppermute | solution.py:1506
  206.3 12.3 %collective-permute-start.35 = (bf16[27,8,512]{2,1,0:T(8,128)(2,1)S(1)}, bf16[27,8,512]{2,1,0:T(8,128)(2,1)S(1)}, u32[]{:S(2)}, u32[]{:S(2)}) collective-permute-start(bf16[27,8,512]{2,1,0:T(8,128)(2,1)S(1)} %add_convert_fusion.3.mine_ref), channel_id=1, source_target_pairs={{0,2},{1,3},{2,0},{3,1},{4,6},{5,7},{6,4},{7,5},{8,10},{9,11},{10,... | collective-permute-start | bytes 663560 | tf_op jit(solution)/shard_map/ppermute | solution.py:106
  214.6 3.9 %collective-permute-start.37 = (bf16[27,8,512]{2,1,0:T(8,128)(2,1)S(1)}, bf16[27,8,512]{2,1,0:T(8,128)(2,1)S(1)}, u32[]{:S(2)}, u32[]{:S(2)}) collective-permute-start(bf16[27,8,512]{2,1,0:T(8,128)(2,1)S(1)} %add_convert_fusion.3.mine_ref), channel_id=1, source_target_pairs={{0,1},{1,0},{2,3},{3,2},{4,5},{5,4},{6,7},{7,6},{8,9},{9,8},{10,11... | collective-permute-start | bytes 663560 | tf_op jit(solution)/shard_map/ppermute | solution.py:106
  218.5 5.4 %collective-permute-start.36 = (bf16[27,8,512]{2,1,0:T(8,128)(2,1)S(1)}, bf16[27,8,512]{2,1,0:T(8,128)(2,1)S(1)}, u32[]{:S(2)}, u32[]{:S(2)}) collective-permute-start(bf16[27,8,512]{2,1,0:T(8,128)(2,1)S(1)} %collective-permute-done.35.mine_ref), channel_id=1, source_target_pairs={{0,1},{1,0},{2,3},{3,2},{4,5},{5,4},{6,7},{7,6},{8,9},{9,8},{10,11... | collective-permute-start | bytes 663560 | tf_op jit(solution)/shard_map/ppermute | solution.py:106
  (26 other events, 90.0 us)

commit v7 on v5

--- a/solution.py
+++ b/solution.py
@@ -43,7 +43,7 @@
 CHUNK = 768
 HALF_BIN = 384
 PAIR = 5
-ADAM_BLOCK = 9
+ADAM_BLOCK = 27
 LANE = 128
 AXES = ("rows", "seq")
 
@@ -241,7 +241,7 @@
         return carry
 
     lax.fori_loop(0, owners, name, 0)
-    lax.fori_loop(0, owners * slots, clear, 0)
+    lax.fori_loop(0, owners * slots, clear, 0, unroll=8)
     lax.fori_loop(0, NB, place, 0)
     own = rel[row_at]
 
@@ -346,12 +346,15 @@
 
 
 def place_parts(places, counts, core, pieces, table, sem, slots, owners, start):
+    done = {}
     for index, ref in enumerate(pieces):
         side = core if index % 2 == 0 else 1 - core
         owner = owners[index // 2]
-
-        def one(s, carry, ref=ref, side=side, owner=owner):
-            bucket = places[0, owner * slots + s]
+        first = done.get((owner, index % 2), 0)
+        done[owner, index % 2] = first + ref.shape[0]
+
+        def one(s, carry, ref=ref, side=side, owner=owner, first=first):
+            bucket = places[0, owner * slots + first + s]
             at = pl.multiple_of(bucket * BR + side * HALF, HALF)
             copy = pltpu.make_async_copy(ref.at[s], table.at[pl.ds(at, HALF), :], sem)
             if start:
@@ -360,7 +363,8 @@
                 copy.wait()
             return carry
 
-        lax.fori_loop(0, counts[0, owner], one, 0)
+        held = jnp.clip(counts[0, owner] - first, 0, ref.shape[0])
+        lax.fori_loop(0, held, one, 0)
 
 
 def assemble_body(meta, places, counts, *refs, slots, owners):
@@ -456,6 +460,8 @@
         for other in others[at:until]:
             other()
         at = until
+    for other in others[at:]:
+        other()
 
 
 def forward_body(meta, places, counts, x_ref, low_ref, high_ref, order_ref, cot_ref, *rest, owners, slots, tiles, count, utts):
@@ -636,18 +642,13 @@
     def grad_dot(c):
         grad[c : c + 256, :] += dot(hg_old[:, c : c + 256], normed_old[...], TN)
 
-    interleave(
-        head_dots(logs_ref, 0) + head_dots(angle_ref, BIN_PAD),
-        [functools.partial(convolve, at, size) for at, size in spans(TILE, 32)],
-    )
-    interleave(
-        [functools.partial(hidden_dot, c) for c in range(0, FF, 256)]
-        + [functools.partial(grad_dot, c) for c in range(0, 2 * BIN_PAD, 256)],
-        [functools.partial(head, at, size, sincos) for at, size in spans(TILE, 16)],
-    )
-
-    @pl.when((step > 0) & (slow[0] > 0))
-    def _():
+    def ngrad_dot(c):
+        ngrad_ref[:, c : c + 256] = dot(hg[...], w_head[:, c : c + 256], NN)
+
+    def branch_dot(c):
+        slim[:, c : c + 256] = dot(act_ref[...], table[FF : 2 * FF, c : c + 256], NN)
+
+    def head_again():
         def again(i, carry):
             rows = pl.ds(pl.multiple_of(i * 32, 32), 32)
             for c in range(0, BIN_PAD, LANE):
@@ -668,8 +669,7 @@
 
         lax.fori_loop(0, TILE // 32, again, 0)
 
-    @pl.when(step == 0)
-    def _():
+    def build_head():
         last = vecs[...]
         line = jnp.concatenate([last[25:26], last[26:27], last[27:28]], axis=1)
         line = jnp.broadcast_to(line, (16, 3 * channels))
@@ -697,36 +697,62 @@
         bound = 1.05 * normed_length * jnp.max(jnp.sqrt(longest)) + jnp.max(jnp.abs(b_head[:, BIN_PAD:]))
         slow[0] = jnp.where(bound < ANGLE_LIMIT, 0, 1)
 
-    def ngrad_dot(c):
-        ngrad_ref[:, c : c + 256] = dot(hg[...], w_head[:, c : c + 256], NN)
-
-    def branch_dot(c):
-        slim[:, c : c + 256] = dot(act_ref[...], table[FF : 2 * FF, c : c + 256], NN)
-
-    interleave(
-        [functools.partial(ngrad_dot, c) for c in range(0, channels, 256)],
-        [functools.partial(gelu, at, size, c) for c in range(IN_ROWS) for at, size in spans(TILE, 32)],
-    )
-    sums = [sums_ref[v] for v in range(4)]
-
-    def back(at, size):
-        sums[:] = second_norm_back(at, size, sums)
-
-    interleave(
-        [functools.partial(branch_dot, c) for c in range(0, channels, 256)],
-        [functools.partial(back, at, size) for at, size in spans(TILE, 16)],
-    )
-    for v in range(4):
-        sums_ref[v] = sums[v]
-    for c in range(0, 2 * BIN_PAD, 512):
-        total = bsum_ref[:, c : c + 512]
-        for at, size in spans(TILE, 32):
-            total = total + fold(hg[at : at + size, c : c + 512].astype(F32))
-        bsum_ref[:, c : c + 512] = total
-    hg_old[...] = hg[...]
-    normed_old[...] = normed[...]
-    for at, size in spans(TILE, 16):
-        second_norm(at, size)
+    def over_all(call, values):
+        return [functools.partial(call, v) for v in values]
+
+    def in_spans(call, size, *more):
+        return [functools.partial(call, at, length, *more) for at, length in spans(TILE, size)]
+
+    def work(first, second):
+        interleave(
+            head_dots(logs_ref, 0) + head_dots(angle_ref, BIN_PAD) if second else [],
+            in_spans(convolve, 32) if first else [],
+        )
+        interleave(
+            (over_all(hidden_dot, range(0, FF, 256)) if first else [])
+            + (over_all(grad_dot, range(0, 2 * BIN_PAD, 256)) if second else []),
+            in_spans(head, 16, sincos) if second else [],
+        )
+        if second:
+            pl.when(slow[0] > 0)(head_again)
+        interleave(
+            over_all(ngrad_dot, range(0, channels, 256)) if second else [],
+            [call for c in range(IN_ROWS) for call in in_spans(gelu, 32, c)] if first else [],
+        )
+        sums = [sums_ref[v] for v in range(4)]
+
+        def back(at, size):
+            sums[:] = second_norm_back(at, size, sums)
+
+        interleave(
+            over_all(branch_dot, range(0, channels, 256)) if first else [],
+            in_spans(back, 16) if second else [],
+        )
+        if second:
+            for v in range(4):
+                sums_ref[v] = sums[v]
+            for c in range(0, 2 * BIN_PAD, 512):
+                total = bsum_ref[:, c : c + 512]
+                for at, size in spans(TILE, 32):
+                    total = total + fold(hg[at : at + size, c : c + 512].astype(F32))
+                bsum_ref[:, c : c + 512] = total
+            hg_old[...] = hg[...]
+            normed_old[...] = normed[...]
+        if first:
+            interleave([], in_spans(second_norm, 16))
+
+    @pl.when(step == 0)
+    def _():
+        work(True, False)
+        build_head()
+
+    @pl.when((step > 0) & (step < count))
+    def _():
+        work(True, True)
+
+    @pl.when(step == count)
+    def _():
+        work(False, True)
 
     @pl.when(step == count)
     def _():
@@ -747,12 +773,11 @@
         store().wait()
 
 
-def forward(owners, meta, places, counts, x, low, high, order, cot, pieces, table, utts):
+def forward(owners, slots, meta, places, counts, x, low, high, order, cot, pieces, table, utts):
     rows, frames, channels = x.shape
     tiles = frames // TILE
     steps = rows * tiles
     count = rows * frames
-    slots = pieces[0].shape[0]
     ahead = lambda i: jnp.minimum(i, steps - 1)
     behind = lambda i: jnp.maximum(i - 1, 0)
     wide = pl.BlockSpec((TILE, FF), lambda i: (ahead(i), 0))
@@ -1228,7 +1253,7 @@
             out[slot_of[0, start + b]] = value.astype(BF16)
             return carry
 
-        lax.fori_loop(0, stop - start, one, 0)
+        lax.fori_loop(0, stop - start, one, 0, unroll=8)
     total = last_refs[0][0:QUART, :]
     for ref in last_refs[1:]:
         total = total + ref[0:QUART, :]
@@ -1372,19 +1397,19 @@
                 arrived += [ahead, seq_swap(ahead, 1), back, seq_swap(back, 1)]
         arrived = [ahead, seq_swap(ahead, 1)]
         owned = (owners - 1,)
-        part_places, part_counts = places, counts
+        part_places, part_counts, part_slots = places, counts, slots
     else:
         gathered = lax.all_gather(mine, "rows", axis=0, tiled=True)
         arrived = [gathered, seq_swap(gathered, 1)]
         owned = (0,)
         arrived = [take_slots(slot_of, a) for a in arrived]
         part_places = jnp.arange(NB, dtype=jnp.int32)[None, :]
-        part_counts = jnp.full((1, 1), NB, jnp.int32)
+        part_counts, part_slots = jnp.full((1, 1), NB, jnp.int32), NB
         partial_table = jnp.zeros((NB * BR, channels), BF16)
         cot = spectrum_cotangent(0, tiles, cot, meta, lines, later, synth, win, rows, utts)
 
     (table, spec, act, der, ada, low_grad, resg, xc, rc, send, keep, tail, sums, hsum) = forward(
-        owned, meta, part_places, part_counts, frames_in, low, high, order, cot, arrived, partial_table, utts
+        owned, part_slots, meta, part_places, part_counts, frames_in, low, high, order, cot, arrived, partial_table, utts
     )
     halo = shifted(spec[:, frames - EDGE :], 1)
 

time: 236 us -> 228 us (0.966)
  Pallas kernels: 162 us -> 155 us
  waiting for transfers between devices: 19.7 us -> 23.2 us
    pallas_call x1, Pallas kernels: 56.1 us -> 51.6 us  [forward(): pl.pallas_call(functools.partial(forward_body, owners=owners, slots=slots...]
  transfers between devices with their start and end apart: 38 -> 38, of which waited for: 12 -> 13; matrix products, arithmetic and copies ran while one was open for 2% -> 2% of each run, Pallas kernels for 43% -> 43%
where the time goes in v7:
time: 228 us; the launch traced here: 227 us
  Pallas kernels  155 us (68%)
  starting transfers between devices  36 us (16%)
  waiting for transfers between devices  23.2 us (10%)
  local copies, waits for them, and re-layouts  10.6 us (5%)
    pallas_call x1, Pallas kernels, forward(): pl.pallas_call(functools.partial(forward_body, owners=owners, slots=slots...  51.6 us
    pallas_call x2, Pallas kernels, mlp_backward(): pl.pallas_call(functools.partial(mlp_body, utts=utts), grid=(count // til...  21.1 us
    pallas_call x2, Pallas kernels, norm_backward(): pl.pallas_call(functools.partial(norm_body, row=row, tiles=tiles, utts=ut...  20.6 us
    pallas_call x2, Pallas kernels, spectrum_cotangent(): pl.pallas_call(functools.partial(pre_body, start=start, tiles=tiles, rows...  15.1 us
    ppermute x20, starting transfers between devices, seq_swap(): return lax.ppermute(value, 'seq', [(s, s ^ bit) for s in range(count)])  14.4 us
    pallas_call x2, Pallas kernels, wave_forward(): pl.pallas_call(functools.partial(wave_body, start=start, rows=rows, utts=...  14.1 us
    ppermute x20, waiting for transfers between devices, seq_swap(): return lax.ppermute(value, 'seq', [(s, s ^ bit) for s in range(count)])  12.8 us
    pallas_call x2, Pallas kernels, conv_backward(): pl.pallas_call(functools.partial(conv_body, row=row, tiles=tiles, utts=ut...  9.58 us
  transfers between devices with their start and end apart: 38, of which 13 were waited for; matrix products, arithmetic and copies ran while one was open for 2% of the time, Pallas kernels for 43%

profile of v7, /device:TPU:0, one launch (start us, length us, event | category | flops | bytes accessed | tf_op | source)
XLA Modules:
  0.0 227.1 jit_solution(7687417084167212623)
XLA Ops:
  0.6 1.2 dynamic-slice_convert_fusion.refs_0_
  1.9 3.1 %collective-permute-start = (bf16[27,16,512]{2,1,0:T(8,128)(2,1)S(1)}, bf16[27,16,512]{2,1,0:T(8,128)(2,1)S(1)}, u32[]{:S(2)}, u32[]{:S(2)}) collective-permute-start(bf16[27,16,512]{2,1,0:T(8,128)(2,1)S(1)} %dynamic-slice_convert_fusion.refs_0_), channel_id=1, source_target_pairs={{0,8},{1,9},{2,10},{3,11},{8,16},{9,17},{10,18},{11,19},{16,24},{1... | collective-permute-start | bytes 1327112 | tf_op jit(solution)/shard_map/ppermute | solution.py:1382
  5.8 1.4 collective-permute-start.2
  7.2 1.3 collective-permute-start.3
  9.3 1.3 collective-permute-start.4
  11.2 4.2 %plan.1 = (s32[2,12]{1,0:T(2,128)}, s32[1,216]{1,0:T(1,128)}, s32[1,27]{1,0:T(1,128)}, s32[1,137]{1,0:T(1,128)}, s32[1,8]{1,0:T(1,128)}) custom-call(s32[2]{0:T(128)} %pad_add_fusion.ids, s32[2,4]{1,0:T(2,128)} %lengths.1, s32[2,4]{1,0:T(2,128)} %bw_ids.1, s32[137]{0:T(256)} %owner_list.1, s32[8]{0:T(128)} %constant.54.clone.order, s32[8]{0:T(128)} %constant.55.clone.offsets), custom_call_target="tpu_custom_call" | custom-call | flops 8000 | bytes 8192 | tf_op jit(solution)/shard_map/plan/pallas_call | solution.py:259
  15.4 1.2 collective-permute-done.1.refs_4_
  16.6 1.6 collective-permute-start.5
  18.7 7.5 %spectrum_cotangent_0.1.rest_0_ = bf16[2,1024,1536]{2,1,0:T(8,128)(2,1)} custom-call(s32[2,12]{1,0:T(2,128)} %get-tuple-element.110.meta, bf16[5120,128]{1,0:T(8,128)(2,1)} %bitcast.33, bf16[80,128]{1,0:T(8,128)(2,1)} %copy-done.29, bf16[2,768,768]{2,1,0:T(8,128)(2,1)} %constant.52.clone.synth_ref, f32[8,384]{1,0:T(8,128)} %constant.53.clone.win_ref), custom_call_target="tpu_custom_call" | custom-call | flops 2415919104 | bytes 7340032 | tf_op jit(solution)/shard_map/spectrum_cotangent_0/pallas_call | solution.py:329
  26.2 1.3 collective-permute-done.5.refs_6_
  27.5 1.9 collective-permute-done.6.refs_8_
  29.3 1.6 collective-permute-start.7
  31.4 1.2 collective-permute-start.10
  33.1 7.6 %spectrum_cotangent_2.1.cot_ref = bf16[2,1024,1536]{2,1,0:T(8,128)(2,1)} custom-call(s32[2,12]{1,0:T(2,128)} %get-tuple-element.110.meta, bf16[5120,128]{1,0:T(8,128)(2,1)} %bitcast.34, bf16[80,128]{1,0:T(8,128)(2,1)} %copy-done.29, bf16[2,768,768]{2,1,0:T(8,128)(2,1)} %constant.52.clone.synth_ref, ...), custom_call_target="tpu_custom_call", output_to_operand_aliasing={{}: (5, {})} | custom-call | flops 2415919104 | bytes 7340032 | tf_op jit(solution)/shard_map/spectrum_cotangent_2/pallas_call | solution.py:329
  40.7 0.9 collective-permute-done.7.refs_10_
  41.6 0.9 collective-permute-start.13
  42.5 1.0 collective-permute-done.8.refs_12_
  44.3 1.4 collective-permute-start.9
  47.4 5.8 %assemble.1.rest_2_ = bf16[4384,512]{1,0:T(8,128)(2,1)} custom-call(s32[2,12]{1,0:T(2,128)} %get-tuple-element.110.meta, s32[1,216]{1,0:T(1,128)} %get-tuple-element.126.places, s32[1,8]{1,0:T(1,128)} %get-tuple-element.112.counts, bf16[27,16,512]{2,1,0:T(8,128)(2,1)} %copy-done, bf16[27,16,512]{2,1,0:T(8,128)(2,1)} %copy-done.14, ...), custom_call_target="tpu_custom_call" | custom-call | bytes 12582912 | tf_op jit(solution)/shard_map/assemble/pallas_call | solution.py:379
  53.2 3.4 %collective-permute-done.9.rest_0_ = bf16[27,16,512]{2,1,0:T(8,128)(2,1)S(1)} collective-permute-done((bf16[27,16,512]{2,1,0:T(8,128)(2,1)S(1)}, bf16[27,16,512]{2,1,0:T(8,128)(2,1)S(1)}, u32[]{:S(2)}, u32[]{:S(2)}) %collective-permute-start.9) | collective-permute-done | bytes 442400 | tf_op jit(solution)/shard_map/ppermute | solution.py:1382
  56.6 1.8 collective-permute-done.17.rest_1_
  59.2 51.6 %forward.1 = (bf16[4384,512]{1,0:T(8,128)(2,1)}, bf16[2,1024,1536]{2,1,0:T(8,128)(2,1)}, bf16[2048,1536]{1,0:T(8,128)(2,1)}, bf16[2048,1536]{1,0:T(8,128)(2,1)},...) custom-call(s32[2,12]{1,0:T(2,128)} %get-tuple-element.110.meta, ...), custom_call_target="tpu_custom_call" | custom-call | flops 16106127360 | bytes 41943040 | tf_op jit(solution)/shard_map/forward/pallas_call | solution.py:787
  111.0 10.5 %mlp_backward_0.1 = (bf16[2048,1536]{1,0:T(8,128)(2,1)}, bf16[48,16,512]{2,1,0:T(8,128)(2,1)}, bf16[48,16,512]{2,1,0:T(8,128)(2,1)}, f32[8,768]{1,0:T(8,128)}) custom-call(s32[2,12]{1,0:T(2,128)} %get-tuple-element.110.meta, bf16[2048,512]{1,0:T(8,128)(2,1)} %get-tuple-element.131.low_ref, bf16[2048,1536]{1,0:T(8,128)(2,1)} %get-tuple-element.132.act_ref, ...), custom_call_target="tpu_custom_call" | custom-call | flops 4831838208 | bytes 16777216 | tf_op jit(solution)/shard_map/mlp_backward_0/pallas_call | solution.py:898
  123.0 4.6 %collective-permute-start.21 = (bf16[40,8,512]{2,1,0:T(8,128)(2,1)S(1)}, bf16[40,8,512]{2,1,0:T(8,128)(2,1)S(1)}, u32[]{:S(2)}, u32[]{:S(2)}) collective-permute-start(bf16[40,8,512]{2,1,0:T(8,128)(2,1)S(1)} %get-tuple-element.221), channel_id=1, source_target_pairs={{0,2},{1,3},{2,0},{3,1},{4,6},{5,7},{6,4},{7,5},{8,10},{9,11},{10,... | collective-permute-start | bytes 983048 | tf_op jit(solution)/shard_map/ppermute | solution.py:106
  127.6 10.6 %mlp_backward_1.1 = (bf16[2048,1536]{1,0:T(8,128)(2,1)}, bf16[48,16,512]{2,1,0:T(8,128)(2,1)}, bf16[48,16,512]{2,1,0:T(8,128)(2,1)}, f32[8,768]{1,0:T(8,128)}) custom-call(s32[2,12]{1,0:T(2,128)} %get-tuple-element.110.meta, bf16[2048,512]{1,0:T(8,128)(2,1)} %get-tuple-element.131.low_ref, ...), custom_call_target="tpu_custom_call", output_to_operand_aliasing={{0}: (6, {})} | custom-call | flops 4831838208 | bytes 16777216 | tf_op jit(solution)/shard_map/mlp_backward_1/pallas_call | solution.py:898
  138.5 0.8 constant_dynamic-slice_fusion.2
  139.6 9.1 %norm_backward_0.1 = (bf16[1024,512]{1,0:T(8,128)(2,1)}, f32[2,8,512]{2,1,0:T(8,128)}, f32[16,8,512]{2,1,0:T(8,128)}) custom-call(s32[2,12]{1,0:T(2,128)} %get-tuple-element.110.meta, bf16[2,1024,512]{2,1,0:T(8,128)(2,1)} %x_ref.5, bf16[2,16,512]{2,1,0:T(8,128)(2,1)} %copy-done.27, bf16[2,16,512]{2,1,0:T(8,128)(2,1)} %copy-done.28, ...), custom_call_target="tpu_custom_call" | custom-call | flops 1610612736 | bytes 12582912 | tf_op jit(solution)/shard_map/norm_backward_0/pallas_call | solution.py:1079
  148.6 2.2 collective-permute-done.22.refs_4_
  151.2 0.8 constant_dynamic-slice_fusion
  152.3 0.9 slice.37
  153.2 1.4 collective-permute-start.29
  154.6 11.6 %norm_backward_1.1 = (bf16[1024,512]{1,0:T(8,128)(2,1)}, f32[2,8,512]{2,1,0:T(8,128)}, f32[16,8,512]{2,1,0:T(8,128)}, f32[8,512]{1,0:T(8,128)}, f32[24,512]{1,0:...) custom-call(s32[2,12]{1,0:T(2,128)} %get-tuple-element.110.meta, bf16[2,1024,512]{2,1,0:T(8,128)(2,1)} %x_ref.5, ...), custom_call_target="tpu_custom_call" | custom-call | flops 1610612736 | bytes 12582912 | tf_op jit(solution)/shard_map/norm_backward_1/pallas_call | solution.py:1079
  166.1 2.5 %collective-permute-start.24 = (f32[24,512]{1,0:T(8,128)}, f32[24,512]{1,0:T(8,128)S(1)}, u32[]{:S(2)}, u32[]{:S(2)}) collective-permute-start(f32[24,512]{1,0:T(8,128)} %get-tuple-element.169), channel_id=1, source_target_pairs={{0,1},{1,0},{2,3},{3,2},{4,5},{5,4},{6,7},{7,6},{8,9},{9,8},{10,11... | collective-permute-start | bytes 147464 | tf_op jit(solution)/shard_map/ppermute | solution.py:106
  168.7 1.7 collective-permute-start.25
  170.4 2.9 %collective-permute-done.25.refs_8_ = f32[8,512]{1,0:T(8,128)S(1)} collective-permute-done((f32[8,512]{1,0:T(8,128)}, f32[8,512]{1,0:T(8,128)S(1)}, u32[]{:S(2)}, u32[]{:S(2)}) %collective-permute-start.25) | collective-permute-done | bytes 16416 | tf_op jit(solution)/shard_map/ppermute | solution.py:106
  174.1 3.3 %to_slots.1 = (bf16[216,8,512]{2,1,0:T(8,128)(2,1)}, bf16[27,8,512]{2,1,0:T(8,128)(2,1)}, bf16[27,8,512]{2,1,0:T(8,128)(2,1)}) custom-call(s32[1,137]{1,0:T(1,128)} %get-tuple-element.108.slot_of, bf16[40,8,512]{2,1,0:T(8,128)(2,1)} %get-tuple-element.222.refs_0_, bf16[48,8,512]{2,1,0:T(8,128)(2,1)} %get-tuple-element.220.refs_1_, ...), custom_call_target="tpu_custom_call" | custom-call | bytes 6291456 | tf_op jit(solution)/shard_map/to_slots/pallas_call | solution.py:1267
  177.3 1.4 collective-permute-start.27
  180.0 7.1 %wave_forward_0.1.rest_0_ = f32[5120,128]{1,0:T(8,128)} custom-call(s32[2,12]{1,0:T(2,128)} %get-tuple-element.110.meta, bf16[2,1024,1536]{2,1,0:T(8,128)(2,1)} %get-tuple-element.189.spec_ref.prev_ref, bf16[2,1024,1536]{2,1,0:T(8,128)(2,1)} %get-tuple-element.189.spec_ref.prev_ref, bf16[2,16,1536]{2,1,0:T(8,128)(2,1)} %copy-done.20, ...), custom_call_target="tpu_custom_call" | custom-call | flops 2415919104 | bytes 10485760 | tf_op jit(solution)/shard_map/wave_forward_0/pallas_call | solution.py:1219
  187.2 1.5 collective-permute-start.30
  189.3 4.8 %conv_backward_0.1.rest_0_ = f32[2,1024,512]{2,1,0:T(8,128)} custom-call(s32[2,12]{1,0:T(2,128)} %get-tuple-element.110.meta, bf16[1024,512]{1,0:T(8,128)(2,1)} %get-tuple-element.185.cg_ref.before_ref.after_ref, bf16[1024,512]{1,0:T(8,128)(2,1)} %get-tuple-element.185.cg_ref.before_ref.after_ref, ...), custom_call_target="tpu_custom_call" | custom-call | flops 8388608 | bytes 6291456 | tf_op jit(solution)/shard_map/conv_backward_0/pallas_call | solution.py:1147
  194.9 1.4 collective-permute-start.32
  197.0 7.0 %wave_forward_2.1 = f32[5120,128]{1,0:T(8,128)} custom-call(s32[2,12]{1,0:T(2,128)} %get-tuple-element.110.meta, bf16[2,1024,1536]{2,1,0:T(8,128)(2,1)} %get-tuple-element.189.spec_ref.prev_ref, bf16[2,1024,1536]{2,1,0:T(8,128)(2,1)} %get-tuple-element.189.spec_ref.prev_ref, bf16[2,16,1536]{2,1,0:T(8,128)(2,1)} %copy-done.20, ...), custom_call_target="tpu_custom_call", output_to_operand_aliasing={{}: (6, {})} | custom-call | flops 2415919104 | bytes 10485760 | tf_op jit(solution)/shard_map/wave_forward_2/pallas_call | solution.py:1219
  204.1 1.5 collective-permute-start.34
  205.6 4.8 %conv_backward_1.1 = f32[2,1024,512]{2,1,0:T(8,128)} custom-call(s32[2,12]{1,0:T(2,128)} %get-tuple-element.110.meta, bf16[1024,512]{1,0:T(8,128)(2,1)} %get-tuple-element.195.cg_ref.before_ref.after_ref, bf16[1024,512]{1,0:T(8,128)(2,1)} %get-tuple-element.195.cg_ref.before_ref.after_ref, ...), custom_call_target="tpu_custom_call", output_to_operand_aliasing={{}: (8, {})} | custom-call | flops 8388608 | bytes 6291456 | tf_op jit(solution)/shard_map/conv_backward_1/pallas_call | solution.py:1147
  210.5 0.9 collective-permute-start.35
  211.4 5.1 %collective-permute-done.35.mine_ref = bf16[27,8,512]{2,1,0:T(8,128)(2,1)S(1)} collective-permute-done((bf16[27,8,512]{2,1,0:T(8,128)(2,1)S(1)}, bf16[27,8,512]{2,1,0:T(8,128)(2,1)S(1)}, u32[]{:S(2)}, u32[]{:S(2)}) %collective-permute-start.35) | collective-permute-done | bytes 221216 | tf_op jit(solution)/shard_map/ppermute | solution.py:106
  217.2 4.6 %adam_first.1 = (f32[27,2,2,8,512]{4,3,2,1,0:T(8,128)}, f32[27,2,2,8,512]{4,3,2,1,0:T(8,128)}, f32[27,2,2,8,512]{4,3,2,1,0:T(8,128)}) custom-call(s32[1,27]{1,0:T(1,128)} %get-tuple-element.198.places, s32[2,12]{1,0:T(2,128)} %get-tuple-element.110.meta, bf16[27,8,512]{2,1,0:T(8,128)(2,1)} %copy-done.2, bf16[27,8,512]{2,1,0:T(8,128)(2,1)} %copy-done.26, ...), custom_call_target="tpu_custom_call" | custom-call | bytes 6291456 | tf_op jit(solution)/shard_map/adam_first/pallas_call | solution.py:1310
  222.5 4.6 %adam_second.1 = (f32[27,2,2,8,512]{4,3,2,1,0:T(8,128)}, f32[27,2,2,8,512]{4,3,2,1,0:T(8,128)}, f32[27,2,2,8,512]{4,3,2,1,0:T(8,128)}) custom-call(s32[1,27]{1,0:T(1,128)} %get-tuple-element.198.places, s32[2,12]{1,0:T(2,128)} %get-tuple-element.110.meta, bf16[27,8,512]{2,1,0:T(8,128)(2,1)} %copy-done.24, ...), custom_call_target="tpu_custom_call", output_to_operand_aliasing={{0}: (7, {}), {1}: (8, {}), {2}: (9, {})} | custom-call | bytes 6291456 | tf_op jit(solution)/shard_map/adam_second/pallas_call | solution.py:1310
  (125 shorter events, 15.4 us)
Async XLA Ops:
  1.9 29.5 %copy-start = (bf16[27,16,512]{2,1,0:T(8,128)(2,1)}, bf16[27,16,512]{2,1,0:T(8,128)(2,1)S(1)}, u32[]{:S(2)}) copy-start(bf16[27,16,512]{2,1,0:T(8,128)(2,1)S(1)} %dynamic-slice_convert_fusion.refs_0_) | copy-start | bytes 1327108
  1.9 13.5 %collective-permute-start = (bf16[27,16,512]{2,1,0:T(8,128)(2,1)S(1)}, bf16[27,16,512]{2,1,0:T(8,128)(2,1)S(1)}, u32[]{:S(2)}, u32[]{:S(2)}) collective-permute-start(bf16[27,16,512]{2,1,0:T(8,128)(2,1)S(1)} %dynamic-slice_convert_fusion.refs_0_), channel_id=1, source_target_pairs={{0,8},{1,9},{2,10},{3,11},{8,16},{9,17},{10,18},{11,19},{16,24},{1... | collective-permute-start | bytes 1327112 | tf_op jit(solution)/shard_map/ppermute | solution.py:1382
  5.0 11.6 %collective-permute-start.1 = (bf16[27,16,512]{2,1,0:T(8,128)(2,1)S(1)}, bf16[27,16,512]{2,1,0:T(8,128)(2,1)S(1)}, u32[]{:S(2)}, u32[]{:S(2)}) collective-permute-start(bf16[27,16,512]{2,1,0:T(8,128)(2,1)S(1)} %dynamic-slice_convert_fusion.refs_0_), channel_id=1, source_target_pairs={{0,4},{1,5},{2,6},{3,7},{8,0},{9,1},{10,2},{11,3},{16,8},{17,9},{1... | collective-permute-start | bytes 1327112 | tf_op jit(solution)/shard_map/ppermute | solution.py:1384
  5.8 9.6 %collective-permute-start.2 = (bf16[2,16,512]{2,1,0:T(8,128)(2,1)S(1)}, bf16[2,16,512]{2,1,0:T(8,128)(2,1)S(1)}, u32[]{:S(2)}, u32[]{:S(2)}) collective-permute-start(bf16[2,16,512]{2,1,0:T(8,128)(2,1)S(1)} %get-tuple-element.212), channel_id=1, source_target_pairs={{0,1},{1,2},{2,3},{4,5},{5,6},{6,7},{8,9},{9,10},{10,11},{12,13},{... | collective-permute-start | bytes 98312 | tf_op jit(solution)/shard_map/ppermute | solution.py:116
  7.2 8.2 %collective-permute-start.3 = (bf16[2,16,512]{2,1,0:T(8,128)(2,1)S(1)}, bf16[2,16,512]{2,1,0:T(8,128)(2,1)S(1)}, u32[]{:S(2)}, u32[]{:S(2)}) collective-permute-start(bf16[2,16,512]{2,1,0:T(8,128)(2,1)S(1)} %get-tuple-element.211), channel_id=1, source_target_pairs={{1,0},{2,1},{3,2},{5,4},{6,5},{7,6},{9,8},{10,9},{11,10},{13,12},{... | collective-permute-start | bytes 98312 | tf_op jit(solution)/shard_map/ppermute | solution.py:116
  9.3 6.1 %collective-permute-start.4 = (bf16[80,128]{1,0:T(8,128)(2,1)S(1)}, bf16[80,128]{1,0:T(8,128)(2,1)S(1)}, u32[]{:S(2)}, u32[]{:S(2)}) collective-permute-start(bf16[80,128]{1,0:T(8,128)(2,1)S(1)} %bitcast.38), channel_id=1, source_target_pairs={{1,0},{2,1},{3,2},{5,4},{6,5},{7,6},{9,8},{10,9},{11,10},{13,12},{... | collective-permute-start | bytes 61448 | tf_op jit(solution)/shard_map/ppermute | solution.py:116
  15.4 17.2 %copy-start.8 = (bf16[27,16,512]{2,1,0:T(8,128)(2,1)}, bf16[27,16,512]{2,1,0:T(8,128)(2,1)S(1)}, u32[]{:S(2)}) copy-start(bf16[27,16,512]{2,1,0:T(8,128)(2,1)S(1)} %collective-permute-done.refs_2_) | copy-start | bytes 1327108
  16.6 16.0 %copy-start.9 = (bf16[27,16,512]{2,1,0:T(8,128)(2,1)}, bf16[27,16,512]{2,1,0:T(8,128)(2,1)S(1)}, u32[]{:S(2)}) copy-start(bf16[27,16,512]{2,1,0:T(8,128)(2,1)S(1)} %collective-permute-done.1.refs_4_) | copy-start | bytes 1327108
  16.6 10.9 %collective-permute-start.5 = (bf16[27,16,512]{2,1,0:T(8,128)(2,1)S(1)}, bf16[27,16,512]{2,1,0:T(8,128)(2,1)S(1)}, u32[]{:S(2)}, u32[]{:S(2)}) collective-permute-start(bf16[27,16,512]{2,1,0:T(8,128)(2,1)S(1)} %collective-permute-done.refs_2_), channel_id=1, source_target_pairs={{0,8},{1,9},{2,10},{3,11},{8,16},{9,17},{10,18},{11,19},{16,24},{1... | collective-permute-start | bytes 1327112 | tf_op jit(solution)/shard_map/ppermute | solution.py:1382
  18.2 11.1 %collective-permute-start.6 = (bf16[27,16,512]{2,1,0:T(8,128)(2,1)S(1)}, bf16[27,16,512]{2,1,0:T(8,128)(2,1)S(1)}, u32[]{:S(2)}, u32[]{:S(2)}) collective-permute-start(bf16[27,16,512]{2,1,0:T(8,128)(2,1)S(1)} %collective-permute-done.1.refs_4_), channel_id=1, source_target_pairs={{0,4},{1,5},{2,6},{3,7},{8,0},{9,1},{10,2},{11,3},{16,8},{17,9},{1... | collective-permute-start | bytes 1327112 | tf_op jit(solution)/shard_map/ppermute | solution.py:1384
  27.5 14.1 %copy-start.10 = (bf16[27,16,512]{2,1,0:T(8,128)(2,1)}, bf16[27,16,512]{2,1,0:T(8,128)(2,1)S(1)}, u32[]{:S(2)}) copy-start(bf16[27,16,512]{2,1,0:T(8,128)(2,1)S(1)} %collective-permute-done.5.refs_6_) | copy-start | bytes 1327108
  29.3 14.2 %copy-start.11 = (bf16[27,16,512]{2,1,0:T(8,128)(2,1)}, bf16[27,16,512]{2,1,0:T(8,128)(2,1)S(1)}, u32[]{:S(2)}) copy-start(bf16[27,16,512]{2,1,0:T(8,128)(2,1)S(1)} %collective-permute-done.6.refs_8_) | copy-start | bytes 1327108
  29.3 12.3 %collective-permute-start.7 = (bf16[27,16,512]{2,1,0:T(8,128)(2,1)S(1)}, bf16[27,16,512]{2,1,0:T(8,128)(2,1)S(1)}, u32[]{:S(2)}, u32[]{:S(2)}) collective-permute-start(bf16[27,16,512]{2,1,0:T(8,128)(2,1)S(1)} %collective-permute-done.5.refs_6_), channel_id=1, source_target_pairs={{0,8},{1,9},{2,10},{3,11},{8,16},{9,17},{10,18},{11,19},{16,24},{1... | collective-permute-start | bytes 1327112 | tf_op jit(solution)/shard_map/ppermute | solution.py:1382
  30.9 12.6 %collective-permute-start.8 = (bf16[27,16,512]{2,1,0:T(8,128)(2,1)S(1)}, bf16[27,16,512]{2,1,0:T(8,128)(2,1)S(1)}, u32[]{:S(2)}, u32[]{:S(2)}) collective-permute-start(bf16[27,16,512]{2,1,0:T(8,128)(2,1)S(1)} %collective-permute-done.6.refs_8_), channel_id=1, source_target_pairs={{0,4},{1,5},{2,6},{3,7},{8,0},{9,1},{10,2},{11,3},{16,8},{17,9},{1... | collective-permute-start | bytes 1327112 | tf_op jit(solution)/shard_map/ppermute | solution.py:1384
  31.4 12.4 %collective-permute-start.10 = (bf16[27,16,512]{2,1,0:T(8,128)(2,1)S(1)}, bf16[27,16,512]{2,1,0:T(8,128)(2,1)S(1)}, u32[]{:S(2)}, u32[]{:S(2)}) collective-permute-start(bf16[27,16,512]{2,1,0:T(8,128)(2,1)S(1)} %dynamic-slice_convert_fusion.refs_0_), channel_id=1, source_target_pairs={{0,1},{1,0},{2,3},{3,2},{4,5},{5,4},{6,7},{7,6},{8,9},{9,8},{10,11... | collective-permute-start | bytes 1327112 | tf_op jit(solution)/shard_map/ppermute | solution.py:106
  32.6 11.4 %collective-permute-start.11 = (bf16[27,16,512]{2,1,0:T(8,128)(2,1)S(1)}, bf16[27,16,512]{2,1,0:T(8,128)(2,1)S(1)}, u32[]{:S(2)}, u32[]{:S(2)}) collective-permute-start(bf16[27,16,512]{2,1,0:T(8,128)(2,1)S(1)} %collective-permute-done.refs_2_), channel_id=1, source_target_pairs={{0,1},{1,0},{2,3},{3,2},{4,5},{5,4},{6,7},{7,6},{8,9},{9,8},{10,11... | collective-permute-start | bytes 1327112 | tf_op jit(solution)/shard_map/ppermute | solution.py:106
  32.7 11.7 %collective-permute-start.12 = (bf16[27,16,512]{2,1,0:T(8,128)(2,1)S(1)}, bf16[27,16,512]{2,1,0:T(8,128)(2,1)}, u32[]{:S(2)}, u32[]{:S(2)}) collective-permute-start(bf16[27,16,512]{2,1,0:T(8,128)(2,1)S(1)} %collective-permute-done.1.refs_4_), channel_id=1, source_target_pairs={{0,1},{1,0},{2,3},{3,2},{4,5},{5,4},{6,7},{7,6},{8,9},{9,8},{10,11... | collective-permute-start | bytes 1327112 | tf_op jit(solution)/shard_map/ppermute | solution.py:106
  41.6 4.1 %collective-permute-start.13 = (bf16[27,16,512]{2,1,0:T(8,128)(2,1)S(1)}, bf16[27,16,512]{2,1,0:T(8,128)(2,1)S(1)}, u32[]{:S(2)}, u32[]{:S(2)}) collective-permute-start(bf16[27,16,512]{2,1,0:T(8,128)(2,1)S(1)} %collective-permute-done.5.refs_6_), channel_id=1, source_target_pairs={{0,1},{1,0},{2,3},{3,2},{4,5},{5,4},{6,7},{7,6},{8,9},{9,8},{10,11... | collective-permute-start | bytes 1327112 | tf_op jit(solution)/shard_map/ppermute | solution.py:106
  43.5 2.2 collective-permute-start.14
  43.8 2.1 collective-permute-start.15
  44.0 2.5 %collective-permute-start.16 = (bf16[27,16,512]{2,1,0:T(8,128)(2,1)S(1)}, bf16[27,16,512]{2,1,0:T(8,128)(2,1)S(1)}, u32[]{:S(2)}, u32[]{:S(2)}) collective-permute-start(bf16[27,16,512]{2,1,0:T(8,128)(2,1)S(1)} %collective-permute-done.8.refs_12_), channel_id=1, source_target_pairs={{0,1},{1,0},{2,3},{3,2},{4,5},{5,4},{6,7},{7,6},{8,9},{9,8},{10,11... | collective-permute-start | bytes 1327112 | tf_op jit(solution)/shard_map/ppermute | solution.py:106
  44.3 12.3 %collective-permute-start.9 = (bf16[27,16,512]{2,1,0:T(8,128)(2,1)S(1)}, bf16[27,16,512]{2,1,0:T(8,128)(2,1)S(1)}, u32[]{:S(2)}, u32[]{:S(2)}) collective-permute-start(bf16[27,16,512]{2,1,0:T(8,128)(2,1)S(1)} %collective-permute-done.7.refs_10_), channel_id=1, source_target_pairs={{0,8},{1,9},{2,10},{3,11},{8,16},{9,17},{10,18},{11,19},{16,24},{1... | collective-permute-start | bytes 1327112 | tf_op jit(solution)/shard_map/ppermute | solution.py:1382
  56.6 1.8 collective-permute-start.17
  110.8 10.7 %collective-permute-start.18 = (bf16[40,16,512]{2,1,0:T(8,128)(2,1)}, bf16[40,16,512]{2,1,0:T(8,128)(2,1)S(1)}, u32[]{:S(2)}, u32[]{:S(2)}) collective-permute-start(bf16[40,16,512]{2,1,0:T(8,128)(2,1)} %get-tuple-element.130), channel_id=1, source_target_pairs={{0,1},{1,0},{2,3},{3,2},{4,5},{5,4},{6,7},{7,6},{8,9},{9,8},{10,11... | collective-permute-start | bytes 1966088 | tf_op jit(solution)/shard_map/ppermute | solution.py:106
  111.0 11.0 %copy-start.5 = (bf16[40,16,512]{2,1,0:T(8,128)(2,1)S(1)}, bf16[40,16,512]{2,1,0:T(8,128)(2,1)}, u32[]{:S(2)}) copy-start(bf16[40,16,512]{2,1,0:T(8,128)(2,1)} %get-tuple-element.129) | copy-start | bytes 1966084
  121.5 16.6 %collective-permute-start.19 = (bf16[48,16,512]{2,1,0:T(8,128)(2,1)}, bf16[48,16,512]{2,1,0:T(8,128)(2,1)S(1)}, u32[]{:S(2)}, u32[]{:S(2)}) collective-permute-start(bf16[48,16,512]{2,1,0:T(8,128)(2,1)} %get-tuple-element.141), channel_id=1, source_target_pairs={{0,1},{1,0},{2,3},{3,2},{4,5},{5,4},{6,7},{7,6},{8,9},{9,8},{10,11... | collective-permute-start | bytes 2359304 | tf_op jit(solution)/shard_map/ppermute | solution.py:106
  123.0 15.2 %copy-start.4 = (bf16[48,16,512]{2,1,0:T(8,128)(2,1)S(1)}, bf16[48,16,512]{2,1,0:T(8,128)(2,1)}, u32[]{:S(2)}) copy-start(bf16[48,16,512]{2,1,0:T(8,128)(2,1)} %get-tuple-element.140) | copy-start | bytes 2359300
  123.0 16.6 %collective-permute-start.21 = (bf16[40,8,512]{2,1,0:T(8,128)(2,1)S(1)}, bf16[40,8,512]{2,1,0:T(8,128)(2,1)S(1)}, u32[]{:S(2)}, u32[]{:S(2)}) collective-permute-start(bf16[40,8,512]{2,1,0:T(8,128)(2,1)S(1)} %get-tuple-element.221), channel_id=1, source_target_pairs={{0,2},{1,3},{2,0},{3,1},{4,6},{5,7},{6,4},{7,5},{8,10},{9,11},{10,... | collective-permute-start | bytes 983048 | tf_op jit(solution)/shard_map/ppermute | solution.py:106
  138.1 12.7 %collective-permute-start.20 = (bf16[48,16,512]{2,1,0:T(8,128)(2,1)}, bf16[48,16,512]{2,1,0:T(8,128)(2,1)S(1)}, u32[]{:S(2)}, u32[]{:S(2)}) collective-permute-start(bf16[48,16,512]{2,1,0:T(8,128)(2,1)} %get-tuple-element.148), channel_id=1, source_target_pairs={{0,1},{1,0},{2,3},{3,2},{4,5},{5,4},{6,7},{7,6},{8,9},{9,8},{10,11... | collective-permute-start | bytes 2359304 | tf_op jit(solution)/shard_map/ppermute | solution.py:106
  139.3 11.5 %collective-permute-start.22 = (bf16[48,8,512]{2,1,0:T(8,128)(2,1)S(1)}, bf16[48,8,512]{2,1,0:T(8,128)(2,1)S(1)}, u32[]{:S(2)}, u32[]{:S(2)}) collective-permute-start(bf16[48,8,512]{2,1,0:T(8,128)(2,1)S(1)} %get-tuple-element.219), channel_id=1, source_target_pairs={{0,2},{1,3},{2,0},{3,1},{4,6},{5,7},{6,4},{7,5},{8,10},{9,11},{10,... | collective-permute-start | bytes 1179656 | tf_op jit(solution)/shard_map/ppermute | solution.py:106
  139.6 9.1 %copy-start.23 = (bf16[40,8,512]{2,1,0:T(8,128)(2,1)}, bf16[40,8,512]{2,1,0:T(8,128)(2,1)S(1)}, u32[]{:S(2)}) copy-start(bf16[40,8,512]{2,1,0:T(8,128)(2,1)S(1)} %collective-permute-done.21.refs_3_) | copy-start | bytes 983044
  139.6 11.3 %copy-start.3 = (bf16[48,16,512]{2,1,0:T(8,128)(2,1)S(1)}, bf16[48,16,512]{2,1,0:T(8,128)(2,1)}, u32[]{:S(2)}) copy-start(bf16[48,16,512]{2,1,0:T(8,128)(2,1)} %get-tuple-element.147) | copy-start | bytes 2359300
  152.0 21.3 %collective-permute-start.23 = (bf16[48,8,512]{2,1,0:T(8,128)(2,1)S(1)}, bf16[48,8,512]{2,1,0:T(8,128)(2,1)S(1)}, u32[]{:S(2)}, u32[]{:S(2)}) collective-permute-start(bf16[48,8,512]{2,1,0:T(8,128)(2,1)S(1)} %get-tuple-element.217), channel_id=1, source_target_pairs={{0,2},{1,3},{2,0},{3,1},{4,6},{5,7},{6,4},{7,5},{8,10},{9,11},{10,... | collective-permute-start | bytes 1179656 | tf_op jit(solution)/shard_map/ppermute | solution.py:106
  153.2 26.2 %collective-permute-start.29 = (bf16[2,16,1536]{2,1,0:T(8,128)(2,1)S(1)}, bf16[2,16,1536]{2,1,0:T(8,128)(2,1)S(1)}, u32[]{:S(2)}, u32[]{:S(2)}) collective-permute-start(bf16[2,16,1536]{2,1,0:T(8,128)(2,1)S(1)} %slice.37), channel_id=1, source_target_pairs={{0,1},{1,2},{2,3},{4,5},{5,6},{6,7},{8,9},{9,10},{10,11},{12,13},{... | collective-permute-start | bytes 294920 | tf_op jit(solution)/shard_map/ppermute | solution.py:116
  166.1 7.1 %collective-permute-start.24 = (f32[24,512]{1,0:T(8,128)}, f32[24,512]{1,0:T(8,128)S(1)}, u32[]{:S(2)}, u32[]{:S(2)}) collective-permute-start(f32[24,512]{1,0:T(8,128)} %get-tuple-element.169), channel_id=1, source_target_pairs={{0,1},{1,0},{2,3},{3,2},{4,5},{5,4},{6,7},{7,6},{8,9},{9,8},{10,11... | collective-permute-start | bytes 147464 | tf_op jit(solution)/shard_map/ppermute | solution.py:106
  168.7 4.6 %collective-permute-start.26 = (f32[24,512]{1,0:T(8,128)}, f32[24,512]{1,0:T(8,128)S(1)}, u32[]{:S(2)}, u32[]{:S(2)}) collective-permute-start(f32[24,512]{1,0:T(8,128)} %get-tuple-element.171), channel_id=1, source_target_pairs={{0,3},{1,2},{2,1},{3,0},{4,7},{5,6},{6,5},{7,4},{8,11},{9,10},{10,... | collective-permute-start | bytes 147464 | tf_op jit(solution)/shard_map/ppermute | solution.py:106
  168.7 4.6 %collective-permute-start.25 = (f32[8,512]{1,0:T(8,128)}, f32[8,512]{1,0:T(8,128)S(1)}, u32[]{:S(2)}, u32[]{:S(2)}) collective-permute-start(f32[8,512]{1,0:T(8,128)} %get-tuple-element.170), channel_id=1, source_target_pairs={{0,2},{1,3},{2,0},{3,1},{4,6},{5,7},{6,4},{7,5},{8,10},{9,11},{10,... | collective-permute-start | bytes 49160 | tf_op jit(solution)/shard_map/ppermute | solution.py:106
  177.3 9.7 %collective-permute-start.27 = (bf16[27,8,512]{2,1,0:T(8,128)(2,1)}, bf16[27,8,512]{2,1,0:T(8,128)(2,1)S(1)}, u32[]{:S(2)}, u32[]{:S(2)}) collective-permute-start(bf16[27,8,512]{2,1,0:T(8,128)(2,1)} %get-tuple-element.177), channel_id=1, source_target_pairs={{0,8},{1,9},{2,10},{3,11},{8,16},{9,17},{10,18},{11,19},{16,24},{1... | collective-permute-start | bytes 663560 | tf_op jit(solution)/shard_map/ppermute | solution.py:1486
  178.8 8.3 %copy-start.1 = (bf16[216,8,512]{2,1,0:T(8,128)(2,1)S(1)}, bf16[216,8,512]{2,1,0:T(8,128)(2,1)}, u32[]{:S(2)}) copy-start(bf16[216,8,512]{2,1,0:T(8,128)(2,1)} %get-tuple-element.182) | copy-start | bytes 5308420
  178.8 8.3 %collective-permute-start.28 = (bf16[27,8,512]{2,1,0:T(8,128)(2,1)}, bf16[27,8,512]{2,1,0:T(8,128)(2,1)S(1)}, u32[]{:S(2)}, u32[]{:S(2)}) collective-permute-start(bf16[27,8,512]{2,1,0:T(8,128)(2,1)} %get-tuple-element.178), channel_id=1, source_target_pairs={{0,4},{1,5},{2,6},{3,7},{8,0},{9,1},{10,2},{11,3},{16,8},{17,9},{1... | collective-permute-start | bytes 663560 | tf_op jit(solution)/shard_map/ppermute | solution.py:1488
  187.2 6.9 %collective-permute-start.30 = (bf16[27,8,512]{2,1,0:T(8,128)(2,1)S(1)}, bf16[27,8,512]{2,1,0:T(8,128)(2,1)S(1)}, u32[]{:S(2)}, u32[]{:S(2)}) collective-permute-start(bf16[27,8,512]{2,1,0:T(8,128)(2,1)S(1)} %get-tuple-element.216), channel_id=1, source_target_pairs={{0,8},{1,9},{2,10},{3,11},{8,16},{9,17},{10,18},{11,19},{16,24},{1... | collective-permute-start | bytes 663560 | tf_op jit(solution)/shard_map/ppermute | solution.py:1486
  188.7 6.1 %collective-permute-start.31 = (bf16[27,8,512]{2,1,0:T(8,128)(2,1)S(1)}, bf16[27,8,512]{2,1,0:T(8,128)(2,1)S(1)}, u32[]{:S(2)}, u32[]{:S(2)}) collective-permute-start(bf16[27,8,512]{2,1,0:T(8,128)(2,1)S(1)} %get-tuple-element.215), channel_id=1, source_target_pairs={{0,4},{1,5},{2,6},{3,7},{8,0},{9,1},{10,2},{11,3},{16,8},{17,9},{1... | collective-permute-start | bytes 663560 | tf_op jit(solution)/shard_map/ppermute | solution.py:1488
  194.9 9.1 %collective-permute-start.32 = (bf16[27,8,512]{2,1,0:T(8,128)(2,1)S(1)}, bf16[27,8,512]{2,1,0:T(8,128)(2,1)S(1)}, u32[]{:S(2)}, u32[]{:S(2)}) collective-permute-start(bf16[27,8,512]{2,1,0:T(8,128)(2,1)S(1)} %get-tuple-element.214), channel_id=1, source_target_pairs={{0,8},{1,9},{2,10},{3,11},{8,16},{9,17},{10,18},{11,19},{16,24},{1... | collective-permute-start | bytes 663560 | tf_op jit(solution)/shard_map/ppermute | solution.py:1486
  196.4 7.7 %collective-permute-start.33 = (bf16[27,8,512]{2,1,0:T(8,128)(2,1)S(1)}, bf16[27,8,512]{2,1,0:T(8,128)(2,1)S(1)}, u32[]{:S(2)}, u32[]{:S(2)}) collective-permute-start(bf16[27,8,512]{2,1,0:T(8,128)(2,1)S(1)} %get-tuple-element.213), channel_id=1, source_target_pairs={{0,4},{1,5},{2,6},{3,7},{8,0},{9,1},{10,2},{11,3},{16,8},{17,9},{1... | collective-permute-start | bytes 663560 | tf_op jit(solution)/shard_map/ppermute | solution.py:1488
  204.1 6.2 %collective-permute-start.34 = (bf16[27,8,512]{2,1,0:T(8,128)(2,1)S(1)}, bf16[27,8,512]{2,1,0:T(8,128)(2,1)S(1)}, u32[]{:S(2)}, u32[]{:S(2)}) collective-permute-start(bf16[27,8,512]{2,1,0:T(8,128)(2,1)S(1)} %add_convert_fusion.4), channel_id=1, source_target_pairs={{0,8},{1,9},{2,10},{3,11},{8,16},{9,17},{10,18},{11,19},{16,24},{1... | collective-permute-start | bytes 663560 | tf_op jit(solution)/shard_map/ppermute | solution.py:1486
  210.5 6.0 %collective-permute-start.35 = (bf16[27,8,512]{2,1,0:T(8,128)(2,1)S(1)}, bf16[27,8,512]{2,1,0:T(8,128)(2,1)S(1)}, u32[]{:S(2)}, u32[]{:S(2)}) collective-permute-start(bf16[27,8,512]{2,1,0:T(8,128)(2,1)S(1)} %add_convert_fusion.3.mine_ref), channel_id=1, source_target_pairs={{0,2},{1,3},{2,0},{3,1},{4,6},{5,7},{6,4},{7,5},{8,10},{9,11},{10,... | collective-permute-start | bytes 663560 | tf_op jit(solution)/shard_map/ppermute | solution.py:106
  211.4 5.1 %collective-permute-start.37 = (bf16[27,8,512]{2,1,0:T(8,128)(2,1)S(1)}, bf16[27,8,512]{2,1,0:T(8,128)(2,1)S(1)}, u32[]{:S(2)}, u32[]{:S(2)}) collective-permute-start(bf16[27,8,512]{2,1,0:T(8,128)(2,1)S(1)} %add_convert_fusion.3.mine_ref), channel_id=1, source_target_pairs={{0,1},{1,0},{2,3},{3,2},{4,5},{5,4},{6,7},{7,6},{8,9},{9,8},{10,11... | collective-permute-start | bytes 663560 | tf_op jit(solution)/shard_map/ppermute | solution.py:106
  216.5 5.4 %collective-permute-start.36 = (bf16[27,8,512]{2,1,0:T(8,128)(2,1)S(1)}, bf16[27,8,512]{2,1,0:T(8,128)(2,1)S(1)}, u32[]{:S(2)}, u32[]{:S(2)}) collective-permute-start(bf16[27,8,512]{2,1,0:T(8,128)(2,1)S(1)} %collective-permute-done.35.mine_ref), channel_id=1, source_target_pairs={{0,1},{1,0},{2,3},{3,2},{4,5},{5,4},{6,7},{7,6},{8,9},{9,8},{10,11... | collective-permute-start | bytes 663560 | tf_op jit(solution)/shard_map/ppermute | solution.py:106
  (23 other events, 42.6 us)

commit v8 on v7

--- a/solution.py
+++ b/solution.py
@@ -674,9 +674,10 @@
         line = jnp.concatenate([last[25:26], last[26:27], last[27:28]], axis=1)
         line = jnp.broadcast_to(line, (16, 3 * channels))
         moved = pltpu.roll(line, 3 * channels - BINS, 1)
-        for at, value in ((0, line), (BIN_PAD, moved)):
-            picked = dot(value[:, 0:BIN_PAD].astype(BF16), order_ref[...], NN)
-            b_head[:, at : at + BIN_PAD] = picked[0:8]
+        both = jnp.concatenate([line[0:8, 0:BIN_PAD], moved[0:8, 0:BIN_PAD]], axis=0)
+        picked = dot(both.astype(BF16), order_ref[...], NN)
+        b_head[:, 0:BIN_PAD] = picked[0:8]
+        b_head[:, BIN_PAD:] = picked[8:16]
         inside = lax.broadcasted_iota(jnp.int32, (336, LANE), 0)
         for c in range(lane_tiles):
             cut = slice(c * LANE, (c + 1) * LANE)
@@ -1033,16 +1034,17 @@
                     line[:, c * channels : (c + 1) * channels], axis=0, keepdims=True
                 )
 
-            def bins(value):
-                value = jnp.broadcast_to(jnp.sum(value, axis=0, keepdims=True), (16, BIN_PAD))
-                total = jnp.zeros((16, BIN_PAD), F32)
+            parts = []
+            for at in (0, BIN_PAD):
+                value = jnp.sum(hsum_ref[:, at : at + BIN_PAD], axis=0, keepdims=True)
+                value = jnp.broadcast_to(value, (8, BIN_PAD))
                 for _ in range(3):
-                    part = value.astype(BF16)
-                    value = value - part.astype(F32)
-                    total = total + dot(part, order_ref[...], NT)
-                return total[0:8]
-
-            flat = jnp.concatenate([bins(hsum_ref[:, 0:BIN_PAD]), bins(hsum_ref[:, BIN_PAD:])], axis=1)
+                    part = value.astype(BF16).astype(F32)
+                    value = value - part
+                    parts.append(part)
+            moved = dot(jnp.concatenate(parts, axis=0).astype(BF16), order_ref[...], NT)
+            halves = [moved[at : at + 8] + moved[at + 8 : at + 16] + moved[at + 16 : at + 24] for at in (0, 24)]
+            flat = jnp.concatenate(halves, axis=1)
             column = lax.broadcasted_iota(jnp.int32, (8, 3 * channels), 1)
             moved = pltpu.roll(flat, 2 * BIN_PAD - (BIN_PAD - BINS), 1)
             joined = jnp.where(column < BINS, flat, moved)

time: 228 us -> 227 us (level)
  no operation moved by 1% of the time
where the time goes in v8:
time: 227 us; the launch traced here: 226 us
  Pallas kernels  153 us (67%)
  starting transfers between devices  36 us (16%)
  waiting for transfers between devices  23.4 us (10%)
  local copies, waits for them, and re-layouts  10.6 us (5%)
    pallas_call x1, Pallas kernels, forward(): pl.pallas_call(functools.partial(forward_body, owners=owners, slots=slots...  51.5 us
    pallas_call x2, Pallas kernels, mlp_backward(): pl.pallas_call(functools.partial(mlp_body, utts=utts), grid=(count // til...  21.1 us
    pallas_call x2, Pallas kernels, norm_backward(): pl.pallas_call(functools.partial(norm_body, row=row, tiles=tiles, utts=ut...  19.1 us
    pallas_call x2, Pallas kernels, spectrum_cotangent(): pl.pallas_call(functools.partial(pre_body, start=start, tiles=tiles, rows...  15.1 us
    ppermute x20, starting transfers between devices, seq_swap(): return lax.ppermute(value, 'seq', [(s, s ^ bit) for s in range(count)])  14.2 us
    pallas_call x2, Pallas kernels, wave_forward(): pl.pallas_call(functools.partial(wave_body, start=start, rows=rows, utts=...  14.1 us
    ppermute x20, waiting for transfers between devices, seq_swap(): return lax.ppermute(value, 'seq', [(s, s ^ bit) for s in range(count)])  12.9 us
    pallas_call x2, Pallas kernels, conv_backward(): pl.pallas_call(functools.partial(conv_body, row=row, tiles=tiles, utts=ut...  9.58 us
  transfers between devices with their start and end apart: 38, of which 13 were waited for; matrix products, arithmetic and copies ran while one was open for 2% of the time, Pallas kernels for 43%

profile of v8, /device:TPU:0, one launch (start us, length us, event | category | flops | bytes accessed | tf_op | source)
XLA Modules:
  0.0 225.8 jit_solution(5524620752660067587)
XLA Ops:
  0.6 1.2 dynamic-slice_convert_fusion.refs_0_
  1.9 3.1 %collective-permute-start = (bf16[27,16,512]{2,1,0:T(8,128)(2,1)S(1)}, bf16[27,16,512]{2,1,0:T(8,128)(2,1)S(1)}, u32[]{:S(2)}, u32[]{:S(2)}) collective-permute-start(bf16[27,16,512]{2,1,0:T(8,128)(2,1)S(1)} %dynamic-slice_convert_fusion.refs_0_), channel_id=1, source_target_pairs={{0,8},{1,9},{2,10},{3,11},{8,16},{9,17},{10,18},{11,19},{16,24},{1... | collective-permute-start | bytes 1327112 | tf_op jit(solution)/shard_map/ppermute | solution.py:1384
  5.8 1.4 collective-permute-start.2
  7.2 1.3 collective-permute-start.3
  9.3 1.3 collective-permute-start.4
  11.2 4.2 %plan.1 = (s32[2,12]{1,0:T(2,128)}, s32[1,216]{1,0:T(1,128)}, s32[1,27]{1,0:T(1,128)}, s32[1,137]{1,0:T(1,128)}, s32[1,8]{1,0:T(1,128)}) custom-call(s32[2]{0:T(128)} %pad_add_fusion.ids, s32[2,4]{1,0:T(2,128)} %lengths.1, s32[2,4]{1,0:T(2,128)} %bw_ids.1, s32[137]{0:T(256)} %owner_list.1, s32[8]{0:T(128)} %constant.54.clone.order, s32[8]{0:T(128)} %constant.55.clone.offsets), custom_call_target="tpu_custom_call" | custom-call | flops 8000 | bytes 8192 | tf_op jit(solution)/shard_map/plan/pallas_call | solution.py:259
  15.4 1.2 collective-permute-done.1.refs_4_
  16.6 1.6 collective-permute-start.5
  18.7 7.5 %spectrum_cotangent_0.1.rest_0_ = bf16[2,1024,1536]{2,1,0:T(8,128)(2,1)} custom-call(s32[2,12]{1,0:T(2,128)} %get-tuple-element.110.meta, bf16[5120,128]{1,0:T(8,128)(2,1)} %bitcast.33, bf16[80,128]{1,0:T(8,128)(2,1)} %copy-done.29, bf16[2,768,768]{2,1,0:T(8,128)(2,1)} %constant.52.clone.synth_ref, f32[8,384]{1,0:T(8,128)} %constant.53.clone.win_ref), custom_call_target="tpu_custom_call" | custom-call | flops 2415919104 | bytes 7340032 | tf_op jit(solution)/shard_map/spectrum_cotangent_0/pallas_call | solution.py:329
  26.2 1.3 collective-permute-done.5.refs_6_
  27.5 1.9 collective-permute-done.6.refs_8_
  29.3 1.6 collective-permute-start.7
  31.4 1.2 collective-permute-start.10
  33.1 7.6 %spectrum_cotangent_2.1.cot_ref = bf16[2,1024,1536]{2,1,0:T(8,128)(2,1)} custom-call(s32[2,12]{1,0:T(2,128)} %get-tuple-element.110.meta, bf16[5120,128]{1,0:T(8,128)(2,1)} %bitcast.34, bf16[80,128]{1,0:T(8,128)(2,1)} %copy-done.29, bf16[2,768,768]{2,1,0:T(8,128)(2,1)} %constant.52.clone.synth_ref, ...), custom_call_target="tpu_custom_call", output_to_operand_aliasing={{}: (5, {})} | custom-call | flops 2415919104 | bytes 7340032 | tf_op jit(solution)/shard_map/spectrum_cotangent_2/pallas_call | solution.py:329
  40.7 0.9 collective-permute-done.7.refs_10_
  41.6 0.9 collective-permute-start.13
  42.5 1.0 collective-permute-done.8.refs_12_
  44.3 1.4 collective-permute-start.9
  47.4 5.8 %assemble.1.rest_2_ = bf16[4384,512]{1,0:T(8,128)(2,1)} custom-call(s32[2,12]{1,0:T(2,128)} %get-tuple-element.110.meta, s32[1,216]{1,0:T(1,128)} %get-tuple-element.126.places, s32[1,8]{1,0:T(1,128)} %get-tuple-element.112.counts, bf16[27,16,512]{2,1,0:T(8,128)(2,1)} %copy-done, bf16[27,16,512]{2,1,0:T(8,128)(2,1)} %copy-done.14, ...), custom_call_target="tpu_custom_call" | custom-call | bytes 12582912 | tf_op jit(solution)/shard_map/assemble/pallas_call | solution.py:379
  53.2 3.4 %collective-permute-done.9.rest_0_ = bf16[27,16,512]{2,1,0:T(8,128)(2,1)S(1)} collective-permute-done((bf16[27,16,512]{2,1,0:T(8,128)(2,1)S(1)}, bf16[27,16,512]{2,1,0:T(8,128)(2,1)S(1)}, u32[]{:S(2)}, u32[]{:S(2)}) %collective-permute-start.9) | collective-permute-done | bytes 442400 | tf_op jit(solution)/shard_map/ppermute | solution.py:1384
  56.6 1.8 collective-permute-done.17.rest_1_
  59.2 51.5 %forward.1 = (bf16[4384,512]{1,0:T(8,128)(2,1)}, bf16[2,1024,1536]{2,1,0:T(8,128)(2,1)}, bf16[2048,1536]{1,0:T(8,128)(2,1)}, bf16[2048,1536]{1,0:T(8,128)(2,1)},...) custom-call(s32[2,12]{1,0:T(2,128)} %get-tuple-element.110.meta, ...), custom_call_target="tpu_custom_call" | custom-call | flops 16106127360 | bytes 41943040 | tf_op jit(solution)/shard_map/forward/pallas_call | solution.py:788
  110.8 10.5 %mlp_backward_0.1 = (bf16[2048,1536]{1,0:T(8,128)(2,1)}, bf16[48,16,512]{2,1,0:T(8,128)(2,1)}, bf16[48,16,512]{2,1,0:T(8,128)(2,1)}, f32[8,768]{1,0:T(8,128)}) custom-call(s32[2,12]{1,0:T(2,128)} %get-tuple-element.110.meta, bf16[2048,512]{1,0:T(8,128)(2,1)} %get-tuple-element.131.low_ref, bf16[2048,1536]{1,0:T(8,128)(2,1)} %get-tuple-element.132.act_ref, ...), custom_call_target="tpu_custom_call" | custom-call | flops 4831838208 | bytes 16777216 | tf_op jit(solution)/shard_map/mlp_backward_0/pallas_call | solution.py:899
  122.9 4.6 %collective-permute-start.21 = (bf16[40,8,512]{2,1,0:T(8,128)(2,1)S(1)}, bf16[40,8,512]{2,1,0:T(8,128)(2,1)S(1)}, u32[]{:S(2)}, u32[]{:S(2)}) collective-permute-start(bf16[40,8,512]{2,1,0:T(8,128)(2,1)S(1)} %get-tuple-element.221), channel_id=1, source_target_pairs={{0,2},{1,3},{2,0},{3,1},{4,6},{5,7},{6,4},{7,5},{8,10},{9,11},{10,... | collective-permute-start | bytes 983048 | tf_op jit(solution)/shard_map/ppermute | solution.py:106
  127.4 10.6 %mlp_backward_1.1 = (bf16[2048,1536]{1,0:T(8,128)(2,1)}, bf16[48,16,512]{2,1,0:T(8,128)(2,1)}, bf16[48,16,512]{2,1,0:T(8,128)(2,1)}, f32[8,768]{1,0:T(8,128)}) custom-call(s32[2,12]{1,0:T(2,128)} %get-tuple-element.110.meta, bf16[2048,512]{1,0:T(8,128)(2,1)} %get-tuple-element.131.low_ref, ...), custom_call_target="tpu_custom_call", output_to_operand_aliasing={{0}: (6, {})} | custom-call | flops 4831838208 | bytes 16777216 | tf_op jit(solution)/shard_map/mlp_backward_1/pallas_call | solution.py:899
  138.4 0.8 constant_dynamic-slice_fusion.2
  139.4 8.9 %norm_backward_0.1 = (bf16[1024,512]{1,0:T(8,128)(2,1)}, f32[2,8,512]{2,1,0:T(8,128)}, f32[16,8,512]{2,1,0:T(8,128)}) custom-call(s32[2,12]{1,0:T(2,128)} %get-tuple-element.110.meta, bf16[2,1024,512]{2,1,0:T(8,128)(2,1)} %x_ref.5, bf16[2,16,512]{2,1,0:T(8,128)(2,1)} %copy-done.27, bf16[2,16,512]{2,1,0:T(8,128)(2,1)} %copy-done.28, ...), custom_call_target="tpu_custom_call" | custom-call | flops 1610612736 | bytes 12582912 | tf_op jit(solution)/shard_map/norm_backward_0/pallas_call | solution.py:1081
  148.4 2.3 %collective-permute-done.22.refs_4_ = bf16[48,8,512]{2,1,0:T(8,128)(2,1)S(1)} collective-permute-done((bf16[48,8,512]{2,1,0:T(8,128)(2,1)S(1)}, bf16[48,8,512]{2,1,0:T(8,128)(2,1)S(1)}, u32[]{:S(2)}, u32[]{:S(2)}) %collective-permute-start.22) | collective-permute-done | bytes 393248 | tf_op jit(solution)/shard_map/ppermute | solution.py:106
  152.1 0.9 slice.37
  153.0 1.4 collective-permute-start.29
  154.4 10.1 %norm_backward_1.1 = (bf16[1024,512]{1,0:T(8,128)(2,1)}, f32[2,8,512]{2,1,0:T(8,128)}, f32[16,8,512]{2,1,0:T(8,128)}, f32[8,512]{1,0:T(8,128)}, f32[24,512]{1,0:...) custom-call(s32[2,12]{1,0:T(2,128)} %get-tuple-element.110.meta, bf16[2,1024,512]{2,1,0:T(8,128)(2,1)} %x_ref.5, ...), custom_call_target="tpu_custom_call" | custom-call | flops 1610612736 | bytes 12582912 | tf_op jit(solution)/shard_map/norm_backward_1/pallas_call | solution.py:1081
  164.6 2.4 %collective-permute-start.24 = (f32[24,512]{1,0:T(8,128)}, f32[24,512]{1,0:T(8,128)S(1)}, u32[]{:S(2)}, u32[]{:S(2)}) collective-permute-start(f32[24,512]{1,0:T(8,128)} %get-tuple-element.169), channel_id=1, source_target_pairs={{0,1},{1,0},{2,3},{3,2},{4,5},{5,4},{6,7},{7,6},{8,9},{9,8},{10,11... | collective-permute-start | bytes 147464 | tf_op jit(solution)/shard_map/ppermute | solution.py:106
  167.0 1.7 collective-permute-start.25
  168.7 2.9 %collective-permute-done.25.refs_8_ = f32[8,512]{1,0:T(8,128)S(1)} collective-permute-done((f32[8,512]{1,0:T(8,128)}, f32[8,512]{1,0:T(8,128)S(1)}, u32[]{:S(2)}, u32[]{:S(2)}) %collective-permute-start.25) | collective-permute-done | bytes 16416 | tf_op jit(solution)/shard_map/ppermute | solution.py:106
  172.4 3.3 %to_slots.1 = (bf16[216,8,512]{2,1,0:T(8,128)(2,1)}, bf16[27,8,512]{2,1,0:T(8,128)(2,1)}, bf16[27,8,512]{2,1,0:T(8,128)(2,1)}) custom-call(s32[1,137]{1,0:T(1,128)} %get-tuple-element.108.slot_of, bf16[40,8,512]{2,1,0:T(8,128)(2,1)} %get-tuple-element.222.refs_0_, bf16[48,8,512]{2,1,0:T(8,128)(2,1)} %get-tuple-element.220.refs_1_, ...), custom_call_target="tpu_custom_call" | custom-call | bytes 6291456 | tf_op jit(solution)/shard_map/to_slots/pallas_call | solution.py:1269
  175.6 1.6 collective-permute-start.27
  178.3 7.1 %wave_forward_0.1.rest_0_ = f32[5120,128]{1,0:T(8,128)} custom-call(s32[2,12]{1,0:T(2,128)} %get-tuple-element.110.meta, bf16[2,1024,1536]{2,1,0:T(8,128)(2,1)} %get-tuple-element.189.spec_ref.prev_ref, bf16[2,1024,1536]{2,1,0:T(8,128)(2,1)} %get-tuple-element.189.spec_ref.prev_ref, bf16[2,16,1536]{2,1,0:T(8,128)(2,1)} %copy-done.20, ...), custom_call_target="tpu_custom_call" | custom-call | flops 2415919104 | bytes 10485760 | tf_op jit(solution)/shard_map/wave_forward_0/pallas_call | solution.py:1221
  185.5 1.7 collective-permute-start.30
  187.6 4.8 %conv_backward_0.1.rest_0_ = f32[2,1024,512]{2,1,0:T(8,128)} custom-call(s32[2,12]{1,0:T(2,128)} %get-tuple-element.110.meta, bf16[1024,512]{1,0:T(8,128)(2,1)} %get-tuple-element.185.cg_ref.before_ref.after_ref, bf16[1024,512]{1,0:T(8,128)(2,1)} %get-tuple-element.185.cg_ref.before_ref.after_ref, ...), custom_call_target="tpu_custom_call" | custom-call | flops 8388608 | bytes 6291456 | tf_op jit(solution)/shard_map/conv_backward_0/pallas_call | solution.py:1149
  192.4 0.9 collective-permute-done.31
  193.4 1.6 collective-permute-start.32
  195.5 7.0 %wave_forward_2.1 = f32[5120,128]{1,0:T(8,128)} custom-call(s32[2,12]{1,0:T(2,128)} %get-tuple-element.110.meta, bf16[2,1024,1536]{2,1,0:T(8,128)(2,1)} %get-tuple-element.189.spec_ref.prev_ref, bf16[2,1024,1536]{2,1,0:T(8,128)(2,1)} %get-tuple-element.189.spec_ref.prev_ref, bf16[2,16,1536]{2,1,0:T(8,128)(2,1)} %copy-done.20, ...), custom_call_target="tpu_custom_call", output_to_operand_aliasing={{}: (6, {})} | custom-call | flops 2415919104 | bytes 10485760 | tf_op jit(solution)/shard_map/wave_forward_2/pallas_call | solution.py:1221
  202.6 1.6 collective-permute-start.34
  204.2 4.8 %conv_backward_1.1 = f32[2,1024,512]{2,1,0:T(8,128)} custom-call(s32[2,12]{1,0:T(2,128)} %get-tuple-element.110.meta, bf16[1024,512]{1,0:T(8,128)(2,1)} %get-tuple-element.195.cg_ref.before_ref.after_ref, bf16[1024,512]{1,0:T(8,128)(2,1)} %get-tuple-element.195.cg_ref.before_ref.after_ref, ...), custom_call_target="tpu_custom_call", output_to_operand_aliasing={{}: (8, {})} | custom-call | flops 8388608 | bytes 6291456 | tf_op jit(solution)/shard_map/conv_backward_1/pallas_call | solution.py:1149
  209.1 0.9 collective-permute-start.35
  210.0 5.1 %collective-permute-done.35.mine_ref = bf16[27,8,512]{2,1,0:T(8,128)(2,1)S(1)} collective-permute-done((bf16[27,8,512]{2,1,0:T(8,128)(2,1)S(1)}, bf16[27,8,512]{2,1,0:T(8,128)(2,1)S(1)}, u32[]{:S(2)}, u32[]{:S(2)}) %collective-permute-start.35) | collective-permute-done | bytes 221216 | tf_op jit(solution)/shard_map/ppermute | solution.py:106
  215.9 4.6 %adam_first.1 = (f32[27,2,2,8,512]{4,3,2,1,0:T(8,128)}, f32[27,2,2,8,512]{4,3,2,1,0:T(8,128)}, f32[27,2,2,8,512]{4,3,2,1,0:T(8,128)}) custom-call(s32[1,27]{1,0:T(1,128)} %get-tuple-element.198.places, s32[2,12]{1,0:T(2,128)} %get-tuple-element.110.meta, bf16[27,8,512]{2,1,0:T(8,128)(2,1)} %copy-done.2, bf16[27,8,512]{2,1,0:T(8,128)(2,1)} %copy-done.26, ...), custom_call_target="tpu_custom_call" | custom-call | bytes 6291456 | tf_op jit(solution)/shard_map/adam_first/pallas_call | solution.py:1312
  221.2 4.6 %adam_second.1 = (f32[27,2,2,8,512]{4,3,2,1,0:T(8,128)}, f32[27,2,2,8,512]{4,3,2,1,0:T(8,128)}, f32[27,2,2,8,512]{4,3,2,1,0:T(8,128)}) custom-call(s32[1,27]{1,0:T(1,128)} %get-tuple-element.198.places, s32[2,12]{1,0:T(2,128)} %get-tuple-element.110.meta, bf16[27,8,512]{2,1,0:T(8,128)(2,1)} %copy-done.24, ...), custom_call_target="tpu_custom_call", output_to_operand_aliasing={{0}: (7, {}), {1}: (8, {}), {2}: (9, {})} | custom-call | bytes 6291456 | tf_op jit(solution)/shard_map/adam_second/pallas_call | solution.py:1312
  (125 shorter events, 15.0 us)
Async XLA Ops:
  1.9 29.5 %copy-start = (bf16[27,16,512]{2,1,0:T(8,128)(2,1)}, bf16[27,16,512]{2,1,0:T(8,128)(2,1)S(1)}, u32[]{:S(2)}) copy-start(bf16[27,16,512]{2,1,0:T(8,128)(2,1)S(1)} %dynamic-slice_convert_fusion.refs_0_) | copy-start | bytes 1327108
  1.9 13.5 %collective-permute-start = (bf16[27,16,512]{2,1,0:T(8,128)(2,1)S(1)}, bf16[27,16,512]{2,1,0:T(8,128)(2,1)S(1)}, u32[]{:S(2)}, u32[]{:S(2)}) collective-permute-start(bf16[27,16,512]{2,1,0:T(8,128)(2,1)S(1)} %dynamic-slice_convert_fusion.refs_0_), channel_id=1, source_target_pairs={{0,8},{1,9},{2,10},{3,11},{8,16},{9,17},{10,18},{11,19},{16,24},{1... | collective-permute-start | bytes 1327112 | tf_op jit(solution)/shard_map/ppermute | solution.py:1384
  5.0 11.6 %collective-permute-start.1 = (bf16[27,16,512]{2,1,0:T(8,128)(2,1)S(1)}, bf16[27,16,512]{2,1,0:T(8,128)(2,1)S(1)}, u32[]{:S(2)}, u32[]{:S(2)}) collective-permute-start(bf16[27,16,512]{2,1,0:T(8,128)(2,1)S(1)} %dynamic-slice_convert_fusion.refs_0_), channel_id=1, source_target_pairs={{0,4},{1,5},{2,6},{3,7},{8,0},{9,1},{10,2},{11,3},{16,8},{17,9},{1... | collective-permute-start | bytes 1327112 | tf_op jit(solution)/shard_map/ppermute | solution.py:1386
  5.8 9.6 %collective-permute-start.2 = (bf16[2,16,512]{2,1,0:T(8,128)(2,1)S(1)}, bf16[2,16,512]{2,1,0:T(8,128)(2,1)S(1)}, u32[]{:S(2)}, u32[]{:S(2)}) collective-permute-start(bf16[2,16,512]{2,1,0:T(8,128)(2,1)S(1)} %get-tuple-element.212), channel_id=1, source_target_pairs={{0,1},{1,2},{2,3},{4,5},{5,6},{6,7},{8,9},{9,10},{10,11},{12,13},{... | collective-permute-start | bytes 98312 | tf_op jit(solution)/shard_map/ppermute | solution.py:116
  7.2 8.2 %collective-permute-start.3 = (bf16[2,16,512]{2,1,0:T(8,128)(2,1)S(1)}, bf16[2,16,512]{2,1,0:T(8,128)(2,1)S(1)}, u32[]{:S(2)}, u32[]{:S(2)}) collective-permute-start(bf16[2,16,512]{2,1,0:T(8,128)(2,1)S(1)} %get-tuple-element.211), channel_id=1, source_target_pairs={{1,0},{2,1},{3,2},{5,4},{6,5},{7,6},{9,8},{10,9},{11,10},{13,12},{... | collective-permute-start | bytes 98312 | tf_op jit(solution)/shard_map/ppermute | solution.py:116
  9.3 6.1 %collective-permute-start.4 = (bf16[80,128]{1,0:T(8,128)(2,1)S(1)}, bf16[80,128]{1,0:T(8,128)(2,1)S(1)}, u32[]{:S(2)}, u32[]{:S(2)}) collective-permute-start(bf16[80,128]{1,0:T(8,128)(2,1)S(1)} %bitcast.38), channel_id=1, source_target_pairs={{1,0},{2,1},{3,2},{5,4},{6,5},{7,6},{9,8},{10,9},{11,10},{13,12},{... | collective-permute-start | bytes 61448 | tf_op jit(solution)/shard_map/ppermute | solution.py:116
  15.4 17.2 %copy-start.8 = (bf16[27,16,512]{2,1,0:T(8,128)(2,1)}, bf16[27,16,512]{2,1,0:T(8,128)(2,1)S(1)}, u32[]{:S(2)}) copy-start(bf16[27,16,512]{2,1,0:T(8,128)(2,1)S(1)} %collective-permute-done.refs_2_) | copy-start | bytes 1327108
  16.6 16.0 %copy-start.9 = (bf16[27,16,512]{2,1,0:T(8,128)(2,1)}, bf16[27,16,512]{2,1,0:T(8,128)(2,1)S(1)}, u32[]{:S(2)}) copy-start(bf16[27,16,512]{2,1,0:T(8,128)(2,1)S(1)} %collective-permute-done.1.refs_4_) | copy-start | bytes 1327108
  16.6 10.9 %collective-permute-start.5 = (bf16[27,16,512]{2,1,0:T(8,128)(2,1)S(1)}, bf16[27,16,512]{2,1,0:T(8,128)(2,1)S(1)}, u32[]{:S(2)}, u32[]{:S(2)}) collective-permute-start(bf16[27,16,512]{2,1,0:T(8,128)(2,1)S(1)} %collective-permute-done.refs_2_), channel_id=1, source_target_pairs={{0,8},{1,9},{2,10},{3,11},{8,16},{9,17},{10,18},{11,19},{16,24},{1... | collective-permute-start | bytes 1327112 | tf_op jit(solution)/shard_map/ppermute | solution.py:1384
  18.2 11.1 %collective-permute-start.6 = (bf16[27,16,512]{2,1,0:T(8,128)(2,1)S(1)}, bf16[27,16,512]{2,1,0:T(8,128)(2,1)S(1)}, u32[]{:S(2)}, u32[]{:S(2)}) collective-permute-start(bf16[27,16,512]{2,1,0:T(8,128)(2,1)S(1)} %collective-permute-done.1.refs_4_), channel_id=1, source_target_pairs={{0,4},{1,5},{2,6},{3,7},{8,0},{9,1},{10,2},{11,3},{16,8},{17,9},{1... | collective-permute-start | bytes 1327112 | tf_op jit(solution)/shard_map/ppermute | solution.py:1386
  27.5 14.1 %copy-start.10 = (bf16[27,16,512]{2,1,0:T(8,128)(2,1)}, bf16[27,16,512]{2,1,0:T(8,128)(2,1)S(1)}, u32[]{:S(2)}) copy-start(bf16[27,16,512]{2,1,0:T(8,128)(2,1)S(1)} %collective-permute-done.5.refs_6_) | copy-start | bytes 1327108
  29.3 14.2 %copy-start.11 = (bf16[27,16,512]{2,1,0:T(8,128)(2,1)}, bf16[27,16,512]{2,1,0:T(8,128)(2,1)S(1)}, u32[]{:S(2)}) copy-start(bf16[27,16,512]{2,1,0:T(8,128)(2,1)S(1)} %collective-permute-done.6.refs_8_) | copy-start | bytes 1327108
  29.3 12.3 %collective-permute-start.7 = (bf16[27,16,512]{2,1,0:T(8,128)(2,1)S(1)}, bf16[27,16,512]{2,1,0:T(8,128)(2,1)S(1)}, u32[]{:S(2)}, u32[]{:S(2)}) collective-permute-start(bf16[27,16,512]{2,1,0:T(8,128)(2,1)S(1)} %collective-permute-done.5.refs_6_), channel_id=1, source_target_pairs={{0,8},{1,9},{2,10},{3,11},{8,16},{9,17},{10,18},{11,19},{16,24},{1... | collective-permute-start | bytes 1327112 | tf_op jit(solution)/shard_map/ppermute | solution.py:1384
  30.9 12.6 %collective-permute-start.8 = (bf16[27,16,512]{2,1,0:T(8,128)(2,1)S(1)}, bf16[27,16,512]{2,1,0:T(8,128)(2,1)S(1)}, u32[]{:S(2)}, u32[]{:S(2)}) collective-permute-start(bf16[27,16,512]{2,1,0:T(8,128)(2,1)S(1)} %collective-permute-done.6.refs_8_), channel_id=1, source_target_pairs={{0,4},{1,5},{2,6},{3,7},{8,0},{9,1},{10,2},{11,3},{16,8},{17,9},{1... | collective-permute-start | bytes 1327112 | tf_op jit(solution)/shard_map/ppermute | solution.py:1386
  31.4 12.4 %collective-permute-start.10 = (bf16[27,16,512]{2,1,0:T(8,128)(2,1)S(1)}, bf16[27,16,512]{2,1,0:T(8,128)(2,1)S(1)}, u32[]{:S(2)}, u32[]{:S(2)}) collective-permute-start(bf16[27,16,512]{2,1,0:T(8,128)(2,1)S(1)} %dynamic-slice_convert_fusion.refs_0_), channel_id=1, source_target_pairs={{0,1},{1,0},{2,3},{3,2},{4,5},{5,4},{6,7},{7,6},{8,9},{9,8},{10,11... | collective-permute-start | bytes 1327112 | tf_op jit(solution)/shard_map/ppermute | solution.py:106
  32.6 11.4 %collective-permute-start.11 = (bf16[27,16,512]{2,1,0:T(8,128)(2,1)S(1)}, bf16[27,16,512]{2,1,0:T(8,128)(2,1)S(1)}, u32[]{:S(2)}, u32[]{:S(2)}) collective-permute-start(bf16[27,16,512]{2,1,0:T(8,128)(2,1)S(1)} %collective-permute-done.refs_2_), channel_id=1, source_target_pairs={{0,1},{1,0},{2,3},{3,2},{4,5},{5,4},{6,7},{7,6},{8,9},{9,8},{10,11... | collective-permute-start | bytes 1327112 | tf_op jit(solution)/shard_map/ppermute | solution.py:106
  32.7 11.7 %collective-permute-start.12 = (bf16[27,16,512]{2,1,0:T(8,128)(2,1)S(1)}, bf16[27,16,512]{2,1,0:T(8,128)(2,1)}, u32[]{:S(2)}, u32[]{:S(2)}) collective-permute-start(bf16[27,16,512]{2,1,0:T(8,128)(2,1)S(1)} %collective-permute-done.1.refs_4_), channel_id=1, source_target_pairs={{0,1},{1,0},{2,3},{3,2},{4,5},{5,4},{6,7},{7,6},{8,9},{9,8},{10,11... | collective-permute-start | bytes 1327112 | tf_op jit(solution)/shard_map/ppermute | solution.py:106
  41.6 4.1 %collective-permute-start.13 = (bf16[27,16,512]{2,1,0:T(8,128)(2,1)S(1)}, bf16[27,16,512]{2,1,0:T(8,128)(2,1)S(1)}, u32[]{:S(2)}, u32[]{:S(2)}) collective-permute-start(bf16[27,16,512]{2,1,0:T(8,128)(2,1)S(1)} %collective-permute-done.5.refs_6_), channel_id=1, source_target_pairs={{0,1},{1,0},{2,3},{3,2},{4,5},{5,4},{6,7},{7,6},{8,9},{9,8},{10,11... | collective-permute-start | bytes 1327112 | tf_op jit(solution)/shard_map/ppermute | solution.py:106
  43.5 2.2 collective-permute-start.14
  43.8 2.1 collective-permute-start.15
  44.0 2.5 %collective-permute-start.16 = (bf16[27,16,512]{2,1,0:T(8,128)(2,1)S(1)}, bf16[27,16,512]{2,1,0:T(8,128)(2,1)S(1)}, u32[]{:S(2)}, u32[]{:S(2)}) collective-permute-start(bf16[27,16,512]{2,1,0:T(8,128)(2,1)S(1)} %collective-permute-done.8.refs_12_), channel_id=1, source_target_pairs={{0,1},{1,0},{2,3},{3,2},{4,5},{5,4},{6,7},{7,6},{8,9},{9,8},{10,11... | collective-permute-start | bytes 1327112 | tf_op jit(solution)/shard_map/ppermute | solution.py:106
  44.3 12.3 %collective-permute-start.9 = (bf16[27,16,512]{2,1,0:T(8,128)(2,1)S(1)}, bf16[27,16,512]{2,1,0:T(8,128)(2,1)S(1)}, u32[]{:S(2)}, u32[]{:S(2)}) collective-permute-start(bf16[27,16,512]{2,1,0:T(8,128)(2,1)S(1)} %collective-permute-done.7.refs_10_), channel_id=1, source_target_pairs={{0,8},{1,9},{2,10},{3,11},{8,16},{9,17},{10,18},{11,19},{16,24},{1... | collective-permute-start | bytes 1327112 | tf_op jit(solution)/shard_map/ppermute | solution.py:1384
  56.6 1.8 collective-permute-start.17
  110.6 10.7 %collective-permute-start.18 = (bf16[40,16,512]{2,1,0:T(8,128)(2,1)}, bf16[40,16,512]{2,1,0:T(8,128)(2,1)S(1)}, u32[]{:S(2)}, u32[]{:S(2)}) collective-permute-start(bf16[40,16,512]{2,1,0:T(8,128)(2,1)} %get-tuple-element.130), channel_id=1, source_target_pairs={{0,1},{1,0},{2,3},{3,2},{4,5},{5,4},{6,7},{7,6},{8,9},{9,8},{10,11... | collective-permute-start | bytes 1966088 | tf_op jit(solution)/shard_map/ppermute | solution.py:106
  110.8 11.0 %copy-start.5 = (bf16[40,16,512]{2,1,0:T(8,128)(2,1)S(1)}, bf16[40,16,512]{2,1,0:T(8,128)(2,1)}, u32[]{:S(2)}) copy-start(bf16[40,16,512]{2,1,0:T(8,128)(2,1)} %get-tuple-element.129) | copy-start | bytes 1966084
  121.4 16.6 %collective-permute-start.19 = (bf16[48,16,512]{2,1,0:T(8,128)(2,1)}, bf16[48,16,512]{2,1,0:T(8,128)(2,1)S(1)}, u32[]{:S(2)}, u32[]{:S(2)}) collective-permute-start(bf16[48,16,512]{2,1,0:T(8,128)(2,1)} %get-tuple-element.141), channel_id=1, source_target_pairs={{0,1},{1,0},{2,3},{3,2},{4,5},{5,4},{6,7},{7,6},{8,9},{9,8},{10,11... | collective-permute-start | bytes 2359304 | tf_op jit(solution)/shard_map/ppermute | solution.py:106
  122.9 15.2 %copy-start.4 = (bf16[48,16,512]{2,1,0:T(8,128)(2,1)S(1)}, bf16[48,16,512]{2,1,0:T(8,128)(2,1)}, u32[]{:S(2)}) copy-start(bf16[48,16,512]{2,1,0:T(8,128)(2,1)} %get-tuple-element.140) | copy-start | bytes 2359300
  122.9 16.6 %collective-permute-start.21 = (bf16[40,8,512]{2,1,0:T(8,128)(2,1)S(1)}, bf16[40,8,512]{2,1,0:T(8,128)(2,1)S(1)}, u32[]{:S(2)}, u32[]{:S(2)}) collective-permute-start(bf16[40,8,512]{2,1,0:T(8,128)(2,1)S(1)} %get-tuple-element.221), channel_id=1, source_target_pairs={{0,2},{1,3},{2,0},{3,1},{4,6},{5,7},{6,4},{7,5},{8,10},{9,11},{10,... | collective-permute-start | bytes 983048 | tf_op jit(solution)/shard_map/ppermute | solution.py:106
  138.0 12.7 %collective-permute-start.20 = (bf16[48,16,512]{2,1,0:T(8,128)(2,1)}, bf16[48,16,512]{2,1,0:T(8,128)(2,1)S(1)}, u32[]{:S(2)}, u32[]{:S(2)}) collective-permute-start(bf16[48,16,512]{2,1,0:T(8,128)(2,1)} %get-tuple-element.148), channel_id=1, source_target_pairs={{0,1},{1,0},{2,3},{3,2},{4,5},{5,4},{6,7},{7,6},{8,9},{9,8},{10,11... | collective-permute-start | bytes 2359304 | tf_op jit(solution)/shard_map/ppermute | solution.py:106
  139.2 11.5 %collective-permute-start.22 = (bf16[48,8,512]{2,1,0:T(8,128)(2,1)S(1)}, bf16[48,8,512]{2,1,0:T(8,128)(2,1)S(1)}, u32[]{:S(2)}, u32[]{:S(2)}) collective-permute-start(bf16[48,8,512]{2,1,0:T(8,128)(2,1)S(1)} %get-tuple-element.219), channel_id=1, source_target_pairs={{0,2},{1,3},{2,0},{3,1},{4,6},{5,7},{6,4},{7,5},{8,10},{9,11},{10,... | collective-permute-start | bytes 1179656 | tf_op jit(solution)/shard_map/ppermute | solution.py:106
  139.4 9.0 %copy-start.23 = (bf16[40,8,512]{2,1,0:T(8,128)(2,1)}, bf16[40,8,512]{2,1,0:T(8,128)(2,1)S(1)}, u32[]{:S(2)}) copy-start(bf16[40,8,512]{2,1,0:T(8,128)(2,1)S(1)} %collective-permute-done.21.refs_3_) | copy-start | bytes 983044
  139.4 11.3 %copy-start.3 = (bf16[48,16,512]{2,1,0:T(8,128)(2,1)S(1)}, bf16[48,16,512]{2,1,0:T(8,128)(2,1)}, u32[]{:S(2)}) copy-start(bf16[48,16,512]{2,1,0:T(8,128)(2,1)} %get-tuple-element.147) | copy-start | bytes 2359300
  151.8 19.8 %collective-permute-start.23 = (bf16[48,8,512]{2,1,0:T(8,128)(2,1)S(1)}, bf16[48,8,512]{2,1,0:T(8,128)(2,1)S(1)}, u32[]{:S(2)}, u32[]{:S(2)}) collective-permute-start(bf16[48,8,512]{2,1,0:T(8,128)(2,1)S(1)} %get-tuple-element.217), channel_id=1, source_target_pairs={{0,2},{1,3},{2,0},{3,1},{4,6},{5,7},{6,4},{7,5},{8,10},{9,11},{10,... | collective-permute-start | bytes 1179656 | tf_op jit(solution)/shard_map/ppermute | solution.py:106
  153.0 24.6 %collective-permute-start.29 = (bf16[2,16,1536]{2,1,0:T(8,128)(2,1)S(1)}, bf16[2,16,1536]{2,1,0:T(8,128)(2,1)S(1)}, u32[]{:S(2)}, u32[]{:S(2)}) collective-permute-start(bf16[2,16,1536]{2,1,0:T(8,128)(2,1)S(1)} %slice.37), channel_id=1, source_target_pairs={{0,1},{1,2},{2,3},{4,5},{5,6},{6,7},{8,9},{9,10},{10,11},{12,13},{... | collective-permute-start | bytes 294920 | tf_op jit(solution)/shard_map/ppermute | solution.py:116
  164.6 7.0 %collective-permute-start.24 = (f32[24,512]{1,0:T(8,128)}, f32[24,512]{1,0:T(8,128)S(1)}, u32[]{:S(2)}, u32[]{:S(2)}) collective-permute-start(f32[24,512]{1,0:T(8,128)} %get-tuple-element.169), channel_id=1, source_target_pairs={{0,1},{1,0},{2,3},{3,2},{4,5},{5,4},{6,7},{7,6},{8,9},{9,8},{10,11... | collective-permute-start | bytes 147464 | tf_op jit(solution)/shard_map/ppermute | solution.py:106
  167.0 4.6 %collective-permute-start.26 = (f32[24,512]{1,0:T(8,128)}, f32[24,512]{1,0:T(8,128)S(1)}, u32[]{:S(2)}, u32[]{:S(2)}) collective-permute-start(f32[24,512]{1,0:T(8,128)} %get-tuple-element.171), channel_id=1, source_target_pairs={{0,3},{1,2},{2,1},{3,0},{4,7},{5,6},{6,5},{7,4},{8,11},{9,10},{10,... | collective-permute-start | bytes 147464 | tf_op jit(solution)/shard_map/ppermute | solution.py:106
  167.0 4.6 %collective-permute-start.25 = (f32[8,512]{1,0:T(8,128)}, f32[8,512]{1,0:T(8,128)S(1)}, u32[]{:S(2)}, u32[]{:S(2)}) collective-permute-start(f32[8,512]{1,0:T(8,128)} %get-tuple-element.170), channel_id=1, source_target_pairs={{0,2},{1,3},{2,0},{3,1},{4,6},{5,7},{6,4},{7,5},{8,10},{9,11},{10,... | collective-permute-start | bytes 49160 | tf_op jit(solution)/shard_map/ppermute | solution.py:106
  175.6 9.7 %collective-permute-start.27 = (bf16[27,8,512]{2,1,0:T(8,128)(2,1)}, bf16[27,8,512]{2,1,0:T(8,128)(2,1)S(1)}, u32[]{:S(2)}, u32[]{:S(2)}) collective-permute-start(bf16[27,8,512]{2,1,0:T(8,128)(2,1)} %get-tuple-element.177), channel_id=1, source_target_pairs={{0,8},{1,9},{2,10},{3,11},{8,16},{9,17},{10,18},{11,19},{16,24},{1... | collective-permute-start | bytes 663560 | tf_op jit(solution)/shard_map/ppermute | solution.py:1488
  177.2 8.1 %copy-start.1 = (bf16[216,8,512]{2,1,0:T(8,128)(2,1)S(1)}, bf16[216,8,512]{2,1,0:T(8,128)(2,1)}, u32[]{:S(2)}) copy-start(bf16[216,8,512]{2,1,0:T(8,128)(2,1)} %get-tuple-element.182) | copy-start | bytes 5308420
  177.3 8.1 %collective-permute-start.28 = (bf16[27,8,512]{2,1,0:T(8,128)(2,1)}, bf16[27,8,512]{2,1,0:T(8,128)(2,1)S(1)}, u32[]{:S(2)}, u32[]{:S(2)}) collective-permute-start(bf16[27,8,512]{2,1,0:T(8,128)(2,1)} %get-tuple-element.178), channel_id=1, source_target_pairs={{0,4},{1,5},{2,6},{3,7},{8,0},{9,1},{10,2},{11,3},{16,8},{17,9},{1... | collective-permute-start | bytes 663560 | tf_op jit(solution)/shard_map/ppermute | solution.py:1490
  185.5 6.9 %collective-permute-start.30 = (bf16[27,8,512]{2,1,0:T(8,128)(2,1)S(1)}, bf16[27,8,512]{2,1,0:T(8,128)(2,1)S(1)}, u32[]{:S(2)}, u32[]{:S(2)}) collective-permute-start(bf16[27,8,512]{2,1,0:T(8,128)(2,1)S(1)} %get-tuple-element.216), channel_id=1, source_target_pairs={{0,8},{1,9},{2,10},{3,11},{8,16},{9,17},{10,18},{11,19},{16,24},{1... | collective-permute-start | bytes 663560 | tf_op jit(solution)/shard_map/ppermute | solution.py:1488
  187.2 6.1 %collective-permute-start.31 = (bf16[27,8,512]{2,1,0:T(8,128)(2,1)S(1)}, bf16[27,8,512]{2,1,0:T(8,128)(2,1)S(1)}, u32[]{:S(2)}, u32[]{:S(2)}) collective-permute-start(bf16[27,8,512]{2,1,0:T(8,128)(2,1)S(1)} %get-tuple-element.215), channel_id=1, source_target_pairs={{0,4},{1,5},{2,6},{3,7},{8,0},{9,1},{10,2},{11,3},{16,8},{17,9},{1... | collective-permute-start | bytes 663560 | tf_op jit(solution)/shard_map/ppermute | solution.py:1490
  193.4 9.1 %collective-permute-start.32 = (bf16[27,8,512]{2,1,0:T(8,128)(2,1)S(1)}, bf16[27,8,512]{2,1,0:T(8,128)(2,1)S(1)}, u32[]{:S(2)}, u32[]{:S(2)}) collective-permute-start(bf16[27,8,512]{2,1,0:T(8,128)(2,1)S(1)} %get-tuple-element.214), channel_id=1, source_target_pairs={{0,8},{1,9},{2,10},{3,11},{8,16},{9,17},{10,18},{11,19},{16,24},{1... | collective-permute-start | bytes 663560 | tf_op jit(solution)/shard_map/ppermute | solution.py:1488
  195.0 7.5 %collective-permute-start.33 = (bf16[27,8,512]{2,1,0:T(8,128)(2,1)S(1)}, bf16[27,8,512]{2,1,0:T(8,128)(2,1)S(1)}, u32[]{:S(2)}, u32[]{:S(2)}) collective-permute-start(bf16[27,8,512]{2,1,0:T(8,128)(2,1)S(1)} %get-tuple-element.213), channel_id=1, source_target_pairs={{0,4},{1,5},{2,6},{3,7},{8,0},{9,1},{10,2},{11,3},{16,8},{17,9},{1... | collective-permute-start | bytes 663560 | tf_op jit(solution)/shard_map/ppermute | solution.py:1490
  202.6 6.4 %collective-permute-start.34 = (bf16[27,8,512]{2,1,0:T(8,128)(2,1)S(1)}, bf16[27,8,512]{2,1,0:T(8,128)(2,1)S(1)}, u32[]{:S(2)}, u32[]{:S(2)}) collective-permute-start(bf16[27,8,512]{2,1,0:T(8,128)(2,1)S(1)} %add_convert_fusion.4), channel_id=1, source_target_pairs={{0,8},{1,9},{2,10},{3,11},{8,16},{9,17},{10,18},{11,19},{16,24},{1... | collective-permute-start | bytes 663560 | tf_op jit(solution)/shard_map/ppermute | solution.py:1488
  209.1 6.0 %collective-permute-start.35 = (bf16[27,8,512]{2,1,0:T(8,128)(2,1)S(1)}, bf16[27,8,512]{2,1,0:T(8,128)(2,1)S(1)}, u32[]{:S(2)}, u32[]{:S(2)}) collective-permute-start(bf16[27,8,512]{2,1,0:T(8,128)(2,1)S(1)} %add_convert_fusion.3.mine_ref), channel_id=1, source_target_pairs={{0,2},{1,3},{2,0},{3,1},{4,6},{5,7},{6,4},{7,5},{8,10},{9,11},{10,... | collective-permute-start | bytes 663560 | tf_op jit(solution)/shard_map/ppermute | solution.py:106
  210.0 5.1 %collective-permute-start.37 = (bf16[27,8,512]{2,1,0:T(8,128)(2,1)S(1)}, bf16[27,8,512]{2,1,0:T(8,128)(2,1)S(1)}, u32[]{:S(2)}, u32[]{:S(2)}) collective-permute-start(bf16[27,8,512]{2,1,0:T(8,128)(2,1)S(1)} %add_convert_fusion.3.mine_ref), channel_id=1, source_target_pairs={{0,1},{1,0},{2,3},{3,2},{4,5},{5,4},{6,7},{7,6},{8,9},{9,8},{10,11... | collective-permute-start | bytes 663560 | tf_op jit(solution)/shard_map/ppermute | solution.py:106
  215.1 5.4 %collective-permute-start.36 = (bf16[27,8,512]{2,1,0:T(8,128)(2,1)S(1)}, bf16[27,8,512]{2,1,0:T(8,128)(2,1)S(1)}, u32[]{:S(2)}, u32[]{:S(2)}) collective-permute-start(bf16[27,8,512]{2,1,0:T(8,128)(2,1)S(1)} %collective-permute-done.35.mine_ref), channel_id=1, source_target_pairs={{0,1},{1,0},{2,3},{3,2},{4,5},{5,4},{6,7},{7,6},{8,9},{9,8},{10,11... | collective-permute-start | bytes 663560 | tf_op jit(solution)/shard_map/ppermute | solution.py:106
  (23 other events, 42.6 us)

commit v9 on v8

--- a/solution.py
+++ b/solution.py
@@ -1255,7 +1255,7 @@
             out[slot_of[0, start + b]] = value.astype(BF16)
             return carry
 
-        lax.fori_loop(0, stop - start, one, 0, unroll=8)
+        lax.fori_loop(0, stop - start, one, 0, unroll=True)
     total = last_refs[0][0:QUART, :]
     for ref in last_refs[1:]:
         total = total + ref[0:QUART, :]

time: 227 us -> 227 us (level)
  no operation moved by 1% of the time
where the time goes in v9:
time: 227 us; the launch traced here: 226 us
  Pallas kernels  153 us (67%)
  starting transfers between devices  36.1 us (16%)
  waiting for transfers between devices  23.2 us (10%)
  local copies, waits for them, and re-layouts  10.6 us (5%)
    pallas_call x1, Pallas kernels, forward(): pl.pallas_call(functools.partial(forward_body, owners=owners, slots=slots...  51.4 us
    pallas_call x2, Pallas kernels, mlp_backward(): pl.pallas_call(functools.partial(mlp_body, utts=utts), grid=(count // til...  21.1 us
    pallas_call x2, Pallas kernels, norm_backward(): pl.pallas_call(functools.partial(norm_body, row=row, tiles=tiles, utts=ut...  19.1 us
    pallas_call x2, Pallas kernels, spectrum_cotangent(): pl.pallas_call(functools.partial(pre_body, start=start, tiles=tiles, rows...  15.1 us
    ppermute x20, starting transfers between devices, seq_swap(): return lax.ppermute(value, 'seq', [(s, s ^ bit) for s in range(count)])  14.4 us
    pallas_call x2, Pallas kernels, wave_forward(): pl.pallas_call(functools.partial(wave_body, start=start, rows=rows, utts=...  14.1 us
    ppermute x20, waiting for transfers between devices, seq_swap(): return lax.ppermute(value, 'seq', [(s, s ^ bit) for s in range(count)])  12.9 us
    pallas_call x2, Pallas kernels, conv_backward(): pl.pallas_call(functools.partial(conv_body, row=row, tiles=tiles, utts=ut...  9.58 us
  transfers between devices with their start and end apart: 38, of which 13 were waited for; matrix products, arithmetic and copies ran while one was open for 2% of the time, Pallas kernels for 43%

profile of v9, /device:TPU:0, one launch (start us, length us, event | category | flops | bytes accessed | tf_op | source)
XLA Modules:
  0.0 225.6 jit_solution(16732493384413551748)
XLA Ops:
  0.6 1.2 dynamic-slice_convert_fusion.refs_0_
  1.9 3.1 %collective-permute-start = (bf16[27,16,512]{2,1,0:T(8,128)(2,1)S(1)}, bf16[27,16,512]{2,1,0:T(8,128)(2,1)S(1)}, u32[]{:S(2)}, u32[]{:S(2)}) collective-permute-start(bf16[27,16,512]{2,1,0:T(8,128)(2,1)S(1)} %dynamic-slice_convert_fusion.refs_0_), channel_id=1, source_target_pairs={{0,8},{1,9},{2,10},{3,11},{8,16},{9,17},{10,18},{11,19},{16,24},{1... | collective-permute-start | bytes 1327112 | tf_op jit(solution)/shard_map/ppermute | solution.py:1384
  5.8 1.4 collective-permute-start.2
  7.2 1.3 collective-permute-start.3
  9.3 1.3 collective-permute-start.4
  11.2 4.2 %plan.1 = (s32[2,12]{1,0:T(2,128)}, s32[1,216]{1,0:T(1,128)}, s32[1,27]{1,0:T(1,128)}, s32[1,137]{1,0:T(1,128)}, s32[1,8]{1,0:T(1,128)}) custom-call(s32[2]{0:T(128)} %pad_add_fusion.ids, s32[2,4]{1,0:T(2,128)} %lengths.1, s32[2,4]{1,0:T(2,128)} %bw_ids.1, s32[137]{0:T(256)} %owner_list.1, s32[8]{0:T(128)} %constant.54.clone.order, s32[8]{0:T(128)} %constant.55.clone.offsets), custom_call_target="tpu_custom_call" | custom-call | flops 8000 | bytes 8192 | tf_op jit(solution)/shard_map/plan/pallas_call | solution.py:259
  15.4 1.2 collective-permute-done.1.refs_4_
  16.6 1.6 collective-permute-start.5
  18.7 7.5 %spectrum_cotangent_0.1.rest_0_ = bf16[2,1024,1536]{2,1,0:T(8,128)(2,1)} custom-call(s32[2,12]{1,0:T(2,128)} %get-tuple-element.110.meta, bf16[5120,128]{1,0:T(8,128)(2,1)} %bitcast.33, bf16[80,128]{1,0:T(8,128)(2,1)} %copy-done.29, bf16[2,768,768]{2,1,0:T(8,128)(2,1)} %constant.52.clone.synth_ref, f32[8,384]{1,0:T(8,128)} %constant.53.clone.win_ref), custom_call_target="tpu_custom_call" | custom-call | flops 2415919104 | bytes 7340032 | tf_op jit(solution)/shard_map/spectrum_cotangent_0/pallas_call | solution.py:329
  26.2 1.3 collective-permute-done.5.refs_6_
  27.5 1.9 collective-permute-done.6.refs_8_
  29.3 1.6 collective-permute-start.7
  31.4 1.2 collective-permute-start.10
  33.1 7.6 %spectrum_cotangent_2.1.cot_ref = bf16[2,1024,1536]{2,1,0:T(8,128)(2,1)} custom-call(s32[2,12]{1,0:T(2,128)} %get-tuple-element.110.meta, bf16[5120,128]{1,0:T(8,128)(2,1)} %bitcast.34, bf16[80,128]{1,0:T(8,128)(2,1)} %copy-done.29, bf16[2,768,768]{2,1,0:T(8,128)(2,1)} %constant.52.clone.synth_ref, ...), custom_call_target="tpu_custom_call", output_to_operand_aliasing={{}: (5, {})} | custom-call | flops 2415919104 | bytes 7340032 | tf_op jit(solution)/shard_map/spectrum_cotangent_2/pallas_call | solution.py:329
  40.7 0.9 collective-permute-done.7.refs_10_
  41.6 0.9 collective-permute-start.13
  42.5 1.0 collective-permute-done.8.refs_12_
  44.3 1.4 collective-permute-start.9
  47.4 5.9 %assemble.1.rest_2_ = bf16[4384,512]{1,0:T(8,128)(2,1)} custom-call(s32[2,12]{1,0:T(2,128)} %get-tuple-element.110.meta, s32[1,216]{1,0:T(1,128)} %get-tuple-element.126.places, s32[1,8]{1,0:T(1,128)} %get-tuple-element.112.counts, bf16[27,16,512]{2,1,0:T(8,128)(2,1)} %copy-done, bf16[27,16,512]{2,1,0:T(8,128)(2,1)} %copy-done.14, ...), custom_call_target="tpu_custom_call" | custom-call | bytes 12582912 | tf_op jit(solution)/shard_map/assemble/pallas_call | solution.py:379
  53.4 3.3 %collective-permute-done.9.rest_0_ = bf16[27,16,512]{2,1,0:T(8,128)(2,1)S(1)} collective-permute-done((bf16[27,16,512]{2,1,0:T(8,128)(2,1)S(1)}, bf16[27,16,512]{2,1,0:T(8,128)(2,1)S(1)}, u32[]{:S(2)}, u32[]{:S(2)}) %collective-permute-start.9) | collective-permute-done | bytes 442400 | tf_op jit(solution)/shard_map/ppermute | solution.py:1384
  56.6 1.8 collective-permute-done.17.rest_1_
  59.2 51.4 %forward.1 = (bf16[4384,512]{1,0:T(8,128)(2,1)}, bf16[2,1024,1536]{2,1,0:T(8,128)(2,1)}, bf16[2048,1536]{1,0:T(8,128)(2,1)}, bf16[2048,1536]{1,0:T(8,128)(2,1)},...) custom-call(s32[2,12]{1,0:T(2,128)} %get-tuple-element.110.meta, ...), custom_call_target="tpu_custom_call" | custom-call | flops 16106127360 | bytes 41943040 | tf_op jit(solution)/shard_map/forward/pallas_call | solution.py:788
  110.8 10.5 %mlp_backward_0.1 = (bf16[2048,1536]{1,0:T(8,128)(2,1)}, bf16[48,16,512]{2,1,0:T(8,128)(2,1)}, bf16[48,16,512]{2,1,0:T(8,128)(2,1)}, f32[8,768]{1,0:T(8,128)}) custom-call(s32[2,12]{1,0:T(2,128)} %get-tuple-element.110.meta, bf16[2048,512]{1,0:T(8,128)(2,1)} %get-tuple-element.131.low_ref, bf16[2048,1536]{1,0:T(8,128)(2,1)} %get-tuple-element.132.act_ref, ...), custom_call_target="tpu_custom_call" | custom-call | flops 4831838208 | bytes 16777216 | tf_op jit(solution)/shard_map/mlp_backward_0/pallas_call | solution.py:899
  122.8 4.6 %collective-permute-start.21 = (bf16[40,8,512]{2,1,0:T(8,128)(2,1)S(1)}, bf16[40,8,512]{2,1,0:T(8,128)(2,1)S(1)}, u32[]{:S(2)}, u32[]{:S(2)}) collective-permute-start(bf16[40,8,512]{2,1,0:T(8,128)(2,1)S(1)} %get-tuple-element.221), channel_id=1, source_target_pairs={{0,2},{1,3},{2,0},{3,1},{4,6},{5,7},{6,4},{7,5},{8,10},{9,11},{10,... | collective-permute-start | bytes 983048 | tf_op jit(solution)/shard_map/ppermute | solution.py:106
  127.4 10.6 %mlp_backward_1.1 = (bf16[2048,1536]{1,0:T(8,128)(2,1)}, bf16[48,16,512]{2,1,0:T(8,128)(2,1)}, bf16[48,16,512]{2,1,0:T(8,128)(2,1)}, f32[8,768]{1,0:T(8,128)}) custom-call(s32[2,12]{1,0:T(2,128)} %get-tuple-element.110.meta, bf16[2048,512]{1,0:T(8,128)(2,1)} %get-tuple-element.131.low_ref, ...), custom_call_target="tpu_custom_call", output_to_operand_aliasing={{0}: (6, {})} | custom-call | flops 4831838208 | bytes 16777216 | tf_op jit(solution)/shard_map/mlp_backward_1/pallas_call | solution.py:899
  138.3 0.8 constant_dynamic-slice_fusion.2
  139.4 8.9 %norm_backward_0.1 = (bf16[1024,512]{1,0:T(8,128)(2,1)}, f32[2,8,512]{2,1,0:T(8,128)}, f32[16,8,512]{2,1,0:T(8,128)}) custom-call(s32[2,12]{1,0:T(2,128)} %get-tuple-element.110.meta, bf16[2,1024,512]{2,1,0:T(8,128)(2,1)} %x_ref.5, bf16[2,16,512]{2,1,0:T(8,128)(2,1)} %copy-done.27, bf16[2,16,512]{2,1,0:T(8,128)(2,1)} %copy-done.28, ...), custom_call_target="tpu_custom_call" | custom-call | flops 1610612736 | bytes 12582912 | tf_op jit(solution)/shard_map/norm_backward_0/pallas_call | solution.py:1081
  148.3 2.3 %collective-permute-done.22.refs_4_ = bf16[48,8,512]{2,1,0:T(8,128)(2,1)S(1)} collective-permute-done((bf16[48,8,512]{2,1,0:T(8,128)(2,1)S(1)}, bf16[48,8,512]{2,1,0:T(8,128)(2,1)S(1)}, u32[]{:S(2)}, u32[]{:S(2)}) %collective-permute-start.22) | collective-permute-done | bytes 393248 | tf_op jit(solution)/shard_map/ppermute | solution.py:106
  151.0 0.8 constant_dynamic-slice_fusion
  152.1 0.9 slice.37
  153.0 1.4 collective-permute-start.29
  154.4 10.1 %norm_backward_1.1 = (bf16[1024,512]{1,0:T(8,128)(2,1)}, f32[2,8,512]{2,1,0:T(8,128)}, f32[16,8,512]{2,1,0:T(8,128)}, f32[8,512]{1,0:T(8,128)}, f32[24,512]{1,0:...) custom-call(s32[2,12]{1,0:T(2,128)} %get-tuple-element.110.meta, bf16[2,1024,512]{2,1,0:T(8,128)(2,1)} %x_ref.5, ...), custom_call_target="tpu_custom_call" | custom-call | flops 1610612736 | bytes 12582912 | tf_op jit(solution)/shard_map/norm_backward_1/pallas_call | solution.py:1081
  164.5 2.5 %collective-permute-start.24 = (f32[24,512]{1,0:T(8,128)}, f32[24,512]{1,0:T(8,128)S(1)}, u32[]{:S(2)}, u32[]{:S(2)}) collective-permute-start(f32[24,512]{1,0:T(8,128)} %get-tuple-element.169), channel_id=1, source_target_pairs={{0,1},{1,0},{2,3},{3,2},{4,5},{5,4},{6,7},{7,6},{8,9},{9,8},{10,11... | collective-permute-start | bytes 147464 | tf_op jit(solution)/shard_map/ppermute | solution.py:106
  167.0 1.7 collective-permute-start.25
  168.7 2.9 %collective-permute-done.25.refs_8_ = f32[8,512]{1,0:T(8,128)S(1)} collective-permute-done((f32[8,512]{1,0:T(8,128)}, f32[8,512]{1,0:T(8,128)S(1)}, u32[]{:S(2)}, u32[]{:S(2)}) %collective-permute-start.25) | collective-permute-done | bytes 16416 | tf_op jit(solution)/shard_map/ppermute | solution.py:106
  172.4 3.2 %to_slots.1 = (bf16[216,8,512]{2,1,0:T(8,128)(2,1)}, bf16[27,8,512]{2,1,0:T(8,128)(2,1)}, bf16[27,8,512]{2,1,0:T(8,128)(2,1)}) custom-call(s32[1,137]{1,0:T(1,128)} %get-tuple-element.108.slot_of, bf16[40,8,512]{2,1,0:T(8,128)(2,1)} %get-tuple-element.222.refs_0_, bf16[48,8,512]{2,1,0:T(8,128)(2,1)} %get-tuple-element.220.refs_1_, ...), custom_call_target="tpu_custom_call" | custom-call | bytes 6291456 | tf_op jit(solution)/shard_map/to_slots/pallas_call | solution.py:1269
  175.6 1.5 collective-permute-start.27
  178.3 7.1 %wave_forward_0.1.rest_0_ = f32[5120,128]{1,0:T(8,128)} custom-call(s32[2,12]{1,0:T(2,128)} %get-tuple-element.110.meta, bf16[2,1024,1536]{2,1,0:T(8,128)(2,1)} %get-tuple-element.189.spec_ref.prev_ref, bf16[2,1024,1536]{2,1,0:T(8,128)(2,1)} %get-tuple-element.189.spec_ref.prev_ref, bf16[2,16,1536]{2,1,0:T(8,128)(2,1)} %copy-done.20, ...), custom_call_target="tpu_custom_call" | custom-call | flops 2415919104 | bytes 10485760 | tf_op jit(solution)/shard_map/wave_forward_0/pallas_call | solution.py:1221
  185.5 1.5 collective-permute-start.30
  187.6 4.8 %conv_backward_0.1.rest_0_ = f32[2,1024,512]{2,1,0:T(8,128)} custom-call(s32[2,12]{1,0:T(2,128)} %get-tuple-element.110.meta, bf16[1024,512]{1,0:T(8,128)(2,1)} %get-tuple-element.185.cg_ref.before_ref.after_ref, bf16[1024,512]{1,0:T(8,128)(2,1)} %get-tuple-element.185.cg_ref.before_ref.after_ref, ...), custom_call_target="tpu_custom_call" | custom-call | flops 8388608 | bytes 6291456 | tf_op jit(solution)/shard_map/conv_backward_0/pallas_call | solution.py:1149
  193.2 1.6 collective-permute-start.32
  195.3 7.0 %wave_forward_2.1 = f32[5120,128]{1,0:T(8,128)} custom-call(s32[2,12]{1,0:T(2,128)} %get-tuple-element.110.meta, bf16[2,1024,1536]{2,1,0:T(8,128)(2,1)} %get-tuple-element.189.spec_ref.prev_ref, bf16[2,1024,1536]{2,1,0:T(8,128)(2,1)} %get-tuple-element.189.spec_ref.prev_ref, bf16[2,16,1536]{2,1,0:T(8,128)(2,1)} %copy-done.20, ...), custom_call_target="tpu_custom_call", output_to_operand_aliasing={{}: (6, {})} | custom-call | flops 2415919104 | bytes 10485760 | tf_op jit(solution)/shard_map/wave_forward_2/pallas_call | solution.py:1221
  202.4 1.6 collective-permute-start.34
  204.0 4.8 %conv_backward_1.1 = f32[2,1024,512]{2,1,0:T(8,128)} custom-call(s32[2,12]{1,0:T(2,128)} %get-tuple-element.110.meta, bf16[1024,512]{1,0:T(8,128)(2,1)} %get-tuple-element.195.cg_ref.before_ref.after_ref, bf16[1024,512]{1,0:T(8,128)(2,1)} %get-tuple-element.195.cg_ref.before_ref.after_ref, ...), custom_call_target="tpu_custom_call", output_to_operand_aliasing={{}: (8, {})} | custom-call | flops 8388608 | bytes 6291456 | tf_op jit(solution)/shard_map/conv_backward_1/pallas_call | solution.py:1149
  208.9 0.9 collective-permute-start.35
  209.8 5.1 %collective-permute-done.35.mine_ref = bf16[27,8,512]{2,1,0:T(8,128)(2,1)S(1)} collective-permute-done((bf16[27,8,512]{2,1,0:T(8,128)(2,1)S(1)}, bf16[27,8,512]{2,1,0:T(8,128)(2,1)S(1)}, u32[]{:S(2)}, u32[]{:S(2)}) %collective-permute-start.35) | collective-permute-done | bytes 221216 | tf_op jit(solution)/shard_map/ppermute | solution.py:106
  215.7 4.6 %adam_first.1 = (f32[27,2,2,8,512]{4,3,2,1,0:T(8,128)}, f32[27,2,2,8,512]{4,3,2,1,0:T(8,128)}, f32[27,2,2,8,512]{4,3,2,1,0:T(8,128)}) custom-call(s32[1,27]{1,0:T(1,128)} %get-tuple-element.198.places, s32[2,12]{1,0:T(2,128)} %get-tuple-element.110.meta, bf16[27,8,512]{2,1,0:T(8,128)(2,1)} %copy-done.2, bf16[27,8,512]{2,1,0:T(8,128)(2,1)} %copy-done.26, ...), custom_call_target="tpu_custom_call" | custom-call | bytes 6291456 | tf_op jit(solution)/shard_map/adam_first/pallas_call | solution.py:1312
  221.0 4.6 %adam_second.1 = (f32[27,2,2,8,512]{4,3,2,1,0:T(8,128)}, f32[27,2,2,8,512]{4,3,2,1,0:T(8,128)}, f32[27,2,2,8,512]{4,3,2,1,0:T(8,128)}) custom-call(s32[1,27]{1,0:T(1,128)} %get-tuple-element.198.places, s32[2,12]{1,0:T(2,128)} %get-tuple-element.110.meta, bf16[27,8,512]{2,1,0:T(8,128)(2,1)} %copy-done.24, ...), custom_call_target="tpu_custom_call", output_to_operand_aliasing={{0}: (7, {}), {1}: (8, {}), {2}: (9, {})} | custom-call | bytes 6291456 | tf_op jit(solution)/shard_map/adam_second/pallas_call | solution.py:1312
  (125 shorter events, 15.3 us)
Async XLA Ops:
  1.9 29.5 %copy-start = (bf16[27,16,512]{2,1,0:T(8,128)(2,1)}, bf16[27,16,512]{2,1,0:T(8,128)(2,1)S(1)}, u32[]{:S(2)}) copy-start(bf16[27,16,512]{2,1,0:T(8,128)(2,1)S(1)} %dynamic-slice_convert_fusion.refs_0_) | copy-start | bytes 1327108
  1.9 13.5 %collective-permute-start = (bf16[27,16,512]{2,1,0:T(8,128)(2,1)S(1)}, bf16[27,16,512]{2,1,0:T(8,128)(2,1)S(1)}, u32[]{:S(2)}, u32[]{:S(2)}) collective-permute-start(bf16[27,16,512]{2,1,0:T(8,128)(2,1)S(1)} %dynamic-slice_convert_fusion.refs_0_), channel_id=1, source_target_pairs={{0,8},{1,9},{2,10},{3,11},{8,16},{9,17},{10,18},{11,19},{16,24},{1... | collective-permute-start | bytes 1327112 | tf_op jit(solution)/shard_map/ppermute | solution.py:1384
  5.0 11.6 %collective-permute-start.1 = (bf16[27,16,512]{2,1,0:T(8,128)(2,1)S(1)}, bf16[27,16,512]{2,1,0:T(8,128)(2,1)S(1)}, u32[]{:S(2)}, u32[]{:S(2)}) collective-permute-start(bf16[27,16,512]{2,1,0:T(8,128)(2,1)S(1)} %dynamic-slice_convert_fusion.refs_0_), channel_id=1, source_target_pairs={{0,4},{1,5},{2,6},{3,7},{8,0},{9,1},{10,2},{11,3},{16,8},{17,9},{1... | collective-permute-start | bytes 1327112 | tf_op jit(solution)/shard_map/ppermute | solution.py:1386
  5.8 9.6 %collective-permute-start.2 = (bf16[2,16,512]{2,1,0:T(8,128)(2,1)S(1)}, bf16[2,16,512]{2,1,0:T(8,128)(2,1)S(1)}, u32[]{:S(2)}, u32[]{:S(2)}) collective-permute-start(bf16[2,16,512]{2,1,0:T(8,128)(2,1)S(1)} %get-tuple-element.212), channel_id=1, source_target_pairs={{0,1},{1,2},{2,3},{4,5},{5,6},{6,7},{8,9},{9,10},{10,11},{12,13},{... | collective-permute-start | bytes 98312 | tf_op jit(solution)/shard_map/ppermute | solution.py:116
  7.2 8.2 %collective-permute-start.3 = (bf16[2,16,512]{2,1,0:T(8,128)(2,1)S(1)}, bf16[2,16,512]{2,1,0:T(8,128)(2,1)S(1)}, u32[]{:S(2)}, u32[]{:S(2)}) collective-permute-start(bf16[2,16,512]{2,1,0:T(8,128)(2,1)S(1)} %get-tuple-element.211), channel_id=1, source_target_pairs={{1,0},{2,1},{3,2},{5,4},{6,5},{7,6},{9,8},{10,9},{11,10},{13,12},{... | collective-permute-start | bytes 98312 | tf_op jit(solution)/shard_map/ppermute | solution.py:116
  9.3 6.1 %collective-permute-start.4 = (bf16[80,128]{1,0:T(8,128)(2,1)S(1)}, bf16[80,128]{1,0:T(8,128)(2,1)S(1)}, u32[]{:S(2)}, u32[]{:S(2)}) collective-permute-start(bf16[80,128]{1,0:T(8,128)(2,1)S(1)} %bitcast.38), channel_id=1, source_target_pairs={{1,0},{2,1},{3,2},{5,4},{6,5},{7,6},{9,8},{10,9},{11,10},{13,12},{... | collective-permute-start | bytes 61448 | tf_op jit(solution)/shard_map/ppermute | solution.py:116
  15.4 17.2 %copy-start.8 = (bf16[27,16,512]{2,1,0:T(8,128)(2,1)}, bf16[27,16,512]{2,1,0:T(8,128)(2,1)S(1)}, u32[]{:S(2)}) copy-start(bf16[27,16,512]{2,1,0:T(8,128)(2,1)S(1)} %collective-permute-done.refs_2_) | copy-start | bytes 1327108
  16.6 16.0 %copy-start.9 = (bf16[27,16,512]{2,1,0:T(8,128)(2,1)}, bf16[27,16,512]{2,1,0:T(8,128)(2,1)S(1)}, u32[]{:S(2)}) copy-start(bf16[27,16,512]{2,1,0:T(8,128)(2,1)S(1)} %collective-permute-done.1.refs_4_) | copy-start | bytes 1327108
  16.6 10.9 %collective-permute-start.5 = (bf16[27,16,512]{2,1,0:T(8,128)(2,1)S(1)}, bf16[27,16,512]{2,1,0:T(8,128)(2,1)S(1)}, u32[]{:S(2)}, u32[]{:S(2)}) collective-permute-start(bf16[27,16,512]{2,1,0:T(8,128)(2,1)S(1)} %collective-permute-done.refs_2_), channel_id=1, source_target_pairs={{0,8},{1,9},{2,10},{3,11},{8,16},{9,17},{10,18},{11,19},{16,24},{1... | collective-permute-start | bytes 1327112 | tf_op jit(solution)/shard_map/ppermute | solution.py:1384
  18.2 11.1 %collective-permute-start.6 = (bf16[27,16,512]{2,1,0:T(8,128)(2,1)S(1)}, bf16[27,16,512]{2,1,0:T(8,128)(2,1)S(1)}, u32[]{:S(2)}, u32[]{:S(2)}) collective-permute-start(bf16[27,16,512]{2,1,0:T(8,128)(2,1)S(1)} %collective-permute-done.1.refs_4_), channel_id=1, source_target_pairs={{0,4},{1,5},{2,6},{3,7},{8,0},{9,1},{10,2},{11,3},{16,8},{17,9},{1... | collective-permute-start | bytes 1327112 | tf_op jit(solution)/shard_map/ppermute | solution.py:1386
  27.5 14.1 %copy-start.10 = (bf16[27,16,512]{2,1,0:T(8,128)(2,1)}, bf16[27,16,512]{2,1,0:T(8,128)(2,1)S(1)}, u32[]{:S(2)}) copy-start(bf16[27,16,512]{2,1,0:T(8,128)(2,1)S(1)} %collective-permute-done.5.refs_6_) | copy-start | bytes 1327108
  29.3 14.2 %copy-start.11 = (bf16[27,16,512]{2,1,0:T(8,128)(2,1)}, bf16[27,16,512]{2,1,0:T(8,128)(2,1)S(1)}, u32[]{:S(2)}) copy-start(bf16[27,16,512]{2,1,0:T(8,128)(2,1)S(1)} %collective-permute-done.6.refs_8_) | copy-start | bytes 1327108
  29.3 12.3 %collective-permute-start.7 = (bf16[27,16,512]{2,1,0:T(8,128)(2,1)S(1)}, bf16[27,16,512]{2,1,0:T(8,128)(2,1)S(1)}, u32[]{:S(2)}, u32[]{:S(2)}) collective-permute-start(bf16[27,16,512]{2,1,0:T(8,128)(2,1)S(1)} %collective-permute-done.5.refs_6_), channel_id=1, source_target_pairs={{0,8},{1,9},{2,10},{3,11},{8,16},{9,17},{10,18},{11,19},{16,24},{1... | collective-permute-start | bytes 1327112 | tf_op jit(solution)/shard_map/ppermute | solution.py:1384
  30.9 12.6 %collective-permute-start.8 = (bf16[27,16,512]{2,1,0:T(8,128)(2,1)S(1)}, bf16[27,16,512]{2,1,0:T(8,128)(2,1)S(1)}, u32[]{:S(2)}, u32[]{:S(2)}) collective-permute-start(bf16[27,16,512]{2,1,0:T(8,128)(2,1)S(1)} %collective-permute-done.6.refs_8_), channel_id=1, source_target_pairs={{0,4},{1,5},{2,6},{3,7},{8,0},{9,1},{10,2},{11,3},{16,8},{17,9},{1... | collective-permute-start | bytes 1327112 | tf_op jit(solution)/shard_map/ppermute | solution.py:1386
  31.4 12.4 %collective-permute-start.10 = (bf16[27,16,512]{2,1,0:T(8,128)(2,1)S(1)}, bf16[27,16,512]{2,1,0:T(8,128)(2,1)S(1)}, u32[]{:S(2)}, u32[]{:S(2)}) collective-permute-start(bf16[27,16,512]{2,1,0:T(8,128)(2,1)S(1)} %dynamic-slice_convert_fusion.refs_0_), channel_id=1, source_target_pairs={{0,1},{1,0},{2,3},{3,2},{4,5},{5,4},{6,7},{7,6},{8,9},{9,8},{10,11... | collective-permute-start | bytes 1327112 | tf_op jit(solution)/shard_map/ppermute | solution.py:106
  32.6 11.4 %collective-permute-start.11 = (bf16[27,16,512]{2,1,0:T(8,128)(2,1)S(1)}, bf16[27,16,512]{2,1,0:T(8,128)(2,1)S(1)}, u32[]{:S(2)}, u32[]{:S(2)}) collective-permute-start(bf16[27,16,512]{2,1,0:T(8,128)(2,1)S(1)} %collective-permute-done.refs_2_), channel_id=1, source_target_pairs={{0,1},{1,0},{2,3},{3,2},{4,5},{5,4},{6,7},{7,6},{8,9},{9,8},{10,11... | collective-permute-start | bytes 1327112 | tf_op jit(solution)/shard_map/ppermute | solution.py:106
  32.7 11.7 %collective-permute-start.12 = (bf16[27,16,512]{2,1,0:T(8,128)(2,1)S(1)}, bf16[27,16,512]{2,1,0:T(8,128)(2,1)}, u32[]{:S(2)}, u32[]{:S(2)}) collective-permute-start(bf16[27,16,512]{2,1,0:T(8,128)(2,1)S(1)} %collective-permute-done.1.refs_4_), channel_id=1, source_target_pairs={{0,1},{1,0},{2,3},{3,2},{4,5},{5,4},{6,7},{7,6},{8,9},{9,8},{10,11... | collective-permute-start | bytes 1327112 | tf_op jit(solution)/shard_map/ppermute | solution.py:106
  41.6 4.1 %collective-permute-start.13 = (bf16[27,16,512]{2,1,0:T(8,128)(2,1)S(1)}, bf16[27,16,512]{2,1,0:T(8,128)(2,1)S(1)}, u32[]{:S(2)}, u32[]{:S(2)}) collective-permute-start(bf16[27,16,512]{2,1,0:T(8,128)(2,1)S(1)} %collective-permute-done.5.refs_6_), channel_id=1, source_target_pairs={{0,1},{1,0},{2,3},{3,2},{4,5},{5,4},{6,7},{7,6},{8,9},{9,8},{10,11... | collective-permute-start | bytes 1327112 | tf_op jit(solution)/shard_map/ppermute | solution.py:106
  43.5 2.2 collective-permute-start.14
  43.8 2.1 collective-permute-start.15
  44.0 2.5 %collective-permute-start.16 = (bf16[27,16,512]{2,1,0:T(8,128)(2,1)S(1)}, bf16[27,16,512]{2,1,0:T(8,128)(2,1)S(1)}, u32[]{:S(2)}, u32[]{:S(2)}) collective-permute-start(bf16[27,16,512]{2,1,0:T(8,128)(2,1)S(1)} %collective-permute-done.8.refs_12_), channel_id=1, source_target_pairs={{0,1},{1,0},{2,3},{3,2},{4,5},{5,4},{6,7},{7,6},{8,9},{9,8},{10,11... | collective-permute-start | bytes 1327112 | tf_op jit(solution)/shard_map/ppermute | solution.py:106
  44.3 12.3 %collective-permute-start.9 = (bf16[27,16,512]{2,1,0:T(8,128)(2,1)S(1)}, bf16[27,16,512]{2,1,0:T(8,128)(2,1)S(1)}, u32[]{:S(2)}, u32[]{:S(2)}) collective-permute-start(bf16[27,16,512]{2,1,0:T(8,128)(2,1)S(1)} %collective-permute-done.7.refs_10_), channel_id=1, source_target_pairs={{0,8},{1,9},{2,10},{3,11},{8,16},{9,17},{10,18},{11,19},{16,24},{1... | collective-permute-start | bytes 1327112 | tf_op jit(solution)/shard_map/ppermute | solution.py:1384
  56.6 1.8 collective-permute-start.17
  110.6 10.8 %collective-permute-start.18 = (bf16[40,16,512]{2,1,0:T(8,128)(2,1)}, bf16[40,16,512]{2,1,0:T(8,128)(2,1)S(1)}, u32[]{:S(2)}, u32[]{:S(2)}) collective-permute-start(bf16[40,16,512]{2,1,0:T(8,128)(2,1)} %get-tuple-element.130), channel_id=1, source_target_pairs={{0,1},{1,0},{2,3},{3,2},{4,5},{5,4},{6,7},{7,6},{8,9},{9,8},{10,11... | collective-permute-start | bytes 1966088 | tf_op jit(solution)/shard_map/ppermute | solution.py:106
  110.8 11.0 %copy-start.5 = (bf16[40,16,512]{2,1,0:T(8,128)(2,1)S(1)}, bf16[40,16,512]{2,1,0:T(8,128)(2,1)}, u32[]{:S(2)}) copy-start(bf16[40,16,512]{2,1,0:T(8,128)(2,1)} %get-tuple-element.129) | copy-start | bytes 1966084
  121.3 16.6 %collective-permute-start.19 = (bf16[48,16,512]{2,1,0:T(8,128)(2,1)}, bf16[48,16,512]{2,1,0:T(8,128)(2,1)S(1)}, u32[]{:S(2)}, u32[]{:S(2)}) collective-permute-start(bf16[48,16,512]{2,1,0:T(8,128)(2,1)} %get-tuple-element.141), channel_id=1, source_target_pairs={{0,1},{1,0},{2,3},{3,2},{4,5},{5,4},{6,7},{7,6},{8,9},{9,8},{10,11... | collective-permute-start | bytes 2359304 | tf_op jit(solution)/shard_map/ppermute | solution.py:106
  122.8 15.2 %copy-start.4 = (bf16[48,16,512]{2,1,0:T(8,128)(2,1)S(1)}, bf16[48,16,512]{2,1,0:T(8,128)(2,1)}, u32[]{:S(2)}) copy-start(bf16[48,16,512]{2,1,0:T(8,128)(2,1)} %get-tuple-element.140) | copy-start | bytes 2359300
  122.8 16.6 %collective-permute-start.21 = (bf16[40,8,512]{2,1,0:T(8,128)(2,1)S(1)}, bf16[40,8,512]{2,1,0:T(8,128)(2,1)S(1)}, u32[]{:S(2)}, u32[]{:S(2)}) collective-permute-start(bf16[40,8,512]{2,1,0:T(8,128)(2,1)S(1)} %get-tuple-element.221), channel_id=1, source_target_pairs={{0,2},{1,3},{2,0},{3,1},{4,6},{5,7},{6,4},{7,5},{8,10},{9,11},{10,... | collective-permute-start | bytes 983048 | tf_op jit(solution)/shard_map/ppermute | solution.py:106
  137.9 12.7 %collective-permute-start.20 = (bf16[48,16,512]{2,1,0:T(8,128)(2,1)}, bf16[48,16,512]{2,1,0:T(8,128)(2,1)S(1)}, u32[]{:S(2)}, u32[]{:S(2)}) collective-permute-start(bf16[48,16,512]{2,1,0:T(8,128)(2,1)} %get-tuple-element.148), channel_id=1, source_target_pairs={{0,1},{1,0},{2,3},{3,2},{4,5},{5,4},{6,7},{7,6},{8,9},{9,8},{10,11... | collective-permute-start | bytes 2359304 | tf_op jit(solution)/shard_map/ppermute | solution.py:106
  139.1 11.5 %collective-permute-start.22 = (bf16[48,8,512]{2,1,0:T(8,128)(2,1)S(1)}, bf16[48,8,512]{2,1,0:T(8,128)(2,1)S(1)}, u32[]{:S(2)}, u32[]{:S(2)}) collective-permute-start(bf16[48,8,512]{2,1,0:T(8,128)(2,1)S(1)} %get-tuple-element.219), channel_id=1, source_target_pairs={{0,2},{1,3},{2,0},{3,1},{4,6},{5,7},{6,4},{7,5},{8,10},{9,11},{10,... | collective-permute-start | bytes 1179656 | tf_op jit(solution)/shard_map/ppermute | solution.py:106
  139.4 9.0 %copy-start.23 = (bf16[40,8,512]{2,1,0:T(8,128)(2,1)}, bf16[40,8,512]{2,1,0:T(8,128)(2,1)S(1)}, u32[]{:S(2)}) copy-start(bf16[40,8,512]{2,1,0:T(8,128)(2,1)S(1)} %collective-permute-done.21.refs_3_) | copy-start | bytes 983044
  139.4 11.3 %copy-start.3 = (bf16[48,16,512]{2,1,0:T(8,128)(2,1)S(1)}, bf16[48,16,512]{2,1,0:T(8,128)(2,1)}, u32[]{:S(2)}) copy-start(bf16[48,16,512]{2,1,0:T(8,128)(2,1)} %get-tuple-element.147) | copy-start | bytes 2359300
  151.8 19.9 %collective-permute-start.23 = (bf16[48,8,512]{2,1,0:T(8,128)(2,1)S(1)}, bf16[48,8,512]{2,1,0:T(8,128)(2,1)S(1)}, u32[]{:S(2)}, u32[]{:S(2)}) collective-permute-start(bf16[48,8,512]{2,1,0:T(8,128)(2,1)S(1)} %get-tuple-element.217), channel_id=1, source_target_pairs={{0,2},{1,3},{2,0},{3,1},{4,6},{5,7},{6,4},{7,5},{8,10},{9,11},{10,... | collective-permute-start | bytes 1179656 | tf_op jit(solution)/shard_map/ppermute | solution.py:106
  153.0 24.7 %collective-permute-start.29 = (bf16[2,16,1536]{2,1,0:T(8,128)(2,1)S(1)}, bf16[2,16,1536]{2,1,0:T(8,128)(2,1)S(1)}, u32[]{:S(2)}, u32[]{:S(2)}) collective-permute-start(bf16[2,16,1536]{2,1,0:T(8,128)(2,1)S(1)} %slice.37), channel_id=1, source_target_pairs={{0,1},{1,2},{2,3},{4,5},{5,6},{6,7},{8,9},{9,10},{10,11},{12,13},{... | collective-permute-start | bytes 294920 | tf_op jit(solution)/shard_map/ppermute | solution.py:116
  164.5 7.1 %collective-permute-start.24 = (f32[24,512]{1,0:T(8,128)}, f32[24,512]{1,0:T(8,128)S(1)}, u32[]{:S(2)}, u32[]{:S(2)}) collective-permute-start(f32[24,512]{1,0:T(8,128)} %get-tuple-element.169), channel_id=1, source_target_pairs={{0,1},{1,0},{2,3},{3,2},{4,5},{5,4},{6,7},{7,6},{8,9},{9,8},{10,11... | collective-permute-start | bytes 147464 | tf_op jit(solution)/shard_map/ppermute | solution.py:106
  167.0 4.6 %collective-permute-start.26 = (f32[24,512]{1,0:T(8,128)}, f32[24,512]{1,0:T(8,128)S(1)}, u32[]{:S(2)}, u32[]{:S(2)}) collective-permute-start(f32[24,512]{1,0:T(8,128)} %get-tuple-element.171), channel_id=1, source_target_pairs={{0,3},{1,2},{2,1},{3,0},{4,7},{5,6},{6,5},{7,4},{8,11},{9,10},{10,... | collective-permute-start | bytes 147464 | tf_op jit(solution)/shard_map/ppermute | solution.py:106
  167.0 4.6 %collective-permute-start.25 = (f32[8,512]{1,0:T(8,128)}, f32[8,512]{1,0:T(8,128)S(1)}, u32[]{:S(2)}, u32[]{:S(2)}) collective-permute-start(f32[8,512]{1,0:T(8,128)} %get-tuple-element.170), channel_id=1, source_target_pairs={{0,2},{1,3},{2,0},{3,1},{4,6},{5,7},{6,4},{7,5},{8,10},{9,11},{10,... | collective-permute-start | bytes 49160 | tf_op jit(solution)/shard_map/ppermute | solution.py:106
  175.6 9.7 %collective-permute-start.27 = (bf16[27,8,512]{2,1,0:T(8,128)(2,1)}, bf16[27,8,512]{2,1,0:T(8,128)(2,1)S(1)}, u32[]{:S(2)}, u32[]{:S(2)}) collective-permute-start(bf16[27,8,512]{2,1,0:T(8,128)(2,1)} %get-tuple-element.177), channel_id=1, source_target_pairs={{0,8},{1,9},{2,10},{3,11},{8,16},{9,17},{10,18},{11,19},{16,24},{1... | collective-permute-start | bytes 663560 | tf_op jit(solution)/shard_map/ppermute | solution.py:1488
  177.1 8.3 %copy-start.1 = (bf16[216,8,512]{2,1,0:T(8,128)(2,1)S(1)}, bf16[216,8,512]{2,1,0:T(8,128)(2,1)}, u32[]{:S(2)}) copy-start(bf16[216,8,512]{2,1,0:T(8,128)(2,1)} %get-tuple-element.182) | copy-start | bytes 5308420
  177.1 8.3 %collective-permute-start.28 = (bf16[27,8,512]{2,1,0:T(8,128)(2,1)}, bf16[27,8,512]{2,1,0:T(8,128)(2,1)S(1)}, u32[]{:S(2)}, u32[]{:S(2)}) collective-permute-start(bf16[27,8,512]{2,1,0:T(8,128)(2,1)} %get-tuple-element.178), channel_id=1, source_target_pairs={{0,4},{1,5},{2,6},{3,7},{8,0},{9,1},{10,2},{11,3},{16,8},{17,9},{1... | collective-permute-start | bytes 663560 | tf_op jit(solution)/shard_map/ppermute | solution.py:1490
  185.5 6.9 %collective-permute-start.30 = (bf16[27,8,512]{2,1,0:T(8,128)(2,1)S(1)}, bf16[27,8,512]{2,1,0:T(8,128)(2,1)S(1)}, u32[]{:S(2)}, u32[]{:S(2)}) collective-permute-start(bf16[27,8,512]{2,1,0:T(8,128)(2,1)S(1)} %get-tuple-element.216), channel_id=1, source_target_pairs={{0,8},{1,9},{2,10},{3,11},{8,16},{9,17},{10,18},{11,19},{16,24},{1... | collective-permute-start | bytes 663560 | tf_op jit(solution)/shard_map/ppermute | solution.py:1488
  187.0 6.1 %collective-permute-start.31 = (bf16[27,8,512]{2,1,0:T(8,128)(2,1)S(1)}, bf16[27,8,512]{2,1,0:T(8,128)(2,1)S(1)}, u32[]{:S(2)}, u32[]{:S(2)}) collective-permute-start(bf16[27,8,512]{2,1,0:T(8,128)(2,1)S(1)} %get-tuple-element.215), channel_id=1, source_target_pairs={{0,4},{1,5},{2,6},{3,7},{8,0},{9,1},{10,2},{11,3},{16,8},{17,9},{1... | collective-permute-start | bytes 663560 | tf_op jit(solution)/shard_map/ppermute | solution.py:1490
  193.2 9.1 %collective-permute-start.32 = (bf16[27,8,512]{2,1,0:T(8,128)(2,1)S(1)}, bf16[27,8,512]{2,1,0:T(8,128)(2,1)S(1)}, u32[]{:S(2)}, u32[]{:S(2)}) collective-permute-start(bf16[27,8,512]{2,1,0:T(8,128)(2,1)S(1)} %get-tuple-element.214), channel_id=1, source_target_pairs={{0,8},{1,9},{2,10},{3,11},{8,16},{9,17},{10,18},{11,19},{16,24},{1... | collective-permute-start | bytes 663560 | tf_op jit(solution)/shard_map/ppermute | solution.py:1488
  194.8 7.6 %collective-permute-start.33 = (bf16[27,8,512]{2,1,0:T(8,128)(2,1)S(1)}, bf16[27,8,512]{2,1,0:T(8,128)(2,1)S(1)}, u32[]{:S(2)}, u32[]{:S(2)}) collective-permute-start(bf16[27,8,512]{2,1,0:T(8,128)(2,1)S(1)} %get-tuple-element.213), channel_id=1, source_target_pairs={{0,4},{1,5},{2,6},{3,7},{8,0},{9,1},{10,2},{11,3},{16,8},{17,9},{1... | collective-permute-start | bytes 663560 | tf_op jit(solution)/shard_map/ppermute | solution.py:1490
  202.4 6.4 %collective-permute-start.34 = (bf16[27,8,512]{2,1,0:T(8,128)(2,1)S(1)}, bf16[27,8,512]{2,1,0:T(8,128)(2,1)S(1)}, u32[]{:S(2)}, u32[]{:S(2)}) collective-permute-start(bf16[27,8,512]{2,1,0:T(8,128)(2,1)S(1)} %add_convert_fusion.4), channel_id=1, source_target_pairs={{0,8},{1,9},{2,10},{3,11},{8,16},{9,17},{10,18},{11,19},{16,24},{1... | collective-permute-start | bytes 663560 | tf_op jit(solution)/shard_map/ppermute | solution.py:1488
  208.9 6.0 %collective-permute-start.35 = (bf16[27,8,512]{2,1,0:T(8,128)(2,1)S(1)}, bf16[27,8,512]{2,1,0:T(8,128)(2,1)S(1)}, u32[]{:S(2)}, u32[]{:S(2)}) collective-permute-start(bf16[27,8,512]{2,1,0:T(8,128)(2,1)S(1)} %add_convert_fusion.3.mine_ref), channel_id=1, source_target_pairs={{0,2},{1,3},{2,0},{3,1},{4,6},{5,7},{6,4},{7,5},{8,10},{9,11},{10,... | collective-permute-start | bytes 663560 | tf_op jit(solution)/shard_map/ppermute | solution.py:106
  209.8 5.1 %collective-permute-start.37 = (bf16[27,8,512]{2,1,0:T(8,128)(2,1)S(1)}, bf16[27,8,512]{2,1,0:T(8,128)(2,1)S(1)}, u32[]{:S(2)}, u32[]{:S(2)}) collective-permute-start(bf16[27,8,512]{2,1,0:T(8,128)(2,1)S(1)} %add_convert_fusion.3.mine_ref), channel_id=1, source_target_pairs={{0,1},{1,0},{2,3},{3,2},{4,5},{5,4},{6,7},{7,6},{8,9},{9,8},{10,11... | collective-permute-start | bytes 663560 | tf_op jit(solution)/shard_map/ppermute | solution.py:106
  214.9 5.4 %collective-permute-start.36 = (bf16[27,8,512]{2,1,0:T(8,128)(2,1)S(1)}, bf16[27,8,512]{2,1,0:T(8,128)(2,1)S(1)}, u32[]{:S(2)}, u32[]{:S(2)}) collective-permute-start(bf16[27,8,512]{2,1,0:T(8,128)(2,1)S(1)} %collective-permute-done.35.mine_ref), channel_id=1, source_target_pairs={{0,1},{1,0},{2,3},{3,2},{4,5},{5,4},{6,7},{7,6},{8,9},{9,8},{10,11... | collective-permute-start | bytes 663560 | tf_op jit(solution)/shard_map/ppermute | solution.py:106
  (23 other events, 42.6 us)
